TPU v7x, 32 devices: a whole 2x2x4 slice. The times are simulated.
32 devices in a mesh: dp: 4 (over y, core), gx: 2 (over x), gy: 4 (over z).
Axes of the slice: x: 2, y: 2, z: 4, core: 2. Of those that a mesh axis runs over, the one named last changes fastest.
Arguments:
- inputs: bfloat16 [8, 1024, 2048], P('dp', 'gx', 'gy'), may hold values from -6 to 6
- lengths: int32 [8], P('dp'), may hold values from 384 to 1024, as said below
- attn_gain: bfloat16 [2048], P('gy'), may hold values from 0.5 to 1.5
- ffn_gain: bfloat16 [2048], P('gy'), may hold values from 0.5 to 1.5
- query_key: bfloat16 [2048, 32, 2, 64], P('gy', 'gx'), may hold values from -0.046875 to 0.046875
- value_proj: bfloat16 [2048, 32, 64], P('gy', 'gx'), may hold values from -0.125 to 0.125
- out_proj: bfloat16 [32, 64, 2048], P('gx', None, 'gy'), may hold values from -1.5 to 1.5
- gate_up: bfloat16 [2048, 32, 2, 160], P('gy', 'gx'), may hold values from -0.125 to 0.125
- down_proj: bfloat16 [32, 160, 2048], P('gx', None, 'gy'), may hold values from -0.078125 to 0.078125
- bias_table: bfloat16 [32, 32], P(None, ('gx', 'gy')), may hold values from -5 to 5
- cotangent: bfloat16 [8, 1024, 2048], P('dp', 'gx', 'gy'), may hold values from -6 to 6
Outputs:
- outputs: bfloat16 [8, 1024, 2048], P('dp', 'gx', 'gy')
- input_grad: float32 [8, 1024, 2048], P('dp', 'gx', 'gy')
- attn_gain_grad: float32 [2048], P('gy')
- ffn_gain_grad: float32 [2048], P('gy')
- query_key_grad: float32 [2048, 32, 2, 64], P('gy', 'gx')
- value_grad: float32 [2048, 32, 64], P('gy', 'gx')
- out_proj_grad: float32 [32, 64, 2048], P('gx', None, 'gy')
- gate_up_grad: float32 [2048, 32, 2, 160], P('gy', 'gx')
- down_grad: float32 [32, 160, 2048], P('gx', None, 'gy')
- table_grad: float32 [32, 32], P(None, ('gx', 'gy'))
Inputs may be any that keep to these rules, and one draw needn't show every extreme that they name: lengths[s] counts the live leading slots of sequence s; one sequence has exactly 1024 and another exactly 384.
All inputs are finite; a program needn't handle non-finite values.
Results may differ from a plain program's by a relative error of at most 0.018.
Values may be sent and summed in bfloat16 or wider, within the bound.
No kernel may reach another device: no remote copies, remote signals or barrier semaphores. Data moves between devices by JAX's collectives and lax.ppermute only.
A program may use at most 256 MiB of HBM per device.

v0:
```python
import jax
import jax.numpy as jnp
from jax import lax
from jax.sharding import PartitionSpec as P

D = 2048
QBLK = 512


norm_eps = 1e-06
masked_score = -1e30
bucket_edges = (12, 16, 23, 32, 46, 64, 91)
highest = lax.Precision.HIGHEST


def bucket_index(offset):
    magnitude = jnp.abs(offset)
    far_bucket = 8 + sum(((magnitude >= boundary).astype(jnp.int32) for boundary in bucket_edges))
    near_bucket = jnp.where(magnitude < 8, magnitude, far_bucket)
    return near_bucket + 16 * (offset > 0).astype(jnp.int32)


def spread(local_rows, product):
    gathered = lax.all_gather(local_rows, "gx", axis=0, tiled=True)
    return (gathered, lax.psum_scatter(product(gathered), "gy", scatter_dimension=1, tiled=True))


def collect(local_parts, product):
    gathered = lax.all_gather(local_parts, "gy", axis=1, tiled=True)
    return (gathered, lax.psum_scatter(product(gathered), "gx", scatter_dimension=0, tiled=True))


def feature_sums(values):
    return lax.psum(values, "gy")


def norm_forward(tokens, gain):
    squares = feature_sums(jnp.sum(tokens * tokens, axis=1))
    scale = lax.rsqrt(squares / D + norm_eps)[:, None]
    return (scale, (tokens * scale * gain.astype(jnp.float32)).astype(jnp.bfloat16))


def norm_backward(tokens, scale, gain, upstream):
    gain_wide = gain.astype(jnp.float32)
    inner = feature_sums(jnp.sum(tokens * gain_wide * upstream, axis=1))[:, None]
    grad_tokens = scale * gain_wide * upstream - tokens * (scale * scale * scale) * inner / D
    return (grad_tokens, jnp.sum(tokens * scale * upstream, axis=0))


def window_bias(bias_table, first_row, key_total):
    head_count = bias_table.shape[1]
    span_total = QBLK + key_total + 1
    offsets = jnp.arange(span_total, dtype=jnp.int32) - QBLK - first_row
    selector = (
        bucket_index(offsets)[:, None] == jnp.arange(bias_table.shape[0], dtype=jnp.int32)[None, :]
    ).astype(jnp.float32)
    window = jnp.dot(selector, bias_table.astype(jnp.float32), precision=highest)
    sheared = jnp.broadcast_to(jnp.transpose(window)[:, None, :], (head_count, QBLK, span_total))
    flattened = sheared.reshape(head_count, QBLK * span_total)[:, : QBLK * (QBLK + key_total)]
    return (flattened.reshape(head_count, QBLK, QBLK + key_total)[:, :, QBLK:], selector)


def window_grad(grad_scores, selector):
    head_count = grad_scores.shape[0]
    key_total = grad_scores.shape[2]
    padded = jnp.pad(grad_scores, ((0, 0), (0, 0), (QBLK, 0))).reshape(
        head_count, QBLK * (QBLK + key_total)
    )
    padded = jnp.pad(padded, ((0, 0), (0, QBLK))).reshape(head_count, QBLK, QBLK + key_total + 1)
    column_sums = jnp.sum(padded, axis=1)
    return jnp.transpose(jnp.dot(column_sums, selector, precision=highest))


def block_scores(block_queries, key_vecs, position_bias, key_live):
    scores = (
        jnp.einsum("qhs,khs->hqk", block_queries, key_vecs, preferred_element_type=jnp.float32)
        + position_bias
    )
    return jnp.where(key_live, scores, masked_score)


def attend_forward(projected, length, bias_table):
    key_total = projected.shape[0]
    queries = projected[:, :, 0]
    key_vecs = projected[:, :, 1]
    value_vecs = projected[:, :, 2]
    key_live = (jnp.arange(key_total, dtype=jnp.int32) < length)[None, None, :]

    def one_block(first_row):
        position_bias, selector = window_bias(bias_table, first_row, key_total)
        block_queries = lax.dynamic_slice_in_dim(queries, first_row, QBLK, 0)
        scores = block_scores(block_queries, key_vecs, position_bias, key_live)
        largest = jnp.max(scores, axis=2, keepdims=True)
        raised = jnp.exp(scores - largest)
        totals = jnp.sum(raised, axis=2, keepdims=True)
        weights = (raised / totals).astype(jnp.bfloat16)
        block_out = jnp.einsum(
            "hqk,khs->qhs", weights, value_vecs, preferred_element_type=jnp.float32
        )
        return (block_out.astype(jnp.bfloat16), (largest + jnp.log(totals))[:, :, 0])

    starts = jnp.arange(0, key_total, QBLK, dtype=jnp.int32)
    block_outs, log_totals = lax.map(one_block, starts)
    return (block_outs.reshape(key_total, queries.shape[1], queries.shape[2]), log_totals)


def attend_backward(projected, length, bias_table, log_totals, grad_out):
    key_total = projected.shape[0]
    queries = projected[:, :, 0]
    key_vecs = projected[:, :, 1]
    value_vecs = projected[:, :, 2]
    key_live = (jnp.arange(key_total, dtype=jnp.int32) < length)[None, None, :]

    def one_block(sums_carry, block_item):
        key_grad, value_grad, table_grad = sums_carry
        first_row, block_lse = block_item
        position_bias, selector = window_bias(bias_table, first_row, key_total)
        block_queries = lax.dynamic_slice_in_dim(queries, first_row, QBLK, 0)
        scores = block_scores(block_queries, key_vecs, position_bias, key_live)
        weights = jnp.exp(scores - block_lse[:, :, None])
        block_grad = lax.dynamic_slice_in_dim(grad_out, first_row, QBLK, 0)
        grad_weights = jnp.einsum(
            "qhs,khs->hqk", block_grad, value_vecs, preferred_element_type=jnp.float32
        )
        inner = jnp.sum(weights * grad_weights, axis=2, keepdims=True)
        grad_scores = (weights * (grad_weights - inner)).astype(jnp.bfloat16)
        query_grad = jnp.einsum(
            "hqk,khs->qhs", grad_scores, key_vecs, preferred_element_type=jnp.float32
        )
        key_grad = key_grad + jnp.einsum(
            "hqk,qhs->khs", grad_scores, block_queries, preferred_element_type=jnp.float32
        )
        value_grad = value_grad + jnp.einsum(
            "hqk,qhs->khs",
            weights.astype(jnp.bfloat16),
            block_grad,
            preferred_element_type=jnp.float32,
        )
        table_grad = table_grad + window_grad(grad_scores.astype(jnp.float32), selector)
        return ((key_grad, value_grad, table_grad), query_grad)

    empty_grad = jnp.zeros(key_vecs.shape, jnp.float32)
    starts = jnp.arange(0, key_total, QBLK, dtype=jnp.int32)
    sums_done, query_blocks = lax.scan(
        one_block,
        (empty_grad, empty_grad, jnp.zeros(bias_table.shape, jnp.float32)),
        (starts, log_totals),
    )
    query_grad = query_blocks.reshape(key_vecs.shape)
    grad_projected = jnp.stack([query_grad, sums_done[0], sums_done[1]], axis=2).astype(
        jnp.bfloat16
    )
    return (grad_projected, sums_done[2])


def body(
    inputs,
    lengths,
    attn_gain,
    ffn_gain,
    query_key,
    value_proj,
    out_proj,
    gate_up,
    down_proj,
    bias_table,
    cotangent,
):
    proj_block = jnp.concatenate([query_key, value_proj[:, :, None, :]], axis=2)
    local_rows = inputs.shape[1]
    slot_ids = lax.axis_index("gx") * local_rows + jnp.arange(local_rows, dtype=jnp.int32)
    start_totals = (
        jnp.zeros(proj_block.shape, jnp.float32),
        jnp.zeros(out_proj.shape, jnp.float32),
        jnp.zeros(gate_up.shape, jnp.float32),
        jnp.zeros(down_proj.shape, jnp.float32),
        jnp.zeros(bias_table.shape, jnp.float32),
    )
    start_gains = (jnp.zeros(attn_gain.shape, jnp.float32), jnp.zeros(ffn_gain.shape, jnp.float32))

    def micro_step(carry, micro_item):
        totals, gain_totals = carry
        token_block, cot_block, length = micro_item
        tokens = token_block.astype(jnp.float32)
        live_rows = (slot_ids < length).astype(jnp.float32)[:, None]
        scale_one, normed = norm_forward(tokens, attn_gain)
        normed_rows, projected = spread(
            normed,
            lambda rows_all: jnp.einsum(
                "td,dhcs->thcs", rows_all, proj_block, preferred_element_type=jnp.float32
            ),
        )
        projected = projected.astype(jnp.bfloat16)
        attended, log_totals = attend_forward(projected, length, bias_table)
        heads_all, attn_branch = collect(
            attended,
            lambda part_rows: jnp.einsum(
                "ths,hsd->td", part_rows, out_proj, preferred_element_type=jnp.float32
            ),
        )
        hidden = tokens + attn_branch
        scale_two, normed_two = norm_forward(hidden, ffn_gain)
        ffn_rows, gate_and_up = spread(
            normed_two,
            lambda rows_all: jnp.einsum(
                "td,dgcu->tgcu", rows_all, gate_up, preferred_element_type=jnp.float32
            ),
        )
        activated_wide, gelu_pullback = jax.vjp(
            lambda gate_part, up_part: jax.nn.gelu(gate_part, approximate=True) * up_part,
            gate_and_up[:, :, 0],
            gate_and_up[:, :, 1],
        )
        activated = activated_wide.astype(jnp.bfloat16)
        act_all, ffn_branch = collect(
            activated,
            lambda part_rows: jnp.einsum(
                "tgu,gud->td", part_rows, down_proj, preferred_element_type=jnp.float32
            ),
        )
        layer_out = (live_rows * (hidden + ffn_branch)).astype(jnp.bfloat16)
        upstream = live_rows * cot_block.astype(jnp.float32)
        grad_rows, grad_act = spread(
            upstream.astype(jnp.bfloat16),
            lambda rows_all: jnp.einsum(
                "td,gud->tgu", rows_all, down_proj, preferred_element_type=jnp.float32
            ),
        )
        down_term = jnp.einsum(
            "tgu,td->gud", act_all, grad_rows, preferred_element_type=jnp.float32
        )
        grad_gate, grad_up = gelu_pullback(grad_act)
        grad_gate_up = jnp.stack([grad_gate, grad_up], axis=2).astype(jnp.bfloat16)
        gate_up_all, grad_normed_two = collect(
            grad_gate_up,
            lambda part_rows: jnp.einsum(
                "tgcu,dgcu->td", part_rows, gate_up, preferred_element_type=jnp.float32
            ),
        )
        gate_up_term = jnp.einsum(
            "td,tgcu->dgcu", ffn_rows, gate_up_all, preferred_element_type=jnp.float32
        )
        grad_hidden_norm, ffn_gain_term = norm_backward(
            hidden, scale_two, ffn_gain, grad_normed_two
        )
        grad_hidden = upstream + grad_hidden_norm
        branch_rows, grad_attended = spread(
            grad_hidden.astype(jnp.bfloat16),
            lambda rows_all: jnp.einsum(
                "td,hsd->ths", rows_all, out_proj, preferred_element_type=jnp.float32
            ),
        )
        out_term = jnp.einsum(
            "ths,td->hsd", heads_all, branch_rows, preferred_element_type=jnp.float32
        )
        grad_projected, table_term = attend_backward(
            projected, length, bias_table, log_totals, grad_attended.astype(jnp.bfloat16)
        )
        proj_all, grad_normed = collect(
            grad_projected,
            lambda part_rows: jnp.einsum(
                "thcs,dhcs->td", part_rows, proj_block, preferred_element_type=jnp.float32
            ),
        )
        proj_term = jnp.einsum(
            "td,thcs->dhcs", normed_rows, proj_all, preferred_element_type=jnp.float32
        )
        grad_tokens, attn_gain_term = norm_backward(tokens, scale_one, attn_gain, grad_normed)
        layer_grad = grad_hidden + grad_tokens
        gain_totals = (gain_totals[0] + attn_gain_term, gain_totals[1] + ffn_gain_term)
        terms = (proj_term, out_term, gate_up_term, down_term, table_term)
        totals = tuple((running + addend for running, addend in zip(totals, terms)))
        return ((totals, gain_totals), (layer_out, layer_grad))

    final_carry, stacked = lax.scan(
        micro_step, (start_totals, start_gains), (inputs, cotangent, lengths)
    )
    totals, gain_totals = final_carry
    totals = (
        lax.psum(totals[0].astype(jnp.bfloat16), "dp").astype(jnp.float32),
        lax.psum(totals[1].astype(jnp.bfloat16), "dp").astype(jnp.float32),
        lax.psum(totals[2].astype(jnp.bfloat16), "dp").astype(jnp.float32),
        lax.psum(totals[3].astype(jnp.bfloat16), "dp").astype(jnp.float32),
        lax.psum(totals[4].astype(jnp.bfloat16), "dp").astype(jnp.float32),
    )
    gain_grads = lax.psum((gain_totals[0], gain_totals[1]), ("dp", "gx"))
    return (
        stacked[0],
        stacked[1],
        gain_grads[0],
        gain_grads[1],
        totals[0][:, :, :2],
        totals[0][:, :, 2],
        totals[1],
        totals[2],
        totals[3],
        totals[4],
    )


def solution(mesh):
    return jax.shard_map(
        body,
        mesh=mesh,
        in_specs=(
            P("dp", "gx", "gy"),
            P("dp"),
            P("gy"),
            P("gy"),
            P("gy", "gx", None, None),
            P("gy", "gx", None),
            P("gx", None, "gy"),
            P("gy", "gx", None, None),
            P("gx", None, "gy"),
            P(None, ("gx", "gy")),
            P("dp", "gx", "gy"),
        ),
        out_specs=(
            P("dp", "gx", "gy"),
            P("dp", "gx", "gy"),
            P("gy"),
            P("gy"),
            P("gy", "gx", None, None),
            P("gy", "gx", None),
            P("gx", None, "gy"),
            P("gy", "gx", None, None),
            P("gx", None, "gy"),
            P(None, ("gx", "gy")),
        ),
        check_vma=False,
    )
```

profile of v0, /device:TPU:0, one launch (start us, length us, event | category | flops | bytes accessed | tf_op | source)
XLA Modules:
  0.0 5007.0 jit_solution(14606844352781935068)
XLA Ops:
  17.0 4735.7 %while.99 = (s32[]{:T(128)}, f32[512,16,3,64]{0,3,2,1:T(8,128)}, f32[16,64,512]{2,1,0:T(8,128)}, f32[512,16,2,160]{0,3,2,1:T(8,128)}, f32[16,160,512]{2,1,0:T(8,...) while((s32[]{:T(128)}, f32[512,16,3,64]{0,3,2,1:T(8,128)}, ...), condition=%wide.region_27.28_spmd.clone, body=%wide.region_0.27_spmd.clone.sunk | while | flops 39021813760 | bytes 1298249216 | solution.py:275
  61.1 211.4 %reduce-scatter.11.cloned.1.call-done = f32[1024,4,3,64]{0,3,2,1:T(8,128)} async-done(((f32[1024,16,3,64]{0,3,2,1:T(8,128)}), f32[1024,4,3,64]{0,3,2,1:T(8,128)}) %reduce-scatter.11.cloned.1.call-update) | async-done | bytes 3145744 | tf_op jit(solution)/shard_map/while/body/eval_jaxpr/reduce_scatter | solution.py:25
  274.8 169.2 %while.100 = (s32[]{:T(128)}, bf16[2,512,4,64]{1,3,2,0:T(8,128)(2,1)}, f32[2,4,512]{2,1,0:T(4,128)S(1)}, s32[2]{0:T(128)S(1)}, bf16[1024,4,64]{0,2,1:T(8,128)(2,...) while((s32[]{:T(128)}, ...), condition=%wide.region_7.7_spmd.clone, body=%wide.region_4.6_spmd.clone.sunk | while | flops 554265408 | bytes 152738320 | solution.py:103
  445.9 47.1 all-gather.11.cloned.1.call-done
  592.5 162.7 %reduce-scatter.15.cloned.1.call-done = f32[1024,4,160]{0,2,1:T(8,128)} async-done(((f32[1024,16,160]{0,2,1:T(8,128)}), f32[1024,4,160]{0,2,1:T(8,128)}) %reduce-scatter.15.cloned.1.call-update) | async-done | bytes 2621456 | tf_op jit(solution)/shard_map/while/body/eval_jaxpr/reduce_scatter | solution.py:25
  755.2 701.4 %all-reduce.12.cloned.1.call-done = f32[1024,16,2,160]{0,3,1,2:T(8,128)} async-done(((f32[1024,16,2,160]{0,3,1,2:T(8,128)}), f32[1024,16,2,160]{0,3,1,2:T(8,128)}) %all-reduce.12.cloned.1.call-update) | async-done | bytes 20971536 | tf_op jit(solution)/shard_map/while
  1463.7 183.0 %all-gather.17.cloned.1.call-done = bf16[1024,16,2,160]{0,3,1,2:T(8,128)(2,1)} async-done(((bf16[1024,4,2,160]{0,3,1,2:T(8,128)(2,1)}), bf16[1024,16,2,160]{0,3,1,2:T(8,128)(2,1)}) %all-gather.17.cloned.1.call-update) | async-done | bytes 10485776 | tf_op jit(solution)/shard_map/while/body/eval_jaxpr/all_gather | solution.py:29
  1657.5 30.1 reduce-scatter.17.cloned.1.call-done
  1728.0 94.7 %all-gather.23.cloned.1.call-done = bf16[1024,16,160]{0,2,1:T(8,128)(2,1)} async-done(((bf16[1024,4,160]{0,2,1:T(8,128)(2,1)}), bf16[1024,16,160]{0,2,1:T(8,128)(2,1)}) %all-gather.23.cloned.1.call-update) | async-done | bytes 5242896 | tf_op jit(solution)/shard_map/while/body/eval_jaxpr/all_gather | solution.py:29
  1830.3 70.5 %reduce-scatter.19.cloned.1.call-done = f32[1024,4,64]{0,2,1:T(8,128)} async-done(((f32[1024,16,64]{0,2,1:T(8,128)}), f32[1024,4,64]{0,2,1:T(8,128)}) %reduce-scatter.19.cloned.1.call-update) | async-done | bytes 1048592 | tf_op jit(solution)/shard_map/while/body/eval_jaxpr/reduce_scatter | solution.py:25
  1902.1 301.1 %while.101 = (s32[]{:T(128)}, f32[1024,4,64]{0,2,1:T(8,128)}, f32[1024,4,64]{0,2,1:T(8,128)S(1)}, f32[32,4]{0,1:T(4,128)S(1)}, bf16[2,512,4,64]{1,3,2,0:T(8,128)...) while((s32[]{:T(128)}, f32[1024,4,64]{0,2,1:T(8,128)}, ...), condition=%wide.region_20.20_spmd.clone, body=%wide.region_17.19_spmd.clone.sunk | while | flops 1371286016 | bytes 351524864 | solution.py:144
  2228.3 95.7 %all-gather.21.cloned.1.call-done = bf16[1024,16,3,64]{0,3,2,1:T(8,128)(2,1)} async-done(((bf16[1024,4,3,64]{0,3,2,1:T(8,128)(2,1)}), bf16[1024,16,3,64]{0,3,2,1:T(8,128)(2,1)}) %all-gather.21.cloned.1.call-update) | async-done | bytes 6291472 | tf_op jit(solution)/shard_map/while/body/eval_jaxpr/all_gather | solution.py:29
  2422.2 211.4 %reduce-scatter.11.cloned.1.call-done = f32[1024,4,3,64]{0,3,2,1:T(8,128)} async-done(((f32[1024,16,3,64]{0,3,2,1:T(8,128)}), f32[1024,4,3,64]{0,3,2,1:T(8,128)}) %reduce-scatter.11.cloned.1.call-update) | async-done | bytes 3145744 | tf_op jit(solution)/shard_map/while/body/eval_jaxpr/reduce_scatter | solution.py:25
  2635.8 169.0 %while.100 = (s32[]{:T(128)}, bf16[2,512,4,64]{1,3,2,0:T(8,128)(2,1)}, f32[2,4,512]{2,1,0:T(4,128)S(1)}, s32[2]{0:T(128)S(1)}, bf16[1024,4,64]{0,2,1:T(8,128)(2,...) while((s32[]{:T(128)}, ...), condition=%wide.region_7.7_spmd.clone, body=%wide.region_4.6_spmd.clone.sunk | while | flops 554265408 | bytes 152738320 | solution.py:103
  2806.9 47.1 all-gather.11.cloned.1.call-done
  2953.8 162.7 %reduce-scatter.15.cloned.1.call-done = f32[1024,4,160]{0,2,1:T(8,128)} async-done(((f32[1024,16,160]{0,2,1:T(8,128)}), f32[1024,4,160]{0,2,1:T(8,128)}) %reduce-scatter.15.cloned.1.call-update) | async-done | bytes 2621456 | tf_op jit(solution)/shard_map/while/body/eval_jaxpr/reduce_scatter | solution.py:25
  3116.5 701.3 %all-reduce.12.cloned.1.call-done = f32[1024,16,2,160]{0,3,1,2:T(8,128)} async-done(((f32[1024,16,2,160]{0,3,1,2:T(8,128)}), f32[1024,16,2,160]{0,3,1,2:T(8,128)}) %all-reduce.12.cloned.1.call-update) | async-done | bytes 20971536 | tf_op jit(solution)/shard_map/while
  3824.8 183.0 %all-gather.17.cloned.1.call-done = bf16[1024,16,2,160]{0,3,1,2:T(8,128)(2,1)} async-done(((bf16[1024,4,2,160]{0,3,1,2:T(8,128)(2,1)}), bf16[1024,16,2,160]{0,3,1,2:T(8,128)(2,1)}) %all-gather.17.cloned.1.call-update) | async-done | bytes 10485776 | tf_op jit(solution)/shard_map/while/body/eval_jaxpr/all_gather | solution.py:29
  4018.6 30.1 reduce-scatter.17.cloned.1.call-done
  4089.1 94.8 %all-gather.23.cloned.1.call-done = bf16[1024,16,160]{0,2,1:T(8,128)(2,1)} async-done(((bf16[1024,4,160]{0,2,1:T(8,128)(2,1)}), bf16[1024,16,160]{0,2,1:T(8,128)(2,1)}) %all-gather.23.cloned.1.call-update) | async-done | bytes 5242896 | tf_op jit(solution)/shard_map/while/body/eval_jaxpr/all_gather | solution.py:29
  4191.5 70.5 %reduce-scatter.19.cloned.1.call-done = f32[1024,4,64]{0,2,1:T(8,128)} async-done(((f32[1024,16,64]{0,2,1:T(8,128)}), f32[1024,4,64]{0,2,1:T(8,128)}) %reduce-scatter.19.cloned.1.call-update) | async-done | bytes 1048592 | tf_op jit(solution)/shard_map/while/body/eval_jaxpr/reduce_scatter | solution.py:25
  4263.3 301.1 %while.101 = (s32[]{:T(128)}, f32[1024,4,64]{0,2,1:T(8,128)}, f32[1024,4,64]{0,2,1:T(8,128)S(1)}, f32[32,4]{0,1:T(4,128)S(1)}, bf16[2,512,4,64]{1,3,2,0:T(8,128)...) while((s32[]{:T(128)}, f32[1024,4,64]{0,2,1:T(8,128)}, ...), condition=%wide.region_20.20_spmd.clone, body=%wide.region_17.19_spmd.clone.sunk | while | flops 1371286016 | bytes 351524864 | solution.py:144
  4590.2 95.1 %all-gather.21.cloned.1.call-done = bf16[1024,16,3,64]{0,3,2,1:T(8,128)(2,1)} async-done(((bf16[1024,4,3,64]{0,3,2,1:T(8,128)(2,1)}), bf16[1024,16,3,64]{0,3,2,1:T(8,128)(2,1)}) %all-gather.21.cloned.1.call-update) | async-done | bytes 6291472 | tf_op jit(solution)/shard_map/while/body/eval_jaxpr/all_gather | solution.py:29
  4790.2 190.7 %all-reduce.10.cloned.1.call-done = (bf16[512,16,3,64]{0,3,1,2:T(8,128)(2,1)}, bf16[16,64,512]{2,1,0:T(8,128)(2,1)}, bf16[512,16,2,160]{0,3,2,1:T(8,128)(2,1)}, bf16[16,160,512]{2,1,0:T(8,128)(2,1)}) async-done(((bf16[512,16,3,64]{0,3,1,2:T(8,128)(2,1)}, bf16[16,64,512]{2,1,0:T(8,128)(2,1)}, bf16[512,16,2,160]{0,3,2,1:T(8,128)(2,1)}, bf16[16,160,512]{2,1,0:T(8,128)(2,1)}), ...) | async-done | bytes 12058640 | tf_op jit(solution)/shard_map/psum | solution.py:280
  (650 shorter events, 1543.2 us)
Async XLA Ops:
  33.2 239.4 %reduce-scatter.11.cloned.1.call-start = ((), (), s32[]{:S(2)}) async-start(), calls=%async_computation.9 | async-start | bytes 15728640 | tf_op jit(solution)/shard_map/while/body/eval_jaxpr/reduce_scatter | solution.py:25
  60.5 432.5 %all-gather.11.cloned.1.call-start = ((), (), s32[]{:S(2)}) async-start(), calls=%async_computation.10 | async-start | bytes 2621440 | tf_op jit(solution)/shard_map/while/body/eval_jaxpr/all_gather | solution.py:29
  542.2 213.0 %reduce-scatter.15.cloned.1.call-start = ((), (), s32[]{:S(2)}) async-start(), calls=%async_computation.15 | async-start | bytes 13107200 | tf_op jit(solution)/shard_map/while/body/eval_jaxpr/reduce_scatter | solution.py:25
  560.3 896.3 %all-reduce.12.cloned.1.call-start = ((), (), s32[]{:S(2)}) async-start(), calls=%async_computation.13 | async-start | bytes 41943040 | tf_op jit(solution)/shard_map/while
  590.7 1055.9 %all-gather.17.cloned.1.call-start = ((), (), s32[]{:S(2)}) async-start(), calls=%async_computation.16 | async-start | bytes 13107200 | tf_op jit(solution)/shard_map/while/body/eval_jaxpr/all_gather | solution.py:29
  1463.6 224.0 %reduce-scatter.17.cloned.1.call-start = ((), (), s32[]{:S(2)}) async-start(), calls=%async_computation.17 | async-start | bytes 3145728 | tf_op jit(solution)/shard_map/while/body/eval_jaxpr/reduce_scatter | solution.py:30
  1704.3 118.3 %all-gather.23.cloned.1.call-start = ((), (), s32[]{:S(2)}) async-start(), calls=%async_computation.21 | async-start | bytes 6553600 | tf_op jit(solution)/shard_map/while/body/eval_jaxpr/all_gather | solution.py:29
  1704.9 195.9 %reduce-scatter.19.cloned.1.call-start = ((), (), s32[]{:S(2)}) async-start(), calls=%async_computation.19 | async-start | bytes 5242880 | tf_op jit(solution)/shard_map/while/body/eval_jaxpr/reduce_scatter | solution.py:25
  1727.9 487.4 %reduce-scatter.23.cloned.1.call-start = ((), (), s32[]{:S(2)}) async-start(), calls=%async_computation.23 | async-start | bytes 3145728 | tf_op jit(solution)/shard_map/while/body/eval_jaxpr/reduce_scatter | solution.py:30
  1830.2 493.8 %all-gather.21.cloned.1.call-start = ((), (), s32[]{:S(2)}) async-start(), calls=%async_computation.20 | async-start | bytes 7864320 | tf_op jit(solution)/shard_map/while/body/eval_jaxpr/all_gather | solution.py:29
  2208.0 160.5 %reduce-scatter.21.cloned.1.call-start = ((), (), s32[]{:S(2)}) async-start(), calls=%async_computation.22 | async-start | bytes 3145728 | tf_op jit(solution)/shard_map/while/body/eval_jaxpr/reduce_scatter | solution.py:30
  2394.2 239.4 %reduce-scatter.11.cloned.1.call-start = ((), (), s32[]{:S(2)}) async-start(), calls=%async_computation.9 | async-start | bytes 15728640 | tf_op jit(solution)/shard_map/while/body/eval_jaxpr/reduce_scatter | solution.py:25
  2421.5 432.4 %all-gather.11.cloned.1.call-start = ((), (), s32[]{:S(2)}) async-start(), calls=%async_computation.10 | async-start | bytes 2621440 | tf_op jit(solution)/shard_map/while/body/eval_jaxpr/all_gather | solution.py:29
  2806.8 82.1 %reduce-scatter.13.cloned.1.call-start = ((), (), s32[]{:S(2)}) async-start(), calls=%async_computation.11 | async-start | bytes 3145728 | tf_op jit(solution)/shard_map/while/body/eval_jaxpr/reduce_scatter | solution.py:30
  2903.1 213.4 %reduce-scatter.15.cloned.1.call-start = ((), (), s32[]{:S(2)}) async-start(), calls=%async_computation.15 | async-start | bytes 13107200 | tf_op jit(solution)/shard_map/while/body/eval_jaxpr/reduce_scatter | solution.py:25
  2921.4 896.3 %all-reduce.12.cloned.1.call-start = ((), (), s32[]{:S(2)}) async-start(), calls=%async_computation.13 | async-start | bytes 41943040 | tf_op jit(solution)/shard_map/while
  2951.9 1055.8 %all-gather.17.cloned.1.call-start = ((), (), s32[]{:S(2)}) async-start(), calls=%async_computation.16 | async-start | bytes 13107200 | tf_op jit(solution)/shard_map/while/body/eval_jaxpr/all_gather | solution.py:29
  3824.7 224.0 %reduce-scatter.17.cloned.1.call-start = ((), (), s32[]{:S(2)}) async-start(), calls=%async_computation.17 | async-start | bytes 3145728 | tf_op jit(solution)/shard_map/while/body/eval_jaxpr/reduce_scatter | solution.py:30
  4065.4 118.5 %all-gather.23.cloned.1.call-start = ((), (), s32[]{:S(2)}) async-start(), calls=%async_computation.21 | async-start | bytes 6553600 | tf_op jit(solution)/shard_map/while/body/eval_jaxpr/all_gather | solution.py:29
  4066.2 195.9 %reduce-scatter.19.cloned.1.call-start = ((), (), s32[]{:S(2)}) async-start(), calls=%async_computation.19 | async-start | bytes 5242880 | tf_op jit(solution)/shard_map/while/body/eval_jaxpr/reduce_scatter | solution.py:25
  4089.0 488.3 %reduce-scatter.23.cloned.1.call-start = ((), (), s32[]{:S(2)}) async-start(), calls=%async_computation.23 | async-start | bytes 3145728 | tf_op jit(solution)/shard_map/while/body/eval_jaxpr/reduce_scatter | solution.py:30
  4191.4 493.8 %all-gather.21.cloned.1.call-start = ((), (), s32[]{:S(2)}) async-start(), calls=%async_computation.20 | async-start | bytes 7864320 | tf_op jit(solution)/shard_map/while/body/eval_jaxpr/all_gather | solution.py:29
  4569.2 166.4 %reduce-scatter.21.cloned.1.call-start = ((), (), s32[]{:S(2)}) async-start(), calls=%async_computation.22 | async-start | bytes 3145728 | tf_op jit(solution)/shard_map/while/body/eval_jaxpr/reduce_scatter | solution.py:30
  4752.6 228.3 %all-reduce.10.cloned.1.call-start = ((), (), s32[]{:S(2)}) async-start(), calls=%async_computation.7 | async-start | bytes 24117248 | tf_op jit(solution)/shard_map/psum | solution.py:280
  (147 other events, 7738.3 us)
Sparse Core Ops, SparseCore 0:
  60.6 211.8 reduce-scatter.10
  446.0 46.9 all-gather.10
  497.4 30.5 reduce-scatter.12
  577.2 177.9 reduce-scatter.14
  757.9 698.6 all-reduce.11
  1463.7 182.8 all-gather.16
  1657.6 29.9 reduce-scatter.16
  1724.5 98.0 all-gather.22
  1825.6 75.1 reduce-scatter.18
  1903.5 32.3 reduce-scatter.22
  2208.1 115.8 all-gather.20
  2331.7 30.0 reduce-scatter.20
  2421.7 211.8 reduce-scatter.10
  2806.9 46.9 all-gather.10
  2858.3 30.5 reduce-scatter.12
  2938.4 178.0 reduce-scatter.14
  3119.0 698.6 all-reduce.11
  3824.8 182.8 all-gather.16
  4018.7 29.9 reduce-scatter.16
  4085.8 98.0 all-gather.22
  4186.9 75.1 reduce-scatter.18
  4264.7 32.3 reduce-scatter.22
  4569.4 115.8 all-gather.20
  4693.0 30.0 reduce-scatter.20
  (8 shorter events, 160.9 us)
Sparse Core Ops, SparseCore 1:
  4768.4 212.4 all-reduce.9
where the time goes:
time: 5010 us
  waiting for transfers between devices  3550 us (71%)
  local copies, waits for them, and re-layouts  789 us (16%)
  matrix products  277 us (6%)
  other arithmetic  203 us (4%)
  blocking collectives  108 us (2%)
  loops' own time  65.1 us (1%)
    while x34, waiting for transfers between devices  1400 us
    reduce_scatter x6, waiting for transfers between devices, spread(): lax.psum_scatter(product(gathered), 'gy', scatter_dimension=1, tiled=True)  889 us
    all_gather x8, waiting for transfers between devices, collect(): gathered = lax.all_gather(local_parts, 'gy', axis=1, tiled=True)  840 us
    while x278, local copies, waits for them, and re-layouts  384 us
    psum x1, waiting for transfers between devices, body(): lax.psum(totals[0].astype(jnp.bfloat16), 'dp').astype(jnp.float32)  191 us
    reshape x8, local copies, waits for them, and re-layouts, window_bias(): sheared.reshape(head_count, QBLK * span_total)  120 us
    reduce_scatter x8, waiting for transfers between devices, collect(): lax.psum_scatter(product(gathered), 'gx', scatter_dimension=0, tiled=True)  116 us
    all_gather x8, waiting for transfers between devices, spread(): gathered = lax.all_gather(local_rows, 'gx', axis=0, tiled=True)  107 us
  transfers between devices with their start and end apart: 33, of which 29 were waited for; matrix products, arithmetic and copies ran while one was open for 16% of the time, Pallas kernels for 0%

commit v1 on v0

v1 whole, which is shorter than its diff:
```python
import functools
import math

import jax
import jax.numpy as jnp
from jax import lax
from jax.experimental import pallas as pl
from jax.experimental.pallas import tpu as pltpu
from jax.sharding import Mesh
from jax.sharding import PartitionSpec as P

norm_eps = 1e-06
masked_score = -1e30
bucket_edges = (12, 16, 23, 32, 46, 64, 91)
BF = jnp.bfloat16
F32 = jnp.float32
LB = 128
VMEM = 60 * 1024 * 1024
swap = [(0, 1), (1, 0)]
gelu_a = math.sqrt(2.0 / math.pi)
gelu_b = 0.044715


def bucket_index(offset):
    magnitude = jnp.abs(offset)
    far_bucket = 8 + sum(((magnitude >= boundary).astype(jnp.int32) for boundary in bucket_edges))
    near_bucket = jnp.where(magnitude < 8, magnitude, far_bucket)
    return near_bucket + 16 * (offset > 0).astype(jnp.int32)


def cost(flops, moved):
    return pl.CostEstimate(flops=int(flops), bytes_accessed=int(moved), transcendentals=0)


def params(steps):
    return pltpu.CompilerParams(
        dimension_semantics=("arbitrary",) * steps, vmem_limit_bytes=VMEM
    )


def dot_nt(a, b):
    return lax.dot_general(a, b, (((1,), (1,)), ((), ())), preferred_element_type=F32)


def dot_nn(a, b):
    return lax.dot_general(a, b, (((1,), (0,)), ((), ())), preferred_element_type=F32)


def nt_kernel(act_ref, w_ref, out_ref):
    nz, total, _ = act_ref.shape
    for m in range(0, total, 256):
        acc = dot_nt(act_ref[0, m : m + 256], w_ref[0, 0])
        for z in range(1, nz):
            acc += dot_nt(act_ref[z, m : m + 256], w_ref[z, 0])
        out_ref[m : m + 256, :] = acc.astype(BF)


def mm_nt(act, w, first, rows):
    nz, total, width = act.shape
    nc = w.shape[1]
    if rows % 256:
        part = lax.slice_in_dim(w, first, first + rows, axis=2)
        out = jnp.einsum("ztf,zcrf->tcr", act, part, preferred_element_type=F32)
        return out.astype(BF).reshape(total, nc * rows)
    count, skip = rows // 256, first // 256
    return pl.pallas_call(
        nt_kernel,
        grid=(nc, count),
        in_specs=[
            pl.BlockSpec((nz, total, width), lambda c, i: (0, 0, 0)),
            pl.BlockSpec((nz, 1, 256, width), lambda c, i: (0, c, skip + i, 0)),
        ],
        out_specs=pl.BlockSpec((total, 256), lambda c, i: (0, c * count + i)),
        out_shape=jax.ShapeDtypeStruct((total, nc * rows), BF),
        compiler_params=params(2),
        cost_estimate=cost(
            2 * nz * total * width * nc * rows, 2 * nz * width * (total + nc * rows) + 2 * total * nc * rows
        ),
        name="product_nt",
    )(act, w)


def nn_kernel(grad_ref, w_ref, out_ref):
    total = grad_ref.shape[0]
    nc, rows = w_ref.shape[1], w_ref.shape[2]
    for m in range(0, total, 256):
        acc = dot_nn(grad_ref[m : m + 256, :rows], w_ref[0, 0])
        for c in range(1, nc):
            acc += dot_nn(grad_ref[m : m + 256, c * rows : (c + 1) * rows], w_ref[0, c])
        out_ref[0, m : m + 256] = acc.astype(BF)


def mm_nn(grad, w, first, rows):
    total = grad.shape[0]
    nz, nc, _, width = w.shape
    if rows % 128:
        part = lax.slice_in_dim(w, first, first + rows, axis=2)
        out = jnp.einsum(
            "tcr,zcrf->ztf", grad.reshape(total, nc, rows), part, preferred_element_type=F32
        )
        return out.astype(BF)
    skip = first // rows
    return pl.pallas_call(
        nn_kernel,
        grid=(nz,),
        in_specs=[
            pl.BlockSpec((total, nc * rows), lambda z: (0, 0)),
            pl.BlockSpec((1, nc, rows, width), lambda z: (z, 0, skip, 0)),
        ],
        out_specs=pl.BlockSpec((1, total, width), lambda z: (z, 0, 0)),
        out_shape=jax.ShapeDtypeStruct((nz, total, width), BF),
        compiler_params=params(1),
        cost_estimate=cost(
            2 * nz * total * width * nc * rows, 2 * nz * width * (total + nc * rows) + 2 * total * nc * rows
        ),
        name="product_nn",
    )(grad, w)


def tn_kernel(grad_ref, act_ref, out_ref):
    turned = grad_ref[...].T
    for z in range(act_ref.shape[0]):
        out_ref[z] = dot_nn(turned, act_ref[z]).astype(BF)


def mm_tn(grad, act):
    total, rows = grad.shape
    nz, _, width = act.shape
    if rows % 256:
        return jnp.einsum("tr,ztf->zrf", grad, act, preferred_element_type=F32).astype(BF)
    return pl.pallas_call(
        tn_kernel,
        grid=(rows // 256,),
        in_specs=[
            pl.BlockSpec((total, 256), lambda i: (0, i)),
            pl.BlockSpec((nz, total, width), lambda i: (0, 0, 0)),
        ],
        out_specs=pl.BlockSpec((nz, 256, width), lambda i: (0, i, 0)),
        out_shape=jax.ShapeDtypeStruct((nz, rows, width), BF),
        compiler_params=params(1),
        cost_estimate=cost(
            2 * nz * total * width * rows, 2 * nz * width * (total + rows) + 2 * total * rows
        ),
        name="product_tn",
    )(grad, act)


def gelu_parts(gate):
    curve = jnp.tanh(gelu_a * (gate + gelu_b * gate * gate * gate))
    value = 0.5 * gate * (1.0 + curve)
    slope = 0.5 * (1.0 + curve) + 0.5 * gate * (1.0 - curve * curve) * gelu_a * (
        1.0 + 3.0 * gelu_b * gate * gate
    )
    return value, slope


def ffn_in_kernel(act_ref, w_ref, gu_ref, active_ref):
    nz, total, _ = act_ref.shape
    half = active_ref.shape[1]
    for m in range(0, total, 256):
        acc = dot_nt(act_ref[0, m : m + 256], w_ref[0, 0])
        for z in range(1, nz):
            acc += dot_nt(act_ref[z, m : m + 256], w_ref[z, 0])
        gu_ref[m : m + 256, :] = acc.astype(BF)
        gate = acc[:, :half]
        value = 0.5 * gate * (1.0 + jnp.tanh(gelu_a * (gate + gelu_b * gate * gate * gate)))
        active_ref[m : m + 256, :] = (value * acc[:, half:]).astype(BF)


def ffn_in(act, w):
    nz, total, width = act.shape
    nc, rows = w.shape[1], w.shape[2]
    half = rows // 2
    if half % 128:
        gate_up = jnp.einsum("ztf,zcrf->tcr", act, w, preferred_element_type=F32)
        value, _ = gelu_parts(gate_up[:, :, :half])
        active = (value * gate_up[:, :, half:]).astype(BF)
        return gate_up.astype(BF).reshape(total, nc * rows), active.reshape(total, nc * half)
    block = total // 2
    return pl.pallas_call(
        ffn_in_kernel,
        grid=(nc, 2),
        in_specs=[
            pl.BlockSpec((nz, block, width), lambda c, m: (0, m, 0)),
            pl.BlockSpec((nz, 1, rows, width), lambda c, m: (0, c, 0, 0)),
        ],
        out_specs=[
            pl.BlockSpec((block, rows), lambda c, m: (m, c)),
            pl.BlockSpec((block, half), lambda c, m: (m, c)),
        ],
        out_shape=[
            jax.ShapeDtypeStruct((total, nc * rows), BF),
            jax.ShapeDtypeStruct((total, nc * half), BF),
        ],
        compiler_params=params(2),
        cost_estimate=cost(
            2 * nz * total * width * nc * rows, 2 * nz * width * (total + nc * rows) + 3 * total * nc * rows
        ),
        name="ffn_in",
    )(act, w)


def ffn_back_kernel(grad_ref, w_ref, gu_ref, out_ref):
    nz, total, _ = grad_ref.shape
    half = w_ref.shape[2]
    for m in range(0, total, 256):
        acc = dot_nt(grad_ref[0, m : m + 256], w_ref[0, 0])
        for z in range(1, nz):
            acc += dot_nt(grad_ref[z, m : m + 256], w_ref[z, 0])
        gate = gu_ref[m : m + 256, :half].astype(F32)
        up = gu_ref[m : m + 256, half:].astype(F32)
        value, slope = gelu_parts(gate)
        out_ref[m : m + 256, :half] = (acc * up * slope).astype(BF)
        out_ref[m : m + 256, half:] = (acc * value).astype(BF)


def ffn_back(grad, w, gate_up):
    nz, total, width = grad.shape
    nc, half = w.shape[1], w.shape[2]
    if half % 128:
        grad_act = jnp.einsum("ztf,zcrf->tcr", grad, w, preferred_element_type=F32)
        kept = gate_up.astype(F32).reshape(total, nc, 2 * half)
        value, slope = gelu_parts(kept[:, :, :half])
        both = jnp.concatenate([grad_act * kept[:, :, half:] * slope, grad_act * value], axis=2)
        return both.astype(BF).reshape(total, nc * 2 * half)
    block = total // 2
    return pl.pallas_call(
        ffn_back_kernel,
        grid=(nc, 2),
        in_specs=[
            pl.BlockSpec((nz, block, width), lambda c, m: (0, m, 0)),
            pl.BlockSpec((nz, 1, half, width), lambda c, m: (0, c, 0, 0)),
            pl.BlockSpec((block, 2 * half), lambda c, m: (m, c)),
        ],
        out_specs=pl.BlockSpec((block, 2 * half), lambda c, m: (m, c)),
        out_shape=jax.ShapeDtypeStruct((total, nc * 2 * half), BF),
        compiler_params=params(2),
        cost_estimate=cost(
            2 * nz * total * width * nc * half, 2 * nz * width * (total + nc * half) + 8 * total * nc * half
        ),
        name="ffn_back",
    )(grad, w, gate_up)


def near_buckets(tile, total):
    first = (total // LB - 2 + tile) * LB
    rows = lax.broadcasted_iota(jnp.int32, (LB, LB), 0)
    lanes = lax.broadcasted_iota(jnp.int32, (LB, LB), 1)
    return bucket_index(first + rows - (total - LB) - lanes)


def build_strips(table_ref, strip_ref, total, group):
    heads = strip_ref.shape[0]
    near = (total // LB - 2) * LB
    for h in range(heads):
        head = group * heads + h
        strip_ref[h, :near] = jnp.full((near, LB), table_ref[head, 15], F32)
        strip_ref[h, near + 3 * LB :] = jnp.full((near, LB), table_ref[head, 31], F32)

    def one_tile(tile, _):
        index = near_buckets(tile, total)
        vals = [jnp.full((LB, LB), table_ref[group * heads + h, 0], F32) for h in range(heads)]
        for b in range(1, 32):
            hit = index == b
            vals = [
                jnp.where(hit, table_ref[group * heads + h, b], vals[h]) for h in range(heads)
            ]
        for h in range(heads):
            strip_ref[h, pl.ds(pl.multiple_of(near + tile * LB, LB), LB)] = vals[h]
        return 0

    lax.fori_loop(0, 3, one_tile, 0)


def head_lanes(shape, h):
    lanes = lax.broadcasted_iota(jnp.int32, shape, 1)
    return lanes // 64 == h, lanes == ((h + 1) % 4) * 64


def mask_keys(keys, length, h):
    own, spare = head_lanes(keys.shape, h)
    dead = lax.broadcasted_iota(jnp.int32, keys.shape, 0) >= length
    mask = jnp.where(jnp.logical_and(spare, dead), masked_score, 0.0)
    return jnp.where(own, keys.astype(F32), mask).astype(BF)


def with_one(queries, h):
    _, spare = head_lanes(queries.shape, h)
    return jnp.where(spare, 1.0, queries.astype(F32)).astype(BF)


def own_lanes(values, h):
    own, _ = head_lanes(values.shape, h)
    return jnp.where(own, values.astype(F32), 0.0).astype(BF)


def block_bias(strip_ref, h, block, total):
    first = total - LB - 2 * block * LB
    left = strip_ref[h, pl.ds(pl.multiple_of(first, LB), total)]
    right = strip_ref[h, pl.ds(pl.multiple_of(first - LB, LB), total)]
    return jnp.concatenate([left, right], axis=1)


def attend_kernel(length_ref, table_ref, q_ref, k_ref, v_ref, out_ref, lse_ref, strip, heads_k, turned_v, turned_out):
    total = q_ref.shape[0]
    heads = strip.shape[0]
    build_strips(table_ref, strip, total, pl.program_id(0))
    turned_v[...] = v_ref[...].astype(F32).T.astype(BF)
    for h in range(heads):
        heads_k[h] = mask_keys(k_ref[...], length_ref[0], h)

    def one_block(block, _):
        spot = pl.ds(pl.multiple_of(block * 256, 256), 256)
        queries = q_ref[spot]
        for h in range(heads):
            scores = dot_nt(heads_k[h], with_one(queries, h)) + block_bias(strip, h, block, total)
            largest = jnp.max(scores, axis=0, keepdims=True)
            raised = jnp.exp(scores - largest)
            totals = jnp.sum(raised, axis=0, keepdims=True)
            out = dot_nn(turned_v[h * 64 : (h + 1) * 64], raised.astype(BF))
            turned_out[h * 64 : (h + 1) * 64, spot] = out * (1.0 / totals)
            lse_ref[0, h : h + 1, spot] = largest + jnp.log(totals)
        return 0

    lax.fori_loop(0, total // 256, one_block, 0)
    out_ref[...] = turned_out[...].T.astype(BF)


def attend_back_kernel(
    length_ref, table_ref, q_ref, k_ref, v_ref, grad_ref, lse_ref, out_ref, table_grad_ref,
    strip, strip_grad, heads_k, turned_k, turned_q, ds_ref, p_ref, dk_ref, dv_ref,
):
    total = q_ref.shape[0]
    heads = strip.shape[0]
    build_strips(table_ref, strip, total, pl.program_id(0))
    strip_grad[...] = jnp.zeros_like(strip_grad)
    dk_ref[...] = jnp.zeros_like(dk_ref)
    dv_ref[...] = jnp.zeros_like(dv_ref)
    turned_k[...] = k_ref[...].astype(F32).T.astype(BF)
    for h in range(heads):
        heads_k[h] = mask_keys(k_ref[...], length_ref[0], h)

    def one_block(block, _):
        spot = pl.ds(pl.multiple_of(block * 256, 256), 256)
        queries, grads = q_ref[spot], grad_ref[spot]
        own_q, own_g = [], []
        for h in range(heads):
            own_q.append(own_lanes(queries, h))
            own_g.append(own_lanes(grads, h))
            scores = dot_nt(heads_k[h], with_one(queries, h)) + block_bias(strip, h, block, total)
            probs = jnp.exp(scores - lse_ref[0, h : h + 1, spot])
            weighed = probs * dot_nt(v_ref[...], own_g[h])
            delta = jnp.sum(weighed, axis=0, keepdims=True)
            grad_scores = weighed - probs * delta
            first = total - LB - 2 * block * LB
            left = pl.ds(pl.multiple_of(first, LB), total)
            right = pl.ds(pl.multiple_of(first - LB, LB), total)
            strip_grad[h, left] += grad_scores[:, :LB]
            strip_grad[h, right] += grad_scores[:, LB:]
            rounded = grad_scores.astype(BF)
            ds_ref[:, h * 256 : (h + 1) * 256] = rounded
            p_ref[:, h * 256 : (h + 1) * 256] = probs.astype(BF)
            turned_q[h * 64 : (h + 1) * 64, spot] = dot_nn(turned_k[h * 64 : (h + 1) * 64], rounded)
        dk_ref[...] += dot_nn(ds_ref[...], jnp.concatenate(own_q, axis=0))
        dv_ref[...] += dot_nn(p_ref[...], jnp.concatenate(own_g, axis=0))
        return 0

    lax.fori_loop(0, total // 256, one_block, 0)
    out_ref[:, :256] = turned_q[...].T.astype(BF)
    out_ref[:, 256:512] = dk_ref[...].astype(BF)
    out_ref[:, 512:] = dv_ref[...].astype(BF)

    near = (total // LB - 2) * LB
    for h in range(heads):
        table_grad_ref[0, h] = jnp.zeros((32, LB), F32)
        table_grad_ref[0, h, 15:16] = jnp.sum(strip_grad[h, :near], axis=0, keepdims=True)
        table_grad_ref[0, h, 31:32] = jnp.sum(strip_grad[h, near + 3 * LB :], axis=0, keepdims=True)

    def one_tile(tile, _):
        index = near_buckets(tile, total)
        spot = pl.ds(pl.multiple_of(near + tile * LB, LB), LB)
        for h in range(heads):
            grads = strip_grad[h, spot]
            for b in range(32):
                picked = jnp.where(index == b, grads, 0.0)
                table_grad_ref[0, h, b : b + 1] += jnp.sum(picked, axis=0, keepdims=True)
        return 0

    lax.fori_loop(0, 3, one_tile, 0)


def block_specs(total):
    return [
        pl.BlockSpec(memory_space=pltpu.SMEM),
        pl.BlockSpec(memory_space=pltpu.SMEM),
        pl.BlockSpec((total, 256), lambda c: (0, 3 * c)),
        pl.BlockSpec((total, 256), lambda c: (0, 3 * c + 1)),
        pl.BlockSpec((total, 256), lambda c: (0, 3 * c + 2)),
    ]


def attend(projected, length, table, groups, heads):
    total = projected.shape[0]
    strip_rows = 2 * total - LB
    return pl.pallas_call(
        attend_kernel,
        grid=(groups,),
        in_specs=block_specs(total),
        out_specs=[
            pl.BlockSpec((total, 256), lambda c: (0, c)),
            pl.BlockSpec((1, 8, total), lambda c: (c, 0, 0)),
        ],
        out_shape=[
            jax.ShapeDtypeStruct((total, groups * 256), BF),
            jax.ShapeDtypeStruct((groups, 8, total), F32),
        ],
        scratch_shapes=[
            pltpu.VMEM((heads, strip_rows, LB), F32),
            pltpu.VMEM((heads, total, 256), BF),
            pltpu.VMEM((256, total), BF),
            pltpu.VMEM((256, total), F32),
        ],
        compiler_params=params(1),
        cost_estimate=cost(groups * heads * total * total * 2 * 256 * 2, 4 * total * groups * 256 * 2),
        name="attend",
    )(length, table, projected, projected, projected)


def attend_back(projected, length, table, grad_out, lse, groups, heads):
    total = projected.shape[0]
    strip_rows = 2 * total - LB
    return pl.pallas_call(
        attend_back_kernel,
        grid=(groups,),
        in_specs=block_specs(total)
        + [
            pl.BlockSpec((total, 256), lambda c: (0, c)),
            pl.BlockSpec((1, 8, total), lambda c: (c, 0, 0)),
        ],
        out_specs=[
            pl.BlockSpec((total, 768), lambda c: (0, c)),
            pl.BlockSpec((1, heads, 32, LB), lambda c: (c, 0, 0, 0)),
        ],
        out_shape=[
            jax.ShapeDtypeStruct((total, groups * 768), BF),
            jax.ShapeDtypeStruct((groups, heads, 32, LB), F32),
        ],
        scratch_shapes=[
            pltpu.VMEM((heads, strip_rows, LB), F32),
            pltpu.VMEM((heads, strip_rows, LB), F32),
            pltpu.VMEM((heads, total, 256), BF),
            pltpu.VMEM((256, total), BF),
            pltpu.VMEM((256, total), F32),
            pltpu.VMEM((total, heads * 256), BF),
            pltpu.VMEM((total, heads * 256), BF),
            pltpu.VMEM((total, 256), F32),
            pltpu.VMEM((total, 256), F32),
        ],
        compiler_params=params(1),
        cost_estimate=cost(groups * heads * total * total * 2 * 256 * 5, 8 * total * groups * 256 * 2),
        name="attend_back",
    )(length, table, projected, projected, projected, grad_out, lse)


def split_heads(projected, groups, heads):
    parts = projected.reshape(projected.shape[0], groups, 3, heads, 64)
    return [parts[:, :, i].reshape(projected.shape[0], groups * heads, 64) for i in range(3)]


def plain_scores(queries, keys, length, table):
    slots = jnp.arange(keys.shape[0], dtype=jnp.int32)
    picked = (bucket_index(slots[None, :] - slots[:, None])[:, :, None] == jnp.arange(32)).astype(F32)
    bias = jnp.einsum("qkb,hb->hqk", picked, table, precision=lax.Precision.HIGHEST)
    scores = jnp.einsum("qhs,khs->hqk", queries, keys, preferred_element_type=F32) + bias
    return jnp.where(slots < length[0], scores, masked_score), picked


def attend_plain(projected, length, table, groups, heads):
    queries, keys, values = split_heads(projected, groups, heads)
    scores, _ = plain_scores(queries, keys, length, table)
    lse = jax.nn.logsumexp(scores, axis=2)
    probs = jnp.exp(scores - lse[:, :, None]).astype(BF)
    out = jnp.einsum("hqk,khs->qhs", probs, values, preferred_element_type=F32)
    return out.astype(BF).reshape(projected.shape[0], -1), lse


def attend_back_plain(projected, length, table, grad_out, lse, groups, heads):
    total = projected.shape[0]
    queries, keys, values = split_heads(projected, groups, heads)
    grads = grad_out.reshape(queries.shape)
    scores, picked = plain_scores(queries, keys, length, table)
    probs = jnp.exp(scores - lse[:, :, None])
    weighed = probs * jnp.einsum("qhs,khs->hqk", grads, values, preferred_element_type=F32)
    wide = weighed - probs * jnp.sum(weighed, axis=2, keepdims=True)
    rounded = wide.astype(BF)
    parts = [
        jnp.einsum("hqk,khs->qhs", rounded, keys, preferred_element_type=F32),
        jnp.einsum("hqk,qhs->khs", rounded, queries, preferred_element_type=F32),
        jnp.einsum("hqk,qhs->khs", probs.astype(BF), grads, preferred_element_type=F32),
    ]
    parts = [part.astype(BF).reshape(total, groups, 1, heads * 64) for part in parts]
    table_grad = jnp.einsum("hqk,qkb->hb", wide, picked, precision=lax.Precision.HIGHEST)
    return (
        jnp.concatenate(parts, axis=2).reshape(total, -1),
        table_grad.reshape(groups, heads, 32, 1),
    )


def hop(value, axis):
    return lax.ppermute(value, axis, swap)


def pick(value, index, axis):
    return lax.dynamic_index_in_dim(value, index, axis, keepdims=False)


def paired(mine, other, axis):
    return jnp.where(
        lax.axis_index(axis) == 0, jnp.stack([mine, other]), jnp.stack([other, mine])
    )


def gather_tokens(part, nx):
    nz, t, width = part.shape
    if nx != 2:
        return lax.all_gather(part, ("x", "y"), axis=1, tiled=True)
    low, high = part[: nz // 2], part[nz // 2 :]
    low_x, high_y = hop(low, "x"), hop(high, "y")
    low_y, high_x = hop(low, "y"), hop(high, "x")
    low_xy, high_xy = hop(low_x, "y"), hop(high_y, "x")
    low_all = paired(paired(low, low_y, "y"), paired(low_x, low_xy, "y"), "x")
    high_all = paired(paired(high, high_y, "y"), paired(high_x, high_xy, "y"), "x")
    both = jnp.concatenate([low_all, high_all], axis=2)
    return both.transpose(2, 0, 1, 3, 4).reshape(nz, nx * 2 * t, width)


def scatter_tokens(whole, nx):
    nz, total, width = whole.shape
    if nx != 2:
        summed = lax.psum_scatter(
            whole.astype(F32), ("x", "y"), scatter_dimension=1, tiled=True
        )
        return summed
    x, y = lax.axis_index("x"), lax.axis_index("y")
    parts = whole.reshape(nz, nx, 2, total // (2 * nx), width)
    low, high = parts[: nz // 2], parts[nz // 2 :]
    low_in = hop(pick(low, 1 - x, 1), "x")
    high_in = hop(pick(high, 1 - y, 2), "y")
    low_own, high_own = pick(low, x, 1), pick(high, y, 2)

    def add(a, b, index):
        return pick(a, index, 1).astype(F32) + pick(b, index, 1).astype(F32)

    low_last = hop(add(low_own, low_in, 1 - y).astype(BF), "y")
    high_last = hop(add(high_own, high_in, 1 - x).astype(BF), "x")
    return jnp.concatenate(
        [
            add(low_own, low_in, y) + low_last.astype(F32),
            add(high_own, high_in, x) + high_last.astype(F32),
        ],
        axis=0,
    )


def to_groups(stored):
    count, slots, width = stored.shape
    y = lax.axis_index("y")
    halves = stored.reshape(count, 2, slots // 2, width)
    other = hop(pick(halves, 1 - y, 1), "y")
    both = paired(pick(halves, y, 1), other, "y").reshape(2 * count, slots // 2, width)
    return lax.all_to_all(both, "z", 0, 0, tiled=True)


def from_groups(mine):
    nz, t, width = mine.shape
    y = lax.axis_index("y")
    back = lax.all_to_all(mine, "z", 0, 0, tiled=True).reshape(2, nz // 2, t, width)
    other = hop(pick(back, 1 - y, 0), "y")
    both = paired(pick(back, y, 0), other, "y")
    return both.transpose(1, 0, 2, 3).reshape(nz // 2, 2 * t, width)


def body(
    nx, nz, nc, inputs, lengths, attn_gain, ffn_gain, query_key, value_proj, out_proj, gate_up, down_proj, bias_table, cotangent
):
    x, y = lax.axis_index("x"), lax.axis_index("y")
    c, z = lax.axis_index("c"), lax.axis_index("z")
    width = inputs.shape[2]
    features = nz * width
    quarter = y * nc + c
    parts = 2 * nc

    qkv_rows = jnp.concatenate(
        [jnp.transpose(query_key, (1, 2, 3, 0)), jnp.transpose(value_proj, (1, 2, 0))[:, None]], axis=1
    )
    gate_up_rows = jnp.transpose(gate_up, (1, 2, 3, 0))
    heads = qkv_rows.shape[0] // parts
    units = gate_up_rows.shape[0] // parts
    unit = gate_up_rows.shape[2]

    def own(rows, count):
        return lax.dynamic_slice_in_dim(rows, quarter * count, count, 0)

    def spread(rows):
        gathered = lax.all_gather(rows, ("z", "c"), axis=0, tiled=True)
        return gathered.reshape(nz, nc, rows.shape[0], width)

    own_qkv = own(qkv_rows, heads).transpose(1, 0, 2, 3).reshape(3 * heads * 64, width)
    own_out = own(out_proj, heads).reshape(heads * 64, width)
    own_gate_up = own(gate_up_rows, units).transpose(1, 0, 2, 3).reshape(2 * units * unit, width)
    own_down = own(down_proj, units).reshape(units * unit, width)
    qkv_count, out_count = 3 * heads * 64, heads * 64
    w_attn = spread(jnp.concatenate([own_qkv, own_out], axis=0))
    w_gate_up = spread(own_gate_up)
    w_down = spread(own_down)

    both_lengths = jnp.stack([lengths, lax.ppermute(lengths, "y", swap)])
    both_lengths = jnp.where(y == 0, both_lengths, both_lengths[::-1]).reshape(-1)
    length = lax.dynamic_slice_in_dim(both_lengths, z, 1, 0)
    small = jnp.concatenate([attn_gain, ffn_gain, bias_table.reshape(-1)])
    small = lax.all_gather(small, "z", axis=0)
    gain_one = small[:, None, :width].astype(F32)
    gain_two = small[:, None, width : 2 * width].astype(F32)
    table = small[:, 2 * width :].reshape(nz, bias_table.shape[0], -1).transpose(0, 2, 1)
    local_heads = nc * heads
    table = table.reshape(-1, bias_table.shape[0]).astype(F32)
    table = lax.dynamic_slice_in_dim(table, y * local_heads, local_heads, 0)

    tokens = to_groups(inputs).astype(F32)
    count = tokens.shape[1]
    slots = (x * 2 + y) * count + jnp.arange(count, dtype=jnp.int32)
    live = (slots < length).astype(F32)[None, :, None]
    upstream = live * to_groups(cotangent).astype(F32)

    def scale_of(values):
        squares = jnp.sum(values * values, axis=(0, 2), keepdims=True)
        return lax.rsqrt(squares / features + norm_eps)

    def norm_back(values, scale, gain, grad):
        inner = jnp.sum(values * gain * grad, axis=(0, 2), keepdims=True)
        out = scale * gain * grad - values * (scale * scale * scale) * inner / features
        return out, jnp.sum(values * scale * grad, axis=1)

    fits = heads == 4
    forward = attend if fits else attend_plain
    backward = attend_back if fits else attend_back_plain

    scale_one = scale_of(tokens)
    normed = gather_tokens((tokens * scale_one * gain_one).astype(BF), nx)
    grad_ffn = gather_tokens(upstream.astype(BF), nx)
    projected = mm_nt(normed, w_attn, 0, qkv_count)
    attended, lse = forward(projected, length, table, nc, heads)
    hidden = tokens + scatter_tokens(mm_nn(attended, w_attn, qkv_count, out_count), nx)
    scale_two = scale_of(hidden)
    normed_two = gather_tokens((hidden * scale_two * gain_two).astype(BF), nx)
    kept, activated = ffn_in(normed_two, w_gate_up)
    branch = scatter_tokens(mm_nn(activated, w_down, 0, units * unit), nx)
    outputs = from_groups((live * (hidden + branch)).astype(BF))

    def reduce(partial):
        flat = partial.reshape(nz * partial.shape[1], width)
        return lax.psum_scatter(flat, ("z", "c"), scatter_dimension=0, tiled=True)

    def share(part):
        return lax.all_gather(part, ("y", "c"), axis=0)

    down_part = reduce(mm_tn(activated, grad_ffn))
    grad_gate_up = ffn_back(grad_ffn, w_down, kept)
    grad_two = scatter_tokens(mm_nn(grad_gate_up, w_gate_up, 0, 2 * units * unit), nx)
    gate_up_part = reduce(mm_tn(grad_gate_up, normed_two))
    through, ffn_gain_part = norm_back(hidden, scale_two, gain_two, grad_two)
    grad_hidden = upstream + through
    grad_branch = gather_tokens(grad_hidden.astype(BF), nx)
    grad_attended = mm_nt(grad_branch, w_attn, qkv_count, out_count)
    grad_projected, table_part = backward(
        projected, length, table, grad_attended, lse, nc, heads
    )
    grad_one = scatter_tokens(mm_nn(grad_projected, w_attn, 0, qkv_count), nx)
    out_part = reduce(mm_tn(attended, grad_branch))
    qkv_part = reduce(mm_tn(grad_projected, normed))
    through, attn_gain_part = norm_back(tokens, scale_one, gain_one, grad_one)
    input_grad = from_groups((grad_hidden + through).astype(BF)).astype(F32)

    down_all = share(down_part).astype(F32).reshape(down_proj.shape)
    out_all = share(out_part).astype(F32).reshape(out_proj.shape)
    gate_up_all = share(gate_up_part).reshape(parts, 2, units, unit, width)
    gate_up_all = gate_up_all.transpose(4, 0, 2, 1, 3).astype(F32).reshape(gate_up.shape)
    qkv_all = share(qkv_part).reshape(parts, 3, heads, 64, width)
    qkv_all = qkv_all.transpose(4, 0, 2, 1, 3).astype(F32).reshape(width, parts * heads, 3, 64)

    table_part = jnp.sum(table_part, axis=3).reshape(local_heads, -1)
    every = jnp.zeros((nx * 2 * local_heads, table_part.shape[1]), F32)
    every = lax.dynamic_update_slice_in_dim(every, table_part, (x * 2 + y) * local_heads, 0)
    sums = lax.psum(
        (attn_gain_part, ffn_gain_part, every), ("y", "c", "x", "z")
    )
    mine = bias_table.shape[1]
    table_grad = lax.dynamic_slice_in_dim(sums[2], (x * nz + z) * mine, mine, 0).T
    return (
        outputs,
        input_grad,
        pick(sums[0], z, 0),
        pick(sums[1], z, 0),
        qkv_all[:, :, :2],
        qkv_all[:, :, 2],
        out_all,
        gate_up_all,
        down_all,
        table_grad,
    )


def solution(mesh):
    dp, nx, nz = (mesh.shape[name] for name in ("dp", "gx", "gy"))
    nc = dp // 2
    split = Mesh(mesh.devices.reshape(2, nc, nx, nz), ("y", "c", "x", "z"))
    seq = ("y", "c")
    return jax.shard_map(
        functools.partial(body, nx, nz, nc),
        mesh=split,
        in_specs=(
            P(seq, "x", "z"),
            P(seq),
            P("z"),
            P("z"),
            P("z", "x", None, None),
            P("z", "x", None),
            P("x", None, "z"),
            P("z", "x", None, None),
            P("x", None, "z"),
            P(None, ("x", "z")),
            P(seq, "x", "z"),
        ),
        out_specs=(
            P(seq, "x", "z"),
            P(seq, "x", "z"),
            P("z"),
            P("z"),
            P("z", "x", None, None),
            P("z", "x", None),
            P("x", None, "z"),
            P("z", "x", None, None),
            P("x", None, "z"),
            P(None, ("x", "z")),
        ),
        check_vma=False,
    )
```

time: 5010 us -> 946 us (0.19)
  waiting for transfers between devices: 3550 us -> 397 us
  local copies, waits for them, and re-layouts: 789 us -> 61.5 us
  matrix products: 277 us -> 0 us
  Pallas kernels: 0 us -> 223 us
  other arithmetic: 203 us -> 60.3 us
  starting transfers between devices: 1.42 us -> 70.7 us
  loops' own time: 65.1 us -> 0 us
    while x34 -> x0, waiting for transfers between devices: 1400 us -> none
    all_gather x16 -> x7, waiting for transfers between devices: 947 us -> 0.01 us  [the longest x4 0.01 us: share(): return lax.all_gather(part, ('y', 'c'), axis=0)]
    reduce_scatter x14 -> x4, waiting for transfers between devices: 1010 us -> 174 us  [reduce(): return lax.psum_scatter(flat, ('z', 'c'), scatter_dimension=0, tiled=True)]
    while x279 -> x0, local copies, waits for them, and re-layouts: 389 us -> none
    pallas_call x0 -> x14, Pallas kernels: none -> 223 us  [the longest x1 55.1 us: attend_back(): pl.pallas_call(attend_back_kernel, grid=(groups,), in_specs=block_specs(t...]
    dot_general x56 -> x0, matrix products: 211 us -> none  [the longest x8 50.4 us: block_scores(): jnp.einsum('qhs,khs->hqk', block_queries, key_vecs, preferred_element_typ...]
    reshape x16 -> x4, local copies, waits for them, and re-layouts: 208 us -> 11.1 us  [the longest x1 8.15 us: body(): gate_up_all.transpose(4, 0, 2, 1, 3).astype(F32).reshape(gate_up.shape)]
    ppermute x0 -> x45, waiting for transfers between devices: none -> 196 us  [the longest x44 196 us: hop(): return lax.ppermute(value, axis, swap)]
  transfers between devices with their start and end apart: 33 -> 60, of which waited for: 29 -> 28; matrix products, arithmetic and copies ran while one was open for 16% -> 10% of each run, Pallas kernels for 0% -> 20%
where the time goes in v1:
time: 946 us; the launch traced here: 939 us
  waiting for transfers between devices  397 us (42%)
  Pallas kernels  223 us (24%)
  blocking collectives  112 us (12%)
  starting transfers between devices  70.7 us (7%)
  local copies, waits for them, and re-layouts  61.5 us (7%)
  other arithmetic  60.3 us (6%)
  between operations  15 us (2%)
    ppermute x44, waiting for transfers between devices, hop(): return lax.ppermute(value, axis, swap)  196 us
    reduce_scatter x4, waiting for transfers between devices, reduce(): return lax.psum_scatter(flat, ('z', 'c'), scatter_dimension=0, tiled=True)  174 us
    psum x1, blocking collectives, body(): lax.psum((attn_gain_part, ffn_gain_part, every), ('y', 'c', 'x', 'z'))  55.9 us
    all_gather x1, blocking collectives, body(): small = lax.all_gather(small, 'z', axis=0)  55.7 us
    pallas_call x1, Pallas kernels, attend_back(): pl.pallas_call(attend_back_kernel, grid=(groups,), in_specs=block_specs(t...  55.1 us
    ppermute x44, starting transfers between devices, hop(): return lax.ppermute(value, axis, swap)  51.4 us
    pallas_call x4, Pallas kernels, mm_tn(): pl.pallas_call(tn_kernel, grid=(rows // 256,), in_specs=[pl.BlockSpec((to...  44.3 us
    pallas_call x4, Pallas kernels, mm_nn(): pl.pallas_call(nn_kernel, grid=(nz,), in_specs=[pl.BlockSpec((total, nc *...  43.5 us
  transfers between devices with their start and end apart: 60, of which 28 were waited for; matrix products, arithmetic and copies ran while one was open for 10% of the time, Pallas kernels for 20%

profile of v1, /device:TPU:0, one launch (start us, length us, event | category | flops | bytes accessed | tf_op | source)
XLA Modules:
  0.0 939.3 jit_solution(542660349913271286)
XLA Ops:
  21.5 12.2 %collective-permute-done.1 = bf16[2,256,512]{2,1,0:T(8,128)(2,1)} collective-permute-done((bf16[2,256,512]{2,1,0:T(8,128)(2,1)}, bf16[2,256,512]{2,1,0:T(8,128)(2,1)}, u32[]{:S(2)}, u32[]{:S(2)}) %collective-permute-start.1) | collective-permute-done | bytes 524320 | tf_op jit(solution)/shard_map/ppermute | solution.py:510
  46.6 55.7 %all-gather.5 = bf16[4,1,1152]{2,1,0:T(2,128)(2,1)S(1)} all-gather(bf16[1,1,1152]{2,1,0:T(2,128)(2,1)S(1)} %reshape.1329), channel_id=2, replica_groups=mesh['y'=2,'c'=2,'x'=2,'z'=4] {'z'}, dimensions={0}, use_global_device_ids=true | all-gather | bytes 11520 | tf_op jit(solution)/shard_map/all_gather | solution.py:621
  112.9 9.5 %collective-permute-done.5 = bf16[2,256,512]{2,1,0:T(8,128)(2,1)} collective-permute-done((bf16[2,256,512]{2,1,0:T(8,128)(2,1)}, bf16[2,256,512]{2,1,0:T(8,128)(2,1)}, u32[]{:S(2)}, u32[]{:S(2)}) %collective-permute-start.5) | collective-permute-done | bytes 524320 | tf_op jit(solution)/shard_map/ppermute | solution.py:510
  148.6 11.7 %product_nt.2.q_ref.k_ref.v_ref = bf16[1024,1536]{1,0:T(8,128)(2,1)} custom-call(bf16[4,1024,512]{2,1,0:T(8,128)(2,1)} %bitcast.329, bf16[4,2,1024,512]{3,2,1,0:T(8,128)(2,1)} %bitcast.286), custom_call_target="tpu_custom_call" | custom-call | flops 6442450944 | bytes 13631488 | tf_op jit(solution)/shard_map/product_nt/pallas_call | solution.py:66
  160.3 30.8 %attend.1 = (bf16[1024,512]{1,0:T(8,128)(2,1)}, f32[2,8,1024]{2,1,0:T(8,128)}) custom-call(s32[1]{0:T(128)} %dynamic_slice.182.length_ref, f32[8,32]{1,0:T(8,128)} %constant_dynamic-slice_fusion.14.table_ref, bf16[1024,1536]{1,0:T(8,128)(2,1)} %product_nt.2.q_ref.k_ref.v_ref, bf16[1024,1536]{1,0:T(8,128)(2,1)} %product_nt.2.q_ref.k_ref.v_ref, ...), custom_call_target="tpu_custom_call" | custom-call | flops 8589934592 | bytes 4194304 | tf_op jit(solution)/shard_map/attend/pallas_call | solution.py:405
  208.9 18.5 %collective-permute-done.10 = bf16[2,2,256,512]{3,2,0,1:T(8,128)(2,1)} collective-permute-done((bf16[2,2,256,512]{3,2,0,1:T(8,128)(2,1)}, bf16[2,2,256,512]{3,2,0,1:T(8,128)(2,1)}, u32[]{:S(2)}, u32[]{:S(2)}) %collective-permute-start.10) | collective-permute-done | bytes 1048608 | tf_op jit(solution)/shard_map/ppermute | solution.py:510
  252.7 9.9 %collective-permute-done.11 = bf16[2,256,512]{2,1,0:T(8,128)(2,1)S(1)} collective-permute-done((bf16[2,256,512]{2,1,0:T(8,128)(2,1)S(1)}, bf16[2,256,512]{2,1,0:T(8,128)(2,1)S(1)}, u32[]{:S(2)}, u32[]{:S(2)}) %collective-permute-start.11) | collective-permute-done | bytes 524320 | tf_op jit(solution)/shard_map/ppermute | solution.py:510
  305.1 17.1 %ffn_in.1 = (bf16[1024,2560]{1,0:T(8,128)(2,1)}, bf16[1024,1280]{1,0:T(8,128)(2,1)}) custom-call(bf16[4,1024,512]{2,1,0:T(8,128)(2,1)} %bitcast.331, bf16[4,2,1280,512]{3,2,1,0:T(8,128)(2,1)} %bitcast.377), custom_call_target="tpu_custom_call" | custom-call | flops 10737418240 | bytes 22544384 | tf_op jit(solution)/shard_map/ffn_in/pallas_call | solution.py:180
  322.2 14.7 %ffn_back.1.grad_ref = bf16[1024,2560]{1,0:T(8,128)(2,1)} custom-call(bf16[4,1024,512]{2,1,0:T(8,128)(2,1)} %bitcast.292, bf16[4,2,640,512]{3,2,1,0:T(8,128)(2,1)} %bitcast.326, bf16[1024,2560]{1,0:T(8,128)(2,1)} %get-tuple-element.18.gu_ref), custom_call_target="tpu_custom_call" | custom-call | flops 5368709120 | bytes 19922944 | tf_op jit(solution)/shard_map/ffn_back/pallas_call | solution.py:227
  336.9 15.8 %product_nn.6 = bf16[4,1024,512]{2,1,0:T(8,128)(2,1)} custom-call(bf16[1024,2560]{1,0:T(8,128)(2,1)} %ffn_back.1.grad_ref, bf16[4,2,1280,512]{3,2,1,0:T(8,128)(2,1)} %bitcast.378), custom_call_target="tpu_custom_call" | custom-call | flops 10737418240 | bytes 19922944 | tf_op jit(solution)/shard_map/product_nn/pallas_call | solution.py:103
  359.3 10.7 %product_nn.5 = bf16[4,1024,512]{2,1,0:T(8,128)(2,1)} custom-call(bf16[1024,1280]{1,0:T(8,128)(2,1)} %get-tuple-element.17.grad_ref, bf16[4,2,640,512]{3,2,1,0:T(8,128)(2,1)} %bitcast.327), custom_call_target="tpu_custom_call" | custom-call | flops 5368709120 | bytes 12058624 | tf_op jit(solution)/shard_map/product_nn/pallas_call | solution.py:103
  388.0 16.8 %collective-permute-done.20 = bf16[2,2,256,512]{3,2,0,1:T(8,128)(2,1)S(1)} collective-permute-done((bf16[2,2,256,512]{3,2,0,1:T(8,128)(2,1)S(1)}, bf16[2,2,256,512]{3,2,0,1:T(8,128)(2,1)S(1)}, u32[]{:S(2)}, u32[]{:S(2)}) %collective-permute-start.20) | collective-permute-done | bytes 1048608 | tf_op jit(solution)/shard_map/ppermute | solution.py:510
  430.4 10.8 %collective-permute-done.37 = bf16[2,256,512]{2,1,0:T(8,128)(2,1)S(1)} collective-permute-done((bf16[2,256,512]{2,1,0:T(8,128)(2,1)S(1)}, bf16[2,256,512]{2,1,0:T(8,128)(2,1)S(1)}, u32[]{:S(2)}, u32[]{:S(2)}) %collective-permute-start.37) | collective-permute-done | bytes 524320 | tf_op jit(solution)/shard_map/ppermute | solution.py:510
  466.4 10.1 %product_tn.7 = bf16[4,1280,512]{2,1,0:T(8,128)(2,1)} custom-call(bf16[1024,1280]{1,0:T(8,128)(2,1)} %get-tuple-element.17.grad_ref, bf16[4,1024,512]{2,1,0:T(8,128)(2,1)} %bitcast.293), custom_call_target="tpu_custom_call" | custom-call | flops 5368709120 | bytes 12058624 | tf_op jit(solution)/shard_map/product_tn/pallas_call | solution.py:131
  482.6 55.1 %attend_back.1 = (bf16[1024,1536]{1,0:T(8,128)(2,1)}, f32[2,4,32,128]{3,2,1,0:T(8,128)}) custom-call(s32[1]{0:T(128)} %dynamic_slice.182.length_ref, f32[8,32]{1,0:T(8,128)} %constant_dynamic-slice_fusion.14.table_ref, bf16[1024,1536]{1,0:T(8,128)(2,1)} %product_nt.2.q_ref.k_ref.v_ref, bf16[1024,1536]{1,0:T(8,128)(2,1)} %product_nt.2.q_ref.k_ref.v_ref, ...), custom_call_target="tpu_custom_call" | custom-call | flops 21474836480 | bytes 8388608 | tf_op jit(solution)/shard_map/attend_back/pallas_call | solution.py:432
  537.7 11.4 %product_tn.4 = bf16[4,1536,512]{2,1,0:T(8,128)(2,1)} custom-call(bf16[1024,1536]{1,0:T(8,128)(2,1)} %get-tuple-element.20.grad_ref, bf16[4,1024,512]{2,1,0:T(8,128)(2,1)} %bitcast.330), custom_call_target="tpu_custom_call" | custom-call | flops 6442450944 | bytes 13631488 | tf_op jit(solution)/shard_map/product_tn/pallas_call | solution.py:131
  549.3 16.9 %product_tn.6 = bf16[4,2560,512]{2,1,0:T(8,128)(2,1)} custom-call(bf16[1024,2560]{1,0:T(8,128)(2,1)} %ffn_back.1.grad_ref, bf16[4,1024,512]{2,1,0:T(8,128)(2,1)} %bitcast.332), custom_call_target="tpu_custom_call" | custom-call | flops 10737418240 | bytes 19922944 | tf_op jit(solution)/shard_map/product_tn/pallas_call | solution.py:131
  567.7 63.6 %reduce-scatter.5.cloned.1.call-done = bf16[768,512]{1,0:T(8,128)(2,1)} async-done(((bf16[6144,512]{1,0:T(8,128)(2,1)}), bf16[768,512]{1,0:T(8,128)(2,1)}) %reduce-scatter.5.cloned.1.call-update) | async-done | bytes 786448 | tf_op jit(solution)/shard_map/reduce_scatter | solution.py:662
  631.4 110.6 %reduce-scatter.9.cloned.1.call-done = bf16[1280,512]{1,0:T(8,128)(2,1)} async-done(((bf16[10240,512]{1,0:T(8,128)(2,1)}), bf16[1280,512]{1,0:T(8,128)(2,1)}) %reduce-scatter.9.cloned.1.call-update) | async-done | bytes 1310736 | tf_op jit(solution)/shard_map/reduce_scatter | solution.py:662
  742.1 10.9 %product_nn.7 = bf16[4,1024,512]{2,1,0:T(8,128)(2,1)} custom-call(bf16[1024,1536]{1,0:T(8,128)(2,1)} %get-tuple-element.20.grad_ref, bf16[4,2,1024,512]{3,2,1,0:T(8,128)(2,1)} %bitcast.289), custom_call_target="tpu_custom_call" | custom-call | flops 6442450944 | bytes 13631488 | tf_op jit(solution)/shard_map/product_nn/pallas_call | solution.py:103
  759.5 29.8 %collective-permute-done.42 = bf16[2,2,256,512]{3,2,0,1:T(8,128)(2,1)S(1)} collective-permute-done((bf16[2,2,256,512]{3,2,0,1:T(8,128)(2,1)S(1)}, bf16[2,2,256,512]{3,2,0,1:T(8,128)(2,1)S(1)}, u32[]{:S(2)}, u32[]{:S(2)}) %collective-permute-start.42) | collective-permute-done | bytes 1048608 | tf_op jit(solution)/shard_map/ppermute | solution.py:510
  800.9 10.1 %collective-permute-done.41 = bf16[2,256,512]{2,1,0:T(8,128)(2,1)S(1)} collective-permute-done((bf16[2,256,512]{2,1,0:T(8,128)(2,1)S(1)}, bf16[2,256,512]{2,1,0:T(8,128)(2,1)S(1)}, u32[]{:S(2)}, u32[]{:S(2)}) %collective-permute-start.41) | collective-permute-done | bytes 524320 | tf_op jit(solution)/shard_map/ppermute | solution.py:510
  825.8 23.1 %all-to-all-done.3 = bf16[4,256,512]{2,1,0:T(8,128)(2,1)S(1)} async-done(((bf16[4,256,512]{2,1,0:T(8,128)(2,1)}), bf16[4,256,512]{2,1,0:T(8,128)(2,1)S(1)}, u32[]{:S(2)}, u32[]{:S(2)}) %all-to-all-start.3) | async-done | bytes 1048608 | tf_op jit(solution)/shard_map/all_to_all | solution.py:577
  850.4 55.9 %all-reduce = (f32[4,512]{1,0:T(4,128)S(1)}, f32[4,512]{1,0:T(4,128)S(1)}, f32[32,32]{1,0:T(8,128)S(1)}) all-reduce(f32[4,512]{1,0:T(4,128)S(1)} %get-tuple-element.64, f32[4,512]{1,0:T(4,128)S(1)} %get-tuple-element.62, f32[32,32]{1,0:T(8,128)S(1)} %constant_dynamic-update-slice_fusion), channel_id=1, replica_groups=mesh['y'=2,'c'=2,'x'=2,'z'=4] {'y','c','x','z'}, use_global_device_ids=true, to_apply=%region_5.6 | all-reduce | flops 5120 | bytes 40960 | tf_op jit(solution)/shard_map/psum | solution.py:694
  (294 shorter events, 292.3 us)
Async XLA Ops:
  7.2 141.5 %all-gather.14.cloned.1.call-start = ((), (), s32[]{:S(2)}) async-start(), calls=%async_computation.8 | async-start | bytes 9437184 | tf_op jit(solution)/shard_map/all_gather | solution.py:605
  13.8 291.3 %all-gather.16.cloned.1.call-start = ((), (), s32[]{:S(2)}) async-start(), calls=%async_computation.9 | async-start | bytes 11796480 | tf_op jit(solution)/shard_map/all_gather | solution.py:605
  36.1 66.3 %all-to-all-start = ((bf16[4,256,512]{2,1,0:T(8,128)(2,1)}), bf16[4,256,512]{2,1,0:T(8,128)(2,1)}, u32[]{:S(2)}, u32[]{:S(2)}) async-start(bf16[4,256,512]{2,1,0:T(8,128)(2,1)} %bitcast.333), calls=%async_computation | async-start | bytes 2097152 | tf_op jit(solution)/shard_map/all_to_all | solution.py:571
  41.2 281.0 %all-gather.18.cloned.1.call-start = ((), (), s32[]{:S(2)}) async-start(), calls=%async_computation.10 | async-start | bytes 5898240 | tf_op jit(solution)/shard_map/all_gather | solution.py:605
  41.3 69.8 %collective-permute-start = (s32[2]{0:T(128)S(1)}, s32[2]{0:T(128)S(1)}, u32[]{:S(2)}, u32[]{:S(2)}) collective-permute-start(s32[2]{0:T(128)S(1)} %copy-done.22), channel_id=1, source_target_pairs={{0,16},{16,0},{1,17},{17,1},{2,18},{18,2},{3,19},{19,3},{4,20},{20... | collective-permute-start | bytes 32 | tf_op jit(solution)/shard_map/ppermute | solution.py:617
  45.0 81.2 %collective-permute-start.23 = (bf16[2,256,512]{2,1,0:T(8,128)(2,1)}, bf16[2,256,512]{2,1,0:T(8,128)(2,1)}, u32[]{:S(2)}, u32[]{:S(2)}) collective-permute-start(bf16[2,256,512]{2,1,0:T(8,128)(2,1)} %get-tuple-element.95), channel_id=1, source_target_pairs={{0,16},{16,0},{1,17},{17,1},{2,18},{18,2},{3,19},{19,3},{4,20},{20... | collective-permute-start | bytes 1572872 | tf_op jit(solution)/shard_map/ppermute | solution.py:510
  128.6 75.3 %all-to-all-start.2 = ((bf16[4,256,512]{2,1,0:T(8,128)(2,1)}), bf16[4,256,512]{2,1,0:T(8,128)(2,1)S(1)}, u32[]{:S(2)}, u32[]{:S(2)}) async-start(bf16[4,256,512]{2,1,0:T(8,128)(2,1)} %bitcast.75), calls=%async_computation.2 | async-start | bytes 2097152 | tf_op jit(solution)/shard_map/all_to_all | solution.py:571
  133.0 433.3 %reduce-scatter.7.cloned.1.call-start = ((), (), s32[]{:S(2)}) async-start(), calls=%async_computation.12 | async-start | bytes 2359296 | tf_op jit(solution)/shard_map/reduce_scatter | solution.py:662
  202.5 39.0 %collective-permute-start.8 = (bf16[2,2,256,512]{3,2,0,1:T(8,128)(2,1)}, bf16[2,2,256,512]{3,2,0,1:T(8,128)(2,1)}, u32[]{:S(2)}, u32[]{:S(2)}) collective-permute-start(bf16[2,2,256,512]{3,2,0,1:T(8,128)(2,1)} %copy_bitcast_fusion.8), channel_id=1, source_target_pairs={{0,4},{4,0},{1,5},{5,1},{2,6},{6,2},{3,7},{7,3},{8,12},{12,8},{9,1... | collective-permute-start | bytes 3145736 | tf_op jit(solution)/shard_map/ppermute | solution.py:510
  205.3 33.4 %collective-permute-start.27 = (bf16[2,256,512]{2,1,0:T(8,128)(2,1)}, bf16[2,256,512]{2,1,0:T(8,128)(2,1)}, u32[]{:S(2)}, u32[]{:S(2)}) collective-permute-start(bf16[2,256,512]{2,1,0:T(8,128)(2,1)} %get-tuple-element.90), channel_id=1, source_target_pairs={{0,16},{16,0},{1,17},{17,1},{2,18},{18,2},{3,19},{19,3},{4,20},{20... | collective-permute-start | bytes 1572872 | tf_op jit(solution)/shard_map/ppermute | solution.py:510
  206.9 64.0 %collective-permute-start.28 = (bf16[2,256,512]{2,1,0:T(8,128)(2,1)}, bf16[2,256,512]{2,1,0:T(8,128)(2,1)S(1)}, u32[]{:S(2)}, u32[]{:S(2)}) collective-permute-start(bf16[2,256,512]{2,1,0:T(8,128)(2,1)} %get-tuple-element.90), channel_id=1, source_target_pairs={{0,4},{4,0},{1,5},{5,1},{2,6},{6,2},{3,7},{7,3},{8,12},{12,8},{9,1... | collective-permute-start | bytes 1572872 | tf_op jit(solution)/shard_map/ppermute | solution.py:510
  207.5 43.8 %collective-permute-start.25 = (bf16[2,256,512]{2,1,0:T(8,128)(2,1)}, bf16[2,256,512]{2,1,0:T(8,128)(2,1)S(1)}, u32[]{:S(2)}, u32[]{:S(2)}) collective-permute-start(bf16[2,256,512]{2,1,0:T(8,128)(2,1)} %get-tuple-element.91), channel_id=1, source_target_pairs={{0,4},{4,0},{1,5},{5,1},{2,6},{6,2},{3,7},{7,3},{8,12},{12,8},{9,1... | collective-permute-start | bytes 1572872 | tf_op jit(solution)/shard_map/ppermute | solution.py:510
  227.4 41.9 %collective-permute-start.24 = (bf16[2,256,512]{2,1,0:T(8,128)(2,1)}, bf16[2,256,512]{2,1,0:T(8,128)(2,1)S(1)}, u32[]{:S(2)}, u32[]{:S(2)}) collective-permute-start(bf16[2,256,512]{2,1,0:T(8,128)(2,1)} %get-tuple-element.91), channel_id=1, source_target_pairs={{0,16},{16,0},{1,17},{17,1},{2,18},{18,2},{3,19},{19,3},{4,20},{20... | collective-permute-start | bytes 1572872 | tf_op jit(solution)/shard_map/ppermute | solution.py:510
  373.7 33.1 %collective-permute-start.18 = (bf16[2,2,256,512]{3,2,0,1:T(8,128)(2,1)S(1)}, bf16[2,2,256,512]{3,2,0,1:T(8,128)(2,1)S(1)}, u32[]{:S(2)}, u32[]{:S(2)}) collective-permute-start(bf16[2,2,256,512]{3,2,0,1:T(8,128)(2,1)S(1)} %copy_bitcast_fusion.6), channel_id=1, source_target_pairs={{0,4},{4,0},{1,5},{5,1},{2,6},{6,2},{3,7},{7,3},{8,12},{12,8},{9,1... | collective-permute-start | bytes 3145736 | tf_op jit(solution)/shard_map/ppermute | solution.py:510
  466.3 100.7 %reduce-scatter.11.cloned.1.call-start = ((), (), s32[]{:S(2)}) async-start(), calls=%async_computation.14 | async-start | bytes 5898240 | tf_op jit(solution)/shard_map/reduce_scatter | solution.py:662
  476.5 154.9 %reduce-scatter.5.cloned.1.call-start = ((), (), s32[]{:S(2)}) async-start(), calls=%async_computation.11 | async-start | bytes 7077888 | tf_op jit(solution)/shard_map/reduce_scatter | solution.py:662
  549.2 192.8 %reduce-scatter.9.cloned.1.call-start = ((), (), s32[]{:S(2)}) async-start(), calls=%async_computation.13 | async-start | bytes 11796480 | tf_op jit(solution)/shard_map/reduce_scatter | solution.py:662
  566.2 342.7 %all-gather.22.cloned.1.call-start = ((), (), s32[]{:S(2)}) async-start(), calls=%async_computation.16 | async-start | bytes 1310720 | tf_op jit(solution)/shard_map/all_gather | solution.py:665
  567.0 344.8 %all-gather.26.cloned.1.call-start = ((), (), s32[]{:S(2)}) async-start(), calls=%async_computation.18 | async-start | bytes 3276800 | tf_op jit(solution)/shard_map/all_gather | solution.py:665
  567.7 348.9 %all-gather.20.cloned.1.call-start = ((), (), s32[]{:S(2)}) async-start(), calls=%async_computation.15 | async-start | bytes 3932160 | tf_op jit(solution)/shard_map/all_gather | solution.py:665
  631.4 292.9 %all-gather.24.cloned.1.call-start = ((), (), s32[]{:S(2)}) async-start(), calls=%async_computation.17 | async-start | bytes 6553600 | tf_op jit(solution)/shard_map/all_gather | solution.py:665
  755.6 33.7 %collective-permute-start.42 = (bf16[2,2,256,512]{3,2,0,1:T(8,128)(2,1)S(1)}, bf16[2,2,256,512]{3,2,0,1:T(8,128)(2,1)S(1)}, u32[]{:S(2)}, u32[]{:S(2)}) collective-permute-start(bf16[2,2,256,512]{3,2,0,1:T(8,128)(2,1)S(1)} %copy_bitcast_fusion.1), channel_id=1, source_target_pairs={{0,16},{16,0},{1,17},{17,1},{2,18},{18,2},{3,19},{19,3},{4,20},{20... | collective-permute-start | bytes 3145736 | tf_op jit(solution)/shard_map/ppermute | solution.py:510
  758.1 37.8 %collective-permute-start.40 = (bf16[2,2,256,512]{3,2,0,1:T(8,128)(2,1)}, bf16[2,2,256,512]{3,2,0,1:T(8,128)(2,1)}, u32[]{:S(2)}, u32[]{:S(2)}) collective-permute-start(bf16[2,2,256,512]{3,2,0,1:T(8,128)(2,1)} %copy_bitcast_fusion.2), channel_id=1, source_target_pairs={{0,4},{4,0},{1,5},{5,1},{2,6},{6,2},{3,7},{7,3},{8,12},{12,8},{9,1... | collective-permute-start | bytes 3145736 | tf_op jit(solution)/shard_map/ppermute | solution.py:510
  849.0 58.5 %collective-permute-start.44 = (bf16[2,256,512]{2,1,0:T(8,128)(2,1)S(1)}, bf16[2,256,512]{2,1,0:T(8,128)(2,1)S(1)}, u32[]{:S(2)}, u32[]{:S(2)}) collective-permute-start(bf16[2,256,512]{2,1,0:T(8,128)(2,1)S(1)} %get-tuple-element.83), channel_id=1, source_target_pairs={{0,16},{16,0},{1,17},{17,1},{2,18},{18,2},{3,19},{19,3},{4,20},{20... | collective-permute-start | bytes 1572872 | tf_op jit(solution)/shard_map/ppermute | solution.py:510
  (62 other events, 1013.2 us)
Sparse Core Ops, SparseCore 0:
  13.9 107.2 all-gather.13
  123.3 111.3 all-gather.15
  236.3 53.4 all-gather.17
  466.4 33.2 reduce-scatter.6
  502.4 58.5 reduce-scatter.10
  563.2 68.1 reduce-scatter.4
  634.3 107.7 reduce-scatter.8
  743.6 15.9 all-gather.21
  761.1 34.1 all-gather.25
  796.7 29.9 all-gather.19
  828.3 52.0 all-gather.23

commit v2 on v1

v2 whole, which is shorter than its diff:
```python
import functools
import math

import jax
import jax.numpy as jnp
from jax import lax
from jax.experimental import pallas as pl
from jax.experimental.pallas import tpu as pltpu
from jax.sharding import Mesh
from jax.sharding import PartitionSpec as P

norm_eps = 1e-06
masked_score = -1e30
bucket_edges = (12, 16, 23, 32, 46, 64, 91)
BF = jnp.bfloat16
F32 = jnp.float32
LB = 128
VMEM = 60 * 1024 * 1024
swap = [(0, 1), (1, 0)]
gelu_a = math.sqrt(2.0 / math.pi)
gelu_b = 0.044715


def bucket_index(offset):
    magnitude = jnp.abs(offset)
    far_bucket = 8 + sum(((magnitude >= boundary).astype(jnp.int32) for boundary in bucket_edges))
    near_bucket = jnp.where(magnitude < 8, magnitude, far_bucket)
    return near_bucket + 16 * (offset > 0).astype(jnp.int32)


def cost(flops, moved):
    return pl.CostEstimate(flops=int(flops), bytes_accessed=int(moved), transcendentals=0)


def params(steps):
    return pltpu.CompilerParams(
        dimension_semantics=("arbitrary",) * steps, vmem_limit_bytes=VMEM
    )


def dot_nt(a, b):
    return lax.dot_general(a, b, (((1,), (1,)), ((), ())), preferred_element_type=F32)


def dot_nn(a, b):
    return lax.dot_general(a, b, (((1,), (0,)), ((), ())), preferred_element_type=F32)


def spot_of(starts_ref, d, count):
    return pl.ds(pl.multiple_of(starts_ref[d], 256), count)


def piece_specs(pieces):
    shape = pieces[0].shape
    return [pl.BlockSpec(shape, lambda *_: (0, 0, 0)) for _ in pieces]


def nt_sum(piece_refs, d, w_of):
    half = piece_refs[0].shape[0]
    acc = None
    for z in range(2 * half):
        part = dot_nt(piece_refs[4 * (z // half) + d][z % half], w_of(z))
        acc = part if acc is None else acc + part
    return acc


def nt_kernel(starts_ref, *refs):
    pieces, (w_ref, out_ref) = refs[:8], refs[8:]
    for d in range(4):
        acc = nt_sum(pieces, d, lambda z: w_ref[z, 0])
        out_ref[spot_of(starts_ref, d, acc.shape[0]), :] = acc.astype(BF)


def mm_nt(pieces, w, first, rows, starts):
    nz, nc, _, width = w.shape
    total = 4 * pieces[0].shape[1]
    count, skip = rows // 256, first // 256
    return pl.pallas_call(
        nt_kernel,
        grid=(nc, count),
        in_specs=[pl.BlockSpec(memory_space=pltpu.SMEM)]
        + piece_specs(pieces)
        + [pl.BlockSpec((nz, 1, 256, width), lambda c, i: (0, c, skip + i, 0))],
        out_specs=pl.BlockSpec((total, 256), lambda c, i: (0, c * count + i)),
        out_shape=jax.ShapeDtypeStruct((total, nc * rows), BF),
        compiler_params=params(2),
        cost_estimate=cost(
            2 * nz * total * width * nc * rows, 2 * nz * width * (total + nc * rows) + 2 * total * nc * rows
        ),
        name="product_nt",
    )(starts, *pieces, w)


def nn_kernel(count, starts_ref, *refs):
    grads, (w_ref, low_out, low_keep, high_out, high_keep) = refs[:count], refs[count:]
    nc, rows, width = w_ref.shape[1:]
    t = grads[0].shape[0] // 4
    in_low = pl.program_id(0) < pl.num_programs(0) // 2
    for d in range(4):
        spot = spot_of(starts_ref, d, t)
        if count == 1:
            value = dot_nn(grads[0][spot, :], w_ref[0].reshape(nc * rows, width))
        else:
            value = sum(dot_nn(grads[c][spot, :], w_ref[0, c]) for c in range(count))
        value = value.astype(BF)
        dx, dy = d // 2, d % 2

        @pl.when(in_low)
        def _():
            (low_out if dx else low_keep)[dy, 0] = value

        @pl.when(jnp.logical_not(in_low))
        def _():
            (high_out if dy else high_keep)[dx, 0] = value


def mm_nn(grads, w, first, rows, starts):
    total = grads[0].shape[0]
    nz, nc, _, width = w.shape
    skip, half, t = first // rows, nz // 2, total // 4
    low = pl.BlockSpec((2, 1, t, width), lambda z: (0, jnp.minimum(z, half - 1), 0, 0))
    high = pl.BlockSpec((2, 1, t, width), lambda z: (0, jnp.maximum(z - half, 0), 0, 0))
    return pl.pallas_call(
        functools.partial(nn_kernel, len(grads)),
        grid=(nz,),
        in_specs=[pl.BlockSpec(memory_space=pltpu.SMEM)]
        + [pl.BlockSpec(grad.shape, lambda z: (0, 0)) for grad in grads]
        + [pl.BlockSpec((1, nc, rows, width), lambda z: (z, 0, skip, 0))],
        out_specs=[low, low, high, high],
        out_shape=[jax.ShapeDtypeStruct((2, half, t, width), BF)] * 4,
        compiler_params=params(1),
        cost_estimate=cost(
            2 * nz * total * width * nc * rows, 2 * nz * width * (total + nc * rows) + 2 * total * nc * rows
        ),
        name="product_nn",
    )(starts, *grads, w)


def tn_kernel(count, starts_ref, *refs):
    grads, pieces, out_ref = refs[:count], refs[count:-1], refs[-1]
    half, t, _ = pieces[0].shape

    def one(grad_ref):
        turned = [grad_ref[spot_of(starts_ref, d, t), :].T for d in range(4)]
        for z in range(2 * half):
            acc = dot_nn(turned[0], pieces[4 * (z // half)][z % half])
            for d in range(1, 4):
                acc += dot_nn(turned[d], pieces[4 * (z // half) + d][z % half])
            out_ref[z] = acc.astype(BF)

    if count == 1:
        one(grads[0])
    else:
        for c in range(count):

            @pl.when(pl.program_id(0) // (pl.num_programs(0) // count) == c)
            def _():
                one(grads[c])


def mm_tn(grads, pieces, starts):
    total, rows = grads[0].shape
    half, _, width = pieces[0].shape
    nz, count = 2 * half, len(grads)
    block = next(b for b in (640, 384, 256) if rows % b == 0)
    steps = rows // block

    def spec(c):
        return pl.BlockSpec((total, block), lambda i: (0, jnp.clip(i - c * steps, 0, steps - 1)))

    return pl.pallas_call(
        functools.partial(tn_kernel, count),
        grid=(count * steps,),
        in_specs=[pl.BlockSpec(memory_space=pltpu.SMEM)]
        + [spec(c) for c in range(count)]
        + piece_specs(pieces),
        out_specs=pl.BlockSpec((nz, block, width), lambda i: (0, i, 0)),
        out_shape=jax.ShapeDtypeStruct((nz, count * rows, width), BF),
        compiler_params=params(1),
        cost_estimate=cost(
            2 * nz * total * width * count * rows, 2 * nz * width * (total + count * rows) + 2 * total * count * rows
        ),
        name="product_tn",
    )(starts, *grads, *pieces)


def gelu_parts(gate):
    curve = jnp.tanh(gelu_a * (gate + gelu_b * gate * gate * gate))
    value = 0.5 * gate * (1.0 + curve)
    slope = 0.5 * (1.0 + curve) + 0.5 * gate * (1.0 - curve * curve) * gelu_a * (
        1.0 + 3.0 * gelu_b * gate * gate
    )
    return value, slope


def ffn_in_kernel(starts_ref, *refs):
    pieces, (w_ref, gate_ref, up_ref, active_ref) = refs[:8], refs[8:]
    _, _, _, block, width = w_ref.shape
    for d in range(4):
        acc = nt_sum(pieces, d, lambda z: w_ref[z, 0].reshape(2 * block, width))
        spot = spot_of(starts_ref, d, acc.shape[0])
        gate, up = acc[:, :block], acc[:, block:]
        value = 0.5 * gate * (1.0 + jnp.tanh(gelu_a * (gate + gelu_b * gate * gate * gate)))
        gate_ref[spot, :] = gate.astype(BF)
        up_ref[spot, :] = up.astype(BF)
        active_ref[spot, :] = (value * up).astype(BF)


def ffn_in(pieces, w, starts):
    nz, nc, rows, width = w.shape
    half, total = rows // 2, 4 * pieces[0].shape[1]
    count = half // 128
    block = pl.BlockSpec((total, 128), lambda c, i: (0, c * count + i))
    return pl.pallas_call(
        ffn_in_kernel,
        grid=(nc, count),
        in_specs=[pl.BlockSpec(memory_space=pltpu.SMEM)]
        + piece_specs(pieces)
        + [pl.BlockSpec((nz, 1, 2, 128, width), lambda c, i: (0, c, 0, i, 0))],
        out_specs=[block, block, block],
        out_shape=[jax.ShapeDtypeStruct((total, nc * half), BF)] * 3,
        compiler_params=params(2),
        cost_estimate=cost(
            2 * nz * total * width * nc * rows, 2 * nz * width * (total + nc * rows) + 3 * total * nc * rows
        ),
        name="ffn_in",
    )(starts, *pieces, w.reshape(nz, nc, 2, half, width))


def ffn_back_kernel(starts_ref, *refs):
    pieces, (w_ref, gate_ref, up_ref, out_ref) = refs[:8], refs[8:]
    half = w_ref.shape[2]
    for d in range(4):
        acc = nt_sum(pieces, d, lambda z: w_ref[z, 0])
        spot = spot_of(starts_ref, d, acc.shape[0])
        value, slope = gelu_parts(gate_ref[spot, :].astype(F32))
        out_ref[spot, :half] = (acc * up_ref[spot, :].astype(F32) * slope).astype(BF)
        out_ref[spot, half:] = (acc * value).astype(BF)


def ffn_back(pieces, w, gate, up, starts):
    nz, nc, half, width = w.shape
    total = gate.shape[0]
    kept = pl.BlockSpec((total, half), lambda c: (0, c))
    return pl.pallas_call(
        ffn_back_kernel,
        grid=(nc,),
        in_specs=[pl.BlockSpec(memory_space=pltpu.SMEM)]
        + piece_specs(pieces)
        + [pl.BlockSpec((nz, 1, half, width), lambda c: (0, c, 0, 0)), kept, kept],
        out_specs=pl.BlockSpec((total, 2 * half), lambda c: (0, c)),
        out_shape=jax.ShapeDtypeStruct((total, nc * 2 * half), BF),
        compiler_params=params(1),
        cost_estimate=cost(
            2 * nz * total * width * nc * half, 2 * nz * width * (total + nc * half) + 8 * total * nc * half
        ),
        name="ffn_back",
    )(starts, *pieces, w, gate, up)


def mm_nt_plain(act, w, first, rows, starts):
    part = lax.slice_in_dim(w, first, first + rows, axis=2)
    out = jnp.einsum("ztf,zcrf->tcr", act, part, preferred_element_type=F32)
    return out.astype(BF).reshape(act.shape[1], -1)


def mm_nn_plain(grads, w, first, rows, starts):
    grad = grads[0]
    part = lax.slice_in_dim(w, first, first + rows, axis=2)
    split = grad.reshape(grad.shape[0], w.shape[1], rows)
    out = jnp.einsum("tcr,zcrf->ztf", split, part, preferred_element_type=F32)
    return [out.astype(BF)]


def mm_tn_plain(grads, act, starts):
    return jnp.einsum("tr,ztf->zrf", grads[0], act, preferred_element_type=F32).astype(BF)


def ffn_in_plain(act, w, starts):
    _, nc, rows, _ = w.shape
    total = act.shape[1]
    both = jnp.einsum("ztf,zcrf->tcr", act, w, preferred_element_type=F32)
    gate, up = both[:, :, : rows // 2], both[:, :, rows // 2 :]
    value, _ = gelu_parts(gate)
    return [part.astype(BF).reshape(total, -1) for part in (gate, up, value * up)]


def ffn_back_plain(act, w, gate, up, starts):
    total, nc = gate.shape[0], w.shape[1]
    grad = jnp.einsum("ztf,zcrf->tcr", act, w, preferred_element_type=F32)
    value, slope = gelu_parts(gate.astype(F32).reshape(grad.shape))
    both = [grad * up.astype(F32).reshape(grad.shape) * slope, grad * value]
    return jnp.concatenate(both, axis=2).astype(BF).reshape(total, -1)


def near_buckets(tile, total):
    first = (total // LB - 2 + tile) * LB
    rows = lax.broadcasted_iota(jnp.int32, (LB, LB), 0)
    lanes = lax.broadcasted_iota(jnp.int32, (LB, LB), 1)
    return bucket_index(first + rows - (total - LB) - lanes)


def build_strips(table_ref, strip_ref, total, group):
    heads = strip_ref.shape[0]
    near = (total // LB - 2) * LB
    for h in range(heads):
        head = group * heads + h
        strip_ref[h, :near] = jnp.full((near, LB), table_ref[head, 15], F32)
        strip_ref[h, near + 3 * LB :] = jnp.full((near, LB), table_ref[head, 31], F32)

    def one_tile(tile, _):
        index = near_buckets(tile, total)
        vals = [jnp.full((LB, LB), table_ref[group * heads + h, 0], F32) for h in range(heads)]
        for b in range(1, 32):
            hit = index == b
            vals = [
                jnp.where(hit, table_ref[group * heads + h, b], vals[h]) for h in range(heads)
            ]
        for h in range(heads):
            strip_ref[h, pl.ds(pl.multiple_of(near + tile * LB, LB), LB)] = vals[h]
        return 0

    lax.fori_loop(0, 3, one_tile, 0)


def head_lanes(shape, h):
    lanes = lax.broadcasted_iota(jnp.int32, shape, 1)
    return lanes // 64 == h, lanes == ((h + 1) % 4) * 64


def mask_keys(keys, length, h):
    own, spare = head_lanes(keys.shape, h)
    dead = lax.broadcasted_iota(jnp.int32, keys.shape, 0) >= length
    mask = jnp.where(jnp.logical_and(spare, dead), masked_score, 0.0)
    return jnp.where(own, keys.astype(F32), mask).astype(BF)


def with_one(queries, h):
    _, spare = head_lanes(queries.shape, h)
    return jnp.where(spare, 1.0, queries.astype(F32)).astype(BF)


def own_lanes(values, h):
    own, _ = head_lanes(values.shape, h)
    return jnp.where(own, values.astype(F32), 0.0).astype(BF)


def block_bias(strip_ref, h, block, total):
    first = total - LB - 2 * block * LB
    left = strip_ref[h, pl.ds(pl.multiple_of(first, LB), total)]
    right = strip_ref[h, pl.ds(pl.multiple_of(first - LB, LB), total)]
    return jnp.concatenate([left, right], axis=1)


def attend_kernel(group, length_ref, table_ref, q_ref, k_ref, v_ref, out_ref, lse_ref, strip, heads_k, turned_v, turned_out):
    total = q_ref.shape[0]
    heads = strip.shape[0]
    build_strips(table_ref, strip, total, group)
    turned_v[...] = v_ref[...].astype(F32).T.astype(BF)
    for h in range(heads):
        heads_k[h] = mask_keys(k_ref[...], length_ref[0], h)

    def one_block(block, _):
        spot = pl.ds(pl.multiple_of(block * 256, 256), 256)
        queries = q_ref[spot]
        for h in range(heads):
            scores = dot_nt(heads_k[h], with_one(queries, h)) + block_bias(strip, h, block, total)
            largest = jnp.max(scores, axis=0, keepdims=True)
            raised = jnp.exp(scores - largest)
            totals = jnp.sum(raised, axis=0, keepdims=True)
            out = dot_nn(turned_v[h * 64 : (h + 1) * 64], raised.astype(BF))
            turned_out[h * 64 : (h + 1) * 64, spot] = out * (1.0 / totals)
            lse_ref[h : h + 1, spot] = largest + jnp.log(totals)
        return 0

    lax.fori_loop(0, total // 256, one_block, 0)
    out_ref[...] = turned_out[...].T.astype(BF)


def attend_back_kernel(
    group, length_ref, table_ref, q_ref, k_ref, v_ref, grad_ref, lse_ref, out_ref, table_grad_ref,
    strip, strip_grad, heads_k, turned_k, turned_q, ds_ref, p_ref, dk_ref, dv_ref,
):
    total = q_ref.shape[0]
    heads = strip.shape[0]
    build_strips(table_ref, strip, total, group)
    strip_grad[...] = jnp.zeros_like(strip_grad)
    dk_ref[...] = jnp.zeros_like(dk_ref)
    dv_ref[...] = jnp.zeros_like(dv_ref)
    turned_k[...] = k_ref[...].astype(F32).T.astype(BF)
    for h in range(heads):
        heads_k[h] = mask_keys(k_ref[...], length_ref[0], h)

    def one_block(block, _):
        spot = pl.ds(pl.multiple_of(block * 256, 256), 256)
        queries, grads = q_ref[spot], grad_ref[spot]
        own_q, own_g = [], []
        for h in range(heads):
            own_q.append(own_lanes(queries, h))
            own_g.append(own_lanes(grads, h))
            scores = dot_nt(heads_k[h], with_one(queries, h)) + block_bias(strip, h, block, total)
            probs = jnp.exp(scores - lse_ref[h : h + 1, spot])
            weighed = probs * dot_nt(v_ref[...], own_g[h])
            delta = jnp.sum(weighed, axis=0, keepdims=True)
            grad_scores = weighed - probs * delta
            first = total - LB - 2 * block * LB
            left = pl.ds(pl.multiple_of(first, LB), total)
            right = pl.ds(pl.multiple_of(first - LB, LB), total)
            strip_grad[h, left] += grad_scores[:, :LB]
            strip_grad[h, right] += grad_scores[:, LB:]
            rounded = grad_scores.astype(BF)
            ds_ref[:, h * 256 : (h + 1) * 256] = rounded
            p_ref[:, h * 256 : (h + 1) * 256] = probs.astype(BF)
            turned_q[h * 64 : (h + 1) * 64, spot] = dot_nn(turned_k[h * 64 : (h + 1) * 64], rounded)
        dk_ref[...] += dot_nn(ds_ref[...], jnp.concatenate(own_q, axis=0))
        dv_ref[...] += dot_nn(p_ref[...], jnp.concatenate(own_g, axis=0))
        return 0

    lax.fori_loop(0, total // 256, one_block, 0)
    out_ref[:, :256] = turned_q[...].T.astype(BF)
    out_ref[:, 256:512] = dk_ref[...].astype(BF)
    out_ref[:, 512:] = dv_ref[...].astype(BF)

    near = (total // LB - 2) * LB
    for h in range(heads):
        table_grad_ref[h] = jnp.zeros((32, LB), F32)
        table_grad_ref[h, 15:16] = jnp.sum(strip_grad[h, :near], axis=0, keepdims=True)
        table_grad_ref[h, 31:32] = jnp.sum(strip_grad[h, near + 3 * LB :], axis=0, keepdims=True)

    def one_tile(tile, _):
        index = near_buckets(tile, total)
        spot = pl.ds(pl.multiple_of(near + tile * LB, LB), LB)
        for h in range(heads):
            grads = strip_grad[h, spot]
            for b in range(32):
                picked = jnp.where(index == b, grads, 0.0)
                table_grad_ref[h, b : b + 1] += jnp.sum(picked, axis=0, keepdims=True)
        return 0

    lax.fori_loop(0, 3, one_tile, 0)


def block_specs(total, group):
    def spec(i):
        return pl.BlockSpec((total, 256), lambda _: (0, 3 * group + i))

    smem = pl.BlockSpec(memory_space=pltpu.SMEM)
    return [smem, smem, spec(0), spec(1), spec(2)]


def attend(group, projected, length, table):
    total = projected.shape[0]
    heads = 4
    return pl.pallas_call(
        functools.partial(attend_kernel, group),
        grid=(1,),
        in_specs=block_specs(total, group),
        out_specs=[
            pl.BlockSpec((total, 256), lambda _: (0, 0)),
            pl.BlockSpec((8, total), lambda _: (0, 0)),
        ],
        out_shape=[
            jax.ShapeDtypeStruct((total, 256), BF),
            jax.ShapeDtypeStruct((8, total), F32),
        ],
        scratch_shapes=[
            pltpu.VMEM((heads, 2 * total - LB, LB), F32),
            pltpu.VMEM((heads, total, 256), BF),
            pltpu.VMEM((256, total), BF),
            pltpu.VMEM((256, total), F32),
        ],
        compiler_params=params(1),
        cost_estimate=cost(heads * total * total * 2 * 256 * 2, 4 * total * 256 * 2),
        name="attend",
    )(length, table, projected, projected, projected)


def attend_back(group, projected, length, table, grad_out, lse):
    total = projected.shape[0]
    heads = 4
    return pl.pallas_call(
        functools.partial(attend_back_kernel, group),
        grid=(1,),
        in_specs=block_specs(total, group)
        + [
            pl.BlockSpec((total, 256), lambda _: (0, group)),
            pl.BlockSpec((8, total), lambda _: (0, 0)),
        ],
        out_specs=[
            pl.BlockSpec((total, 768), lambda _: (0, 0)),
            pl.BlockSpec((heads, 32, LB), lambda _: (0, 0, 0)),
        ],
        out_shape=[
            jax.ShapeDtypeStruct((total, 768), BF),
            jax.ShapeDtypeStruct((heads, 32, LB), F32),
        ],
        scratch_shapes=[
            pltpu.VMEM((heads, 2 * total - LB, LB), F32),
            pltpu.VMEM((heads, 2 * total - LB, LB), F32),
            pltpu.VMEM((heads, total, 256), BF),
            pltpu.VMEM((256, total), BF),
            pltpu.VMEM((256, total), F32),
            pltpu.VMEM((total, heads * 256), BF),
            pltpu.VMEM((total, heads * 256), BF),
            pltpu.VMEM((total, 256), F32),
            pltpu.VMEM((total, 256), F32),
        ],
        compiler_params=params(1),
        cost_estimate=cost(heads * total * total * 2 * 256 * 5, 8 * total * 256 * 2),
        name="attend_back",
    )(length, table, projected, projected, projected, grad_out, lse)


def split_heads(projected, groups, heads):
    parts = projected.reshape(projected.shape[0], groups, 3, heads, 64)
    return [parts[:, :, i].reshape(projected.shape[0], groups * heads, 64) for i in range(3)]


def plain_scores(queries, keys, length, table):
    slots = jnp.arange(keys.shape[0], dtype=jnp.int32)
    picked = (bucket_index(slots[None, :] - slots[:, None])[:, :, None] == jnp.arange(32)).astype(F32)
    bias = jnp.einsum("qkb,hb->hqk", picked, table, precision=lax.Precision.HIGHEST)
    scores = jnp.einsum("qhs,khs->hqk", queries, keys, preferred_element_type=F32) + bias
    return jnp.where(slots < length[0], scores, masked_score), picked


def attend_plain(projected, length, table, groups, heads):
    queries, keys, values = split_heads(projected, groups, heads)
    scores, _ = plain_scores(queries, keys, length, table)
    lse = jax.nn.logsumexp(scores, axis=2)
    probs = jnp.exp(scores - lse[:, :, None]).astype(BF)
    out = jnp.einsum("hqk,khs->qhs", probs, values, preferred_element_type=F32)
    return out.astype(BF).reshape(projected.shape[0], -1), lse


def attend_back_plain(projected, length, table, grad_out, lse, groups, heads):
    total = projected.shape[0]
    queries, keys, values = split_heads(projected, groups, heads)
    grads = grad_out.reshape(queries.shape)
    scores, picked = plain_scores(queries, keys, length, table)
    probs = jnp.exp(scores - lse[:, :, None])
    weighed = probs * jnp.einsum("qhs,khs->hqk", grads, values, preferred_element_type=F32)
    wide = weighed - probs * jnp.sum(weighed, axis=2, keepdims=True)
    rounded = wide.astype(BF)
    parts = [
        jnp.einsum("hqk,khs->qhs", rounded, keys, preferred_element_type=F32),
        jnp.einsum("hqk,qhs->khs", rounded, queries, preferred_element_type=F32),
        jnp.einsum("hqk,qhs->khs", probs.astype(BF), grads, preferred_element_type=F32),
    ]
    parts = [part.astype(BF).reshape(total, groups, 1, heads * 64) for part in parts]
    table_grad = jnp.einsum("hqk,qkb->hb", wide, picked, precision=lax.Precision.HIGHEST)
    return (
        jnp.concatenate(parts, axis=2).reshape(total, -1),
        table_grad.reshape(groups * heads, 32, 1),
    )


def hop(value, axis):
    return lax.ppermute(value, axis, swap)


def pick(value, index, axis):
    return lax.dynamic_index_in_dim(value, index, axis, keepdims=False)


def paired(mine, other, axis, place=0):
    return jnp.where(
        lax.axis_index(axis) == 0,
        jnp.stack([mine, other], axis=place),
        jnp.stack([other, mine], axis=place),
    )


def after(value, *others):
    return lax.optimization_barrier((value, *others))[0]


def gather_plain(part):
    return lax.all_gather(part, ("x", "y"), axis=1, tiled=True), (), ()


def gather_tokens(part):
    half = part.shape[0] // 2
    low, high = part[:half], part[half:]
    low_x, high_y = hop(low, "x"), hop(high, "y")
    low_y, high_x = hop(low, "y"), hop(high, "x")
    low_xy, high_xy = hop(low_x, "y"), hop(high_y, "x")
    pieces = [low, low_y, low_x, low_xy, high, high_y, high_x, high_xy]
    return pieces, (low_x, high_y), (low_y, low_xy, high_x, high_xy)


def scatter_plain(parts):
    whole = parts[0].astype(F32)
    return lax.psum_scatter(whole, ("x", "y"), scatter_dimension=1, tiled=True), (), ()


def scatter_tokens(parts):
    low_out, low_keep, high_out, high_keep = parts
    low_in, high_in = hop(low_out, "x"), hop(high_out, "y")

    def add(keep, arrived, index):
        return keep[index].astype(F32) + arrived[index].astype(F32)

    low_last = hop(add(low_keep, low_in, 1).astype(BF), "y")
    high_last = hop(add(high_keep, high_in, 1).astype(BF), "x")
    low = add(low_keep, low_in, 0) + low_last.astype(F32)
    high = add(high_keep, high_in, 0) + high_last.astype(F32)
    return jnp.concatenate([low, high], axis=0), (low_in, high_in), (low_last, high_last)


def place_kernel(write, here_ref, *refs):
    pieces, outs = refs[:4], refs[4:]
    step = pl.program_id(0)
    for near in range(4):
        y = here_ref[0] if near < 2 else 1 - here_ref[0]
        c = here_ref[1] if near % 2 == 0 else 1 - here_ref[1]

        @pl.when(step == 2 * y + c)
        def _():
            write(pieces[near], outs)


def place(pieces, here, shapes, write):
    return pl.pallas_call(
        functools.partial(place_kernel, write),
        grid=(4,),
        in_specs=[pl.BlockSpec(memory_space=pltpu.SMEM)]
        + [pl.BlockSpec(piece.shape, lambda q: (0, 0)) for piece in pieces],
        out_specs=[
            pl.BlockSpec(shape, lambda q, rank=len(shape): (q,) + (0,) * (rank - 1)) for shape in shapes
        ],
        out_shape=[jax.ShapeDtypeStruct((4 * shape[0], *shape[1:]), F32) for shape in shapes],
        compiler_params=params(1),
        cost_estimate=cost(0, 20 * pieces[0].size),
        name="place",
    )(here, *pieces)


def share(part):
    over_y = hop(part, "y")
    return [part, hop(part, "c"), over_y, hop(over_y, "c")], over_y


def share_plain(part):
    return lax.all_gather(part, ("y", "c"), axis=0), part


def to_groups(halves, other, extra):
    count, _, t, width = halves.shape
    y = lax.axis_index("y")
    both = paired(pick(halves, y, 1), other, "y").reshape(2 * count, t, width)
    if extra is not None:
        wide = jnp.broadcast_to(extra[None], (2 * count, *extra.shape))
        both = jnp.concatenate([both, wide], axis=1)
    return lax.all_to_all(both, "z", 0, 0, tiled=True)


def from_groups(mine):
    nz, t, width = mine.shape
    y = lax.axis_index("y")
    back = lax.all_to_all(mine, "z", 0, 0, tiled=True).reshape(2, nz // 2, t, width)
    other = hop(pick(back, 1 - y, 0), "y")
    both = paired(pick(back, y, 0), other, "y")
    return both.transpose(1, 0, 2, 3).reshape(nz // 2, 2 * t, width)


def sum_all(value, nx, nz):
    value = value + hop(value, "c")
    value = value + hop(value, "y")
    value = value + hop(value, "x") if nx == 2 else lax.psum(value, "x")
    step = 1
    while step < nz:
        value = value + lax.ppermute(value, "z", [(i, i ^ step) for i in range(nz)])
        step *= 2
    return value


def body(
    nx, nz, nc, inputs, lengths, attn_gain, ffn_gain, query_key, value_proj, out_proj, gate_up, down_proj, bias_table, cotangent
):
    x, y = lax.axis_index("x"), lax.axis_index("y")
    c, z = lax.axis_index("c"), lax.axis_index("z")
    width = inputs.shape[2]
    features = nz * width
    quarter = y * nc + c
    parts = 2 * nc
    buckets, mine = bias_table.shape
    count = inputs.shape[1] // 2

    stored_in = inputs.reshape(inputs.shape[0], 2, count, width)
    stored_cot = cotangent.reshape(stored_in.shape)
    leaving = pick(stored_in, 1 - y, 1)
    small = jnp.concatenate(
        [attn_gain[None], ffn_gain[None], jnp.pad(bias_table.reshape(1, -1), ((0, 0), (0, width - buckets * mine)))]
    )
    small = jnp.pad(small, ((0, 5), (0, 0)))

    query_key_rows = jnp.transpose(query_key, (1, 2, 3, 0))
    value_rows = jnp.transpose(value_proj, (1, 2, 0))
    gate_up_rows = jnp.transpose(gate_up, (1, 2, 3, 0))
    heads = value_rows.shape[0] // parts
    units = gate_up_rows.shape[0] // parts
    unit = gate_up_rows.shape[2]
    local_heads = nc * heads

    def own(rows, size):
        return lax.dynamic_slice_in_dim(rows, quarter * size, size, 0)

    def flat(rows):
        return rows.reshape(-1, width)

    def spread(rows):
        gathered = lax.all_gather(rows, ("z", "c"), axis=0, tiled=True)
        return gathered.reshape(nz, nc, rows.shape[0], width)

    own_pair = own(query_key_rows, heads)
    own_attn = [own_pair[:, 0], own_pair[:, 1], own(value_rows, heads), own(out_proj, heads)]
    own_attn = jnp.concatenate([flat(rows) for rows in own_attn])
    w_attn = spread(own_attn)
    other = after(hop(leaving, "y"), own_attn)
    own_pair = own(after(gate_up_rows, other), units)
    own_gate_up = jnp.concatenate([flat(own_pair[:, 0]), flat(own_pair[:, 1])])
    w_gate_up = spread(own_gate_up)
    own_down = flat(own(after(down_proj, other), units))
    w_down = spread(own_down)
    qkv_count, out_count = 3 * heads * 64, heads * 64

    arrived = after(to_groups(stored_in, other, small), own_gate_up, own_down)
    tokens = arrived[:, :count].astype(F32)
    small = arrived[:, count:]
    gain_one = small[:, :1].astype(F32)
    gain_two = small[:, 1:2].astype(F32)
    table = small[:, 2, : buckets * mine].reshape(nz, buckets, mine).transpose(0, 2, 1)
    table = table.reshape(-1, buckets).astype(F32)
    table = lax.dynamic_slice_in_dim(table, y * local_heads, local_heads, 0)

    both_lengths = jnp.stack([lengths, lax.ppermute(lengths, "y", swap)])
    both_lengths = jnp.where(y == 0, both_lengths, both_lengths[::-1]).reshape(-1)
    length = lax.dynamic_slice_in_dim(both_lengths, z, 1, 0)
    slots = (x * 2 + y) * count + jnp.arange(count, dtype=jnp.int32)
    live = (slots < length).astype(F32)[None, :, None]

    def scale_of(values):
        squares = jnp.sum(values * values, axis=(0, 2), keepdims=True)
        return lax.rsqrt(squares / features + norm_eps)

    def norm_back(values, scale, gain, grad):
        inner = jnp.sum(values * gain * grad, axis=(0, 2), keepdims=True)
        out = scale * gain * grad - values * (scale * scale * scale) * inner / features
        return out, jnp.sum(values * scale * grad, axis=1)

    def reduce(partial):
        rows = partial.reshape(nz * partial.shape[1], width)
        return lax.psum_scatter(rows, ("z", "c"), scatter_dimension=0, tiled=True)

    fits = nx == 2 and heads == 4 and count == 256 and units * unit % 640 == 0 and nz % 2 == 0
    if fits:
        forward, backward, gather, scatter = attend, attend_back, gather_tokens, scatter_tokens
        nt, nn, tn, ffn_one, ffn_two = mm_nt, mm_nn, mm_tn, ffn_in, ffn_back
        shared = share
    else:
        forward, backward, gather, scatter = attend_plain, attend_back_plain, gather_plain, scatter_plain
        nt, nn, tn, ffn_one, ffn_two = mm_nt_plain, mm_nn_plain, mm_tn_plain, ffn_in_plain, ffn_back_plain
        shared = share_plain
    near_x, near_y = jnp.array([0, 0, 1, 1]) ^ x, jnp.array([0, 1, 0, 1]) ^ y
    starts = ((near_x * 2 + near_y) * count).astype(jnp.int32)

    def attend_all(*last):
        if not fits:
            out, stats = forward(projected, length, table, nc, heads)
            return (out,), stats
        first = forward(0, projected, length, table)
        second = forward(1, after(projected, *last), length, table)
        return (first[0], second[0]), (first[1], second[1])

    def attend_back_all(grad, *last):
        if not fits:
            grads, table_grad = backward(projected, length, table, grad, lse, nc, heads)
            return (grads,), table_grad
        first = backward(0, projected, length, table, grad, lse[0])
        second = backward(1, after(projected, *last), length, table, grad, lse[1])
        return (first[0], second[0]), jnp.concatenate([first[1], second[1]])

    scale_one = scale_of(tokens)
    normed, _, _ = gather((tokens * scale_one * gain_one).astype(BF))
    cot_other = hop(pick(stored_cot, 1 - y, 1), "y")
    upstream = live * to_groups(stored_cot, after(cot_other, arrived), None).astype(F32)
    grad_ffn, cot_first, cot_last = gather(after(upstream.astype(BF), w_attn))
    projected = nt(normed, w_attn, 0, qkv_count, starts)
    attended, lse = attend_all(*cot_first)
    heads_out = [after(attended[0], *cot_last), *attended[1:]]
    hidden = tokens + scatter(nn(heads_out, w_attn, qkv_count, out_count, starts))[0]
    scale_two = scale_of(hidden)
    normed_two, _, _ = gather((hidden * scale_two * gain_two).astype(BF))
    gate, up, activated = ffn_one(normed_two, w_gate_up, starts)

    down_partial = tn([activated], grad_ffn, starts)
    down_part = reduce(down_partial)
    grad_gate_up = ffn_two(grad_ffn, w_down, after(gate, down_partial), up, starts)
    two_parts = nn([grad_gate_up], w_gate_up, 0, 2 * units * unit, starts)
    grad_two, two_first, _ = scatter(two_parts)
    gate_up_partial = tn([after(grad_gate_up, two_parts[0])], normed_two, starts)
    gate_up_part = reduce(after(gate_up_partial, down_part, *two_first))
    branch_parts = nn([after(activated, gate_up_partial)], w_down, 0, units * unit, starts)
    through, ffn_gain_part = norm_back(hidden, scale_two, gain_two, grad_two)
    grad_hidden = upstream + through
    grad_branch, _, branch_last = gather(after(grad_hidden.astype(BF), branch_parts[0]))
    grad_attended = nt(grad_branch, w_attn, qkv_count, out_count, starts)
    out_partial = tn(attended, grad_branch, starts)
    branch_parts = [after(part, *branch_last) for part in branch_parts]
    branch, branch_first, branch_last = scatter(branch_parts)
    down_pieces, down_last = shared(after(down_part, grad_attended))
    grad_projected, table_part = attend_back_all(after(grad_attended, out_partial), *branch_first)
    out_part = reduce(after(out_partial, gate_up_part, grad_projected[-1]))
    last = after(grad_projected[-1], *branch_last, down_last)
    grad_projected = [*grad_projected[:-1], last]
    qkv_partial = tn(grad_projected, normed, starts)
    qkv_part = reduce(after(qkv_partial, out_part))
    one_parts = nn(grad_projected, w_attn, 0, qkv_count, starts)
    grad_one, _, _ = scatter(one_parts)
    outputs = from_groups((live * (hidden + branch)).astype(BF))
    through, attn_gain_part = norm_back(tokens, scale_one, gain_one, grad_one)
    input_grad = from_groups((grad_hidden + through).astype(BF)).astype(F32)

    gate_up_pieces, _ = shared(after(gate_up_part, attn_gain_part))
    out_pieces, _ = shared(after(out_part, attn_gain_part))
    qkv_pieces, _ = shared(qkv_part)
    if fits:
        here = jnp.stack([y, c]).astype(jnp.int32)

        def write_rows(source, outs):
            outs[0][...] = source[...].astype(F32)

        def write_qkv(source, outs):
            for h in range(heads):
                for i in range(3):
                    value = source[(i * heads + h) * 64 : (i * heads + h + 1) * 64, :].astype(F32)
                    if i == 2:
                        outs[1][h] = value
                    else:
                        outs[0][h, i] = value

        def write_gate_up(source, outs):
            for u in range(units):
                for i in range(2):
                    first = (i * units + u) * unit
                    outs[0][u, i] = source[first : first + unit, :].astype(F32)

        (down_all,) = place(down_pieces, here, [(units * unit, width)], write_rows)
        (out_all,) = place(out_pieces, here, [(heads * 64, width)], write_rows)
        (gate_up_all,) = place(gate_up_pieces, here, [(units, 2, unit, width)], write_gate_up)
        query_key_all, value_all = place(
            qkv_pieces, here, [(heads, 2, 64, width), (heads, 64, width)], write_qkv
        )
    else:
        down_all, out_all = down_pieces.astype(F32), out_pieces.astype(F32)
        gate_up_all = gate_up_pieces.astype(F32).reshape(parts, 2, units, unit, width)
        gate_up_all = gate_up_all.transpose(0, 2, 1, 3, 4).reshape(-1, 2, unit, width)
        qkv_all = qkv_pieces.astype(F32).reshape(parts, 3, heads, 64, width)
        qkv_all = qkv_all.transpose(0, 2, 1, 3, 4).reshape(-1, 3, 64, width)
        query_key_all, value_all = qkv_all[:, :2], qkv_all[:, 2]
    down_all, out_all = down_all.reshape(down_proj.shape), out_all.reshape(out_proj.shape)

    table_part = jnp.sum(table_part, axis=2)
    every = jnp.zeros((nx * 2 * local_heads, table_part.shape[1]), F32)
    every = lax.dynamic_update_slice_in_dim(every, table_part, (x * 2 + y) * local_heads, 0)
    every = every.reshape(-1, width) if every.size % width == 0 else every
    if every.shape[1] == width:
        both = sum_all(jnp.concatenate([ffn_gain_part, every]), nx, nz)
        ffn_gain_grad, every = both[:nz], both[nz:].reshape(-1, buckets)
    else:
        ffn_gain_grad, every = sum_all(ffn_gain_part, nx, nz), sum_all(every, nx, nz)
    attn_gain_grad = sum_all(attn_gain_part, nx, nz)
    table_grad = lax.dynamic_slice_in_dim(every, (x * nz + z) * mine, mine, 0).T
    return (
        outputs,
        input_grad,
        pick(attn_gain_grad, z, 0),
        pick(ffn_gain_grad, z, 0),
        query_key_all.transpose(3, 0, 1, 2),
        value_all.transpose(2, 0, 1),
        out_all,
        gate_up_all.transpose(3, 0, 1, 2),
        down_all,
        table_grad,
    )


def solution(mesh):
    dp, nx, nz = (mesh.shape[name] for name in ("dp", "gx", "gy"))
    nc = dp // 2
    split = Mesh(mesh.devices.reshape(2, nc, nx, nz), ("y", "c", "x", "z"))
    seq = ("y", "c")
    return jax.shard_map(
        functools.partial(body, nx, nz, nc),
        mesh=split,
        in_specs=(
            P(seq, "x", "z"),
            P(seq),
            P("z"),
            P("z"),
            P("z", "x", None, None),
            P("z", "x", None),
            P("x", None, "z"),
            P("z", "x", None, None),
            P("x", None, "z"),
            P(None, ("x", "z")),
            P(seq, "x", "z"),
        ),
        out_specs=(
            P(seq, "x", "z"),
            P(seq, "x", "z"),
            P("z"),
            P("z"),
            P("z", "x", None, None),
            P("z", "x", None),
            P("x", None, "z"),
            P("z", "x", None, None),
            P("x", None, "z"),
            P(None, ("x", "z")),
        ),
        check_vma=False,
    )
```

time: 946 us -> 748 us (0.79)
  blocking collectives: 112 us -> 0 us
  waiting for transfers between devices: 397 us -> 310 us
  local copies, waits for them, and re-layouts: 61.5 us -> 20.2 us
  Pallas kernels: 223 us -> 259 us
  starting transfers between devices: 70.7 us -> 89.5 us
  other arithmetic: 60.3 us -> 48 us
    reduce_scatter x4, waiting for transfers between devices: 174 us -> 1.08 us  [reduce(): return lax.psum_scatter(rows, ('z', 'c'), scatter_dimension=0, tiled=True)]
    psum x1 -> x0, blocking collectives: 55.9 us -> none  [body(): lax.psum((attn_gain_part, ffn_gain_part, every), ('y', 'c', 'x', 'z'))]
    all_gather x1 -> x0, blocking collectives: 55.7 us -> none  [body(): small = lax.all_gather(small, 'z', axis=0)]
    all_to_all x2, waiting for transfers between devices: 0.01 us -> 53.6 us  [to_groups(): return lax.all_to_all(both, 'z', 0, 0, tiled=True)]
    pallas_call x14 -> x20, Pallas kernels: 223 us -> 259 us  [the longest x2 57.8 us: attend_back(): pl.pallas_call(functools.partial(attend_back_kernel, group), grid=(1,), i...]
    ppermute x44 -> x62, waiting for transfers between devices: 196 us -> 214 us  [hop(): return lax.ppermute(value, axis, swap)]
    select_n x26 -> x2, other arithmetic: 14.5 us -> 3.72 us  [paired(): jnp.where(lax.axis_index(axis) == 0, jnp.stack([mine, other], axis=place)...]
    reshape x3, local copies, waits for them, and re-layouts: 11 us -> 0.28 us  [the longest x1 0.11 us: body(): bias_table.reshape(1, -1)]
  transfers between devices with their start and end apart: 60 -> 78, of which waited for: 28 -> 36; matrix products, arithmetic and copies ran while one was open for 10% -> 8% of each run, Pallas kernels for 20% -> 34%
where the time goes in v2:
time: 748 us; the launch traced here: 742 us
  waiting for transfers between devices  310 us (41%)
  Pallas kernels  259 us (35%)
  starting transfers between devices  89.5 us (12%)
  other arithmetic  48 us (6%)
  local copies, waits for them, and re-layouts  20.2 us (3%)
  between operations  15.3 us (2%)
    ppermute x62, waiting for transfers between devices, hop(): return lax.ppermute(value, axis, swap)  214 us
    ppermute x62, starting transfers between devices, hop(): return lax.ppermute(value, axis, swap)  58.2 us
    pallas_call x2, Pallas kernels, attend_back(): pl.pallas_call(functools.partial(attend_back_kernel, group), grid=(1,), i...  57.8 us
    pallas_call x4, Pallas kernels, mm_nn(): pl.pallas_call(functools.partial(nn_kernel, len(grads)), grid=(nz,), in_s...  53.7 us
    all_to_all x2, waiting for transfers between devices, to_groups(): return lax.all_to_all(both, 'z', 0, 0, tiled=True)  53.6 us
    pallas_call x4, Pallas kernels, mm_tn(): pl.pallas_call(functools.partial(tn_kernel, count), grid=(count * steps,)...  43.4 us
    pallas_call x2, Pallas kernels, attend(): pl.pallas_call(functools.partial(attend_kernel, group), grid=(1,), in_spe...  33.6 us
    all_to_all x2, waiting for transfers between devices, from_groups(): lax.all_to_all(mine, 'z', 0, 0, tiled=True).reshape(2, nz // 2, t, width)  23.3 us
  transfers between devices with their start and end apart: 78, of which 36 were waited for; matrix products, arithmetic and copies ran while one was open for 8% of the time, Pallas kernels for 34%

profile of v2, /device:TPU:0, one launch (start us, length us, event | category | flops | bytes accessed | tf_op | source)
XLA Modules:
  0.0 742.1 jit_solution(8554287321792018624)
XLA Ops:
  16.7 12.2 %collective-permute-done.1 = bf16[2,256,512]{2,1,0:T(8,128)(2,1)} collective-permute-done((bf16[2,256,512]{2,1,0:T(8,128)(2,1)}, bf16[2,256,512]{2,1,0:T(8,128)(2,1)}, u32[]{:S(2)}, u32[]{:S(2)}) %collective-permute-start.1) | collective-permute-done | bytes 524320 | tf_op jit(solution)/shard_map/ppermute | solution.py:559
  44.1 10.3 %collective-permute-done = s32[2]{0:T(128)S(1)} collective-permute-done((s32[2]{0:T(128)S(1)}, s32[2]{0:T(128)S(1)}, u32[]{:S(2)}, u32[]{:S(2)}) %collective-permute-start) | collective-permute-done | bytes 40 | tf_op jit(solution)/shard_map/ppermute | solution.py:737
  55.4 39.5 %all-to-all-done = bf16[4,264,512]{2,1,0:T(8,128)(2,1)} async-done(((bf16[4,264,512]{2,1,0:T(8,128)(2,1)}), bf16[4,264,512]{2,1,0:T(8,128)(2,1)}, u32[]{:S(2)}, u32[]{:S(2)}) %all-to-all-start) | async-done | bytes 1081376 | tf_op jit(solution)/shard_map/all_to_all | solution.py:655
  126.2 14.0 %all-to-all-done.1 = bf16[4,256,512]{2,1,0:T(8,128)(2,1)S(1)} async-done(((bf16[4,256,512]{2,1,0:T(8,128)(2,1)}), bf16[4,256,512]{2,1,0:T(8,128)(2,1)S(1)}, u32[]{:S(2)}, u32[]{:S(2)}) %all-to-all-start.1) | async-done | bytes 1048608 | tf_op jit(solution)/shard_map/all_to_all | solution.py:655
  145.0 12.0 %product_nt.2.q_ref.k_ref.v_ref = bf16[1024,1536]{1,0:T(8,128)(2,1)} custom-call(s32[4]{0:T(128)} %add_multiply_fusion.starts_ref, bf16[2,256,512]{2,1,0:T(8,128)(2,1)} %get-tuple-element.143.refs_0_.refs_2_, bf16[2,256,512]{2,1,0:T(8,128)(2,1)} %collective-permute-done.2.refs_1_.refs_3_, bf16[2,256,512]{2,1,0:T(8,128)(2,1)} %collective-permute-done.3.refs_2_.refs_4_, ...), custom_call_target="tpu_custom_call" | custom-call | flops 6442450944 | bytes 13631488 | tf_op jit(solution)/shard_map/product_nt/pallas_call | solution.py:78
  157.0 10.4 %collective-permute-done.10.refs_3_.refs_2_ = bf16[2,256,512]{2,1,0:T(8,128)(2,1)S(1)} collective-permute-done((bf16[2,256,512]{2,1,0:T(8,128)(2,1)S(1)}, bf16[2,256,512]{2,1,0:T(8,128)(2,1)S(1)}, u32[]{:S(2)}, u32[]{:S(2)}) %collective-permute-start.10) | collective-permute-done | bytes 524320 | tf_op jit(solution)/shard_map/ppermute | solution.py:559
  169.5 16.8 %attend.2 = (bf16[1024,256]{1,0:T(8,128)(2,1)}, f32[8,1024]{1,0:T(8,128)}) custom-call(s32[1]{0:T(128)} %dynamic_slice.57.length_ref, f32[8,32]{1,0:T(8,128)} %constant_dynamic-slice_fusion.7.table_ref, bf16[1024,1536]{1,0:T(8,128)(2,1)} %product_nt.2.q_ref.k_ref.v_ref, bf16[1024,1536]{1,0:T(8,128)(2,1)} %product_nt.2.q_ref.k_ref.v_ref, ...), custom_call_target="tpu_custom_call" | custom-call | flops 4294967296 | bytes 2097152 | tf_op jit(solution)/shard_map/attend/pallas_call | solution.py:454
  186.3 16.8 %attend.3 = (bf16[1024,256]{1,0:T(8,128)(2,1)}, f32[8,1024]{1,0:T(8,128)}) custom-call(s32[1]{0:T(128)} %dynamic_slice.57.length_ref, f32[8,32]{1,0:T(8,128)} %constant_dynamic-slice_fusion.7.table_ref, bf16[1024,1536]{1,0:T(8,128)(2,1)} %product_nt.2.q_ref.k_ref.v_ref, bf16[1024,1536]{1,0:T(8,128)(2,1)} %product_nt.2.q_ref.k_ref.v_ref, ...), custom_call_target="tpu_custom_call" | custom-call | flops 4294967296 | bytes 2097152 | tf_op jit(solution)/shard_map/attend/pallas_call | solution.py:454
  213.9 21.9 %collective-permute-done.15 = bf16[2,2,256,512]{3,2,1,0:T(8,128)(2,1)S(1)} collective-permute-done((bf16[2,2,256,512]{3,2,1,0:T(8,128)(2,1)}, bf16[2,2,256,512]{3,2,1,0:T(8,128)(2,1)S(1)}, u32[]{:S(2)}, u32[]{:S(2)}) %collective-permute-start.15) | collective-permute-done | bytes 1048608 | tf_op jit(solution)/shard_map/ppermute | solution.py:559
  257.7 10.8 %collective-permute-done.20.refs_2_.refs_3_ = bf16[2,256,512]{2,1,0:T(8,128)(2,1)S(1)} collective-permute-done((bf16[2,256,512]{2,1,0:T(8,128)(2,1)S(1)}, bf16[2,256,512]{2,1,0:T(8,128)(2,1)S(1)}, u32[]{:S(2)}, u32[]{:S(2)}) %collective-permute-start.20) | collective-permute-done | bytes 524320 | tf_op jit(solution)/shard_map/ppermute | solution.py:559
  287.6 17.7 %ffn_in.1 = (bf16[1024,1280]{1,0:T(8,128)(2,1)}, bf16[1024,1280]{1,0:T(8,128)(2,1)}, bf16[1024,1280]{1,0:T(8,128)(2,1)}) custom-call(s32[4]{0:T(128)} %add_multiply_fusion.starts_ref, bf16[2,256,512]{2,1,0:T(8,128)(2,1)} %copy-done.21, bf16[2,256,512]{2,1,0:T(8,128)(2,1)} %copy-done.41, bf16[2,256,512]{2,1,0:T(8,128)(2,1)} %copy-done.39, ...), custom_call_target="tpu_custom_call" | custom-call | flops 10737418240 | bytes 22544384 | tf_op jit(solution)/shard_map/ffn_in/pallas_call | solution.py:214
  315.4 15.5 %ffn_back.1.refs_0_ = bf16[1024,2560]{1,0:T(8,128)(2,1)} custom-call(s32[4]{0:T(128)} %add_multiply_fusion.starts_ref, bf16[2,256,512]{2,1,0:T(8,128)(2,1)} %copy-done.4, bf16[2,256,512]{2,1,0:T(8,128)(2,1)} %collective-permute-done.9.refs_2_.refs_1_, bf16[2,256,512]{2,1,0:T(8,128)(2,1)} %copy-done.19, ...), custom_call_target="tpu_custom_call" | custom-call | flops 5368709120 | bytes 19922944 | tf_op jit(solution)/shard_map/ffn_back/pallas_call | solution.py:245
  330.9 18.7 %product_nn.5 = (bf16[2,2,256,512]{3,2,1,0:T(8,128)(2,1)}, bf16[2,2,256,512]{3,2,1,0:T(8,128)(2,1)}, bf16[2,2,256,512]{3,2,1,0:T(8,128)(2,1)}, bf16[2,2,256,512]{3,2,1,0:T(8,128)(2,1)}) custom-call(s32[4]{0:T(128)} %add_multiply_fusion.starts_ref, bf16[1024,2560]{1,0:T(8,128)(2,1)} %ffn_back.1.refs_0_, bf16[4,2,1280,512]{3,2,1,0:T(8,128)(2,1)} %bitcast.138), custom_call_target="tpu_custom_call" | custom-call | flops 10737418240 | bytes 19922944 | tf_op jit(solution)/shard_map/product_nn/pallas_call | solution.py:123
  351.5 15.9 %product_tn.5 = bf16[4,2560,512]{2,1,0:T(8,128)(2,1)} custom-call(s32[4]{0:T(128)} %add_multiply_fusion.starts_ref, bf16[1024,2560]{1,0:T(8,128)(2,1)} %ffn_back.1.refs_0_, bf16[2,256,512]{2,1,0:T(8,128)(2,1)} %copy-done.21, bf16[2,256,512]{2,1,0:T(8,128)(2,1)} %copy-done.41, bf16[2,256,512]{2,1,0:T(8,128)(2,1)} %copy-done.39, ...), custom_call_target="tpu_custom_call" | custom-call | flops 10737418240 | bytes 19922944 | tf_op jit(solution)/shard_map/product_tn/pallas_call | solution.py:171
  380.1 12.5 %product_nn.6 = (bf16[2,2,256,512]{3,2,1,0:T(8,128)(2,1)}, bf16[2,2,256,512]{3,2,1,0:T(8,128)(2,1)}, bf16[2,2,256,512]{3,2,1,0:T(8,128)(2,1)}, bf16[2,2,256,512]{3,2,1,0:T(8,128)(2,1)}) custom-call(s32[4]{0:T(128)} %add_multiply_fusion.starts_ref, bf16[1024,1280]{1,0:T(8,128)(2,1)} %get-tuple-element.84.refs_0_, bf16[4,2,640,512]{3,2,1,0:T(8,128)(2,1)} %bitcast.110), custom_call_target="tpu_custom_call" | custom-call | flops 5368709120 | bytes 12058624 | tf_op jit(solution)/shard_map/product_nn/pallas_call | solution.py:123
  402.6 10.8 %collective-permute-done.30.refs_2_.refs_4_ = bf16[2,256,512]{2,1,0:T(8,128)(2,1)S(1)} collective-permute-done((bf16[2,256,512]{2,1,0:T(8,128)(2,1)S(1)}, bf16[2,256,512]{2,1,0:T(8,128)(2,1)S(1)}, u32[]{:S(2)}, u32[]{:S(2)}) %collective-permute-start.30) | collective-permute-done | bytes 524320 | tf_op jit(solution)/shard_map/ppermute | solution.py:559
  415.4 10.5 %collective-permute-done.29.refs_1_.refs_3_ = bf16[2,256,512]{2,1,0:T(8,128)(2,1)S(1)} collective-permute-done((bf16[2,256,512]{2,1,0:T(8,128)(2,1)S(1)}, bf16[2,256,512]{2,1,0:T(8,128)(2,1)S(1)}, u32[]{:S(2)}, u32[]{:S(2)}) %collective-permute-start.29) | collective-permute-done | bytes 524320 | tf_op jit(solution)/shard_map/ppermute | solution.py:559
  454.7 28.8 %attend_back.3 = (bf16[1024,768]{1,0:T(8,128)(2,1)}, f32[4,32,128]{2,1,0:T(8,128)}) custom-call(s32[1]{0:T(128)} %dynamic_slice.57.length_ref, f32[8,32]{1,0:T(8,128)} %constant_dynamic-slice_fusion.7.table_ref, bf16[1024,1536]{1,0:T(8,128)(2,1)} %product_nt.2.q_ref.k_ref.v_ref, bf16[1024,1536]{1,0:T(8,128)(2,1)} %product_nt.2.q_ref.k_ref.v_ref, ...), custom_call_target="tpu_custom_call" | custom-call | flops 10737418240 | bytes 4194304 | tf_op jit(solution)/shard_map/attend_back/pallas_call | solution.py:481
  490.4 29.0 %attend_back.2 = (bf16[1024,768]{1,0:T(8,128)(2,1)}, f32[4,32,128]{2,1,0:T(8,128)}) custom-call(s32[1]{0:T(128)} %dynamic_slice.57.length_ref, f32[8,32]{1,0:T(8,128)} %constant_dynamic-slice_fusion.7.table_ref, bf16[1024,1536]{1,0:T(8,128)(2,1)} %product_nt.2.q_ref.k_ref.v_ref, bf16[1024,1536]{1,0:T(8,128)(2,1)} %product_nt.2.q_ref.k_ref.v_ref, ...), custom_call_target="tpu_custom_call" | custom-call | flops 10737418240 | bytes 4194304 | tf_op jit(solution)/shard_map/attend_back/pallas_call | solution.py:481
  519.5 11.4 %product_tn.7 = bf16[4,1536,512]{2,1,0:T(8,128)(2,1)} custom-call(s32[4]{0:T(128)} %add_multiply_fusion.starts_ref, bf16[1024,768]{1,0:T(8,128)(2,1)} %get-tuple-element.99.refs_0_, bf16[1024,768]{1,0:T(8,128)(2,1)} %get-tuple-element.104.refs_1_, bf16[2,256,512]{2,1,0:T(8,128)(2,1)} %get-tuple-element.143.refs_0_.refs_2_, ...), custom_call_target="tpu_custom_call" | custom-call | flops 6442450944 | bytes 13631488 | tf_op jit(solution)/shard_map/product_tn/pallas_call | solution.py:171
  530.9 13.8 %product_nn.7 = (bf16[2,2,256,512]{3,2,1,0:T(8,128)(2,1)}, bf16[2,2,256,512]{3,2,1,0:T(8,128)(2,1)}, bf16[2,2,256,512]{3,2,1,0:T(8,128)(2,1)}, bf16[2,2,256,512]{3,2,1,0:T(8,128)(2,1)}) custom-call(s32[4]{0:T(128)} %add_multiply_fusion.starts_ref, bf16[1024,768]{1,0:T(8,128)(2,1)} %get-tuple-element.99.refs_0_, ...), custom_call_target="tpu_custom_call" | custom-call | flops 6442450944 | bytes 13631488 | tf_op jit(solution)/shard_map/product_nn/pallas_call | solution.py:123
  549.4 17.1 %collective-permute-done.41 = bf16[2,2,256,512]{3,2,1,0:T(8,128)(2,1)S(1)} collective-permute-done((bf16[2,2,256,512]{3,2,1,0:T(8,128)(2,1)}, bf16[2,2,256,512]{3,2,1,0:T(8,128)(2,1)S(1)}, u32[]{:S(2)}, u32[]{:S(2)}) %collective-permute-start.41) | collective-permute-done | bytes 1048608 | tf_op jit(solution)/shard_map/ppermute | solution.py:559
  595.6 23.3 %all-to-all-done.2 = bf16[4,256,512]{2,1,0:T(8,128)(2,1)S(1)} async-done(((bf16[4,256,512]{2,1,0:T(8,128)(2,1)}), bf16[4,256,512]{2,1,0:T(8,128)(2,1)S(1)}, u32[]{:S(2)}, u32[]{:S(2)}) %all-to-all-start.2) | async-done | bytes 1048608 | tf_op jit(solution)/shard_map/all_to_all | solution.py:661
  629.2 32.9 %collective-permute-done.52 = f32[6,512]{1,0:T(8,128)S(1)} collective-permute-done((f32[6,512]{1,0:T(8,128)S(1)}, f32[6,512]{1,0:T(8,128)S(1)}, u32[]{:S(2)}, u32[]{:S(2)}) %collective-permute-start.52) | collective-permute-done | bytes 12320 | tf_op jit(solution)/shard_map/ppermute | solution.py:559
  (339 shorter events, 304.0 us)
Async XLA Ops:
  7.2 133.5 %all-gather.4.cloned.1.call-start = ((), (), s32[]{:S(2)}) async-start(), calls=%async_computation.8 | async-start | bytes 9437184 | tf_op jit(solution)/shard_map/all_gather | solution.py:713
  11.6 276.1 %all-gather.6.cloned.1.call-start = ((), (), s32[]{:S(2)}) async-start(), calls=%async_computation.9 | async-start | bytes 11796480 | tf_op jit(solution)/shard_map/all_gather | solution.py:713
  34.3 60.7 %all-to-all-start = ((bf16[4,264,512]{2,1,0:T(8,128)(2,1)}), bf16[4,264,512]{2,1,0:T(8,128)(2,1)}, u32[]{:S(2)}, u32[]{:S(2)}) async-start(bf16[4,264,512]{2,1,0:T(8,128)(2,1)} %pad_maximum_fusion.3), calls=%async_computation | async-start | bytes 2162688 | tf_op jit(solution)/shard_map/all_to_all | solution.py:655
  39.5 275.9 %all-gather.8.cloned.1.call-start = ((), (), s32[]{:S(2)}) async-start(), calls=%async_computation.10 | async-start | bytes 5898240 | tf_op jit(solution)/shard_map/all_gather | solution.py:713
  41.6 54.9 %collective-permute-start.8 = (bf16[2,256,512]{2,1,0:T(8,128)(2,1)}, bf16[2,256,512]{2,1,0:T(8,128)(2,1)}, u32[]{:S(2)}, u32[]{:S(2)}) collective-permute-start(bf16[2,256,512]{2,1,0:T(8,128)(2,1)} %get-tuple-element.141), channel_id=1, source_target_pairs={{0,16},{16,0},{1,17},{17,1},{2,18},{18,2},{3,19},{19,3},{4,20},{20... | collective-permute-start | bytes 1572872 | tf_op jit(solution)/shard_map/ppermute | solution.py:559
  98.8 41.4 %all-to-all-start.1 = ((bf16[4,256,512]{2,1,0:T(8,128)(2,1)}), bf16[4,256,512]{2,1,0:T(8,128)(2,1)S(1)}, u32[]{:S(2)}, u32[]{:S(2)}) async-start(bf16[4,256,512]{2,1,0:T(8,128)(2,1)} %bitcast.25), calls=%async_computation.1 | async-start | bytes 2097152 | tf_op jit(solution)/shard_map/all_to_all | solution.py:655
  104.5 268.3 %reduce-scatter.5.cloned.1.call-start = ((), (), s32[]{:S(2)}) async-start(), calls=%async_computation.11 | async-start | bytes 5898240 | tf_op jit(solution)/shard_map/reduce_scatter | solution.py:754
  142.4 60.7 %collective-permute-start.12 = (bf16[2,256,512]{2,1,0:T(8,128)(2,1)S(1)}, bf16[2,256,512]{2,1,0:T(8,128)(2,1)S(1)}, u32[]{:S(2)}, u32[]{:S(2)}) collective-permute-start(bf16[2,256,512]{2,1,0:T(8,128)(2,1)S(1)} %get-tuple-element.138.refs_5_.refs_4_), channel_id=1, source_target_pairs={{0,4},{4,0},{1,5},{5,1},{2,6},{6,2},{3,7},{7,3},{8,12},{12,8},{9,1... | collective-permute-start | bytes 1572872 | tf_op jit(solution)/shard_map/ppermute | solution.py:559
  144.4 58.6 %collective-permute-start.9 = (bf16[2,256,512]{2,1,0:T(8,128)(2,1)S(1)}, bf16[2,256,512]{2,1,0:T(8,128)(2,1)}, u32[]{:S(2)}, u32[]{:S(2)}) collective-permute-start(bf16[2,256,512]{2,1,0:T(8,128)(2,1)S(1)} %get-tuple-element.139.refs_1_.refs_0_), channel_id=1, source_target_pairs={{0,16},{16,0},{1,17},{17,1},{2,18},{18,2},{3,19},{19,3},{4,20},{20... | collective-permute-start | bytes 1572872 | tf_op jit(solution)/shard_map/ppermute | solution.py:559
  167.4 35.6 %collective-permute-start.11 = (bf16[2,256,512]{2,1,0:T(8,128)(2,1)S(1)}, bf16[2,256,512]{2,1,0:T(8,128)(2,1)}, u32[]{:S(2)}, u32[]{:S(2)}) collective-permute-start(bf16[2,256,512]{2,1,0:T(8,128)(2,1)S(1)} %collective-permute-done.10.refs_3_.refs_2_), channel_id=1, source_target_pairs={{0,16},{16,0},{1,17},{17,1},{2,18},{18,2},{3,19},{19,3},{4,20},{20... | collective-permute-start | bytes 1572872 | tf_op jit(solution)/shard_map/ppermute | solution.py:559
  168.0 35.1 %collective-permute-start.14 = (bf16[2,256,512]{2,1,0:T(8,128)(2,1)S(1)}, bf16[2,256,512]{2,1,0:T(8,128)(2,1)}, u32[]{:S(2)}, u32[]{:S(2)}) collective-permute-start(bf16[2,256,512]{2,1,0:T(8,128)(2,1)S(1)} %collective-permute-done.13.refs_6_.refs_5_), channel_id=1, source_target_pairs={{0,4},{4,0},{1,5},{5,1},{2,6},{6,2},{3,7},{7,3},{8,12},{12,8},{9,1... | collective-permute-start | bytes 1572872 | tf_op jit(solution)/shard_map/ppermute | solution.py:559
  315.3 168.2 %reduce-scatter.7.cloned.1.call-start = ((), (), s32[]{:S(2)}) async-start(), calls=%async_computation.12 | async-start | bytes 11796480 | tf_op jit(solution)/shard_map/reduce_scatter | solution.py:754
  372.8 158.1 %reduce-scatter.9.cloned.1.call-start = ((), (), s32[]{:S(2)}) async-start(), calls=%async_computation.13 | async-start | bytes 2359296 | tf_op jit(solution)/shard_map/reduce_scatter | solution.py:754
  483.5 194.4 %reduce-scatter.11.cloned.1.call-start = ((), (), s32[]{:S(2)}) async-start(), calls=%async_computation.14 | async-start | bytes 7077888 | tf_op jit(solution)/shard_map/reduce_scatter | solution.py:754
  485.0 34.5 %collective-permute-start.36 = (bf16[2,256,512]{2,1,0:T(8,128)(2,1)S(1)}, bf16[2,256,512]{2,1,0:T(8,128)(2,1)}, u32[]{:S(2)}, u32[]{:S(2)}) collective-permute-start(bf16[2,256,512]{2,1,0:T(8,128)(2,1)S(1)} %fusion.20), channel_id=1, source_target_pairs={{0,16},{16,0},{1,17},{17,1},{2,18},{18,2},{3,19},{19,3},{4,20},{20... | collective-permute-start | bytes 1572872 | tf_op jit(solution)/shard_map/ppermute | solution.py:559
  570.5 48.4 %all-to-all-start.2 = ((bf16[4,256,512]{2,1,0:T(8,128)(2,1)}), bf16[4,256,512]{2,1,0:T(8,128)(2,1)S(1)}, u32[]{:S(2)}, u32[]{:S(2)}) async-start(bf16[4,256,512]{2,1,0:T(8,128)(2,1)} %fusion.13), calls=%async_computation.2 | async-start | bytes 2097152 | tf_op jit(solution)/shard_map/all_to_all | solution.py:661
  618.8 66.2 %all-to-all-start.3 = ((bf16[4,256,512]{2,1,0:T(8,128)(2,1)}), bf16[4,256,512]{2,1,0:T(8,128)(2,1)S(1)}, u32[]{:S(2)}, u32[]{:S(2)}) async-start(bf16[4,256,512]{2,1,0:T(8,128)(2,1)} %fusion.9), calls=%async_computation.4 | async-start | bytes 2097152 | tf_op jit(solution)/shard_map/all_to_all | solution.py:661
  622.4 60.4 %collective-permute-start.63 = (bf16[1280,512]{1,0:T(8,128)(2,1)}, bf16[1280,512]{1,0:T(8,128)(2,1)}, u32[]{:S(2)}, u32[]{:S(2)}) collective-permute-start(bf16[1280,512]{1,0:T(8,128)(2,1)} %reduce-scatter.7.cloned.1.call-done.refs_0_), channel_id=1, source_target_pairs={{0,16},{16,0},{1,17},{17,1},{2,18},{18,2},{3,19},{19,3},{4,20},{20... | collective-permute-start | bytes 3932168 | tf_op jit(solution)/shard_map/ppermute | solution.py:559
  624.9 54.1 %collective-permute-start.39 = (bf16[2,256,512]{2,1,0:T(8,128)(2,1)}, bf16[2,256,512]{2,1,0:T(8,128)(2,1)}, u32[]{:S(2)}, u32[]{:S(2)}) collective-permute-start(bf16[2,256,512]{2,1,0:T(8,128)(2,1)} %get-tuple-element.133), channel_id=1, source_target_pairs={{0,16},{16,0},{1,17},{17,1},{2,18},{18,2},{3,19},{19,3},{4,20},{20... | collective-permute-start | bytes 1572872 | tf_op jit(solution)/shard_map/ppermute | solution.py:559
  625.6 57.7 %collective-permute-start.65 = (bf16[640,512]{1,0:T(8,128)(2,1)}, bf16[640,512]{1,0:T(8,128)(2,1)S(1)}, u32[]{:S(2)}, u32[]{:S(2)}) collective-permute-start(bf16[640,512]{1,0:T(8,128)(2,1)} %reduce-scatter.5.cloned.1.call-done.refs_0_), channel_id=1, source_target_pairs={{0,8},{8,0},{1,9},{9,1},{2,10},{10,2},{3,11},{11,3},{4,12},{12,4},... | collective-permute-start | bytes 1966088 | tf_op jit(solution)/shard_map/ppermute | solution.py:559
  627.7 34.4 %collective-permute-start.52 = (f32[6,512]{1,0:T(8,128)S(1)}, f32[6,512]{1,0:T(8,128)S(1)}, u32[]{:S(2)}, u32[]{:S(2)}) collective-permute-start(f32[6,512]{1,0:T(8,128)S(1)} %fusion.28), channel_id=1, source_target_pairs={{0,16},{16,0},{1,17},{17,1},{2,18},{18,2},{3,19},{19,3},{4,20},{20... | collective-permute-start | bytes 36872 | tf_op jit(solution)/shard_map/ppermute | solution.py:559
  672.3 43.8 %collective-permute-start.62 = (bf16[1280,512]{1,0:T(8,128)(2,1)}, bf16[1280,512]{1,0:T(8,128)(2,1)}, u32[]{:S(2)}, u32[]{:S(2)}) collective-permute-start(bf16[1280,512]{1,0:T(8,128)(2,1)} %reduce-scatter.7.cloned.1.call-done.refs_0_), channel_id=1, source_target_pairs={{0,8},{8,0},{1,9},{9,1},{2,10},{10,2},{3,11},{11,3},{4,12},{12,4},... | collective-permute-start | bytes 3932168 | tf_op jit(solution)/shard_map/ppermute | solution.py:559
  682.7 36.3 %collective-permute-start.64 = (bf16[1280,512]{1,0:T(8,128)(2,1)}, bf16[1280,512]{1,0:T(8,128)(2,1)}, u32[]{:S(2)}, u32[]{:S(2)}) collective-permute-start(bf16[1280,512]{1,0:T(8,128)(2,1)} %collective-permute-done.63.refs_2_), channel_id=1, source_target_pairs={{0,8},{8,0},{1,9},{9,1},{2,10},{10,2},{3,11},{11,3},{4,12},{12,4},... | collective-permute-start | bytes 3932168 | tf_op jit(solution)/shard_map/ppermute | solution.py:559
  692.5 37.2 %collective-permute-start.56 = (bf16[768,512]{1,0:T(8,128)(2,1)S(1)}, bf16[768,512]{1,0:T(8,128)(2,1)}, u32[]{:S(2)}, u32[]{:S(2)}) collective-permute-start(bf16[768,512]{1,0:T(8,128)(2,1)S(1)} %copy-done.15), channel_id=1, source_target_pairs={{0,8},{8,0},{1,9},{9,1},{2,10},{10,2},{3,11},{11,3},{4,12},{12,4},... | collective-permute-start | bytes 2359304 | tf_op jit(solution)/shard_map/ppermute | solution.py:559
  (98 other events, 1461.7 us)
Sparse Core Ops, SparseCore 0:
  11.7 129.0 all-gather.3
  142.9 97.5 all-gather.5
  242.2 54.4 all-gather.7
  315.5 57.3 reduce-scatter.4
  375.5 107.7 reduce-scatter.6
  486.1 35.9 reduce-scatter.8
  531.0 88.6 reduce-scatter.10

commit v3 on v2

--- a/solution.py
+++ b/solution.py
@@ -96,22 +96,22 @@
     nc, rows, width = w_ref.shape[1:]
     t = grads[0].shape[0] // 4
     in_low = pl.program_id(0) < pl.num_programs(0) // 2
-    for d in range(4):
+
+    def product(d):
         spot = spot_of(starts_ref, d, t)
         if count == 1:
-            value = dot_nn(grads[0][spot, :], w_ref[0].reshape(nc * rows, width))
-        else:
-            value = sum(dot_nn(grads[c][spot, :], w_ref[0, c]) for c in range(count))
-        value = value.astype(BF)
-        dx, dy = d // 2, d % 2
-
-        @pl.when(in_low)
-        def _():
-            (low_out if dx else low_keep)[dy, 0] = value
-
-        @pl.when(jnp.logical_not(in_low))
-        def _():
-            (high_out if dy else high_keep)[dx, 0] = value
+            return dot_nn(grads[0][spot, :], w_ref[0].reshape(nc * rows, width)).astype(BF)
+        return sum(dot_nn(grads[c][spot, :], w_ref[0, c]) for c in range(count)).astype(BF)
+
+    @pl.when(in_low)
+    def _():
+        for d in range(4):
+            (low_out if d // 2 else low_keep)[d % 2, 0] = product(d)
+
+    @pl.when(jnp.logical_not(in_low))
+    def _():
+        for d in range(4):
+            (high_out if d % 2 else high_keep)[d // 2, 0] = product(d)
 
 
 def mm_nn(grads, w, first, rows, starts):
@@ -575,28 +575,32 @@
     return lax.optimization_barrier((value, *others))[0]
 
 
-def gather_plain(part):
+def gather_plain(part, *beside):
     return lax.all_gather(part, ("x", "y"), axis=1, tiled=True), (), ()
 
 
-def gather_tokens(part):
+def gather_tokens(part, *beside):
     half = part.shape[0] // 2
     low, high = part[:half], part[half:]
     low_x, high_y = hop(low, "x"), hop(high, "y")
+    if beside:
+        low_x, high_y = after(low_x, *beside), after(high_y, *beside)
     low_y, high_x = hop(low, "y"), hop(high, "x")
     low_xy, high_xy = hop(low_x, "y"), hop(high_y, "x")
     pieces = [low, low_y, low_x, low_xy, high, high_y, high_x, high_xy]
     return pieces, (low_x, high_y), (low_y, low_xy, high_x, high_xy)
 
 
-def scatter_plain(parts):
+def scatter_plain(parts, *beside):
     whole = parts[0].astype(F32)
     return lax.psum_scatter(whole, ("x", "y"), scatter_dimension=1, tiled=True), (), ()
 
 
-def scatter_tokens(parts):
+def scatter_tokens(parts, *beside):
     low_out, low_keep, high_out, high_keep = parts
     low_in, high_in = hop(low_out, "x"), hop(high_out, "y")
+    if beside:
+        low_in, high_in = after(low_in, *beside), after(high_in, *beside)
 
     def add(keep, arrived, index):
         return keep[index].astype(F32) + arrived[index].astype(F32)
@@ -645,29 +649,93 @@
     return lax.all_gather(part, ("y", "c"), axis=0), part
 
 
-def to_groups(halves, other, extra):
-    count, _, t, width = halves.shape
-    y = lax.axis_index("y")
-    both = paired(pick(halves, y, 1), other, "y").reshape(2 * count, t, width)
-    if extra is not None:
-        wide = jnp.broadcast_to(extra[None], (2 * count, *extra.shape))
-        both = jnp.concatenate([both, wide], axis=1)
-    return lax.all_to_all(both, "z", 0, 0, tiled=True)
+def routes(nz, k):
+    many = nz // 2
+    pairs = []
+    for y in range(2):
+        for z in range(nz):
+            piece = (z + k) % nz
+            pairs.append((y * nz + z, (piece // many) * nz + y * many + piece % many))
+    return pairs
+
+
+def turned(pieces, shift):
+    n = len(pieces)
+    options = [jnp.stack([pieces[(i + s) % n] for i in range(n)]) for s in range(n)]
+    return lax.select_n(lax.rem(shift + n, n), *options)
+
+
+def to_groups(stored, extra, *earlier):
+    count, _, t, width = stored.shape
+    nz = 2 * count
+    y, z = lax.axis_index("y"), lax.axis_index("z")
+    arrived = []
+    for k in range(nz):
+        place = lax.rem(z + k, nz)
+        corner = (lax.rem(place, count), lax.div(place, count), 0, 0)
+        piece = lax.dynamic_slice(stored, corner, (1, 1, t, width)).reshape(t, width)
+        if extra is not None:
+            piece = jnp.concatenate([piece, extra])
+        if earlier:
+            piece = after(piece, *earlier)
+        arrived.append(lax.ppermute(piece, ("y", "z"), routes(nz, k)))
+    mine = y * count + lax.rem(z, count)
+    return [arrived[(nz - i) % nz] for i in range(nz)], nz - mine
 
 
 def from_groups(mine):
     nz, t, width = mine.shape
-    y = lax.axis_index("y")
-    back = lax.all_to_all(mine, "z", 0, 0, tiled=True).reshape(2, nz // 2, t, width)
-    other = hop(pick(back, 1 - y, 0), "y")
-    both = paired(pick(back, y, 0), other, "y")
-    return both.transpose(1, 0, 2, 3).reshape(nz // 2, 2 * t, width)
-
-
-def sum_all(value, nx, nz):
+    y, z = lax.axis_index("y"), lax.axis_index("z")
+    count = nz // 2
+    own = y * count + lax.rem(z, count)
+    arrived = []
+    for k in range(nz):
+        piece = pick(mine, lax.rem(own - k + nz, nz), 0)
+        arrived.append(lax.ppermute(piece, ("y", "z"), [(b, a) for a, b in routes(nz, k)]))
+    return arrived
+
+
+def settle_kernel(shift_ref, *refs):
+    pieces, out_ref = refs[:-1], refs[-1]
+    count = len(pieces)
+    for k in range(count):
+
+        @pl.when(lax.rem(pl.program_id(0) + shift_ref[0], count) == k)
+        def _():
+            out_ref[0, 0] = pieces[k][...].astype(out_ref.dtype)
+
+
+def settle(arrived, dtype):
+    nz = len(arrived)
+    t, width = arrived[0].shape
+    count = nz // 2
+    shift = (nz - lax.axis_index("z")).astype(jnp.int32).reshape(1)
+    out = pl.pallas_call(
+        settle_kernel,
+        grid=(nz,),
+        in_specs=[pl.BlockSpec(memory_space=pltpu.SMEM)]
+        + [pl.BlockSpec((t, width), lambda i: (0, 0))] * nz,
+        out_specs=pl.BlockSpec((1, 1, t, width), lambda i: (lax.rem(i, count), lax.div(i, count), 0, 0)),
+        out_shape=jax.ShapeDtypeStruct((count, 2, t, width), dtype),
+        compiler_params=params(1),
+        cost_estimate=cost(0, 6 * nz * t * width),
+        name="settle",
+    )(shift, *arrived)
+    return out.reshape(count, 2 * t, width)
+
+
+def settle_plain(arrived, dtype):
+    nz = len(arrived)
+    t, width = arrived[0].shape
+    back = turned(arrived, nz - lax.axis_index("z")).reshape(2, nz // 2, t, width)
+    return back.transpose(1, 0, 2, 3).reshape(nz // 2, 2 * t, width).astype(dtype)
+
+
+def sum_all(value, nx, nz, *earlier):
     value = value + hop(value, "c")
+    value = value + hop(value, "x") if nx == 2 else lax.psum(value, "x")
     value = value + hop(value, "y")
-    value = value + hop(value, "x") if nx == 2 else lax.psum(value, "x")
+    value = after(value, *earlier)
     step = 1
     while step < nz:
         value = value + lax.ppermute(value, "z", [(i, i ^ step) for i in range(nz)])
@@ -689,7 +757,6 @@
 
     stored_in = inputs.reshape(inputs.shape[0], 2, count, width)
     stored_cot = cotangent.reshape(stored_in.shape)
-    leaving = pick(stored_in, 1 - y, 1)
     small = jnp.concatenate(
         [attn_gain[None], ffn_gain[None], jnp.pad(bias_table.reshape(1, -1), ((0, 0), (0, width - buckets * mine)))]
     )
@@ -709,23 +776,20 @@
     def flat(rows):
         return rows.reshape(-1, width)
 
-    def spread(rows):
+    def spread(blocks):
+        rows = jnp.concatenate([flat(block) for block in blocks])
         gathered = lax.all_gather(rows, ("z", "c"), axis=0, tiled=True)
         return gathered.reshape(nz, nc, rows.shape[0], width)
 
     own_pair = own(query_key_rows, heads)
     own_attn = [own_pair[:, 0], own_pair[:, 1], own(value_rows, heads), own(out_proj, heads)]
-    own_attn = jnp.concatenate([flat(rows) for rows in own_attn])
-    w_attn = spread(own_attn)
-    other = after(hop(leaving, "y"), own_attn)
-    own_pair = own(after(gate_up_rows, other), units)
-    own_gate_up = jnp.concatenate([flat(own_pair[:, 0]), flat(own_pair[:, 1])])
-    w_gate_up = spread(own_gate_up)
-    own_down = flat(own(after(down_proj, other), units))
-    w_down = spread(own_down)
+    w_attn = spread(own_attn[:-1])
+    w_out = spread(own_attn[-1:])
     qkv_count, out_count = 3 * heads * 64, heads * 64
 
-    arrived = after(to_groups(stored_in, other, small), own_gate_up, own_down)
+    arrived, shift = to_groups(stored_in, small)
+    first_in = arrived[0]
+    arrived = turned(arrived, shift)
     tokens = arrived[:, :count].astype(F32)
     small = arrived[:, count:]
     gain_one = small[:, :1].astype(F32)
@@ -757,39 +821,41 @@
     if fits:
         forward, backward, gather, scatter = attend, attend_back, gather_tokens, scatter_tokens
         nt, nn, tn, ffn_one, ffn_two = mm_nt, mm_nn, mm_tn, ffn_in, ffn_back
-        shared = share
+        shared, stored_from = share, settle
     else:
         forward, backward, gather, scatter = attend_plain, attend_back_plain, gather_plain, scatter_plain
         nt, nn, tn, ffn_one, ffn_two = mm_nt_plain, mm_nn_plain, mm_tn_plain, ffn_in_plain, ffn_back_plain
-        shared = share_plain
+        shared, stored_from = share_plain, settle_plain
     near_x, near_y = jnp.array([0, 0, 1, 1]) ^ x, jnp.array([0, 1, 0, 1]) ^ y
     starts = ((near_x * 2 + near_y) * count).astype(jnp.int32)
-
-    def attend_all(*last):
-        if not fits:
-            out, stats = forward(projected, length, table, nc, heads)
-            return (out,), stats
-        first = forward(0, projected, length, table)
-        second = forward(1, after(projected, *last), length, table)
-        return (first[0], second[0]), (first[1], second[1])
 
     def attend_back_all(grad, *last):
         if not fits:
             grads, table_grad = backward(projected, length, table, grad, lse, nc, heads)
             return (grads,), table_grad
         first = backward(0, projected, length, table, grad, lse[0])
-        second = backward(1, after(projected, *last), length, table, grad, lse[1])
+        second = backward(1, after(projected, first[0], *last), length, table, grad, lse[1])
         return (first[0], second[0]), jnp.concatenate([first[1], second[1]])
 
     scale_one = scale_of(tokens)
-    normed, _, _ = gather((tokens * scale_one * gain_one).astype(BF))
-    cot_other = hop(pick(stored_cot, 1 - y, 1), "y")
-    upstream = live * to_groups(stored_cot, after(cot_other, arrived), None).astype(F32)
-    grad_ffn, cot_first, cot_last = gather(after(upstream.astype(BF), w_attn))
+    normed, normed_first, _ = gather((tokens * scale_one * gain_one).astype(BF))
+    own_pair = own(after(gate_up_rows, *normed_first), units)
+    w_gate_up = spread([own_pair[:, 0], own_pair[:, 1]])
+    w_down = spread([own(after(down_proj, *normed_first), units)])
+    upstream = live * turned(*to_groups(stored_cot, None, first_in)).astype(F32)
+    upstream_rounded = after(upstream.astype(BF), w_attn)
     projected = nt(normed, w_attn, 0, qkv_count, starts)
-    attended, lse = attend_all(*cot_first)
+    if fits:
+        first = forward(0, projected, length, table)
+        grad_ffn, cot_first, cot_last = gather(upstream_rounded, first[0])
+        second = forward(1, after(projected, first[0], *cot_first), length, table)
+        attended, lse = (first[0], second[0]), (first[1], second[1])
+    else:
+        grad_ffn, _, cot_last = gather(upstream_rounded)
+        attended, lse = forward(projected, length, table, nc, heads)
+        attended = (attended,)
     heads_out = [after(attended[0], *cot_last), *attended[1:]]
-    hidden = tokens + scatter(nn(heads_out, w_attn, qkv_count, out_count, starts))[0]
+    hidden = tokens + scatter(nn(heads_out, w_out, 0, out_count, starts))[0]
     scale_two = scale_of(hidden)
     normed_two, _, _ = gather((hidden * scale_two * gain_two).astype(BF))
     gate, up, activated = ffn_one(normed_two, w_gate_up, starts)
@@ -805,26 +871,27 @@
     through, ffn_gain_part = norm_back(hidden, scale_two, gain_two, grad_two)
     grad_hidden = upstream + through
     grad_branch, _, branch_last = gather(after(grad_hidden.astype(BF), branch_parts[0]))
-    grad_attended = nt(grad_branch, w_attn, qkv_count, out_count, starts)
+    grad_attended = nt(grad_branch, w_out, 0, out_count, starts)
     out_partial = tn(attended, grad_branch, starts)
     branch_parts = [after(part, *branch_last) for part in branch_parts]
     branch, branch_first, branch_last = scatter(branch_parts)
     down_pieces, down_last = shared(after(down_part, grad_attended))
     grad_projected, table_part = attend_back_all(after(grad_attended, out_partial), *branch_first)
-    out_part = reduce(after(out_partial, gate_up_part, grad_projected[-1]))
+    out_part = reduce(out_partial)
     last = after(grad_projected[-1], *branch_last, down_last)
     grad_projected = [*grad_projected[:-1], last]
     qkv_partial = tn(grad_projected, normed, starts)
     qkv_part = reduce(after(qkv_partial, out_part))
     one_parts = nn(grad_projected, w_attn, 0, qkv_count, starts)
-    grad_one, _, _ = scatter(one_parts)
+    gate_up_pieces, gate_up_last = shared(after(gate_up_part, grad_projected[0]))
     outputs = from_groups((live * (hidden + branch)).astype(BF))
+    grad_one, _, one_last = scatter(one_parts, gate_up_last, *outputs)
     through, attn_gain_part = norm_back(tokens, scale_one, gain_one, grad_one)
-    input_grad = from_groups((grad_hidden + through).astype(BF)).astype(F32)
-
-    gate_up_pieces, _ = shared(after(gate_up_part, attn_gain_part))
-    out_pieces, _ = shared(after(out_part, attn_gain_part))
-    qkv_pieces, _ = shared(qkv_part)
+    input_grad = input_last = from_groups((grad_hidden + through).astype(BF))
+    outputs = stored_from(outputs, BF)
+
+    out_pieces, _ = shared(after(out_part, *one_last))
+    qkv_pieces, _ = shared(after(qkv_part, *one_last))
     if fits:
         here = jnp.stack([y, c]).astype(jnp.int32)
 
@@ -859,18 +926,20 @@
         qkv_all = qkv_pieces.astype(F32).reshape(parts, 3, heads, 64, width)
         qkv_all = qkv_all.transpose(0, 2, 1, 3, 4).reshape(-1, 3, 64, width)
         query_key_all, value_all = qkv_all[:, :2], qkv_all[:, 2]
+    input_grad = [after(part, down_all, out_all, gate_up_all) for part in input_grad]
+    input_grad = stored_from(input_grad, F32)
     down_all, out_all = down_all.reshape(down_proj.shape), out_all.reshape(out_proj.shape)
 
     table_part = jnp.sum(table_part, axis=2)
     every = jnp.zeros((nx * 2 * local_heads, table_part.shape[1]), F32)
     every = lax.dynamic_update_slice_in_dim(every, table_part, (x * 2 + y) * local_heads, 0)
-    every = every.reshape(-1, width) if every.size % width == 0 else every
-    if every.shape[1] == width:
-        both = sum_all(jnp.concatenate([ffn_gain_part, every]), nx, nz)
-        ffn_gain_grad, every = both[:nz], both[nz:].reshape(-1, buckets)
+    both = jnp.concatenate([attn_gain_part, ffn_gain_part])
+    if every.size % width == 0:
+        both = sum_all(jnp.concatenate([both, every.reshape(-1, width)]), nx, nz, *input_last)
+        every = both[2 * nz :].reshape(-1, buckets)
     else:
-        ffn_gain_grad, every = sum_all(ffn_gain_part, nx, nz), sum_all(every, nx, nz)
-    attn_gain_grad = sum_all(attn_gain_part, nx, nz)
+        both, every = sum_all(both, nx, nz), sum_all(every, nx, nz)
+    attn_gain_grad, ffn_gain_grad = both[:nz], both[nz : 2 * nz]
     table_grad = lax.dynamic_slice_in_dim(every, (x * nz + z) * mine, mine, 0).T
     return (
         outputs,

time: 748 us -> 829 us (1.11)
  starting transfers between devices: 89.5 us -> 142 us
  waiting for transfers between devices: 310 us -> 355 us
  other arithmetic: 48 us -> 36.1 us
    ppermute x0 -> x16, waiting for transfers between devices: none -> 151 us  [the longest x8 101 us: to_groups(): arrived.append(lax.ppermute(piece, ('y', 'z'), routes(nz, k)))]
    ppermute x62 -> x55, waiting for transfers between devices: 214 us -> 127 us  [hop(): return lax.ppermute(value, axis, swap)]
    ppermute x0 -> x16, starting transfers between devices: none -> 85.2 us  [the longest x8 44.5 us: to_groups(): arrived.append(lax.ppermute(piece, ('y', 'z'), routes(nz, k)))]
    all_to_all x4 -> x0, waiting for transfers between devices: 76.8 us -> none  [the longest x2 53.6 us: to_groups(): return lax.all_to_all(both, 'z', 0, 0, tiled=True)]
    reduce_scatter x4, waiting for transfers between devices: 1.08 us -> 67.8 us  [reduce(): return lax.psum_scatter(rows, ('z', 'c'), scatter_dimension=0, tiled=True)]
    all_to_all x4 -> x0, starting transfers between devices: 21.7 us -> none  [the longest x2 10.9 us: to_groups(): return lax.all_to_all(both, 'z', 0, 0, tiled=True)]
    ppermute x1, waiting for transfers between devices: 10.3 us -> 0.01 us  [body(): both_lengths = jnp.stack([lengths, lax.ppermute(lengths, 'y', swap)])]
    pallas_call x4, Pallas kernels: 53.7 us -> 44.5 us  [mm_nn(): pl.pallas_call(functools.partial(nn_kernel, len(grads)), grid=(nz,), in_s...]
  transfers between devices with their start and end apart: 78 -> 82, of which waited for: 36 -> 31; matrix products, arithmetic and copies ran while one was open for 8% -> 6% of each run, Pallas kernels for 34% -> 30%
where the time goes in v3:
time: 829 us; the launch traced here: 824 us
  waiting for transfers between devices  355 us (43%)
  Pallas kernels  255 us (31%)
  starting transfers between devices  142 us (17%)
  other arithmetic  36.1 us (4%)
  local copies, waits for them, and re-layouts  20.4 us (2%)
  between operations  15.8 us (2%)
    ppermute x55, waiting for transfers between devices, hop(): return lax.ppermute(value, axis, swap)  127 us
    ppermute x8, waiting for transfers between devices, to_groups(): arrived.append(lax.ppermute(piece, ('y', 'z'), routes(nz, k)))  101 us
    reduce_scatter x4, waiting for transfers between devices, reduce(): return lax.psum_scatter(rows, ('z', 'c'), scatter_dimension=0, tiled=True)  67.8 us
    pallas_call x2, Pallas kernels, attend_back(): pl.pallas_call(functools.partial(attend_back_kernel, group), grid=(1,), i...  57.4 us
    ppermute x55, starting transfers between devices, hop(): return lax.ppermute(value, axis, swap)  54.3 us
    ppermute x8, waiting for transfers between devices, from_groups(): lax.ppermute(piece, ('y', 'z'), [(b, a) for a, b in routes(nz, k)])  49.9 us
    ppermute x8, starting transfers between devices, to_groups(): arrived.append(lax.ppermute(piece, ('y', 'z'), routes(nz, k)))  44.5 us
    pallas_call x4, Pallas kernels, mm_nn(): pl.pallas_call(functools.partial(nn_kernel, len(grads)), grid=(nz,), in_s...  44.5 us
  transfers between devices with their start and end apart: 82, of which 31 were waited for; matrix products, arithmetic and copies ran while one was open for 6% of the time, Pallas kernels for 30%

profile of v3, /device:TPU:0, one launch (start us, length us, event | category | flops | bytes accessed | tf_op | source)
XLA Modules:
  0.0 824.0 jit_solution(3493917412464826625)
XLA Ops:
  24.3 69.3 %collective-permute-done.3 = bf16[264,512]{1,0:T(8,128)(2,1)S(1)} collective-permute-done((bf16[264,512]{1,0:T(8,128)(2,1)}, bf16[264,512]{1,0:T(8,128)(2,1)S(1)}, u32[]{:S(2)}, u32[]{:S(2)}) %collective-permute-start.3) | collective-permute-done | bytes 270368 | tf_op jit(solution)/shard_map/ppermute | solution.py:681
  117.1 29.5 %collective-permute-start.12 = (bf16[256,512]{1,0:T(8,128)(2,1)}, bf16[256,512]{1,0:T(8,128)(2,1)S(1)}, u32[]{:S(2)}, u32[]{:S(2)}) collective-permute-start(bf16[256,512]{1,0:T(8,128)(2,1)} %get-tuple-element.76), channel_id=1, source_target_pairs={{0,17},{1,0},{2,1},{3,16},{16,19},{17,2},{18,3},{19,18},{4,21},{5,... | collective-permute-start | bytes 786440 | tf_op jit(solution)/shard_map/ppermute | solution.py:681
  160.1 31.5 %collective-permute-done.13 = bf16[256,512]{1,0:T(8,128)(2,1)S(1)} collective-permute-done((bf16[256,512]{1,0:T(8,128)(2,1)}, bf16[256,512]{1,0:T(8,128)(2,1)S(1)}, u32[]{:S(2)}, u32[]{:S(2)}) %collective-permute-start.13) | collective-permute-done | bytes 262176 | tf_op jit(solution)/shard_map/ppermute | solution.py:681
  206.8 11.5 %product_nt.2.q_ref.k_ref.v_ref = bf16[1024,1536]{1,0:T(8,128)(2,1)} custom-call(s32[4]{0:T(128)} %add_multiply_fusion.starts_ref, bf16[2,256,512]{2,1,0:T(8,128)(2,1)} %get-tuple-element.169.refs_0_.refs_2_, bf16[2,256,512]{2,1,0:T(8,128)(2,1)} %collective-permute-done.5.refs_1_.refs_3_, bf16[2,256,512]{2,1,0:T(8,128)(2,1)} %collective-permute-done.6.refs_2_.refs_4_, ...), custom_call_target="tpu_custom_call" | custom-call | flops 6442450944 | bytes 13631488 | tf_op jit(solution)/shard_map/product_nt/pallas_call | solution.py:78
  218.3 16.8 %attend.2 = (bf16[1024,256]{1,0:T(8,128)(2,1)}, f32[8,1024]{1,0:T(8,128)}) custom-call(s32[1]{0:T(128)} %dynamic_slice.80.length_ref, f32[8,32]{1,0:T(8,128)} %constant_dynamic-slice_fusion.8.table_ref, bf16[1024,1536]{1,0:T(8,128)(2,1)} %product_nt.2.q_ref.k_ref.v_ref, bf16[1024,1536]{1,0:T(8,128)(2,1)} %product_nt.2.q_ref.k_ref.v_ref, ...), custom_call_target="tpu_custom_call" | custom-call | flops 4294967296 | bytes 2097152 | tf_op jit(solution)/shard_map/attend/pallas_call | solution.py:454
  238.7 16.9 %attend.3 = (bf16[1024,256]{1,0:T(8,128)(2,1)}, f32[8,1024]{1,0:T(8,128)}) custom-call(s32[1]{0:T(128)} %dynamic_slice.80.length_ref, f32[8,32]{1,0:T(8,128)} %constant_dynamic-slice_fusion.8.table_ref, bf16[1024,1536]{1,0:T(8,128)(2,1)} %product_nt.2.q_ref.k_ref.v_ref, bf16[1024,1536]{1,0:T(8,128)(2,1)} %product_nt.2.q_ref.k_ref.v_ref, ...), custom_call_target="tpu_custom_call" | custom-call | flops 4294967296 | bytes 2097152 | tf_op jit(solution)/shard_map/attend/pallas_call | solution.py:454
  264.9 20.1 %collective-permute-done.21 = bf16[2,2,256,512]{3,2,1,0:T(8,128)(2,1)S(1)} collective-permute-done((bf16[2,2,256,512]{3,2,1,0:T(8,128)(2,1)}, bf16[2,2,256,512]{3,2,1,0:T(8,128)(2,1)S(1)}, u32[]{:S(2)}, u32[]{:S(2)}) %collective-permute-start.21) | collective-permute-done | bytes 1048608 | tf_op jit(solution)/shard_map/ppermute | solution.py:559
  304.4 10.8 %collective-permute-done.26.refs_2_.refs_3_ = bf16[2,256,512]{2,1,0:T(8,128)(2,1)S(1)} collective-permute-done((bf16[2,256,512]{2,1,0:T(8,128)(2,1)S(1)}, bf16[2,256,512]{2,1,0:T(8,128)(2,1)S(1)}, u32[]{:S(2)}, u32[]{:S(2)}) %collective-permute-start.26) | collective-permute-done | bytes 524320 | tf_op jit(solution)/shard_map/ppermute | solution.py:559
  332.4 17.5 %ffn_in.1 = (bf16[1024,1280]{1,0:T(8,128)(2,1)}, bf16[1024,1280]{1,0:T(8,128)(2,1)}, bf16[1024,1280]{1,0:T(8,128)(2,1)}) custom-call(s32[4]{0:T(128)} %add_multiply_fusion.starts_ref, bf16[2,256,512]{2,1,0:T(8,128)(2,1)} %copy-done.32, bf16[2,256,512]{2,1,0:T(8,128)(2,1)} %copy-done.53, bf16[2,256,512]{2,1,0:T(8,128)(2,1)} %copy-done.51, ...), custom_call_target="tpu_custom_call" | custom-call | flops 10737418240 | bytes 22544384 | tf_op jit(solution)/shard_map/ffn_in/pallas_call | solution.py:214
  359.9 15.2 %ffn_back.1.refs_0_ = bf16[1024,2560]{1,0:T(8,128)(2,1)} custom-call(s32[4]{0:T(128)} %add_multiply_fusion.starts_ref, bf16[2,256,512]{2,1,0:T(8,128)(2,1)} %copy-done.8, bf16[2,256,512]{2,1,0:T(8,128)(2,1)} %copy-done.26, bf16[2,256,512]{2,1,0:T(8,128)(2,1)} %copy-done.25, bf16[2,256,512]{2,1,0:T(8,128)(2,1)} %collective-permute-done.17.refs_4_.refs_3_, ...), custom_call_target="tpu_custom_call" | custom-call | flops 5368709120 | bytes 19922944 | tf_op jit(solution)/shard_map/ffn_back/pallas_call | solution.py:245
  375.1 16.4 %product_nn.5 = (bf16[2,2,256,512]{3,2,1,0:T(8,128)(2,1)}, bf16[2,2,256,512]{3,2,1,0:T(8,128)(2,1)}, bf16[2,2,256,512]{3,2,1,0:T(8,128)(2,1)}, bf16[2,2,256,512]{3,2,1,0:T(8,128)(2,1)}) custom-call(s32[4]{0:T(128)} %add_multiply_fusion.starts_ref, bf16[1024,2560]{1,0:T(8,128)(2,1)} %ffn_back.1.refs_0_, bf16[4,2,1280,512]{3,2,1,0:T(8,128)(2,1)} %bitcast.167), custom_call_target="tpu_custom_call" | custom-call | flops 10737418240 | bytes 19922944 | tf_op jit(solution)/shard_map/product_nn/pallas_call | solution.py:123
  393.9 15.9 %product_tn.5 = bf16[4,2560,512]{2,1,0:T(8,128)(2,1)} custom-call(s32[4]{0:T(128)} %add_multiply_fusion.starts_ref, bf16[1024,2560]{1,0:T(8,128)(2,1)} %ffn_back.1.refs_0_, bf16[2,256,512]{2,1,0:T(8,128)(2,1)} %copy-done.32, bf16[2,256,512]{2,1,0:T(8,128)(2,1)} %copy-done.53, bf16[2,256,512]{2,1,0:T(8,128)(2,1)} %copy-done.51, ...), custom_call_target="tpu_custom_call" | custom-call | flops 10737418240 | bytes 19922944 | tf_op jit(solution)/shard_map/product_tn/pallas_call | solution.py:171
  418.6 10.0 %product_nn.6 = (bf16[2,2,256,512]{3,2,1,0:T(8,128)(2,1)}, bf16[2,2,256,512]{3,2,1,0:T(8,128)(2,1)}, bf16[2,2,256,512]{3,2,1,0:T(8,128)(2,1)}, bf16[2,2,256,512]{3,2,1,0:T(8,128)(2,1)}) custom-call(s32[4]{0:T(128)} %add_multiply_fusion.starts_ref, bf16[1024,1280]{1,0:T(8,128)(2,1)} %get-tuple-element.97.refs_0_, bf16[4,2,640,512]{3,2,1,0:T(8,128)(2,1)} %bitcast.126), custom_call_target="tpu_custom_call" | custom-call | flops 5368709120 | bytes 12058624 | tf_op jit(solution)/shard_map/product_nn/pallas_call | solution.py:123
  439.1 10.8 %collective-permute-done.36.refs_2_.refs_4_ = bf16[2,256,512]{2,1,0:T(8,128)(2,1)S(1)} collective-permute-done((bf16[2,256,512]{2,1,0:T(8,128)(2,1)S(1)}, bf16[2,256,512]{2,1,0:T(8,128)(2,1)S(1)}, u32[]{:S(2)}, u32[]{:S(2)}) %collective-permute-start.36) | collective-permute-done | bytes 524320 | tf_op jit(solution)/shard_map/ppermute | solution.py:559
  479.7 28.7 %attend_back.2 = (bf16[1024,768]{1,0:T(8,128)(2,1)}, f32[4,32,128]{2,1,0:T(8,128)}) custom-call(s32[1]{0:T(128)} %dynamic_slice.80.length_ref, f32[8,32]{1,0:T(8,128)} %constant_dynamic-slice_fusion.8.table_ref, bf16[1024,1536]{1,0:T(8,128)(2,1)} %product_nt.2.q_ref.k_ref.v_ref, bf16[1024,1536]{1,0:T(8,128)(2,1)} %product_nt.2.q_ref.k_ref.v_ref, ...), custom_call_target="tpu_custom_call" | custom-call | flops 10737418240 | bytes 4194304 | tf_op jit(solution)/shard_map/attend_back/pallas_call | solution.py:481
  516.1 28.8 %attend_back.3 = (bf16[1024,768]{1,0:T(8,128)(2,1)}, f32[4,32,128]{2,1,0:T(8,128)}) custom-call(s32[1]{0:T(128)} %dynamic_slice.80.length_ref, f32[8,32]{1,0:T(8,128)} %constant_dynamic-slice_fusion.8.table_ref, bf16[1024,1536]{1,0:T(8,128)(2,1)} %product_nt.2.q_ref.k_ref.v_ref, bf16[1024,1536]{1,0:T(8,128)(2,1)} %product_nt.2.q_ref.k_ref.v_ref, ...), custom_call_target="tpu_custom_call" | custom-call | flops 10737418240 | bytes 4194304 | tf_op jit(solution)/shard_map/attend_back/pallas_call | solution.py:481
  544.9 11.6 %product_tn.7 = bf16[4,1536,512]{2,1,0:T(8,128)(2,1)} custom-call(s32[4]{0:T(128)} %add_multiply_fusion.starts_ref, bf16[1024,768]{1,0:T(8,128)(2,1)} %get-tuple-element.112.refs_0_, bf16[1024,768]{1,0:T(8,128)(2,1)} %get-tuple-element.117.refs_1_, bf16[2,256,512]{2,1,0:T(8,128)(2,1)} %get-tuple-element.169.refs_0_.refs_2_, ...), custom_call_target="tpu_custom_call" | custom-call | flops 6442450944 | bytes 13631488 | tf_op jit(solution)/shard_map/product_tn/pallas_call | solution.py:171
  559.1 67.8 %reduce-scatter.7.cloned.1.call-done.refs_0_ = bf16[1280,512]{1,0:T(8,128)(2,1)} async-done(((bf16[10240,512]{1,0:T(8,128)(2,1)}), bf16[1280,512]{1,0:T(8,128)(2,1)}) %reduce-scatter.7.cloned.1.call-update) | async-done | bytes 1310736 | tf_op jit(solution)/shard_map/reduce_scatter | solution.py:818
  628.4 11.2 %product_nn.7 = (bf16[2,2,256,512]{3,2,1,0:T(8,128)(2,1)}, bf16[2,2,256,512]{3,2,1,0:T(8,128)(2,1)}, bf16[2,2,256,512]{3,2,1,0:T(8,128)(2,1)}, bf16[2,2,256,512]{3,2,1,0:T(8,128)(2,1)}) custom-call(s32[4]{0:T(128)} %add_multiply_fusion.starts_ref, bf16[1024,768]{1,0:T(8,128)(2,1)} %get-tuple-element.112.refs_0_, ...), custom_call_target="tpu_custom_call" | custom-call | flops 6442450944 | bytes 13631488 | tf_op jit(solution)/shard_map/product_nn/pallas_call | solution.py:123
  647.4 31.0 %collective-permute-start.47 = (bf16[256,512]{1,0:T(8,128)(2,1)S(1)}, bf16[256,512]{1,0:T(8,128)(2,1)S(1)}, u32[]{:S(2)}, u32[]{:S(2)}) collective-permute-start(bf16[256,512]{1,0:T(8,128)(2,1)S(1)} %get-tuple-element.155), channel_id=1, source_target_pairs={{16,0},{17,1},{0,2},{1,3},{18,16},{19,17},{2,18},{3,19},{20,4},{21... | collective-permute-start | bytes 786440 | tf_op jit(solution)/shard_map/ppermute | solution.py:694
  688.4 25.5 %collective-permute-done.48.refs_3_ = bf16[256,512]{1,0:T(8,128)(2,1)S(1)} collective-permute-done((bf16[256,512]{1,0:T(8,128)(2,1)S(1)}, bf16[256,512]{1,0:T(8,128)(2,1)S(1)}, u32[]{:S(2)}, u32[]{:S(2)}) %collective-permute-start.48) | collective-permute-done | bytes 262176 | tf_op jit(solution)/shard_map/ppermute | solution.py:694
  717.2 10.7 %collective-permute-done.52 = bf16[2,256,512]{2,1,0:T(8,128)(2,1)S(1)} collective-permute-done((bf16[2,256,512]{2,1,0:T(8,128)(2,1)S(1)}, bf16[2,256,512]{2,1,0:T(8,128)(2,1)S(1)}, u32[]{:S(2)}, u32[]{:S(2)}) %collective-permute-start.52) | collective-permute-done | bytes 524320 | tf_op jit(solution)/shard_map/ppermute | solution.py:559
  747.0 11.8 %collective-permute-done.68 = f32[10,512]{1,0:T(8,128)S(1)} collective-permute-done((f32[10,512]{1,0:T(8,128)S(1)}, f32[10,512]{1,0:T(8,128)S(1)}, u32[]{:S(2)}, u32[]{:S(2)}) %collective-permute-start.68) | collective-permute-done | bytes 20512 | tf_op jit(solution)/shard_map/ppermute | solution.py:559
  760.1 14.6 %collective-permute-done.65.refs_3_ = bf16[256,512]{1,0:T(8,128)(2,1)S(1)} collective-permute-done((bf16[256,512]{1,0:T(8,128)(2,1)S(1)}, bf16[256,512]{1,0:T(8,128)(2,1)S(1)}, u32[]{:S(2)}, u32[]{:S(2)}) %collective-permute-start.65) | collective-permute-done | bytes 262176 | tf_op jit(solution)/shard_map/ppermute | solution.py:694
  (373 shorter events, 274.3 us)
Async XLA Ops:
  7.2 185.2 %all-gather.5.cloned.1.call-start = ((), (), s32[]{:S(2)}) async-start(), calls=%async_computation.4 | async-start | bytes 7077888 | tf_op jit(solution)/shard_map/all_gather | solution.py:781
  10.5 246.0 %all-gather.7.cloned.1.call-start = ((), (), s32[]{:S(2)}) async-start(), calls=%async_computation.5 | async-start | bytes 2359296 | tf_op jit(solution)/shard_map/all_gather | solution.py:781
  12.3 320.1 %all-gather.9.cloned.1.call-start = ((), (), s32[]{:S(2)}) async-start(), calls=%async_computation.6 | async-start | bytes 11796480 | tf_op jit(solution)/shard_map/all_gather | solution.py:781
  16.6 77.0 %collective-permute-start.3 = (bf16[264,512]{1,0:T(8,128)(2,1)}, bf16[264,512]{1,0:T(8,128)(2,1)S(1)}, u32[]{:S(2)}, u32[]{:S(2)}) collective-permute-start(bf16[264,512]{1,0:T(8,128)(2,1)} %get-tuple-element.180), channel_id=1, source_target_pairs={{0,16},{1,17},{2,0},{3,1},{16,18},{17,19},{18,2},{19,3},{4,20},{5,... | collective-permute-start | bytes 811016 | tf_op jit(solution)/shard_map/ppermute | solution.py:681
  22.4 71.2 %collective-permute-start.4 = (bf16[264,512]{1,0:T(8,128)(2,1)}, bf16[264,512]{1,0:T(8,128)(2,1)S(1)}, u32[]{:S(2)}, u32[]{:S(2)}) collective-permute-start(bf16[264,512]{1,0:T(8,128)(2,1)} %get-tuple-element.181), channel_id=1, source_target_pairs={{0,1},{1,16},{2,17},{3,0},{16,3},{17,18},{18,19},{19,2},{4,5},{5,2... | collective-permute-start | bytes 811016 | tf_op jit(solution)/shard_map/ppermute | solution.py:681
  24.0 69.6 %collective-permute-start.2 = (bf16[264,512]{1,0:T(8,128)(2,1)}, bf16[264,512]{1,0:T(8,128)(2,1)}, u32[]{:S(2)}, u32[]{:S(2)}) collective-permute-start(bf16[264,512]{1,0:T(8,128)(2,1)} %get-tuple-element.179), channel_id=1, source_target_pairs={{0,17},{1,0},{2,1},{3,16},{16,19},{17,2},{18,3},{19,18},{4,21},{5,... | collective-permute-start | bytes 811016 | tf_op jit(solution)/shard_map/ppermute | solution.py:681
  109.1 250.8 %all-gather.11.cloned.1.call-start = ((), (), s32[]{:S(2)}) async-start(), calls=%async_computation.7 | async-start | bytes 5898240 | tf_op jit(solution)/shard_map/all_gather | solution.py:781
  114.8 356.1 %reduce-scatter.5.cloned.1.call-start = ((), (), s32[]{:S(2)}) async-start(), calls=%async_computation.8 | async-start | bytes 5898240 | tf_op jit(solution)/shard_map/reduce_scatter | solution.py:818
  115.5 41.6 %collective-permute-start.11 = (bf16[256,512]{1,0:T(8,128)(2,1)}, bf16[256,512]{1,0:T(8,128)(2,1)S(1)}, u32[]{:S(2)}, u32[]{:S(2)}) collective-permute-start(bf16[256,512]{1,0:T(8,128)(2,1)} %get-tuple-element.75), channel_id=1, source_target_pairs={{0,0},{1,1},{2,16},{3,17},{16,2},{17,3},{18,18},{19,19},{4,4},{5,5... | collective-permute-start | bytes 786440 | tf_op jit(solution)/shard_map/ppermute | solution.py:681
  117.1 41.5 %collective-permute-start.12 = (bf16[256,512]{1,0:T(8,128)(2,1)}, bf16[256,512]{1,0:T(8,128)(2,1)S(1)}, u32[]{:S(2)}, u32[]{:S(2)}) collective-permute-start(bf16[256,512]{1,0:T(8,128)(2,1)} %get-tuple-element.76), channel_id=1, source_target_pairs={{0,17},{1,0},{2,1},{3,16},{16,19},{17,2},{18,3},{19,18},{4,21},{5,... | collective-permute-start | bytes 786440 | tf_op jit(solution)/shard_map/ppermute | solution.py:681
  146.6 45.0 %collective-permute-start.13 = (bf16[256,512]{1,0:T(8,128)(2,1)}, bf16[256,512]{1,0:T(8,128)(2,1)S(1)}, u32[]{:S(2)}, u32[]{:S(2)}) collective-permute-start(bf16[256,512]{1,0:T(8,128)(2,1)} %get-tuple-element.77), channel_id=1, source_target_pairs={{0,16},{1,17},{2,0},{3,1},{16,18},{17,19},{18,2},{19,3},{4,20},{5,... | collective-permute-start | bytes 786440 | tf_op jit(solution)/shard_map/ppermute | solution.py:681
  150.0 41.6 %collective-permute-start.14 = (bf16[256,512]{1,0:T(8,128)(2,1)}, bf16[256,512]{1,0:T(8,128)(2,1)S(1)}, u32[]{:S(2)}, u32[]{:S(2)}) collective-permute-start(bf16[256,512]{1,0:T(8,128)(2,1)} %get-tuple-element.78), channel_id=1, source_target_pairs={{0,1},{1,16},{2,17},{3,0},{16,3},{17,18},{18,19},{19,2},{4,5},{5,2... | collective-permute-start | bytes 786440 | tf_op jit(solution)/shard_map/ppermute | solution.py:681
  151.4 42.7 %collective-permute-start.5 = (bf16[2,256,512]{2,1,0:T(8,128)(2,1)}, bf16[2,256,512]{2,1,0:T(8,128)(2,1)}, u32[]{:S(2)}, u32[]{:S(2)}) collective-permute-start(bf16[2,256,512]{2,1,0:T(8,128)(2,1)} %get-tuple-element.169.refs_0_.refs_2_), channel_id=1, source_target_pairs={{0,16},{16,0},{1,17},{17,1},{2,18},{18,2},{3,19},{19,3},{4,20},{20... | collective-permute-start | bytes 1572872 | tf_op jit(solution)/shard_map/ppermute | solution.py:559
  192.5 42.6 %collective-permute-start.16 = (bf16[2,256,512]{2,1,0:T(8,128)(2,1)S(1)}, bf16[2,256,512]{2,1,0:T(8,128)(2,1)S(1)}, u32[]{:S(2)}, u32[]{:S(2)}) collective-permute-start(bf16[2,256,512]{2,1,0:T(8,128)(2,1)S(1)} %get-tuple-element.163.refs_1_.refs_0_), channel_id=1, source_target_pairs={{0,4},{4,0},{1,5},{5,1},{2,6},{6,2},{3,7},{7,3},{8,12},{12,8},{9,1... | collective-permute-start | bytes 1572872 | tf_op jit(solution)/shard_map/ppermute | solution.py:559
  194.1 61.5 %collective-permute-start.15 = (bf16[2,256,512]{2,1,0:T(8,128)(2,1)S(1)}, bf16[2,256,512]{2,1,0:T(8,128)(2,1)S(1)}, u32[]{:S(2)}, u32[]{:S(2)}) collective-permute-start(bf16[2,256,512]{2,1,0:T(8,128)(2,1)S(1)} %get-tuple-element.163.refs_1_.refs_0_), channel_id=1, source_target_pairs={{0,16},{16,0},{1,17},{17,1},{2,18},{18,2},{3,19},{19,3},{4,20},{20... | collective-permute-start | bytes 1572872 | tf_op jit(solution)/shard_map/ppermute | solution.py:559
  197.0 58.6 %collective-permute-start.18 = (bf16[2,256,512]{2,1,0:T(8,128)(2,1)S(1)}, bf16[2,256,512]{2,1,0:T(8,128)(2,1)S(1)}, u32[]{:S(2)}, u32[]{:S(2)}) collective-permute-start(bf16[2,256,512]{2,1,0:T(8,128)(2,1)S(1)} %get-tuple-element.162.refs_5_.refs_4_), channel_id=1, source_target_pairs={{0,4},{4,0},{1,5},{5,1},{2,6},{6,2},{3,7},{7,3},{8,12},{12,8},{9,1... | collective-permute-start | bytes 1572872 | tf_op jit(solution)/shard_map/ppermute | solution.py:559
  359.8 196.7 %reduce-scatter.9.cloned.1.call-start = ((), (), s32[]{:S(2)}) async-start(), calls=%async_computation.10 | async-start | bytes 2359296 | tf_op jit(solution)/shard_map/reduce_scatter | solution.py:818
  470.8 156.1 %reduce-scatter.7.cloned.1.call-start = ((), (), s32[]{:S(2)}) async-start(), calls=%async_computation.9 | async-start | bytes 11796480 | tf_op jit(solution)/shard_map/reduce_scatter | solution.py:818
  471.5 245.6 %reduce-scatter.11.cloned.1.call-start = ((), (), s32[]{:S(2)}) async-start(), calls=%async_computation.11 | async-start | bytes 7077888 | tf_op jit(solution)/shard_map/reduce_scatter | solution.py:818
  626.9 87.0 %collective-permute-start.51 = (bf16[1280,512]{1,0:T(8,128)(2,1)}, bf16[1280,512]{1,0:T(8,128)(2,1)}, u32[]{:S(2)}, u32[]{:S(2)}) collective-permute-start(bf16[1280,512]{1,0:T(8,128)(2,1)} %reduce-scatter.7.cloned.1.call-done.refs_0_), channel_id=1, source_target_pairs={{0,16},{16,0},{1,17},{17,1},{2,18},{18,2},{3,19},{19,3},{4,20},{20... | collective-permute-start | bytes 3932168 | tf_op jit(solution)/shard_map/ppermute | solution.py:559
  639.6 74.3 %collective-permute-start.50 = (bf16[2,2,256,512]{3,2,1,0:T(8,128)(2,1)}, bf16[2,2,256,512]{3,2,1,0:T(8,128)(2,1)S(1)}, u32[]{:S(2)}, u32[]{:S(2)}) collective-permute-start(bf16[2,2,256,512]{3,2,1,0:T(8,128)(2,1)} %get-tuple-element.119), channel_id=1, source_target_pairs={{0,4},{4,0},{1,5},{5,1},{2,6},{6,2},{3,7},{7,3},{8,12},{12,8},{9,1... | collective-permute-start | bytes 3145736 | tf_op jit(solution)/shard_map/ppermute | solution.py:559
  642.5 72.4 %collective-permute-start.53 = (bf16[2,2,256,512]{3,2,1,0:T(8,128)(2,1)S(1)}, bf16[2,2,256,512]{3,2,1,0:T(8,128)(2,1)S(1)}, u32[]{:S(2)}, u32[]{:S(2)}) collective-permute-start(bf16[2,2,256,512]{3,2,1,0:T(8,128)(2,1)S(1)} %copy-done.50), channel_id=1, source_target_pairs={{0,16},{16,0},{1,17},{17,1},{2,18},{18,2},{3,19},{19,3},{4,20},{20... | collective-permute-start | bytes 3145736 | tf_op jit(solution)/shard_map/ppermute | solution.py:559
  730.0 48.7 %collective-permute-start.72 = (bf16[768,512]{1,0:T(8,128)(2,1)}, bf16[768,512]{1,0:T(8,128)(2,1)}, u32[]{:S(2)}, u32[]{:S(2)}) collective-permute-start(bf16[768,512]{1,0:T(8,128)(2,1)} %reduce-scatter.11.cloned.1.call-done.refs_0_), channel_id=1, source_target_pairs={{0,16},{16,0},{1,17},{17,1},{2,18},{18,2},{3,19},{19,3},{4,20},{20... | collective-permute-start | bytes 2359304 | tf_op jit(solution)/shard_map/ppermute | solution.py:559
  758.9 41.9 %collective-permute-start.61 = (bf16[1280,512]{1,0:T(8,128)(2,1)S(1)}, bf16[1280,512]{1,0:T(8,128)(2,1)S(1)}, u32[]{:S(2)}, u32[]{:S(2)}) collective-permute-start(bf16[1280,512]{1,0:T(8,128)(2,1)S(1)} %copy-done.9), channel_id=1, source_target_pairs={{0,8},{8,0},{1,9},{9,1},{2,10},{10,2},{3,11},{11,3},{4,12},{12,4},... | collective-permute-start | bytes 3932168 | tf_op jit(solution)/shard_map/ppermute | solution.py:559
  (119 other events, 2252.8 us)
Sparse Core Ops, SparseCore 0:
  10.6 110.8 all-gather.4
  123.7 54.2 all-gather.6
  180.2 103.0 all-gather.8
  284.7 54.9 all-gather.10
  360.0 68.9 reduce-scatter.4
  470.9 44.7 reduce-scatter.8
  518.5 108.2 reduce-scatter.6
  629.2 84.2 reduce-scatter.10

commit v4 on v3

--- a/solution.py
+++ b/solution.py
@@ -649,86 +649,60 @@
     return lax.all_gather(part, ("y", "c"), axis=0), part
 
 
-def routes(nz, k):
-    many = nz // 2
-    pairs = []
-    for y in range(2):
-        for z in range(nz):
-            piece = (z + k) % nz
-            pairs.append((y * nz + z, (piece // many) * nz + y * many + piece % many))
-    return pairs
-
-
-def turned(pieces, shift):
-    n = len(pieces)
-    options = [jnp.stack([pieces[(i + s) % n] for i in range(n)]) for s in range(n)]
-    return lax.select_n(lax.rem(shift + n, n), *options)
-
-
-def to_groups(stored, extra, *earlier):
-    count, _, t, width = stored.shape
-    nz = 2 * count
-    y, z = lax.axis_index("y"), lax.axis_index("z")
-    arrived = []
-    for k in range(nz):
-        place = lax.rem(z + k, nz)
-        corner = (lax.rem(place, count), lax.div(place, count), 0, 0)
-        piece = lax.dynamic_slice(stored, corner, (1, 1, t, width)).reshape(t, width)
-        if extra is not None:
-            piece = jnp.concatenate([piece, extra])
-        if earlier:
-            piece = after(piece, *earlier)
-        arrived.append(lax.ppermute(piece, ("y", "z"), routes(nz, k)))
-    mine = y * count + lax.rem(z, count)
-    return [arrived[(nz - i) % nz] for i in range(nz)], nz - mine
+def to_groups(halves, other, extra):
+    count, _, t, width = halves.shape
+    both = paired(pick(halves, lax.axis_index("y"), 1), other, "y").reshape(2 * count, t, width)
+    if extra is not None:
+        wide = jnp.broadcast_to(extra[None], (2 * count, *extra.shape))
+        both = jnp.concatenate([both, wide], axis=1)
+    return lax.all_to_all(both, "z", 0, 0, tiled=True)
 
 
 def from_groups(mine):
     nz, t, width = mine.shape
-    y, z = lax.axis_index("y"), lax.axis_index("z")
-    count = nz // 2
-    own = y * count + lax.rem(z, count)
-    arrived = []
-    for k in range(nz):
-        piece = pick(mine, lax.rem(own - k + nz, nz), 0)
-        arrived.append(lax.ppermute(piece, ("y", "z"), [(b, a) for a, b in routes(nz, k)]))
-    return arrived
-
-
-def settle_kernel(shift_ref, *refs):
-    pieces, out_ref = refs[:-1], refs[-1]
-    count = len(pieces)
-    for k in range(count):
-
-        @pl.when(lax.rem(pl.program_id(0) + shift_ref[0], count) == k)
-        def _():
-            out_ref[0, 0] = pieces[k][...].astype(out_ref.dtype)
+    back = lax.all_to_all(mine, "z", 0, 0, tiled=True).reshape(2, nz // 2, t, width)
+    leaving = pick(back, 1 - lax.axis_index("y"), 0)
+    return (back, hop(leaving, "y")), leaving
+
+
+def settle_kernel(y_ref, back_ref, other_ref, out_ref):
+    j, y = pl.program_id(0), pl.program_id(1)
+
+    @pl.when(y == y_ref[0])
+    def _():
+        out_ref[0, 0] = back_ref[y, j].astype(out_ref.dtype)
+
+    @pl.when(y != y_ref[0])
+    def _():
+        out_ref[0, 0] = other_ref[j].astype(out_ref.dtype)
 
 
 def settle(arrived, dtype):
-    nz = len(arrived)
-    t, width = arrived[0].shape
-    count = nz // 2
-    shift = (nz - lax.axis_index("z")).astype(jnp.int32).reshape(1)
+    back, other = arrived
+    _, count, t, width = back.shape
+    y = lax.axis_index("y").astype(jnp.int32).reshape(1)
     out = pl.pallas_call(
         settle_kernel,
-        grid=(nz,),
-        in_specs=[pl.BlockSpec(memory_space=pltpu.SMEM)]
-        + [pl.BlockSpec((t, width), lambda i: (0, 0))] * nz,
-        out_specs=pl.BlockSpec((1, 1, t, width), lambda i: (lax.rem(i, count), lax.div(i, count), 0, 0)),
+        grid=(count, 2),
+        in_specs=[
+            pl.BlockSpec(memory_space=pltpu.SMEM),
+            pl.BlockSpec(back.shape, lambda j, y: (0, 0, 0, 0)),
+            pl.BlockSpec(other.shape, lambda j, y: (0, 0, 0)),
+        ],
+        out_specs=pl.BlockSpec((1, 1, t, width), lambda j, y: (j, y, 0, 0)),
         out_shape=jax.ShapeDtypeStruct((count, 2, t, width), dtype),
-        compiler_params=params(1),
-        cost_estimate=cost(0, 6 * nz * t * width),
+        compiler_params=params(2),
+        cost_estimate=cost(0, 12 * count * t * width),
         name="settle",
-    )(shift, *arrived)
+    )(y, back, other)
     return out.reshape(count, 2 * t, width)
 
 
 def settle_plain(arrived, dtype):
-    nz = len(arrived)
-    t, width = arrived[0].shape
-    back = turned(arrived, nz - lax.axis_index("z")).reshape(2, nz // 2, t, width)
-    return back.transpose(1, 0, 2, 3).reshape(nz // 2, 2 * t, width).astype(dtype)
+    back, other = arrived
+    _, count, t, width = back.shape
+    both = paired(pick(back, lax.axis_index("y"), 0), other, "y")
+    return both.transpose(1, 0, 2, 3).reshape(count, 2 * t, width).astype(dtype)
 
 
 def sum_all(value, nx, nz, *earlier):
@@ -761,6 +735,7 @@
         [attn_gain[None], ffn_gain[None], jnp.pad(bias_table.reshape(1, -1), ((0, 0), (0, width - buckets * mine)))]
     )
     small = jnp.pad(small, ((0, 5), (0, 0)))
+    leaving = pick(stored_in, 1 - y, 1)
 
     query_key_rows = jnp.transpose(query_key, (1, 2, 3, 0))
     value_rows = jnp.transpose(value_proj, (1, 2, 0))
@@ -776,20 +751,23 @@
     def flat(rows):
         return rows.reshape(-1, width)
 
-    def spread(blocks):
-        rows = jnp.concatenate([flat(block) for block in blocks])
+    def spread(rows):
         gathered = lax.all_gather(rows, ("z", "c"), axis=0, tiled=True)
         return gathered.reshape(nz, nc, rows.shape[0], width)
 
     own_pair = own(query_key_rows, heads)
     own_attn = [own_pair[:, 0], own_pair[:, 1], own(value_rows, heads), own(out_proj, heads)]
-    w_attn = spread(own_attn[:-1])
-    w_out = spread(own_attn[-1:])
+    own_attn = jnp.concatenate([flat(rows) for rows in own_attn])
+    w_attn = spread(own_attn)
+    other = after(hop(leaving, "y"), own_attn)
+    own_pair = own(after(gate_up_rows, other), units)
+    own_gate_up = jnp.concatenate([flat(own_pair[:, 0]), flat(own_pair[:, 1])])
+    w_gate_up = spread(own_gate_up)
+    own_down = flat(own(after(down_proj, other), units))
+    w_down = spread(own_down)
     qkv_count, out_count = 3 * heads * 64, heads * 64
 
-    arrived, shift = to_groups(stored_in, small)
-    first_in = arrived[0]
-    arrived = turned(arrived, shift)
+    arrived = after(to_groups(stored_in, other, small), own_gate_up, own_down)
     tokens = arrived[:, :count].astype(F32)
     small = arrived[:, count:]
     gain_one = small[:, :1].astype(F32)
@@ -838,11 +816,9 @@
         return (first[0], second[0]), jnp.concatenate([first[1], second[1]])
 
     scale_one = scale_of(tokens)
-    normed, normed_first, _ = gather((tokens * scale_one * gain_one).astype(BF))
-    own_pair = own(after(gate_up_rows, *normed_first), units)
-    w_gate_up = spread([own_pair[:, 0], own_pair[:, 1]])
-    w_down = spread([own(after(down_proj, *normed_first), units)])
-    upstream = live * turned(*to_groups(stored_cot, None, first_in)).astype(F32)
+    normed, _, _ = gather((tokens * scale_one * gain_one).astype(BF))
+    cot_other = hop(pick(stored_cot, 1 - y, 1), "y")
+    upstream = live * to_groups(stored_cot, after(cot_other, arrived), None).astype(F32)
     upstream_rounded = after(upstream.astype(BF), w_attn)
     projected = nt(normed, w_attn, 0, qkv_count, starts)
     if fits:
@@ -855,7 +831,7 @@
         attended, lse = forward(projected, length, table, nc, heads)
         attended = (attended,)
     heads_out = [after(attended[0], *cot_last), *attended[1:]]
-    hidden = tokens + scatter(nn(heads_out, w_out, 0, out_count, starts))[0]
+    hidden = tokens + scatter(nn(heads_out, w_attn, qkv_count, out_count, starts))[0]
     scale_two = scale_of(hidden)
     normed_two, _, _ = gather((hidden * scale_two * gain_two).astype(BF))
     gate, up, activated = ffn_one(normed_two, w_gate_up, starts)
@@ -871,26 +847,26 @@
     through, ffn_gain_part = norm_back(hidden, scale_two, gain_two, grad_two)
     grad_hidden = upstream + through
     grad_branch, _, branch_last = gather(after(grad_hidden.astype(BF), branch_parts[0]))
-    grad_attended = nt(grad_branch, w_out, 0, out_count, starts)
+    grad_attended = nt(grad_branch, w_attn, qkv_count, out_count, starts)
     out_partial = tn(attended, grad_branch, starts)
     branch_parts = [after(part, *branch_last) for part in branch_parts]
     branch, branch_first, branch_last = scatter(branch_parts)
     down_pieces, down_last = shared(after(down_part, grad_attended))
     grad_projected, table_part = attend_back_all(after(grad_attended, out_partial), *branch_first)
-    out_part = reduce(out_partial)
     last = after(grad_projected[-1], *branch_last, down_last)
     grad_projected = [*grad_projected[:-1], last]
     qkv_partial = tn(grad_projected, normed, starts)
-    qkv_part = reduce(after(qkv_partial, out_part))
+    qkv_part = reduce(after(qkv_partial, gate_up_part))
     one_parts = nn(grad_projected, w_attn, 0, qkv_count, starts)
     gate_up_pieces, gate_up_last = shared(after(gate_up_part, grad_projected[0]))
-    outputs = from_groups((live * (hidden + branch)).astype(BF))
-    grad_one, _, one_last = scatter(one_parts, gate_up_last, *outputs)
+    outputs, _ = from_groups((live * (hidden + branch)).astype(BF))
+    grad_one, one_first, one_last = scatter(one_parts, outputs[0], gate_up_last)
+    out_part = reduce(after(out_partial, *one_first))
     through, attn_gain_part = norm_back(tokens, scale_one, gain_one, grad_one)
-    input_grad = input_last = from_groups((grad_hidden + through).astype(BF))
+    input_grad, input_leaves = from_groups((grad_hidden + through).astype(BF))
     outputs = stored_from(outputs, BF)
 
-    out_pieces, _ = shared(after(out_part, *one_last))
+    out_pieces, _ = shared(after(out_part, input_leaves))
     qkv_pieces, _ = shared(after(qkv_part, *one_last))
     if fits:
         here = jnp.stack([y, c]).astype(jnp.int32)
@@ -926,7 +902,8 @@
         qkv_all = qkv_pieces.astype(F32).reshape(parts, 3, heads, 64, width)
         qkv_all = qkv_all.transpose(0, 2, 1, 3, 4).reshape(-1, 3, 64, width)
         query_key_all, value_all = qkv_all[:, :2], qkv_all[:, 2]
-    input_grad = [after(part, down_all, out_all, gate_up_all) for part in input_grad]
+    back, other = input_grad
+    input_grad = back, after(other, down_all, gate_up_all)
     input_grad = stored_from(input_grad, F32)
     down_all, out_all = down_all.reshape(down_proj.shape), out_all.reshape(out_proj.shape)
 
@@ -935,7 +912,7 @@
     every = lax.dynamic_update_slice_in_dim(every, table_part, (x * 2 + y) * local_heads, 0)
     both = jnp.concatenate([attn_gain_part, ffn_gain_part])
     if every.size % width == 0:
-        both = sum_all(jnp.concatenate([both, every.reshape(-1, width)]), nx, nz, *input_last)
+        both = sum_all(jnp.concatenate([both, every.reshape(-1, width)]), nx, nz, input_leaves)
         every = both[2 * nz :].reshape(-1, buckets)
     else:
         both, every = sum_all(both, nx, nz), sum_all(every, nx, nz)

time: 829 us -> 706 us (0.85)
  waiting for transfers between devices: 355 us -> 263 us
  starting transfers between devices: 142 us -> 100 us
  other arithmetic: 36.1 us -> 47 us
    ppermute x16 -> x0, waiting for transfers between devices: 151 us -> none  [the longest x8 101 us: to_groups(): arrived.append(lax.ppermute(piece, ('y', 'z'), routes(nz, k)))]
    ppermute x16 -> x0, starting transfers between devices: 85.2 us -> none  [the longest x8 44.5 us: to_groups(): arrived.append(lax.ppermute(piece, ('y', 'z'), routes(nz, k)))]
    all_to_all x0 -> x4, waiting for transfers between devices: none -> 80.2 us  [the longest x2 53.5 us: to_groups(): return lax.all_to_all(both, 'z', 0, 0, tiled=True)]
    reduce_scatter x4, waiting for transfers between devices: 67.8 us -> 27 us  [reduce(): return lax.psum_scatter(rows, ('z', 'c'), scatter_dimension=0, tiled=True)]
    all_to_all x0 -> x4, starting transfers between devices: none -> 20.9 us  [the longest x2 10.9 us: to_groups(): return lax.all_to_all(both, 'z', 0, 0, tiled=True)]
    ppermute x55 -> x59, waiting for transfers between devices: 127 us -> 144 us  [hop(): return lax.ppermute(value, axis, swap)]
    ppermute x2, starting transfers between devices: 0.17 us -> 14.8 us  [sum_all(): value = value + lax.ppermute(value, 'z', [(i, i ^ step) for i in range(nz)])]
    ppermute x1, waiting for transfers between devices: 0.01 us -> 10.3 us  [body(): both_lengths = jnp.stack([lengths, lax.ppermute(lengths, 'y', swap)])]
  transfers between devices with their start and end apart: 82 -> 73, of which waited for: 31 -> 29; matrix products, arithmetic and copies ran while one was open for 6% -> 8% of each run, Pallas kernels for 30% -> 36%
where the time goes in v4:
time: 706 us; the launch traced here: 701 us
  waiting for transfers between devices  263 us (37%)
  Pallas kernels  256 us (36%)
  starting transfers between devices  100 us (14%)
  other arithmetic  47 us (7%)
  local copies, waits for them, and re-layouts  19 us (3%)
  between operations  15.3 us (2%)
    ppermute x59, waiting for transfers between devices, hop(): return lax.ppermute(value, axis, swap)  144 us
    ppermute x59, starting transfers between devices, hop(): return lax.ppermute(value, axis, swap)  64 us
    pallas_call x2, Pallas kernels, attend_back(): pl.pallas_call(functools.partial(attend_back_kernel, group), grid=(1,), i...  57.7 us
    all_to_all x2, waiting for transfers between devices, to_groups(): return lax.all_to_all(both, 'z', 0, 0, tiled=True)  53.5 us
    pallas_call x4, Pallas kernels, mm_nn(): pl.pallas_call(functools.partial(nn_kernel, len(grads)), grid=(nz,), in_s...  45 us
    pallas_call x4, Pallas kernels, mm_tn(): pl.pallas_call(functools.partial(tn_kernel, count), grid=(count * steps,)...  43.6 us
    pallas_call x2, Pallas kernels, attend(): pl.pallas_call(functools.partial(attend_kernel, group), grid=(1,), in_spe...  33.7 us
    reduce_scatter x4, waiting for transfers between devices, reduce(): return lax.psum_scatter(rows, ('z', 'c'), scatter_dimension=0, tiled=True)  27 us
  transfers between devices with their start and end apart: 73, of which 29 were waited for; matrix products, arithmetic and copies ran while one was open for 8% of the time, Pallas kernels for 36%

profile of v4, /device:TPU:0, one launch (start us, length us, event | category | flops | bytes accessed | tf_op | source)
XLA Modules:
  0.0 700.7 jit_solution(108800898337064433)
XLA Ops:
  16.7 12.2 %collective-permute-done.1 = bf16[2,256,512]{2,1,0:T(8,128)(2,1)} collective-permute-done((bf16[2,256,512]{2,1,0:T(8,128)(2,1)}, bf16[2,256,512]{2,1,0:T(8,128)(2,1)}, u32[]{:S(2)}, u32[]{:S(2)}) %collective-permute-start.1) | collective-permute-done | bytes 524320 | tf_op jit(solution)/shard_map/ppermute | solution.py:559
  44.1 10.3 %collective-permute-done = s32[2]{0:T(128)S(1)} collective-permute-done((s32[2]{0:T(128)S(1)}, s32[2]{0:T(128)S(1)}, u32[]{:S(2)}, u32[]{:S(2)}) %collective-permute-start) | collective-permute-done | bytes 40 | tf_op jit(solution)/shard_map/ppermute | solution.py:779
  55.4 39.5 %all-to-all-done = bf16[4,264,512]{2,1,0:T(8,128)(2,1)} async-done(((bf16[4,264,512]{2,1,0:T(8,128)(2,1)}), bf16[4,264,512]{2,1,0:T(8,128)(2,1)}, u32[]{:S(2)}, u32[]{:S(2)}) %all-to-all-start) | async-done | bytes 1081376 | tf_op jit(solution)/shard_map/all_to_all | solution.py:658
  126.3 14.0 %all-to-all-done.1 = bf16[4,256,512]{2,1,0:T(8,128)(2,1)S(1)} async-done(((bf16[4,256,512]{2,1,0:T(8,128)(2,1)}), bf16[4,256,512]{2,1,0:T(8,128)(2,1)S(1)}, u32[]{:S(2)}, u32[]{:S(2)}) %all-to-all-start.1) | async-done | bytes 1048608 | tf_op jit(solution)/shard_map/all_to_all | solution.py:658
  145.3 12.0 %product_nt.2.q_ref.k_ref.v_ref = bf16[1024,1536]{1,0:T(8,128)(2,1)} custom-call(s32[4]{0:T(128)} %add_multiply_fusion.starts_ref, bf16[2,256,512]{2,1,0:T(8,128)(2,1)} %get-tuple-element.153.refs_0_.refs_2_, bf16[2,256,512]{2,1,0:T(8,128)(2,1)} %collective-permute-done.2.refs_1_.refs_3_, bf16[2,256,512]{2,1,0:T(8,128)(2,1)} %collective-permute-done.3.refs_2_.refs_4_, ...), custom_call_target="tpu_custom_call" | custom-call | flops 6442450944 | bytes 13631488 | tf_op jit(solution)/shard_map/product_nt/pallas_call | solution.py:78
  157.3 16.8 %attend.2 = (bf16[1024,256]{1,0:T(8,128)(2,1)}, f32[8,1024]{1,0:T(8,128)}) custom-call(s32[1]{0:T(128)} %dynamic_slice.51.length_ref, f32[8,32]{1,0:T(8,128)} %constant_dynamic-slice_fusion.4.table_ref, bf16[1024,1536]{1,0:T(8,128)(2,1)} %product_nt.2.q_ref.k_ref.v_ref, bf16[1024,1536]{1,0:T(8,128)(2,1)} %product_nt.2.q_ref.k_ref.v_ref, ...), custom_call_target="tpu_custom_call" | custom-call | flops 4294967296 | bytes 2097152 | tf_op jit(solution)/shard_map/attend/pallas_call | solution.py:454
  177.0 16.8 %attend.3 = (bf16[1024,256]{1,0:T(8,128)(2,1)}, f32[8,1024]{1,0:T(8,128)}) custom-call(s32[1]{0:T(128)} %dynamic_slice.51.length_ref, f32[8,32]{1,0:T(8,128)} %constant_dynamic-slice_fusion.4.table_ref, bf16[1024,1536]{1,0:T(8,128)(2,1)} %product_nt.2.q_ref.k_ref.v_ref, bf16[1024,1536]{1,0:T(8,128)(2,1)} %product_nt.2.q_ref.k_ref.v_ref, ...), custom_call_target="tpu_custom_call" | custom-call | flops 4294967296 | bytes 2097152 | tf_op jit(solution)/shard_map/attend/pallas_call | solution.py:454
  202.2 22.7 %collective-permute-done.15 = bf16[2,2,256,512]{3,2,1,0:T(8,128)(2,1)S(1)} collective-permute-done((bf16[2,2,256,512]{3,2,1,0:T(8,128)(2,1)}, bf16[2,2,256,512]{3,2,1,0:T(8,128)(2,1)S(1)}, u32[]{:S(2)}, u32[]{:S(2)}) %collective-permute-start.15) | collective-permute-done | bytes 1048608 | tf_op jit(solution)/shard_map/ppermute | solution.py:559
  245.8 10.8 %collective-permute-done.20.refs_2_.refs_3_ = bf16[2,256,512]{2,1,0:T(8,128)(2,1)S(1)} collective-permute-done((bf16[2,256,512]{2,1,0:T(8,128)(2,1)S(1)}, bf16[2,256,512]{2,1,0:T(8,128)(2,1)S(1)}, u32[]{:S(2)}, u32[]{:S(2)}) %collective-permute-start.20) | collective-permute-done | bytes 524320 | tf_op jit(solution)/shard_map/ppermute | solution.py:559
  275.7 17.7 %ffn_in.1 = (bf16[1024,1280]{1,0:T(8,128)(2,1)}, bf16[1024,1280]{1,0:T(8,128)(2,1)}, bf16[1024,1280]{1,0:T(8,128)(2,1)}) custom-call(s32[4]{0:T(128)} %add_multiply_fusion.starts_ref, bf16[2,256,512]{2,1,0:T(8,128)(2,1)} %copy-done.21, bf16[2,256,512]{2,1,0:T(8,128)(2,1)} %copy-done.42, bf16[2,256,512]{2,1,0:T(8,128)(2,1)} %copy-done.40, ...), custom_call_target="tpu_custom_call" | custom-call | flops 10737418240 | bytes 22544384 | tf_op jit(solution)/shard_map/ffn_in/pallas_call | solution.py:214
  303.5 15.2 %ffn_back.1.refs_0_ = bf16[1024,2560]{1,0:T(8,128)(2,1)} custom-call(s32[4]{0:T(128)} %add_multiply_fusion.starts_ref, bf16[2,256,512]{2,1,0:T(8,128)(2,1)} %copy-done.6, bf16[2,256,512]{2,1,0:T(8,128)(2,1)} %collective-permute-done.9.refs_2_.refs_1_, bf16[2,256,512]{2,1,0:T(8,128)(2,1)} %copy-done.19, ...), custom_call_target="tpu_custom_call" | custom-call | flops 5368709120 | bytes 19922944 | tf_op jit(solution)/shard_map/ffn_back/pallas_call | solution.py:245
  318.7 16.5 %product_nn.5 = (bf16[2,2,256,512]{3,2,1,0:T(8,128)(2,1)}, bf16[2,2,256,512]{3,2,1,0:T(8,128)(2,1)}, bf16[2,2,256,512]{3,2,1,0:T(8,128)(2,1)}, bf16[2,2,256,512]{3,2,1,0:T(8,128)(2,1)}) custom-call(s32[4]{0:T(128)} %add_multiply_fusion.starts_ref, bf16[1024,2560]{1,0:T(8,128)(2,1)} %ffn_back.1.refs_0_, bf16[4,2,1280,512]{3,2,1,0:T(8,128)(2,1)} %bitcast.141), custom_call_target="tpu_custom_call" | custom-call | flops 10737418240 | bytes 19922944 | tf_op jit(solution)/shard_map/product_nn/pallas_call | solution.py:123
  338.2 15.9 %product_tn.5 = bf16[4,2560,512]{2,1,0:T(8,128)(2,1)} custom-call(s32[4]{0:T(128)} %add_multiply_fusion.starts_ref, bf16[1024,2560]{1,0:T(8,128)(2,1)} %ffn_back.1.refs_0_, bf16[2,256,512]{2,1,0:T(8,128)(2,1)} %copy-done.21, bf16[2,256,512]{2,1,0:T(8,128)(2,1)} %copy-done.42, bf16[2,256,512]{2,1,0:T(8,128)(2,1)} %copy-done.40, ...), custom_call_target="tpu_custom_call" | custom-call | flops 10737418240 | bytes 19922944 | tf_op jit(solution)/shard_map/product_tn/pallas_call | solution.py:171
  369.1 10.2 %product_nn.6 = (bf16[2,2,256,512]{3,2,1,0:T(8,128)(2,1)}, bf16[2,2,256,512]{3,2,1,0:T(8,128)(2,1)}, bf16[2,2,256,512]{3,2,1,0:T(8,128)(2,1)}, bf16[2,2,256,512]{3,2,1,0:T(8,128)(2,1)}) custom-call(s32[4]{0:T(128)} %add_multiply_fusion.starts_ref, bf16[1024,1280]{1,0:T(8,128)(2,1)} %get-tuple-element.93.refs_0_, bf16[4,2,640,512]{3,2,1,0:T(8,128)(2,1)} %bitcast.110), custom_call_target="tpu_custom_call" | custom-call | flops 5368709120 | bytes 12058624 | tf_op jit(solution)/shard_map/product_nn/pallas_call | solution.py:123
  389.3 10.8 %collective-permute-done.30.refs_2_.refs_4_ = bf16[2,256,512]{2,1,0:T(8,128)(2,1)S(1)} collective-permute-done((bf16[2,256,512]{2,1,0:T(8,128)(2,1)S(1)}, bf16[2,256,512]{2,1,0:T(8,128)(2,1)S(1)}, u32[]{:S(2)}, u32[]{:S(2)}) %collective-permute-start.30) | collective-permute-done | bytes 524320 | tf_op jit(solution)/shard_map/ppermute | solution.py:559
  402.1 10.5 %collective-permute-done.29.refs_1_.refs_3_ = bf16[2,256,512]{2,1,0:T(8,128)(2,1)S(1)} collective-permute-done((bf16[2,256,512]{2,1,0:T(8,128)(2,1)S(1)}, bf16[2,256,512]{2,1,0:T(8,128)(2,1)S(1)}, u32[]{:S(2)}, u32[]{:S(2)}) %collective-permute-start.29) | collective-permute-done | bytes 524320 | tf_op jit(solution)/shard_map/ppermute | solution.py:559
  433.8 28.9 %attend_back.2 = (bf16[1024,768]{1,0:T(8,128)(2,1)}, f32[4,32,128]{2,1,0:T(8,128)}) custom-call(s32[1]{0:T(128)} %dynamic_slice.51.length_ref, f32[8,32]{1,0:T(8,128)} %constant_dynamic-slice_fusion.4.table_ref, bf16[1024,1536]{1,0:T(8,128)(2,1)} %product_nt.2.q_ref.k_ref.v_ref, bf16[1024,1536]{1,0:T(8,128)(2,1)} %product_nt.2.q_ref.k_ref.v_ref, ...), custom_call_target="tpu_custom_call" | custom-call | flops 10737418240 | bytes 4194304 | tf_op jit(solution)/shard_map/attend_back/pallas_call | solution.py:481
  468.8 28.8 %attend_back.3 = (bf16[1024,768]{1,0:T(8,128)(2,1)}, f32[4,32,128]{2,1,0:T(8,128)}) custom-call(s32[1]{0:T(128)} %dynamic_slice.51.length_ref, f32[8,32]{1,0:T(8,128)} %constant_dynamic-slice_fusion.4.table_ref, bf16[1024,1536]{1,0:T(8,128)(2,1)} %product_nt.2.q_ref.k_ref.v_ref, bf16[1024,1536]{1,0:T(8,128)(2,1)} %product_nt.2.q_ref.k_ref.v_ref, ...), custom_call_target="tpu_custom_call" | custom-call | flops 10737418240 | bytes 4194304 | tf_op jit(solution)/shard_map/attend_back/pallas_call | solution.py:481
  497.7 11.4 %product_tn.7 = bf16[4,1536,512]{2,1,0:T(8,128)(2,1)} custom-call(s32[4]{0:T(128)} %add_multiply_fusion.starts_ref, bf16[1024,768]{1,0:T(8,128)(2,1)} %get-tuple-element.108.refs_0_, bf16[1024,768]{1,0:T(8,128)(2,1)} %get-tuple-element.113.refs_1_, bf16[2,256,512]{2,1,0:T(8,128)(2,1)} %get-tuple-element.153.refs_0_.refs_2_, ...), custom_call_target="tpu_custom_call" | custom-call | flops 6442450944 | bytes 13631488 | tf_op jit(solution)/shard_map/product_tn/pallas_call | solution.py:171
  520.2 11.4 %product_nn.7 = (bf16[2,2,256,512]{3,2,1,0:T(8,128)(2,1)}, bf16[2,2,256,512]{3,2,1,0:T(8,128)(2,1)}, bf16[2,2,256,512]{3,2,1,0:T(8,128)(2,1)}, bf16[2,2,256,512]{3,2,1,0:T(8,128)(2,1)}) custom-call(s32[4]{0:T(128)} %add_multiply_fusion.starts_ref, bf16[1024,768]{1,0:T(8,128)(2,1)} %get-tuple-element.108.refs_0_, ...), custom_call_target="tpu_custom_call" | custom-call | flops 6442450944 | bytes 13631488 | tf_op jit(solution)/shard_map/product_nn/pallas_call | solution.py:123
  533.1 26.7 %all-to-all-done.2 = bf16[4,256,512]{2,1,0:T(8,128)(2,1)S(1)} async-done(((bf16[4,256,512]{2,1,0:T(8,128)(2,1)}), bf16[4,256,512]{2,1,0:T(8,128)(2,1)S(1)}, u32[]{:S(2)}, u32[]{:S(2)}) %all-to-all-start.2) | async-done | bytes 1048608 | tf_op jit(solution)/shard_map/all_to_all | solution.py:663
  608.7 12.1 %collective-permute-done.53 = f32[10,512]{1,0:T(8,128)S(1)} collective-permute-done((f32[10,512]{1,0:T(8,128)S(1)}, f32[10,512]{1,0:T(8,128)S(1)}, u32[]{:S(2)}, u32[]{:S(2)}) %collective-permute-start.53) | collective-permute-done | bytes 20512 | tf_op jit(solution)/shard_map/ppermute | solution.py:559
  624.6 14.8 %collective-permute-start.54 = (f32[10,512]{1,0:T(8,128)S(1)}, f32[10,512]{1,0:T(8,128)S(1)}, u32[]{:S(2)}, u32[]{:S(2)}) collective-permute-start(f32[10,512]{1,0:T(8,128)S(1)} %add.274), channel_id=1, source_target_pairs={{0,1},{1,0},{2,3},{3,2},{4,5},{5,4},{6,7},{7,6},{8,9},{9,8},{10,11... | collective-permute-start | bytes 61448 | tf_op jit(solution)/shard_map/ppermute | solution.py:715
  639.4 21.5 %reduce-scatter.11.cloned.1.call-done.refs_0_ = bf16[256,512]{1,0:T(8,128)(2,1)} async-done(((bf16[2048,512]{1,0:T(8,128)(2,1)}), bf16[256,512]{1,0:T(8,128)(2,1)}) %reduce-scatter.11.cloned.1.call-update) | async-done | bytes 262160 | tf_op jit(solution)/shard_map/reduce_scatter | solution.py:796
  (325 shorter events, 277.9 us)
Async XLA Ops:
  7.2 133.8 %all-gather.4.cloned.1.call-start = ((), (), s32[]{:S(2)}) async-start(), calls=%async_computation.8 | async-start | bytes 9437184 | tf_op jit(solution)/shard_map/all_gather | solution.py:755
  11.6 264.2 %all-gather.6.cloned.1.call-start = ((), (), s32[]{:S(2)}) async-start(), calls=%async_computation.9 | async-start | bytes 11796480 | tf_op jit(solution)/shard_map/all_gather | solution.py:755
  34.3 60.7 %all-to-all-start = ((bf16[4,264,512]{2,1,0:T(8,128)(2,1)}), bf16[4,264,512]{2,1,0:T(8,128)(2,1)}, u32[]{:S(2)}, u32[]{:S(2)}) async-start(bf16[4,264,512]{2,1,0:T(8,128)(2,1)} %pad_maximum_fusion.3), calls=%async_computation | async-start | bytes 2162688 | tf_op jit(solution)/shard_map/all_to_all | solution.py:658
  39.5 264.0 %all-gather.8.cloned.1.call-start = ((), (), s32[]{:S(2)}) async-start(), calls=%async_computation.10 | async-start | bytes 5898240 | tf_op jit(solution)/shard_map/all_gather | solution.py:755
  41.6 53.4 %collective-permute-start.8 = (bf16[2,256,512]{2,1,0:T(8,128)(2,1)}, bf16[2,256,512]{2,1,0:T(8,128)(2,1)}, u32[]{:S(2)}, u32[]{:S(2)}) collective-permute-start(bf16[2,256,512]{2,1,0:T(8,128)(2,1)} %get-tuple-element.151), channel_id=1, source_target_pairs={{0,16},{16,0},{1,17},{17,1},{2,18},{18,2},{3,19},{19,3},{4,20},{20... | collective-permute-start | bytes 1572872 | tf_op jit(solution)/shard_map/ppermute | solution.py:559
  97.4 42.8 %all-to-all-start.1 = ((bf16[4,256,512]{2,1,0:T(8,128)(2,1)}), bf16[4,256,512]{2,1,0:T(8,128)(2,1)S(1)}, u32[]{:S(2)}, u32[]{:S(2)}) async-start(bf16[4,256,512]{2,1,0:T(8,128)(2,1)} %bitcast.26), calls=%async_computation.1 | async-start | bytes 2097152 | tf_op jit(solution)/shard_map/all_to_all | solution.py:658
  103.1 258.7 %reduce-scatter.5.cloned.1.call-start = ((), (), s32[]{:S(2)}) async-start(), calls=%async_computation.11 | async-start | bytes 5898240 | tf_op jit(solution)/shard_map/reduce_scatter | solution.py:796
  142.7 51.2 %collective-permute-start.12 = (bf16[2,256,512]{2,1,0:T(8,128)(2,1)S(1)}, bf16[2,256,512]{2,1,0:T(8,128)(2,1)S(1)}, u32[]{:S(2)}, u32[]{:S(2)}) collective-permute-start(bf16[2,256,512]{2,1,0:T(8,128)(2,1)S(1)} %get-tuple-element.148.refs_5_.refs_4_), channel_id=1, source_target_pairs={{0,4},{4,0},{1,5},{5,1},{2,6},{6,2},{3,7},{7,3},{8,12},{12,8},{9,1... | collective-permute-start | bytes 1572872 | tf_op jit(solution)/shard_map/ppermute | solution.py:559
  144.7 49.2 %collective-permute-start.9 = (bf16[2,256,512]{2,1,0:T(8,128)(2,1)S(1)}, bf16[2,256,512]{2,1,0:T(8,128)(2,1)}, u32[]{:S(2)}, u32[]{:S(2)}) collective-permute-start(bf16[2,256,512]{2,1,0:T(8,128)(2,1)S(1)} %get-tuple-element.149.refs_1_.refs_0_), channel_id=1, source_target_pairs={{0,16},{16,0},{1,17},{17,1},{2,18},{18,2},{3,19},{19,3},{4,20},{20... | collective-permute-start | bytes 1572872 | tf_op jit(solution)/shard_map/ppermute | solution.py:559
  303.4 205.7 %reduce-scatter.7.cloned.1.call-start = ((), (), s32[]{:S(2)}) async-start(), calls=%async_computation.12 | async-start | bytes 11796480 | tf_op jit(solution)/shard_map/reduce_scatter | solution.py:796
  361.8 236.3 %reduce-scatter.9.cloned.1.call-start = ((), (), s32[]{:S(2)}) async-start(), calls=%async_computation.13 | async-start | bytes 7077888 | tf_op jit(solution)/shard_map/reduce_scatter | solution.py:796
  419.4 43.2 %collective-permute-start.35 = (bf16[2,2,256,512]{3,2,1,0:T(8,128)(2,1)}, bf16[2,2,256,512]{3,2,1,0:T(8,128)(2,1)}, u32[]{:S(2)}, u32[]{:S(2)}) collective-permute-start(bf16[2,2,256,512]{3,2,1,0:T(8,128)(2,1)} %get-tuple-element.101), channel_id=1, source_target_pairs={{0,4},{4,0},{1,5},{5,1},{2,6},{6,2},{3,7},{7,3},{8,12},{12,8},{9,1... | collective-permute-start | bytes 3145736 | tf_op jit(solution)/shard_map/ppermute | solution.py:559
  420.6 42.1 %collective-permute-start.37 = (bf16[2,2,256,512]{3,2,1,0:T(8,128)(2,1)}, bf16[2,2,256,512]{3,2,1,0:T(8,128)(2,1)}, u32[]{:S(2)}, u32[]{:S(2)}) collective-permute-start(bf16[2,2,256,512]{3,2,1,0:T(8,128)(2,1)} %get-tuple-element.105), channel_id=1, source_target_pairs={{0,16},{16,0},{1,17},{17,1},{2,18},{18,2},{3,19},{19,3},{4,20},{20... | collective-permute-start | bytes 3145736 | tf_op jit(solution)/shard_map/ppermute | solution.py:559
  464.0 33.6 %collective-permute-start.36 = (bf16[2,256,512]{2,1,0:T(8,128)(2,1)S(1)}, bf16[2,256,512]{2,1,0:T(8,128)(2,1)}, u32[]{:S(2)}, u32[]{:S(2)}) collective-permute-start(bf16[2,256,512]{2,1,0:T(8,128)(2,1)S(1)} %fusion.19), channel_id=1, source_target_pairs={{0,16},{16,0},{1,17},{17,1},{2,18},{18,2},{3,19},{19,3},{4,20},{20... | collective-permute-start | bytes 1572872 | tf_op jit(solution)/shard_map/ppermute | solution.py:559
  513.3 46.4 %all-to-all-start.2 = ((bf16[4,256,512]{2,1,0:T(8,128)(2,1)}), bf16[4,256,512]{2,1,0:T(8,128)(2,1)S(1)}, u32[]{:S(2)}, u32[]{:S(2)}) async-start(bf16[4,256,512]{2,1,0:T(8,128)(2,1)} %fusion.13), calls=%async_computation.2 | async-start | bytes 2097152 | tf_op jit(solution)/shard_map/all_to_all | solution.py:663
  518.7 142.2 %reduce-scatter.11.cloned.1.call-start = ((), (), s32[]{:S(2)}) async-start(), calls=%async_computation.14 | async-start | bytes 2359296 | tf_op jit(solution)/shard_map/reduce_scatter | solution.py:796
  518.7 41.1 %collective-permute-start.42 = (bf16[1280,512]{1,0:T(8,128)(2,1)S(1)}, bf16[1280,512]{1,0:T(8,128)(2,1)}, u32[]{:S(2)}, u32[]{:S(2)}) collective-permute-start(bf16[1280,512]{1,0:T(8,128)(2,1)S(1)} %copy-done.9), channel_id=1, source_target_pairs={{0,16},{16,0},{1,17},{17,1},{2,18},{18,2},{3,19},{19,3},{4,20},{20... | collective-permute-start | bytes 3932168 | tf_op jit(solution)/shard_map/ppermute | solution.py:559
  532.5 36.5 %collective-permute-start.44 = (bf16[2,2,256,512]{3,2,1,0:T(8,128)(2,1)}, bf16[2,2,256,512]{3,2,1,0:T(8,128)(2,1)}, u32[]{:S(2)}, u32[]{:S(2)}) collective-permute-start(bf16[2,2,256,512]{3,2,1,0:T(8,128)(2,1)} %get-tuple-element.120), channel_id=1, source_target_pairs={{0,16},{16,0},{1,17},{17,1},{2,18},{18,2},{3,19},{19,3},{4,20},{20... | collective-permute-start | bytes 3145736 | tf_op jit(solution)/shard_map/ppermute | solution.py:559
  589.1 34.1 %all-to-all-start.3 = ((bf16[4,256,512]{2,1,0:T(8,128)(2,1)}), bf16[4,256,512]{2,1,0:T(8,128)(2,1)S(1)}, u32[]{:S(2)}, u32[]{:S(2)}) async-start(bf16[4,256,512]{2,1,0:T(8,128)(2,1)} %fusion.9), calls=%async_computation.5 | async-start | bytes 2097152 | tf_op jit(solution)/shard_map/all_to_all | solution.py:663
  596.1 66.4 %collective-permute-start.49 = (bf16[1280,512]{1,0:T(8,128)(2,1)S(1)}, bf16[1280,512]{1,0:T(8,128)(2,1)}, u32[]{:S(2)}, u32[]{:S(2)}) collective-permute-start(bf16[1280,512]{1,0:T(8,128)(2,1)S(1)} %copy-done.9), channel_id=1, source_target_pairs={{0,8},{8,0},{1,9},{9,1},{2,10},{10,2},{3,11},{11,3},{4,12},{12,4},... | collective-permute-start | bytes 3932168 | tf_op jit(solution)/shard_map/ppermute | solution.py:559
  596.1 66.9 %collective-permute-start.50 = (bf16[1280,512]{1,0:T(8,128)(2,1)}, bf16[1280,512]{1,0:T(8,128)(2,1)}, u32[]{:S(2)}, u32[]{:S(2)}) collective-permute-start(bf16[1280,512]{1,0:T(8,128)(2,1)} %collective-permute-done.42.refs_2_), channel_id=1, source_target_pairs={{0,8},{8,0},{1,9},{9,1},{2,10},{10,2},{3,11},{11,3},{4,12},{12,4},... | collective-permute-start | bytes 3932168 | tf_op jit(solution)/shard_map/ppermute | solution.py:559
  622.6 65.8 %collective-permute-start.56 = (bf16[768,512]{1,0:T(8,128)(2,1)}, bf16[768,512]{1,0:T(8,128)(2,1)}, u32[]{:S(2)}, u32[]{:S(2)}) collective-permute-start(bf16[768,512]{1,0:T(8,128)(2,1)} %reduce-scatter.9.cloned.1.call-done.refs_0_), channel_id=1, source_target_pairs={{0,8},{8,0},{1,9},{9,1},{2,10},{10,2},{3,11},{11,3},{4,12},{12,4},... | collective-permute-start | bytes 2359304 | tf_op jit(solution)/shard_map/ppermute | solution.py:559
  622.7 65.8 %collective-permute-start.58 = (bf16[768,512]{1,0:T(8,128)(2,1)}, bf16[768,512]{1,0:T(8,128)(2,1)}, u32[]{:S(2)}, u32[]{:S(2)}) collective-permute-start(bf16[768,512]{1,0:T(8,128)(2,1)} %collective-permute-done.57.refs_2_), channel_id=1, source_target_pairs={{0,8},{8,0},{1,9},{9,1},{2,10},{10,2},{3,11},{11,3},{4,12},{12,4},... | collective-permute-start | bytes 2359304 | tf_op jit(solution)/shard_map/ppermute | solution.py:559
  624.6 36.3 %collective-permute-start.54 = (f32[10,512]{1,0:T(8,128)S(1)}, f32[10,512]{1,0:T(8,128)S(1)}, u32[]{:S(2)}, u32[]{:S(2)}) collective-permute-start(f32[10,512]{1,0:T(8,128)S(1)} %add.274), channel_id=1, source_target_pairs={{0,1},{1,0},{2,3},{3,2},{4,5},{5,4},{6,7},{7,6},{8,9},{9,8},{10,11... | collective-permute-start | bytes 61448 | tf_op jit(solution)/shard_map/ppermute | solution.py:715
  (94 other events, 1547.0 us)
Sparse Core Ops, SparseCore 0:
  11.7 129.2 all-gather.3
  143.2 97.5 all-gather.5
  242.5 54.4 all-gather.7
  303.5 58.1 reduce-scatter.4
  364.5 107.7 reduce-scatter.6
  509.2 88.8 reduce-scatter.8
  601.0 59.8 reduce-scatter.10

commit v5 on v4

--- a/solution.py
+++ b/solution.py
@@ -705,11 +705,13 @@
     return both.transpose(1, 0, 2, 3).reshape(count, 2 * t, width).astype(dtype)
 
 
-def sum_all(value, nx, nz, *earlier):
+def sum_plane(value, nx):
     value = value + hop(value, "c")
     value = value + hop(value, "x") if nx == 2 else lax.psum(value, "x")
-    value = value + hop(value, "y")
-    value = after(value, *earlier)
+    return value + hop(value, "y")
+
+
+def sum_line(value, nz):
     step = 1
     while step < nz:
         value = value + lax.ppermute(value, "z", [(i, i ^ step) for i in range(nz)])
@@ -853,21 +855,31 @@
     branch, branch_first, branch_last = scatter(branch_parts)
     down_pieces, down_last = shared(after(down_part, grad_attended))
     grad_projected, table_part = attend_back_all(after(grad_attended, out_partial), *branch_first)
+    out_part = reduce(after(out_partial, gate_up_part, grad_projected[0], *branch_first))
+    outputs = (live * (hidden + branch)).astype(BF)
     last = after(grad_projected[-1], *branch_last, down_last)
     grad_projected = [*grad_projected[:-1], last]
+    outputs, _ = from_groups(outputs)
     qkv_partial = tn(grad_projected, normed, starts)
-    qkv_part = reduce(after(qkv_partial, gate_up_part))
+    qkv_part = reduce(after(qkv_partial, out_part))
     one_parts = nn(grad_projected, w_attn, 0, qkv_count, starts)
     gate_up_pieces, gate_up_last = shared(after(gate_up_part, grad_projected[0]))
-    outputs, _ = from_groups((live * (hidden + branch)).astype(BF))
-    grad_one, one_first, one_last = scatter(one_parts, outputs[0], gate_up_last)
-    out_part = reduce(after(out_partial, *one_first))
+    grad_one, _, one_last = scatter(one_parts, outputs[0], gate_up_last)
     through, attn_gain_part = norm_back(tokens, scale_one, gain_one, grad_one)
     input_grad, input_leaves = from_groups((grad_hidden + through).astype(BF))
     outputs = stored_from(outputs, BF)
 
-    out_pieces, _ = shared(after(out_part, input_leaves))
-    qkv_pieces, _ = shared(after(qkv_part, *one_last))
+    table_part = jnp.sum(table_part, axis=2)
+    every = jnp.zeros((nx * 2 * local_heads, table_part.shape[1]), F32)
+    every = lax.dynamic_update_slice_in_dim(every, table_part, (x * 2 + y) * local_heads, 0)
+    spare = -every.size % width
+    every = jnp.pad(every.reshape(-1), (0, spare)).reshape(-1, width)
+    sums = sum_plane(jnp.concatenate([attn_gain_part, ffn_gain_part, every]), nx)
+    all_sums = sum_line(after(sums, input_leaves), nz)
+    attn_gain_grad, ffn_gain_grad = all_sums[:nz], all_sums[nz : 2 * nz]
+    every = all_sums[2 * nz :].reshape(-1)[: nx * 2 * local_heads * buckets].reshape(-1, buckets)
+
+    out_pieces, _ = shared(after(out_part, *one_last))
     if fits:
         here = jnp.stack([y, c]).astype(jnp.int32)
 
@@ -892,31 +904,20 @@
         (down_all,) = place(down_pieces, here, [(units * unit, width)], write_rows)
         (out_all,) = place(out_pieces, here, [(heads * 64, width)], write_rows)
         (gate_up_all,) = place(gate_up_pieces, here, [(units, 2, unit, width)], write_gate_up)
+        qkv_part = after(qkv_part, sums, down_all, out_all, gate_up_all, outputs, *one_last)
         query_key_all, value_all = place(
-            qkv_pieces, here, [(heads, 2, 64, width), (heads, 64, width)], write_qkv
+            shared(qkv_part)[0], here, [(heads, 2, 64, width), (heads, 64, width)], write_qkv
         )
     else:
         down_all, out_all = down_pieces.astype(F32), out_pieces.astype(F32)
         gate_up_all = gate_up_pieces.astype(F32).reshape(parts, 2, units, unit, width)
         gate_up_all = gate_up_all.transpose(0, 2, 1, 3, 4).reshape(-1, 2, unit, width)
-        qkv_all = qkv_pieces.astype(F32).reshape(parts, 3, heads, 64, width)
+        qkv_all = shared(qkv_part)[0].astype(F32).reshape(parts, 3, heads, 64, width)
         qkv_all = qkv_all.transpose(0, 2, 1, 3, 4).reshape(-1, 3, 64, width)
         query_key_all, value_all = qkv_all[:, :2], qkv_all[:, 2]
-    back, other = input_grad
-    input_grad = back, after(other, down_all, gate_up_all)
     input_grad = stored_from(input_grad, F32)
     down_all, out_all = down_all.reshape(down_proj.shape), out_all.reshape(out_proj.shape)
 
-    table_part = jnp.sum(table_part, axis=2)
-    every = jnp.zeros((nx * 2 * local_heads, table_part.shape[1]), F32)
-    every = lax.dynamic_update_slice_in_dim(every, table_part, (x * 2 + y) * local_heads, 0)
-    both = jnp.concatenate([attn_gain_part, ffn_gain_part])
-    if every.size % width == 0:
-        both = sum_all(jnp.concatenate([both, every.reshape(-1, width)]), nx, nz, input_leaves)
-        every = both[2 * nz :].reshape(-1, buckets)
-    else:
-        both, every = sum_all(both, nx, nz), sum_all(every, nx, nz)
-    attn_gain_grad, ffn_gain_grad = both[:nz], both[nz : 2 * nz]
     table_grad = lax.dynamic_slice_in_dim(every, (x * nz + z) * mine, mine, 0).T
     return (
         outputs,

time: 706 us -> 694 us (0.983)
  starting transfers between devices: 100 us -> 83.2 us
    reduce_scatter x4, waiting for transfers between devices: 27 us -> 13.8 us  [reduce(): return lax.psum_scatter(rows, ('z', 'c'), scatter_dimension=0, tiled=True)]
    ppermute x59, waiting for transfers between devices: 144 us -> 156 us  [hop(): return lax.ppermute(value, axis, swap)]
    ppermute x2, starting transfers between devices: 14.8 us -> 4.95 us  [sum_line(): value = value + lax.ppermute(value, 'z', [(i, i ^ step) for i in range(nz)])]
  transfers between devices with their start and end apart: 73 -> 73, of which waited for: 29 -> 30; matrix products, arithmetic and copies ran while one was open for 8% -> 9% of each run, Pallas kernels for 36% -> 36%
where the time goes in v5:
time: 694 us; the launch traced here: 688 us
  waiting for transfers between devices  266 us (38%)
  Pallas kernels  256 us (37%)
  starting transfers between devices  83.2 us (12%)
  other arithmetic  48.9 us (7%)
  local copies, waits for them, and re-layouts  19.4 us (3%)
  between operations  15.4 us (2%)
    ppermute x59, waiting for transfers between devices, hop(): return lax.ppermute(value, axis, swap)  156 us
    pallas_call x2, Pallas kernels, attend_back(): pl.pallas_call(functools.partial(attend_back_kernel, group), grid=(1,), i...  57.6 us
    ppermute x59, starting transfers between devices, hop(): return lax.ppermute(value, axis, swap)  57.5 us
    all_to_all x2, waiting for transfers between devices, to_groups(): return lax.all_to_all(both, 'z', 0, 0, tiled=True)  53 us
    pallas_call x4, Pallas kernels, mm_nn(): pl.pallas_call(functools.partial(nn_kernel, len(grads)), grid=(nz,), in_s...  44.8 us
    pallas_call x4, Pallas kernels, mm_tn(): pl.pallas_call(functools.partial(tn_kernel, count), grid=(count * steps,)...  43.5 us
    pallas_call x2, Pallas kernels, attend(): pl.pallas_call(functools.partial(attend_kernel, group), grid=(1,), in_spe...  33.5 us
    all_to_all x2, waiting for transfers between devices, from_groups(): lax.all_to_all(mine, 'z', 0, 0, tiled=True).reshape(2, nz // 2, t, width)  27.7 us
  transfers between devices with their start and end apart: 73, of which 30 were waited for; matrix products, arithmetic and copies ran while one was open for 9% of the time, Pallas kernels for 36%

profile of v5, /device:TPU:0, one launch (start us, length us, event | category | flops | bytes accessed | tf_op | source)
XLA Modules:
  0.0 688.4 jit_solution(12064536889143598157)
XLA Ops:
  16.7 12.2 %collective-permute-done.1 = bf16[2,256,512]{2,1,0:T(8,128)(2,1)} collective-permute-done((bf16[2,256,512]{2,1,0:T(8,128)(2,1)}, bf16[2,256,512]{2,1,0:T(8,128)(2,1)}, u32[]{:S(2)}, u32[]{:S(2)}) %collective-permute-start.1) | collective-permute-done | bytes 524320 | tf_op jit(solution)/shard_map/ppermute | solution.py:559
  44.1 10.3 %collective-permute-done = s32[2]{0:T(128)S(1)} collective-permute-done((s32[2]{0:T(128)S(1)}, s32[2]{0:T(128)S(1)}, u32[]{:S(2)}, u32[]{:S(2)}) %collective-permute-start) | collective-permute-done | bytes 40 | tf_op jit(solution)/shard_map/ppermute | solution.py:781
  55.4 39.5 %all-to-all-done = bf16[4,264,512]{2,1,0:T(8,128)(2,1)} async-done(((bf16[4,264,512]{2,1,0:T(8,128)(2,1)}), bf16[4,264,512]{2,1,0:T(8,128)(2,1)}, u32[]{:S(2)}, u32[]{:S(2)}) %all-to-all-start) | async-done | bytes 1081376 | tf_op jit(solution)/shard_map/all_to_all | solution.py:658
  126.8 13.5 %all-to-all-done.1 = bf16[4,256,512]{2,1,0:T(8,128)(2,1)S(1)} async-done(((bf16[4,256,512]{2,1,0:T(8,128)(2,1)}), bf16[4,256,512]{2,1,0:T(8,128)(2,1)S(1)}, u32[]{:S(2)}, u32[]{:S(2)}) %all-to-all-start.1) | async-done | bytes 1048608 | tf_op jit(solution)/shard_map/all_to_all | solution.py:658
  145.3 12.0 %product_nt.2.q_ref.k_ref.v_ref = bf16[1024,1536]{1,0:T(8,128)(2,1)} custom-call(s32[4]{0:T(128)} %add_multiply_fusion.starts_ref, bf16[2,256,512]{2,1,0:T(8,128)(2,1)} %get-tuple-element.151.refs_0_.refs_2_, bf16[2,256,512]{2,1,0:T(8,128)(2,1)} %collective-permute-done.2.refs_1_.refs_3_, bf16[2,256,512]{2,1,0:T(8,128)(2,1)} %collective-permute-done.3.refs_2_.refs_4_, ...), custom_call_target="tpu_custom_call" | custom-call | flops 6442450944 | bytes 13631488 | tf_op jit(solution)/shard_map/product_nt/pallas_call | solution.py:78
  157.3 16.8 %attend.2 = (bf16[1024,256]{1,0:T(8,128)(2,1)}, f32[8,1024]{1,0:T(8,128)}) custom-call(s32[1]{0:T(128)} %dynamic_slice.51.length_ref, f32[8,32]{1,0:T(8,128)} %constant_dynamic-slice_fusion.4.table_ref, bf16[1024,1536]{1,0:T(8,128)(2,1)} %product_nt.2.q_ref.k_ref.v_ref, bf16[1024,1536]{1,0:T(8,128)(2,1)} %product_nt.2.q_ref.k_ref.v_ref, ...), custom_call_target="tpu_custom_call" | custom-call | flops 4294967296 | bytes 2097152 | tf_op jit(solution)/shard_map/attend/pallas_call | solution.py:454
  177.0 16.8 %attend.3 = (bf16[1024,256]{1,0:T(8,128)(2,1)}, f32[8,1024]{1,0:T(8,128)}) custom-call(s32[1]{0:T(128)} %dynamic_slice.51.length_ref, f32[8,32]{1,0:T(8,128)} %constant_dynamic-slice_fusion.4.table_ref, bf16[1024,1536]{1,0:T(8,128)(2,1)} %product_nt.2.q_ref.k_ref.v_ref, bf16[1024,1536]{1,0:T(8,128)(2,1)} %product_nt.2.q_ref.k_ref.v_ref, ...), custom_call_target="tpu_custom_call" | custom-call | flops 4294967296 | bytes 2097152 | tf_op jit(solution)/shard_map/attend/pallas_call | solution.py:454
  202.1 22.7 %collective-permute-done.15 = bf16[2,2,256,512]{3,2,1,0:T(8,128)(2,1)S(1)} collective-permute-done((bf16[2,2,256,512]{3,2,1,0:T(8,128)(2,1)}, bf16[2,2,256,512]{3,2,1,0:T(8,128)(2,1)S(1)}, u32[]{:S(2)}, u32[]{:S(2)}) %collective-permute-start.15) | collective-permute-done | bytes 1048608 | tf_op jit(solution)/shard_map/ppermute | solution.py:559
  245.8 10.8 %collective-permute-done.20.refs_2_.refs_3_ = bf16[2,256,512]{2,1,0:T(8,128)(2,1)S(1)} collective-permute-done((bf16[2,256,512]{2,1,0:T(8,128)(2,1)S(1)}, bf16[2,256,512]{2,1,0:T(8,128)(2,1)S(1)}, u32[]{:S(2)}, u32[]{:S(2)}) %collective-permute-start.20) | collective-permute-done | bytes 524320 | tf_op jit(solution)/shard_map/ppermute | solution.py:559
  275.8 17.6 %ffn_in.1 = (bf16[1024,1280]{1,0:T(8,128)(2,1)}, bf16[1024,1280]{1,0:T(8,128)(2,1)}, bf16[1024,1280]{1,0:T(8,128)(2,1)}) custom-call(s32[4]{0:T(128)} %add_multiply_fusion.starts_ref, bf16[2,256,512]{2,1,0:T(8,128)(2,1)} %copy-done.22, bf16[2,256,512]{2,1,0:T(8,128)(2,1)} %copy-done.46, bf16[2,256,512]{2,1,0:T(8,128)(2,1)} %copy-done.44, ...), custom_call_target="tpu_custom_call" | custom-call | flops 10737418240 | bytes 22544384 | tf_op jit(solution)/shard_map/ffn_in/pallas_call | solution.py:214
  293.3 9.9 %product_tn.4 = bf16[4,1280,512]{2,1,0:T(8,128)(2,1)} custom-call(s32[4]{0:T(128)} %add_multiply_fusion.starts_ref, bf16[1024,1280]{1,0:T(8,128)(2,1)} %get-tuple-element.92.refs_0_, bf16[2,256,512]{2,1,0:T(8,128)(2,1)} %copy-done.6, bf16[2,256,512]{2,1,0:T(8,128)(2,1)} %collective-permute-done.9.refs_2_.refs_1_, bf16[2,256,512]{2,1,0:T(8,128)(2,1)} %copy-done.20, ...), custom_call_target="tpu_custom_call" | custom-call | flops 5368709120 | bytes 12058624 | tf_op jit(solution)/shard_map/product_tn/pallas_call | solution.py:171
  303.4 15.2 %ffn_back.1.refs_0_ = bf16[1024,2560]{1,0:T(8,128)(2,1)} custom-call(s32[4]{0:T(128)} %add_multiply_fusion.starts_ref, bf16[2,256,512]{2,1,0:T(8,128)(2,1)} %copy-done.6, bf16[2,256,512]{2,1,0:T(8,128)(2,1)} %collective-permute-done.9.refs_2_.refs_1_, bf16[2,256,512]{2,1,0:T(8,128)(2,1)} %copy-done.20, ...), custom_call_target="tpu_custom_call" | custom-call | flops 5368709120 | bytes 19922944 | tf_op jit(solution)/shard_map/ffn_back/pallas_call | solution.py:245
  318.5 16.5 %product_nn.5 = (bf16[2,2,256,512]{3,2,1,0:T(8,128)(2,1)}, bf16[2,2,256,512]{3,2,1,0:T(8,128)(2,1)}, bf16[2,2,256,512]{3,2,1,0:T(8,128)(2,1)}, bf16[2,2,256,512]{3,2,1,0:T(8,128)(2,1)}) custom-call(s32[4]{0:T(128)} %add_multiply_fusion.starts_ref, bf16[1024,2560]{1,0:T(8,128)(2,1)} %ffn_back.1.refs_0_, bf16[4,2,1280,512]{3,2,1,0:T(8,128)(2,1)} %bitcast.141), custom_call_target="tpu_custom_call" | custom-call | flops 10737418240 | bytes 19922944 | tf_op jit(solution)/shard_map/product_nn/pallas_call | solution.py:123
  338.0 15.9 %product_tn.5 = bf16[4,2560,512]{2,1,0:T(8,128)(2,1)} custom-call(s32[4]{0:T(128)} %add_multiply_fusion.starts_ref, bf16[1024,2560]{1,0:T(8,128)(2,1)} %ffn_back.1.refs_0_, bf16[2,256,512]{2,1,0:T(8,128)(2,1)} %copy-done.22, bf16[2,256,512]{2,1,0:T(8,128)(2,1)} %copy-done.46, bf16[2,256,512]{2,1,0:T(8,128)(2,1)} %copy-done.44, ...), custom_call_target="tpu_custom_call" | custom-call | flops 10737418240 | bytes 19922944 | tf_op jit(solution)/shard_map/product_tn/pallas_call | solution.py:171
  368.8 10.2 %product_nn.6 = (bf16[2,2,256,512]{3,2,1,0:T(8,128)(2,1)}, bf16[2,2,256,512]{3,2,1,0:T(8,128)(2,1)}, bf16[2,2,256,512]{3,2,1,0:T(8,128)(2,1)}, bf16[2,2,256,512]{3,2,1,0:T(8,128)(2,1)}) custom-call(s32[4]{0:T(128)} %add_multiply_fusion.starts_ref, bf16[1024,1280]{1,0:T(8,128)(2,1)} %get-tuple-element.92.refs_0_, bf16[4,2,640,512]{3,2,1,0:T(8,128)(2,1)} %bitcast.110), custom_call_target="tpu_custom_call" | custom-call | flops 5368709120 | bytes 12058624 | tf_op jit(solution)/shard_map/product_nn/pallas_call | solution.py:123
  389.0 10.8 %collective-permute-done.30.refs_2_.refs_4_ = bf16[2,256,512]{2,1,0:T(8,128)(2,1)S(1)} collective-permute-done((bf16[2,256,512]{2,1,0:T(8,128)(2,1)S(1)}, bf16[2,256,512]{2,1,0:T(8,128)(2,1)S(1)}, u32[]{:S(2)}, u32[]{:S(2)}) %collective-permute-start.30) | collective-permute-done | bytes 524320 | tf_op jit(solution)/shard_map/ppermute | solution.py:559
  401.9 10.5 %collective-permute-done.29.refs_1_.refs_3_ = bf16[2,256,512]{2,1,0:T(8,128)(2,1)S(1)} collective-permute-done((bf16[2,256,512]{2,1,0:T(8,128)(2,1)S(1)}, bf16[2,256,512]{2,1,0:T(8,128)(2,1)S(1)}, u32[]{:S(2)}, u32[]{:S(2)}) %collective-permute-start.29) | collective-permute-done | bytes 524320 | tf_op jit(solution)/shard_map/ppermute | solution.py:559
  433.6 28.8 %attend_back.2 = (bf16[1024,768]{1,0:T(8,128)(2,1)}, f32[4,32,128]{2,1,0:T(8,128)}) custom-call(s32[1]{0:T(128)} %dynamic_slice.51.length_ref, f32[8,32]{1,0:T(8,128)} %constant_dynamic-slice_fusion.4.table_ref, bf16[1024,1536]{1,0:T(8,128)(2,1)} %product_nt.2.q_ref.k_ref.v_ref, bf16[1024,1536]{1,0:T(8,128)(2,1)} %product_nt.2.q_ref.k_ref.v_ref, ...), custom_call_target="tpu_custom_call" | custom-call | flops 10737418240 | bytes 4194304 | tf_op jit(solution)/shard_map/attend_back/pallas_call | solution.py:481
  462.4 9.7 %reduce-scatter.7.cloned.1.call-done.refs_0_ = bf16[1280,512]{1,0:T(8,128)(2,1)} async-done(((bf16[10240,512]{1,0:T(8,128)(2,1)}), bf16[1280,512]{1,0:T(8,128)(2,1)}) %reduce-scatter.7.cloned.1.call-update) | async-done | bytes 1310736 | tf_op jit(solution)/shard_map/reduce_scatter | solution.py:798
  479.0 28.8 %attend_back.3 = (bf16[1024,768]{1,0:T(8,128)(2,1)}, f32[4,32,128]{2,1,0:T(8,128)}) custom-call(s32[1]{0:T(128)} %dynamic_slice.51.length_ref, f32[8,32]{1,0:T(8,128)} %constant_dynamic-slice_fusion.4.table_ref, bf16[1024,1536]{1,0:T(8,128)(2,1)} %product_nt.2.q_ref.k_ref.v_ref, bf16[1024,1536]{1,0:T(8,128)(2,1)} %product_nt.2.q_ref.k_ref.v_ref, ...), custom_call_target="tpu_custom_call" | custom-call | flops 10737418240 | bytes 4194304 | tf_op jit(solution)/shard_map/attend_back/pallas_call | solution.py:481
  507.9 11.5 %product_tn.7 = bf16[4,1536,512]{2,1,0:T(8,128)(2,1)} custom-call(s32[4]{0:T(128)} %add_multiply_fusion.starts_ref, bf16[1024,768]{1,0:T(8,128)(2,1)} %get-tuple-element.107.refs_0_, bf16[1024,768]{1,0:T(8,128)(2,1)} %get-tuple-element.112.refs_1_, bf16[2,256,512]{2,1,0:T(8,128)(2,1)} %get-tuple-element.151.refs_0_.refs_2_, ...), custom_call_target="tpu_custom_call" | custom-call | flops 6442450944 | bytes 13631488 | tf_op jit(solution)/shard_map/product_tn/pallas_call | solution.py:171
  529.1 11.2 %product_nn.7 = (bf16[2,2,256,512]{3,2,1,0:T(8,128)(2,1)}, bf16[2,2,256,512]{3,2,1,0:T(8,128)(2,1)}, bf16[2,2,256,512]{3,2,1,0:T(8,128)(2,1)}, bf16[2,2,256,512]{3,2,1,0:T(8,128)(2,1)}) custom-call(s32[4]{0:T(128)} %add_multiply_fusion.starts_ref, bf16[1024,768]{1,0:T(8,128)(2,1)} %get-tuple-element.107.refs_0_, ...), custom_call_target="tpu_custom_call" | custom-call | flops 6442450944 | bytes 13631488 | tf_op jit(solution)/shard_map/product_nn/pallas_call | solution.py:123
  541.5 27.7 %all-to-all-done.2 = bf16[4,256,512]{2,1,0:T(8,128)(2,1)S(1)} async-done(((bf16[4,256,512]{2,1,0:T(8,128)(2,1)}), bf16[4,256,512]{2,1,0:T(8,128)(2,1)S(1)}, u32[]{:S(2)}, u32[]{:S(2)}) %all-to-all-start.2) | async-done | bytes 1048608 | tf_op jit(solution)/shard_map/all_to_all | solution.py:663
  637.8 19.3 %collective-permute-done.60.refs_2_ = bf16[768,512]{1,0:T(8,128)(2,1)S(1)} collective-permute-done((bf16[768,512]{1,0:T(8,128)(2,1)}, bf16[768,512]{1,0:T(8,128)(2,1)S(1)}, u32[]{:S(2)}, u32[]{:S(2)}) %collective-permute-start.60) | collective-permute-done | bytes 786464 | tf_op jit(solution)/shard_map/ppermute | solution.py:559
  (333 shorter events, 274.9 us)
Async XLA Ops:
  7.2 133.8 %all-gather.4.cloned.1.call-start = ((), (), s32[]{:S(2)}) async-start(), calls=%async_computation.8 | async-start | bytes 9437184 | tf_op jit(solution)/shard_map/all_gather | solution.py:757
  11.6 264.2 %all-gather.6.cloned.1.call-start = ((), (), s32[]{:S(2)}) async-start(), calls=%async_computation.9 | async-start | bytes 11796480 | tf_op jit(solution)/shard_map/all_gather | solution.py:757
  34.3 60.7 %all-to-all-start = ((bf16[4,264,512]{2,1,0:T(8,128)(2,1)}), bf16[4,264,512]{2,1,0:T(8,128)(2,1)}, u32[]{:S(2)}, u32[]{:S(2)}) async-start(bf16[4,264,512]{2,1,0:T(8,128)(2,1)} %pad_maximum_fusion.3), calls=%async_computation | async-start | bytes 2162688 | tf_op jit(solution)/shard_map/all_to_all | solution.py:658
  39.5 263.9 %all-gather.8.cloned.1.call-start = ((), (), s32[]{:S(2)}) async-start(), calls=%async_computation.10 | async-start | bytes 5898240 | tf_op jit(solution)/shard_map/all_gather | solution.py:757
  41.6 53.4 %collective-permute-start.8 = (bf16[2,256,512]{2,1,0:T(8,128)(2,1)}, bf16[2,256,512]{2,1,0:T(8,128)(2,1)}, u32[]{:S(2)}, u32[]{:S(2)}) collective-permute-start(bf16[2,256,512]{2,1,0:T(8,128)(2,1)} %get-tuple-element.149), channel_id=1, source_target_pairs={{0,16},{16,0},{1,17},{17,1},{2,18},{18,2},{3,19},{19,3},{4,20},{20... | collective-permute-start | bytes 1572872 | tf_op jit(solution)/shard_map/ppermute | solution.py:559
  97.3 42.9 %all-to-all-start.1 = ((bf16[4,256,512]{2,1,0:T(8,128)(2,1)}), bf16[4,256,512]{2,1,0:T(8,128)(2,1)S(1)}, u32[]{:S(2)}, u32[]{:S(2)}) async-start(bf16[4,256,512]{2,1,0:T(8,128)(2,1)} %bitcast.26), calls=%async_computation.1 | async-start | bytes 2097152 | tf_op jit(solution)/shard_map/all_to_all | solution.py:658
  103.0 258.5 %reduce-scatter.5.cloned.1.call-start = ((), (), s32[]{:S(2)}) async-start(), calls=%async_computation.11 | async-start | bytes 5898240 | tf_op jit(solution)/shard_map/reduce_scatter | solution.py:798
  141.1 32.9 %collective-permute-start.13 = (bf16[2,256,512]{2,1,0:T(8,128)(2,1)S(1)}, bf16[2,256,512]{2,1,0:T(8,128)(2,1)S(1)}, u32[]{:S(2)}, u32[]{:S(2)}) collective-permute-start(bf16[2,256,512]{2,1,0:T(8,128)(2,1)S(1)} %get-tuple-element.146.refs_5_.refs_4_), channel_id=1, source_target_pairs={{0,16},{16,0},{1,17},{17,1},{2,18},{18,2},{3,19},{19,3},{4,20},{20... | collective-permute-start | bytes 1572872 | tf_op jit(solution)/shard_map/ppermute | solution.py:559
  142.7 51.1 %collective-permute-start.12 = (bf16[2,256,512]{2,1,0:T(8,128)(2,1)S(1)}, bf16[2,256,512]{2,1,0:T(8,128)(2,1)S(1)}, u32[]{:S(2)}, u32[]{:S(2)}) collective-permute-start(bf16[2,256,512]{2,1,0:T(8,128)(2,1)S(1)} %get-tuple-element.146.refs_5_.refs_4_), channel_id=1, source_target_pairs={{0,4},{4,0},{1,5},{5,1},{2,6},{6,2},{3,7},{7,3},{8,12},{12,8},{9,1... | collective-permute-start | bytes 1572872 | tf_op jit(solution)/shard_map/ppermute | solution.py:559
  144.7 49.0 %collective-permute-start.9 = (bf16[2,256,512]{2,1,0:T(8,128)(2,1)S(1)}, bf16[2,256,512]{2,1,0:T(8,128)(2,1)}, u32[]{:S(2)}, u32[]{:S(2)}) collective-permute-start(bf16[2,256,512]{2,1,0:T(8,128)(2,1)S(1)} %get-tuple-element.147.refs_1_.refs_0_), channel_id=1, source_target_pairs={{0,16},{16,0},{1,17},{17,1},{2,18},{18,2},{3,19},{19,3},{4,20},{20... | collective-permute-start | bytes 1572872 | tf_op jit(solution)/shard_map/ppermute | solution.py:559
  303.3 168.8 %reduce-scatter.7.cloned.1.call-start = ((), (), s32[]{:S(2)}) async-start(), calls=%async_computation.12 | async-start | bytes 11796480 | tf_op jit(solution)/shard_map/reduce_scatter | solution.py:798
  361.6 157.8 %reduce-scatter.9.cloned.1.call-start = ((), (), s32[]{:S(2)}) async-start(), calls=%async_computation.13 | async-start | bytes 2359296 | tf_op jit(solution)/shard_map/reduce_scatter | solution.py:798
  419.2 43.1 %collective-permute-start.35 = (bf16[2,2,256,512]{3,2,1,0:T(8,128)(2,1)}, bf16[2,2,256,512]{3,2,1,0:T(8,128)(2,1)}, u32[]{:S(2)}, u32[]{:S(2)}) collective-permute-start(bf16[2,2,256,512]{3,2,1,0:T(8,128)(2,1)} %get-tuple-element.100), channel_id=1, source_target_pairs={{0,4},{4,0},{1,5},{5,1},{2,6},{6,2},{3,7},{7,3},{8,12},{12,8},{9,1... | collective-permute-start | bytes 3145736 | tf_op jit(solution)/shard_map/ppermute | solution.py:559
  420.4 42.0 %collective-permute-start.37 = (bf16[2,2,256,512]{3,2,1,0:T(8,128)(2,1)}, bf16[2,2,256,512]{3,2,1,0:T(8,128)(2,1)}, u32[]{:S(2)}, u32[]{:S(2)}) collective-permute-start(bf16[2,2,256,512]{3,2,1,0:T(8,128)(2,1)} %get-tuple-element.104), channel_id=1, source_target_pairs={{0,16},{16,0},{1,17},{17,1},{2,18},{18,2},{3,19},{19,3},{4,20},{20... | collective-permute-start | bytes 3145736 | tf_op jit(solution)/shard_map/ppermute | solution.py:559
  472.1 165.2 %reduce-scatter.11.cloned.1.call-start = ((), (), s32[]{:S(2)}) async-start(), calls=%async_computation.14 | async-start | bytes 7077888 | tf_op jit(solution)/shard_map/reduce_scatter | solution.py:798
  473.5 34.4 %collective-permute-start.36 = (bf16[2,256,512]{2,1,0:T(8,128)(2,1)S(1)}, bf16[2,256,512]{2,1,0:T(8,128)(2,1)}, u32[]{:S(2)}, u32[]{:S(2)}) collective-permute-start(bf16[2,256,512]{2,1,0:T(8,128)(2,1)S(1)} %fusion.19), channel_id=1, source_target_pairs={{0,16},{16,0},{1,17},{17,1},{2,18},{18,2},{3,19},{19,3},{4,20},{20... | collective-permute-start | bytes 1572872 | tf_op jit(solution)/shard_map/ppermute | solution.py:559
  477.0 30.9 %collective-permute-start.38 = (bf16[2,256,512]{2,1,0:T(8,128)(2,1)}, bf16[2,256,512]{2,1,0:T(8,128)(2,1)}, u32[]{:S(2)}, u32[]{:S(2)}) collective-permute-start(bf16[2,256,512]{2,1,0:T(8,128)(2,1)} %fusion.20), channel_id=1, source_target_pairs={{0,4},{4,0},{1,5},{5,1},{2,6},{6,2},{3,7},{7,3},{8,12},{12,8},{9,1... | collective-permute-start | bytes 1572872 | tf_op jit(solution)/shard_map/ppermute | solution.py:559
  523.6 45.5 %all-to-all-start.2 = ((bf16[4,256,512]{2,1,0:T(8,128)(2,1)}), bf16[4,256,512]{2,1,0:T(8,128)(2,1)S(1)}, u32[]{:S(2)}, u32[]{:S(2)}) async-start(bf16[4,256,512]{2,1,0:T(8,128)(2,1)} %fusion.13), calls=%async_computation.2 | async-start | bytes 2097152 | tf_op jit(solution)/shard_map/all_to_all | solution.py:663
  527.6 41.6 %collective-permute-start.42 = (bf16[1280,512]{1,0:T(8,128)(2,1)S(1)}, bf16[1280,512]{1,0:T(8,128)(2,1)}, u32[]{:S(2)}, u32[]{:S(2)}) collective-permute-start(bf16[1280,512]{1,0:T(8,128)(2,1)S(1)} %copy-done.9), channel_id=1, source_target_pairs={{0,16},{16,0},{1,17},{17,1},{2,18},{18,2},{3,19},{19,3},{4,20},{20... | collective-permute-start | bytes 3932168 | tf_op jit(solution)/shard_map/ppermute | solution.py:559
  541.0 40.9 %collective-permute-start.44 = (bf16[2,2,256,512]{3,2,1,0:T(8,128)(2,1)}, bf16[2,2,256,512]{3,2,1,0:T(8,128)(2,1)S(1)}, u32[]{:S(2)}, u32[]{:S(2)}) collective-permute-start(bf16[2,2,256,512]{3,2,1,0:T(8,128)(2,1)} %get-tuple-element.119), channel_id=1, source_target_pairs={{0,16},{16,0},{1,17},{17,1},{2,18},{18,2},{3,19},{19,3},{4,20},{20... | collective-permute-start | bytes 3145736 | tf_op jit(solution)/shard_map/ppermute | solution.py:559
  593.2 32.8 %collective-permute-start.57 = (bf16[1280,512]{1,0:T(8,128)(2,1)S(1)}, bf16[1280,512]{1,0:T(8,128)(2,1)}, u32[]{:S(2)}, u32[]{:S(2)}) collective-permute-start(bf16[1280,512]{1,0:T(8,128)(2,1)S(1)} %copy-done.9), channel_id=1, source_target_pairs={{0,8},{8,0},{1,9},{9,1},{2,10},{10,2},{3,11},{11,3},{4,12},{12,4},... | collective-permute-start | bytes 3932168 | tf_op jit(solution)/shard_map/ppermute | solution.py:559
  594.8 31.2 %collective-permute-start.58 = (bf16[1280,512]{1,0:T(8,128)(2,1)}, bf16[1280,512]{1,0:T(8,128)(2,1)}, u32[]{:S(2)}, u32[]{:S(2)}) collective-permute-start(bf16[1280,512]{1,0:T(8,128)(2,1)} %collective-permute-done.42.refs_2_), channel_id=1, source_target_pairs={{0,8},{8,0},{1,9},{9,1},{2,10},{10,2},{3,11},{11,3},{4,12},{12,4},... | collective-permute-start | bytes 3932168 | tf_op jit(solution)/shard_map/ppermute | solution.py:559
  601.6 55.6 %all-to-all-start.3 = ((bf16[4,256,512]{2,1,0:T(8,128)(2,1)}), bf16[4,256,512]{2,1,0:T(8,128)(2,1)S(1)}, u32[]{:S(2)}, u32[]{:S(2)}) async-start(bf16[4,256,512]{2,1,0:T(8,128)(2,1)} %fusion.9), calls=%async_computation.5 | async-start | bytes 2097152 | tf_op jit(solution)/shard_map/all_to_all | solution.py:663
  637.8 38.2 %collective-permute-start.59 = (bf16[768,512]{1,0:T(8,128)(2,1)}, bf16[768,512]{1,0:T(8,128)(2,1)}, u32[]{:S(2)}, u32[]{:S(2)}) collective-permute-start(bf16[768,512]{1,0:T(8,128)(2,1)} %reduce-scatter.11.cloned.1.call-done.refs_0_), channel_id=1, source_target_pairs={{0,8},{8,0},{1,9},{9,1},{2,10},{10,2},{3,11},{11,3},{4,12},{12,4},... | collective-permute-start | bytes 2359304 | tf_op jit(solution)/shard_map/ppermute | solution.py:559
  (98 other events, 1509.0 us)
Sparse Core Ops, SparseCore 0:
  11.7 129.3 all-gather.3
  143.2 97.5 all-gather.5
  242.5 54.4 all-gather.7
  303.4 58.0 reduce-scatter.4
  364.3 107.7 reduce-scatter.6
  474.8 33.9 reduce-scatter.8
  519.5 84.0 reduce-scatter.10

commit v6 on v5

--- a/solution.py
+++ b/solution.py
@@ -29,7 +29,7 @@
 
 
 def cost(flops, moved):
-    return pl.CostEstimate(flops=int(flops), bytes_accessed=int(moved), transcendentals=0)
+    return pl.CostEstimate(flops=int(flops) // 4, bytes_accessed=int(moved) // 4, transcendentals=0)
 
 
 def params(steps):
@@ -591,12 +591,12 @@
     return pieces, (low_x, high_y), (low_y, low_xy, high_x, high_xy)
 
 
-def scatter_plain(parts, *beside):
+def scatter_plain(parts, beside=(), beside_last=()):
     whole = parts[0].astype(F32)
     return lax.psum_scatter(whole, ("x", "y"), scatter_dimension=1, tiled=True), (), ()
 
 
-def scatter_tokens(parts, *beside):
+def scatter_tokens(parts, beside=(), beside_last=()):
     low_out, low_keep, high_out, high_keep = parts
     low_in, high_in = hop(low_out, "x"), hop(high_out, "y")
     if beside:
@@ -607,6 +607,8 @@
 
     low_last = hop(add(low_keep, low_in, 1).astype(BF), "y")
     high_last = hop(add(high_keep, high_in, 1).astype(BF), "x")
+    if beside_last:
+        low_last, high_last = after(low_last, *beside_last), after(high_last, *beside_last)
     low = add(low_keep, low_in, 0) + low_last.astype(F32)
     high = add(high_keep, high_in, 0) + high_last.astype(F32)
     return jnp.concatenate([low, high], axis=0), (low_in, high_in), (low_last, high_last)
@@ -635,13 +637,15 @@
         ],
         out_shape=[jax.ShapeDtypeStruct((4 * shape[0], *shape[1:]), F32) for shape in shapes],
         compiler_params=params(1),
-        cost_estimate=cost(0, 20 * pieces[0].size),
+        cost_estimate=cost(0, pieces[0].size),
         name="place",
     )(here, *pieces)
 
 
-def share(part):
+def share(part, *beside):
     over_y = hop(part, "y")
+    if beside:
+        over_y = after(over_y, *beside)
     return [part, hop(part, "c"), over_y, hop(over_y, "c")], over_y
 
 
@@ -692,7 +696,7 @@
         out_specs=pl.BlockSpec((1, 1, t, width), lambda j, y: (j, y, 0, 0)),
         out_shape=jax.ShapeDtypeStruct((count, 2, t, width), dtype),
         compiler_params=params(2),
-        cost_estimate=cost(0, 12 * count * t * width),
+        cost_estimate=cost(0, count * t * width),
         name="settle",
     )(y, back, other)
     return out.reshape(count, 2 * t, width)
@@ -864,7 +868,7 @@
     qkv_part = reduce(after(qkv_partial, out_part))
     one_parts = nn(grad_projected, w_attn, 0, qkv_count, starts)
     gate_up_pieces, gate_up_last = shared(after(gate_up_part, grad_projected[0]))
-    grad_one, _, one_last = scatter(one_parts, outputs[0], gate_up_last)
+    grad_one, _, one_last = scatter(one_parts, (gate_up_last,), (outputs[0],))
     through, attn_gain_part = norm_back(tokens, scale_one, gain_one, grad_one)
     input_grad, input_leaves = from_groups((grad_hidden + through).astype(BF))
     outputs = stored_from(outputs, BF)
@@ -904,9 +908,9 @@
         (down_all,) = place(down_pieces, here, [(units * unit, width)], write_rows)
         (out_all,) = place(out_pieces, here, [(heads * 64, width)], write_rows)
         (gate_up_all,) = place(gate_up_pieces, here, [(units, 2, unit, width)], write_gate_up)
-        qkv_part = after(qkv_part, sums, down_all, out_all, gate_up_all, outputs, *one_last)
+        qkv_pieces, _ = shared(after(qkv_part, sums, *one_last), down_all, out_all, gate_up_all, outputs)
         query_key_all, value_all = place(
-            shared(qkv_part)[0], here, [(heads, 2, 64, width), (heads, 64, width)], write_qkv
+            qkv_pieces, here, [(heads, 2, 64, width), (heads, 64, width)], write_qkv
         )
     else:
         down_all, out_all = down_pieces.astype(F32), out_pieces.astype(F32)

time: 694 us -> 709 us (1.022)
    all_to_all x2, waiting for transfers between devices: 27.7 us -> 6.42 us  [from_groups(): lax.all_to_all(mine, 'z', 0, 0, tiled=True).reshape(2, nz // 2, t, width)]
    all_to_all x2, waiting for transfers between devices: 53 us -> 68.3 us  [to_groups(): return lax.all_to_all(both, 'z', 0, 0, tiled=True)]
    ppermute x59, waiting for transfers between devices: 156 us -> 170 us  [hop(): return lax.ppermute(value, axis, swap)]
    ppermute x2, starting transfers between devices: 4.95 us -> 13 us  [sum_line(): value = value + lax.ppermute(value, 'z', [(i, i ^ step) for i in range(nz)])]
  transfers between devices with their start and end apart: 73 -> 73, of which waited for: 30 -> 30; matrix products, arithmetic and copies ran while one was open for 9% -> 8% of each run, Pallas kernels for 36% -> 36%
where the time goes in v6:
time: 709 us; the launch traced here: 701 us
  waiting for transfers between devices  273 us (39%)
  Pallas kernels  257 us (36%)
  starting transfers between devices  88.8 us (13%)
  other arithmetic  47.7 us (7%)
  local copies, waits for them, and re-layouts  18.8 us (3%)
  between operations  15.4 us (2%)
    ppermute x59, waiting for transfers between devices, hop(): return lax.ppermute(value, axis, swap)  170 us
    all_to_all x2, waiting for transfers between devices, to_groups(): return lax.all_to_all(both, 'z', 0, 0, tiled=True)  68.3 us
    pallas_call x2, Pallas kernels, attend_back(): pl.pallas_call(functools.partial(attend_back_kernel, group), grid=(1,), i...  57.6 us
    ppermute x59, starting transfers between devices, hop(): return lax.ppermute(value, axis, swap)  56.8 us
    pallas_call x4, Pallas kernels, mm_nn(): pl.pallas_call(functools.partial(nn_kernel, len(grads)), grid=(nz,), in_s...  45.4 us
    pallas_call x4, Pallas kernels, mm_tn(): pl.pallas_call(functools.partial(tn_kernel, count), grid=(count * steps,)...  43.5 us
    pallas_call x2, Pallas kernels, attend(): pl.pallas_call(functools.partial(attend_kernel, group), grid=(1,), in_spe...  33.6 us
    pallas_call x4, Pallas kernels, place(): pl.pallas_call(functools.partial(place_kernel, write), grid=(4,), in_spec...  19.3 us
  transfers between devices with their start and end apart: 73, of which 30 were waited for; matrix products, arithmetic and copies ran while one was open for 8% of the time, Pallas kernels for 36%

profile of v6, /device:TPU:0, one launch (start us, length us, event | category | flops | bytes accessed | tf_op | source)
XLA Modules:
  0.0 700.9 jit_solution(17431223131805083822)
XLA Ops:
  16.7 12.2 %collective-permute-done.1 = bf16[2,256,512]{2,1,0:T(8,128)(2,1)} collective-permute-done((bf16[2,256,512]{2,1,0:T(8,128)(2,1)}, bf16[2,256,512]{2,1,0:T(8,128)(2,1)}, u32[]{:S(2)}, u32[]{:S(2)}) %collective-permute-start.1) | collective-permute-done | bytes 524320 | tf_op jit(solution)/shard_map/ppermute | solution.py:559
  43.2 51.6 %all-to-all-done = bf16[4,264,512]{2,1,0:T(8,128)(2,1)} async-done(((bf16[4,264,512]{2,1,0:T(8,128)(2,1)}), bf16[4,264,512]{2,1,0:T(8,128)(2,1)}, u32[]{:S(2)}, u32[]{:S(2)}) %all-to-all-start) | async-done | bytes 1081376 | tf_op jit(solution)/shard_map/all_to_all | solution.py:662
  123.5 16.7 %all-to-all-done.1 = bf16[4,256,512]{2,1,0:T(8,128)(2,1)S(1)} async-done(((bf16[4,256,512]{2,1,0:T(8,128)(2,1)}), bf16[4,256,512]{2,1,0:T(8,128)(2,1)S(1)}, u32[]{:S(2)}, u32[]{:S(2)}) %all-to-all-start.1) | async-done | bytes 1048608 | tf_op jit(solution)/shard_map/all_to_all | solution.py:662
  149.0 12.3 %product_nt.2.q_ref.k_ref.v_ref = bf16[1024,1536]{1,0:T(8,128)(2,1)} custom-call(s32[4]{0:T(128)} %add_multiply_fusion.starts_ref, bf16[2,256,512]{2,1,0:T(8,128)(2,1)} %copy-done.10, bf16[2,256,512]{2,1,0:T(8,128)(2,1)} %collective-permute-done.2.refs_1_.refs_3_, bf16[2,256,512]{2,1,0:T(8,128)(2,1)} %collective-permute-done.3.refs_2_.refs_4_, ...), custom_call_target="tpu_custom_call" | custom-call | flops 1610612736 | bytes 3407872 | tf_op jit(solution)/shard_map/product_nt/pallas_call | solution.py:78
  161.3 16.8 %attend.2 = (bf16[1024,256]{1,0:T(8,128)(2,1)}, f32[8,1024]{1,0:T(8,128)}) custom-call(s32[1]{0:T(128)} %dynamic_slice.51.length_ref, f32[8,32]{1,0:T(8,128)} %constant_dynamic-slice_fusion.4.table_ref, bf16[1024,1536]{1,0:T(8,128)(2,1)} %product_nt.2.q_ref.k_ref.v_ref, bf16[1024,1536]{1,0:T(8,128)(2,1)} %product_nt.2.q_ref.k_ref.v_ref, ...), custom_call_target="tpu_custom_call" | custom-call | flops 1073741824 | bytes 524288 | tf_op jit(solution)/shard_map/attend/pallas_call | solution.py:454
  181.0 16.8 %attend.3 = (bf16[1024,256]{1,0:T(8,128)(2,1)}, f32[8,1024]{1,0:T(8,128)}) custom-call(s32[1]{0:T(128)} %dynamic_slice.51.length_ref, f32[8,32]{1,0:T(8,128)} %constant_dynamic-slice_fusion.4.table_ref, bf16[1024,1536]{1,0:T(8,128)(2,1)} %product_nt.2.q_ref.k_ref.v_ref, bf16[1024,1536]{1,0:T(8,128)(2,1)} %product_nt.2.q_ref.k_ref.v_ref, ...), custom_call_target="tpu_custom_call" | custom-call | flops 1073741824 | bytes 524288 | tf_op jit(solution)/shard_map/attend/pallas_call | solution.py:454
  206.3 22.8 %collective-permute-done.15 = bf16[2,2,256,512]{3,2,1,0:T(8,128)(2,1)S(1)} collective-permute-done((bf16[2,2,256,512]{3,2,1,0:T(8,128)(2,1)}, bf16[2,2,256,512]{3,2,1,0:T(8,128)(2,1)S(1)}, u32[]{:S(2)}, u32[]{:S(2)}) %collective-permute-start.15) | collective-permute-done | bytes 1048608 | tf_op jit(solution)/shard_map/ppermute | solution.py:559
  250.1 10.8 %collective-permute-done.20.refs_2_.refs_3_ = bf16[2,256,512]{2,1,0:T(8,128)(2,1)S(1)} collective-permute-done((bf16[2,256,512]{2,1,0:T(8,128)(2,1)S(1)}, bf16[2,256,512]{2,1,0:T(8,128)(2,1)S(1)}, u32[]{:S(2)}, u32[]{:S(2)}) %collective-permute-start.20) | collective-permute-done | bytes 524320 | tf_op jit(solution)/shard_map/ppermute | solution.py:559
  280.0 17.6 %ffn_in.1 = (bf16[1024,1280]{1,0:T(8,128)(2,1)}, bf16[1024,1280]{1,0:T(8,128)(2,1)}, bf16[1024,1280]{1,0:T(8,128)(2,1)}) custom-call(s32[4]{0:T(128)} %add_multiply_fusion.starts_ref, bf16[2,256,512]{2,1,0:T(8,128)(2,1)} %copy-done.8, bf16[2,256,512]{2,1,0:T(8,128)(2,1)} %copy-done.18, bf16[2,256,512]{2,1,0:T(8,128)(2,1)} %copy-done.16, ...), custom_call_target="tpu_custom_call" | custom-call | flops 2684354560 | bytes 5636096 | tf_op jit(solution)/shard_map/ffn_in/pallas_call | solution.py:214
  297.6 10.0 %product_tn.4 = bf16[4,1280,512]{2,1,0:T(8,128)(2,1)} custom-call(s32[4]{0:T(128)} %add_multiply_fusion.starts_ref, bf16[1024,1280]{1,0:T(8,128)(2,1)} %get-tuple-element.95.refs_0_, bf16[2,256,512]{2,1,0:T(8,128)(2,1)} %copy-done.6, bf16[2,256,512]{2,1,0:T(8,128)(2,1)} %copy-done.15, bf16[2,256,512]{2,1,0:T(8,128)(2,1)} %copy-done.13, ...), custom_call_target="tpu_custom_call" | custom-call | flops 1342177280 | bytes 3014656 | tf_op jit(solution)/shard_map/product_tn/pallas_call | solution.py:171
  307.7 15.3 %ffn_back.1.refs_0_ = bf16[1024,2560]{1,0:T(8,128)(2,1)} custom-call(s32[4]{0:T(128)} %add_multiply_fusion.starts_ref, bf16[2,256,512]{2,1,0:T(8,128)(2,1)} %copy-done.6, bf16[2,256,512]{2,1,0:T(8,128)(2,1)} %copy-done.15, bf16[2,256,512]{2,1,0:T(8,128)(2,1)} %copy-done.13, bf16[2,256,512]{2,1,0:T(8,128)(2,1)} %collective-permute-done.11.refs_4_.refs_3_, ...), custom_call_target="tpu_custom_call" | custom-call | flops 1342177280 | bytes 4980736 | tf_op jit(solution)/shard_map/ffn_back/pallas_call | solution.py:245
  323.0 16.5 %product_nn.5 = (bf16[2,2,256,512]{3,2,1,0:T(8,128)(2,1)}, bf16[2,2,256,512]{3,2,1,0:T(8,128)(2,1)}, bf16[2,2,256,512]{3,2,1,0:T(8,128)(2,1)}, bf16[2,2,256,512]{3,2,1,0:T(8,128)(2,1)}) custom-call(s32[4]{0:T(128)} %add_multiply_fusion.starts_ref, bf16[1024,2560]{1,0:T(8,128)(2,1)} %ffn_back.1.refs_0_, bf16[4,2,1280,512]{3,2,1,0:T(8,128)(2,1)} %bitcast.101), custom_call_target="tpu_custom_call" | custom-call | flops 2684354560 | bytes 4980736 | tf_op jit(solution)/shard_map/product_nn/pallas_call | solution.py:123
  342.4 15.9 %product_tn.5 = bf16[4,2560,512]{2,1,0:T(8,128)(2,1)} custom-call(s32[4]{0:T(128)} %add_multiply_fusion.starts_ref, bf16[1024,2560]{1,0:T(8,128)(2,1)} %ffn_back.1.refs_0_, bf16[2,256,512]{2,1,0:T(8,128)(2,1)} %copy-done.8, bf16[2,256,512]{2,1,0:T(8,128)(2,1)} %copy-done.18, bf16[2,256,512]{2,1,0:T(8,128)(2,1)} %copy-done.16, ...), custom_call_target="tpu_custom_call" | custom-call | flops 2684354560 | bytes 4980736 | tf_op jit(solution)/shard_map/product_tn/pallas_call | solution.py:171
  373.2 10.2 %product_nn.6 = (bf16[2,2,256,512]{3,2,1,0:T(8,128)(2,1)}, bf16[2,2,256,512]{3,2,1,0:T(8,128)(2,1)}, bf16[2,2,256,512]{3,2,1,0:T(8,128)(2,1)}, bf16[2,2,256,512]{3,2,1,0:T(8,128)(2,1)}) custom-call(s32[4]{0:T(128)} %add_multiply_fusion.starts_ref, bf16[1024,1280]{1,0:T(8,128)(2,1)} %get-tuple-element.95.refs_0_, bf16[4,2,640,512]{3,2,1,0:T(8,128)(2,1)} %bitcast.106), custom_call_target="tpu_custom_call" | custom-call | flops 1342177280 | bytes 3014656 | tf_op jit(solution)/shard_map/product_nn/pallas_call | solution.py:123
  393.4 10.8 %collective-permute-done.30.refs_2_.refs_4_ = bf16[2,256,512]{2,1,0:T(8,128)(2,1)S(1)} collective-permute-done((bf16[2,256,512]{2,1,0:T(8,128)(2,1)S(1)}, bf16[2,256,512]{2,1,0:T(8,128)(2,1)S(1)}, u32[]{:S(2)}, u32[]{:S(2)}) %collective-permute-start.30) | collective-permute-done | bytes 524320 | tf_op jit(solution)/shard_map/ppermute | solution.py:559
  406.2 10.5 %collective-permute-done.29.refs_1_.refs_3_ = bf16[2,256,512]{2,1,0:T(8,128)(2,1)S(1)} collective-permute-done((bf16[2,256,512]{2,1,0:T(8,128)(2,1)S(1)}, bf16[2,256,512]{2,1,0:T(8,128)(2,1)S(1)}, u32[]{:S(2)}, u32[]{:S(2)}) %collective-permute-start.29) | collective-permute-done | bytes 524320 | tf_op jit(solution)/shard_map/ppermute | solution.py:559
  438.0 28.8 %attend_back.2 = (bf16[1024,768]{1,0:T(8,128)(2,1)}, f32[4,32,128]{2,1,0:T(8,128)}) custom-call(s32[1]{0:T(128)} %dynamic_slice.51.length_ref, f32[8,32]{1,0:T(8,128)} %constant_dynamic-slice_fusion.4.table_ref, bf16[1024,1536]{1,0:T(8,128)(2,1)} %product_nt.2.q_ref.k_ref.v_ref, bf16[1024,1536]{1,0:T(8,128)(2,1)} %product_nt.2.q_ref.k_ref.v_ref, ...), custom_call_target="tpu_custom_call" | custom-call | flops 2684354560 | bytes 1048576 | tf_op jit(solution)/shard_map/attend_back/pallas_call | solution.py:481
  483.4 28.8 %attend_back.3 = (bf16[1024,768]{1,0:T(8,128)(2,1)}, f32[4,32,128]{2,1,0:T(8,128)}) custom-call(s32[1]{0:T(128)} %dynamic_slice.51.length_ref, f32[8,32]{1,0:T(8,128)} %constant_dynamic-slice_fusion.4.table_ref, bf16[1024,1536]{1,0:T(8,128)(2,1)} %product_nt.2.q_ref.k_ref.v_ref, bf16[1024,1536]{1,0:T(8,128)(2,1)} %product_nt.2.q_ref.k_ref.v_ref, ...), custom_call_target="tpu_custom_call" | custom-call | flops 2684354560 | bytes 1048576 | tf_op jit(solution)/shard_map/attend_back/pallas_call | solution.py:481
  512.2 11.4 %product_tn.7 = bf16[4,1536,512]{2,1,0:T(8,128)(2,1)} custom-call(s32[4]{0:T(128)} %add_multiply_fusion.starts_ref, bf16[1024,768]{1,0:T(8,128)(2,1)} %get-tuple-element.110.refs_0_, bf16[1024,768]{1,0:T(8,128)(2,1)} %get-tuple-element.115.refs_1_, bf16[2,256,512]{2,1,0:T(8,128)(2,1)} %copy-done.10, ...), custom_call_target="tpu_custom_call" | custom-call | flops 1610612736 | bytes 3407872 | tf_op jit(solution)/shard_map/product_tn/pallas_call | solution.py:171
  526.7 11.7 %product_nn.7 = (bf16[2,2,256,512]{3,2,1,0:T(8,128)(2,1)}, bf16[2,2,256,512]{3,2,1,0:T(8,128)(2,1)}, bf16[2,2,256,512]{3,2,1,0:T(8,128)(2,1)}, bf16[2,2,256,512]{3,2,1,0:T(8,128)(2,1)}) custom-call(s32[4]{0:T(128)} %add_multiply_fusion.starts_ref, bf16[1024,768]{1,0:T(8,128)(2,1)} %get-tuple-element.110.refs_0_, ...), custom_call_target="tpu_custom_call" | custom-call | flops 1610612736 | bytes 3407872 | tf_op jit(solution)/shard_map/product_nn/pallas_call | solution.py:123
  546.3 13.9 %collective-permute-done.41 = bf16[2,2,256,512]{3,2,1,0:T(8,128)(2,1)} collective-permute-done((bf16[2,2,256,512]{3,2,1,0:T(8,128)(2,1)}, bf16[2,2,256,512]{3,2,1,0:T(8,128)(2,1)}, u32[]{:S(2)}, u32[]{:S(2)}) %collective-permute-start.41) | collective-permute-done | bytes 1048608 | tf_op jit(solution)/shard_map/ppermute | solution.py:559
  562.8 15.4 %collective-permute-done.44 = bf16[2,2,256,512]{3,2,1,0:T(8,128)(2,1)} collective-permute-done((bf16[2,2,256,512]{3,2,1,0:T(8,128)(2,1)}, bf16[2,2,256,512]{3,2,1,0:T(8,128)(2,1)}, u32[]{:S(2)}, u32[]{:S(2)}) %collective-permute-start.44) | collective-permute-done | bytes 1048608 | tf_op jit(solution)/shard_map/ppermute | solution.py:559
  618.9 23.3 %collective-permute-done.57.refs_2_ = bf16[256,512]{1,0:T(8,128)(2,1)S(1)} collective-permute-done((bf16[256,512]{1,0:T(8,128)(2,1)}, bf16[256,512]{1,0:T(8,128)(2,1)S(1)}, u32[]{:S(2)}, u32[]{:S(2)}) %collective-permute-start.57) | collective-permute-done | bytes 262176 | tf_op jit(solution)/shard_map/ppermute | solution.py:559
  665.1 12.2 %collective-permute-start.50 = (f32[10,512]{1,0:T(8,128)S(1)}, f32[10,512]{1,0:T(8,128)S(1)}, u32[]{:S(2)}, u32[]{:S(2)}) collective-permute-start(f32[10,512]{1,0:T(8,128)S(1)} %add.274), channel_id=1, source_target_pairs={{0,1},{1,0},{2,3},{3,2},{4,5},{5,4},{6,7},{7,6},{8,9},{9,8},{10,11... | collective-permute-start | bytes 61448 | tf_op jit(solution)/shard_map/ppermute | solution.py:721
  (329 shorter events, 273.3 us)
Async XLA Ops:
  7.2 134.3 %all-gather.4.cloned.1.call-start = ((), (), s32[]{:S(2)}) async-start(), calls=%async_computation.8 | async-start | bytes 9437184 | tf_op jit(solution)/shard_map/all_gather | solution.py:761
  11.6 268.5 %all-gather.6.cloned.1.call-start = ((), (), s32[]{:S(2)}) async-start(), calls=%async_computation.9 | async-start | bytes 11796480 | tf_op jit(solution)/shard_map/all_gather | solution.py:761
  34.3 60.5 %all-to-all-start = ((bf16[4,264,512]{2,1,0:T(8,128)(2,1)}), bf16[4,264,512]{2,1,0:T(8,128)(2,1)}, u32[]{:S(2)}, u32[]{:S(2)}) async-start(bf16[4,264,512]{2,1,0:T(8,128)(2,1)} %pad_maximum_fusion.3), calls=%async_computation | async-start | bytes 2162688 | tf_op jit(solution)/shard_map/all_to_all | solution.py:662
  39.3 268.4 %all-gather.8.cloned.1.call-start = ((), (), s32[]{:S(2)}) async-start(), calls=%async_computation.10 | async-start | bytes 5898240 | tf_op jit(solution)/shard_map/all_gather | solution.py:761
  41.6 53.2 %collective-permute-start.8 = (bf16[2,256,512]{2,1,0:T(8,128)(2,1)S(1)}, bf16[2,256,512]{2,1,0:T(8,128)(2,1)S(1)}, u32[]{:S(2)}, u32[]{:S(2)}) collective-permute-start(bf16[2,256,512]{2,1,0:T(8,128)(2,1)S(1)} %get-tuple-element.155), channel_id=1, source_target_pairs={{0,16},{16,0},{1,17},{17,1},{2,18},{18,2},{3,19},{19,3},{4,20},{20... | collective-permute-start | bytes 1572872 | tf_op jit(solution)/shard_map/ppermute | solution.py:559
  95.9 44.3 %all-to-all-start.1 = ((bf16[4,256,512]{2,1,0:T(8,128)(2,1)}), bf16[4,256,512]{2,1,0:T(8,128)(2,1)S(1)}, u32[]{:S(2)}, u32[]{:S(2)}) async-start(bf16[4,256,512]{2,1,0:T(8,128)(2,1)} %bitcast.26), calls=%async_computation.1 | async-start | bytes 2097152 | tf_op jit(solution)/shard_map/all_to_all | solution.py:662
  101.7 264.2 %reduce-scatter.5.cloned.1.call-start = ((), (), s32[]{:S(2)}) async-start(), calls=%async_computation.11 | async-start | bytes 5898240 | tf_op jit(solution)/shard_map/reduce_scatter | solution.py:802
  142.8 35.3 %collective-permute-start.13 = (bf16[2,256,512]{2,1,0:T(8,128)(2,1)S(1)}, bf16[2,256,512]{2,1,0:T(8,128)(2,1)}, u32[]{:S(2)}, u32[]{:S(2)}) collective-permute-start(bf16[2,256,512]{2,1,0:T(8,128)(2,1)S(1)} %get-tuple-element.152.refs_5_.refs_4_), channel_id=1, source_target_pairs={{0,16},{16,0},{1,17},{17,1},{2,18},{18,2},{3,19},{19,3},{4,20},{20... | collective-permute-start | bytes 1572872 | tf_op jit(solution)/shard_map/ppermute | solution.py:559
  147.9 50.0 %collective-permute-start.12 = (bf16[2,256,512]{2,1,0:T(8,128)(2,1)S(1)}, bf16[2,256,512]{2,1,0:T(8,128)(2,1)S(1)}, u32[]{:S(2)}, u32[]{:S(2)}) collective-permute-start(bf16[2,256,512]{2,1,0:T(8,128)(2,1)S(1)} %get-tuple-element.152.refs_5_.refs_4_), channel_id=1, source_target_pairs={{0,4},{4,0},{1,5},{5,1},{2,6},{6,2},{3,7},{7,3},{8,12},{12,8},{9,1... | collective-permute-start | bytes 1572872 | tf_op jit(solution)/shard_map/ppermute | solution.py:559
  148.4 49.4 %collective-permute-start.9 = (bf16[2,256,512]{2,1,0:T(8,128)(2,1)S(1)}, bf16[2,256,512]{2,1,0:T(8,128)(2,1)S(1)}, u32[]{:S(2)}, u32[]{:S(2)}) collective-permute-start(bf16[2,256,512]{2,1,0:T(8,128)(2,1)S(1)} %get-tuple-element.153.refs_1_.refs_0_), channel_id=1, source_target_pairs={{0,16},{16,0},{1,17},{17,1},{2,18},{18,2},{3,19},{19,3},{4,20},{20... | collective-permute-start | bytes 1572872 | tf_op jit(solution)/shard_map/ppermute | solution.py:559
  307.6 168.8 %reduce-scatter.7.cloned.1.call-start = ((), (), s32[]{:S(2)}) async-start(), calls=%async_computation.12 | async-start | bytes 11796480 | tf_op jit(solution)/shard_map/reduce_scatter | solution.py:802
  365.9 157.7 %reduce-scatter.9.cloned.1.call-start = ((), (), s32[]{:S(2)}) async-start(), calls=%async_computation.13 | async-start | bytes 2359296 | tf_op jit(solution)/shard_map/reduce_scatter | solution.py:802
  423.6 43.2 %collective-permute-start.35 = (bf16[2,2,256,512]{3,2,1,0:T(8,128)(2,1)}, bf16[2,2,256,512]{3,2,1,0:T(8,128)(2,1)}, u32[]{:S(2)}, u32[]{:S(2)}) collective-permute-start(bf16[2,2,256,512]{3,2,1,0:T(8,128)(2,1)} %get-tuple-element.103), channel_id=1, source_target_pairs={{0,4},{4,0},{1,5},{5,1},{2,6},{6,2},{3,7},{7,3},{8,12},{12,8},{9,1... | collective-permute-start | bytes 3145736 | tf_op jit(solution)/shard_map/ppermute | solution.py:559
  424.7 42.1 %collective-permute-start.37 = (bf16[2,2,256,512]{3,2,1,0:T(8,128)(2,1)}, bf16[2,2,256,512]{3,2,1,0:T(8,128)(2,1)}, u32[]{:S(2)}, u32[]{:S(2)}) collective-permute-start(bf16[2,2,256,512]{3,2,1,0:T(8,128)(2,1)} %get-tuple-element.107), channel_id=1, source_target_pairs={{0,16},{16,0},{1,17},{17,1},{2,18},{18,2},{3,19},{19,3},{4,20},{20... | collective-permute-start | bytes 3145736 | tf_op jit(solution)/shard_map/ppermute | solution.py:559
  476.4 140.0 %reduce-scatter.11.cloned.1.call-start = ((), (), s32[]{:S(2)}) async-start(), calls=%async_computation.14 | async-start | bytes 7077888 | tf_op jit(solution)/shard_map/reduce_scatter | solution.py:802
  477.8 34.4 %collective-permute-start.36 = (bf16[2,256,512]{2,1,0:T(8,128)(2,1)S(1)}, bf16[2,256,512]{2,1,0:T(8,128)(2,1)}, u32[]{:S(2)}, u32[]{:S(2)}) collective-permute-start(bf16[2,256,512]{2,1,0:T(8,128)(2,1)S(1)} %fusion.19), channel_id=1, source_target_pairs={{0,16},{16,0},{1,17},{17,1},{2,18},{18,2},{3,19},{19,3},{4,20},{20... | collective-permute-start | bytes 1572872 | tf_op jit(solution)/shard_map/ppermute | solution.py:559
  523.6 36.6 %collective-permute-start.42 = (bf16[1280,512]{1,0:T(8,128)(2,1)}, bf16[1280,512]{1,0:T(8,128)(2,1)}, u32[]{:S(2)}, u32[]{:S(2)}) collective-permute-start(bf16[1280,512]{1,0:T(8,128)(2,1)} %reduce-scatter.7.cloned.1.call-done.refs_0_), channel_id=1, source_target_pairs={{0,16},{16,0},{1,17},{17,1},{2,18},{18,2},{3,19},{19,3},{4,20},{20... | collective-permute-start | bytes 3932168 | tf_op jit(solution)/shard_map/ppermute | solution.py:559
  541.1 37.1 %collective-permute-start.44 = (bf16[2,2,256,512]{3,2,1,0:T(8,128)(2,1)}, bf16[2,2,256,512]{3,2,1,0:T(8,128)(2,1)}, u32[]{:S(2)}, u32[]{:S(2)}) collective-permute-start(bf16[2,2,256,512]{3,2,1,0:T(8,128)(2,1)} %get-tuple-element.123), channel_id=1, source_target_pairs={{0,16},{16,0},{1,17},{17,1},{2,18},{18,2},{3,19},{19,3},{4,20},{20... | collective-permute-start | bytes 3145736 | tf_op jit(solution)/shard_map/ppermute | solution.py:559
  542.7 44.8 %all-to-all-start.2 = ((bf16[4,256,512]{2,1,0:T(8,128)(2,1)}), bf16[4,256,512]{2,1,0:T(8,128)(2,1)S(1)}, u32[]{:S(2)}, u32[]{:S(2)}) async-start(bf16[4,256,512]{2,1,0:T(8,128)(2,1)} %fusion.13), calls=%async_computation.2 | async-start | bytes 2097152 | tf_op jit(solution)/shard_map/all_to_all | solution.py:667
  597.4 65.7 %all-to-all-start.3 = ((bf16[4,256,512]{2,1,0:T(8,128)(2,1)}), bf16[4,256,512]{2,1,0:T(8,128)(2,1)S(1)}, u32[]{:S(2)}, u32[]{:S(2)}) async-start(bf16[4,256,512]{2,1,0:T(8,128)(2,1)} %fusion.9), calls=%async_computation.5 | async-start | bytes 2097152 | tf_op jit(solution)/shard_map/all_to_all | solution.py:667
  603.4 46.8 %collective-permute-start.59 = (bf16[1280,512]{1,0:T(8,128)(2,1)}, bf16[1280,512]{1,0:T(8,128)(2,1)S(1)}, u32[]{:S(2)}, u32[]{:S(2)}) collective-permute-start(bf16[1280,512]{1,0:T(8,128)(2,1)} %reduce-scatter.7.cloned.1.call-done.refs_0_), channel_id=1, source_target_pairs={{0,8},{8,0},{1,9},{9,1},{2,10},{10,2},{3,11},{11,3},{4,12},{12,4},... | collective-permute-start | bytes 3932168 | tf_op jit(solution)/shard_map/ppermute | solution.py:559
  603.4 46.8 %collective-permute-start.60 = (bf16[1280,512]{1,0:T(8,128)(2,1)}, bf16[1280,512]{1,0:T(8,128)(2,1)}, u32[]{:S(2)}, u32[]{:S(2)}) collective-permute-start(bf16[1280,512]{1,0:T(8,128)(2,1)} %collective-permute-done.42.refs_2_), channel_id=1, source_target_pairs={{0,8},{8,0},{1,9},{9,1},{2,10},{10,2},{3,11},{11,3},{4,12},{12,4},... | collective-permute-start | bytes 3932168 | tf_op jit(solution)/shard_map/ppermute | solution.py:559
  616.4 46.7 %collective-permute-start.53 = (bf16[768,512]{1,0:T(8,128)(2,1)}, bf16[768,512]{1,0:T(8,128)(2,1)}, u32[]{:S(2)}, u32[]{:S(2)}) collective-permute-start(bf16[768,512]{1,0:T(8,128)(2,1)} %reduce-scatter.11.cloned.1.call-done.refs_0_), channel_id=1, source_target_pairs={{0,16},{16,0},{1,17},{17,1},{2,18},{18,2},{3,19},{19,3},{4,20},{20... | collective-permute-start | bytes 2359304 | tf_op jit(solution)/shard_map/ppermute | solution.py:559
  618.8 39.3 %collective-permute-start.56 = (bf16[256,512]{1,0:T(8,128)(2,1)}, bf16[256,512]{1,0:T(8,128)(2,1)S(1)}, u32[]{:S(2)}, u32[]{:S(2)}) collective-permute-start(bf16[256,512]{1,0:T(8,128)(2,1)} %reduce-scatter.9.cloned.1.call-done.refs_0_), channel_id=1, source_target_pairs={{0,8},{8,0},{1,9},{9,1},{2,10},{10,2},{3,11},{11,3},{4,12},{12,4},... | collective-permute-start | bytes 786440 | tf_op jit(solution)/shard_map/ppermute | solution.py:559
  (96 other events, 1605.6 us)
Sparse Core Ops, SparseCore 0:
  11.7 129.7 all-gather.3
  143.7 97.5 all-gather.5
  242.9 54.4 all-gather.7
  307.7 58.0 reduce-scatter.4
  368.6 107.7 reduce-scatter.6
  479.1 33.9 reduce-scatter.8
  523.8 86.3 reduce-scatter.10

commit v7 on v6

--- a/solution.py
+++ b/solution.py
@@ -29,7 +29,7 @@
 
 
 def cost(flops, moved):
-    return pl.CostEstimate(flops=int(flops) // 4, bytes_accessed=int(moved) // 4, transcendentals=0)
+    return pl.CostEstimate(flops=int(flops) // 16, bytes_accessed=int(moved) // 16, transcendentals=0)
 
 
 def params(steps):
@@ -709,8 +709,8 @@
     return both.transpose(1, 0, 2, 3).reshape(count, 2 * t, width).astype(dtype)
 
 
-def sum_plane(value, nx):
-    value = value + hop(value, "c")
+def sum_plane(value, nx, *earlier):
+    value = value + after(hop(value, "c"), *earlier)
     value = value + hop(value, "x") if nx == 2 else lax.psum(value, "x")
     return value + hop(value, "y")
 
@@ -852,38 +852,37 @@
     branch_parts = nn([after(activated, gate_up_partial)], w_down, 0, units * unit, starts)
     through, ffn_gain_part = norm_back(hidden, scale_two, gain_two, grad_two)
     grad_hidden = upstream + through
-    grad_branch, _, branch_last = gather(after(grad_hidden.astype(BF), branch_parts[0]))
+    grad_branch, _, branch_here = gather(after(grad_hidden.astype(BF), branch_parts[0]))
     grad_attended = nt(grad_branch, w_attn, qkv_count, out_count, starts)
     out_partial = tn(attended, grad_branch, starts)
-    branch_parts = [after(part, *branch_last) for part in branch_parts]
+    branch_parts = [after(part, *branch_here) for part in branch_parts]
     branch, branch_first, branch_last = scatter(branch_parts)
-    down_pieces, down_last = shared(after(down_part, grad_attended))
+    down_pieces, down_last = shared(after(down_part, *branch_here))
     grad_projected, table_part = attend_back_all(after(grad_attended, out_partial), *branch_first)
-    out_part = reduce(after(out_partial, gate_up_part, grad_projected[0], *branch_first))
+    out_part = reduce(after(out_partial, gate_up_part, grad_projected[0], *branch_first, down_last))
     outputs = (live * (hidden + branch)).astype(BF)
-    last = after(grad_projected[-1], *branch_last, down_last)
-    grad_projected = [*grad_projected[:-1], last]
     outputs, _ = from_groups(outputs)
     qkv_partial = tn(grad_projected, normed, starts)
-    qkv_part = reduce(after(qkv_partial, out_part))
+    gate_up_pieces, gate_up_last = shared(after(gate_up_part, grad_projected[0]))
+    qkv_part = reduce(after(qkv_partial, out_part, *branch_last, gate_up_last))
     one_parts = nn(grad_projected, w_attn, 0, qkv_count, starts)
-    gate_up_pieces, gate_up_last = shared(after(gate_up_part, grad_projected[0]))
-    grad_one, _, one_last = scatter(one_parts, (gate_up_last,), (outputs[0],))
+    grad_one, _, one_last = scatter(one_parts, (), (outputs[0],))
     through, attn_gain_part = norm_back(tokens, scale_one, gain_one, grad_one)
     input_grad, input_leaves = from_groups((grad_hidden + through).astype(BF))
-    outputs = stored_from(outputs, BF)
+
+    out_pieces, out_last = shared(out_part)
 
     table_part = jnp.sum(table_part, axis=2)
     every = jnp.zeros((nx * 2 * local_heads, table_part.shape[1]), F32)
     every = lax.dynamic_update_slice_in_dim(every, table_part, (x * 2 + y) * local_heads, 0)
     spare = -every.size % width
     every = jnp.pad(every.reshape(-1), (0, spare)).reshape(-1, width)
-    sums = sum_plane(jnp.concatenate([attn_gain_part, ffn_gain_part, every]), nx)
+    sums = sum_plane(jnp.concatenate([attn_gain_part, ffn_gain_part, every]), nx, out_last, outputs[1])
     all_sums = sum_line(after(sums, input_leaves), nz)
     attn_gain_grad, ffn_gain_grad = all_sums[:nz], all_sums[nz : 2 * nz]
     every = all_sums[2 * nz :].reshape(-1)[: nx * 2 * local_heads * buckets].reshape(-1, buckets)
 
-    out_pieces, _ = shared(after(out_part, *one_last))
+    outputs = stored_from(outputs, BF)
     if fits:
         here = jnp.stack([y, c]).astype(jnp.int32)
 

time: 709 us -> 686 us (0.968)
  waiting for transfers between devices: 273 us -> 257 us
    ppermute x59, waiting for transfers between devices: 170 us -> 141 us  [hop(): return lax.ppermute(value, axis, swap)]
    all_to_all x2, waiting for transfers between devices: 6.42 us -> 24.4 us  [from_groups(): lax.all_to_all(mine, 'z', 0, 0, tiled=True).reshape(2, nz // 2, t, width)]
  transfers between devices with their start and end apart: 73 -> 73, of which waited for: 30 -> 29; matrix products, arithmetic and copies ran while one was open for 8% -> 9% of each run, Pallas kernels for 36% -> 37%
where the time goes in v7:
time: 686 us; the launch traced here: 680 us
  waiting for transfers between devices  257 us (37%)
  Pallas kernels  257 us (37%)
  starting transfers between devices  84.7 us (12%)
  other arithmetic  48.4 us (7%)
  local copies, waits for them, and re-layouts  17.5 us (3%)
  between operations  15.4 us (2%)
    ppermute x59, waiting for transfers between devices, hop(): return lax.ppermute(value, axis, swap)  141 us
    all_to_all x2, waiting for transfers between devices, to_groups(): return lax.all_to_all(both, 'z', 0, 0, tiled=True)  68.3 us
    ppermute x59, starting transfers between devices, hop(): return lax.ppermute(value, axis, swap)  57.8 us
    pallas_call x2, Pallas kernels, attend_back(): pl.pallas_call(functools.partial(attend_back_kernel, group), grid=(1,), i...  57.6 us
    pallas_call x4, Pallas kernels, mm_nn(): pl.pallas_call(functools.partial(nn_kernel, len(grads)), grid=(nz,), in_s...  45.3 us
    pallas_call x4, Pallas kernels, mm_tn(): pl.pallas_call(functools.partial(tn_kernel, count), grid=(count * steps,)...  43.4 us
    pallas_call x2, Pallas kernels, attend(): pl.pallas_call(functools.partial(attend_kernel, group), grid=(1,), in_spe...  33.6 us
    all_to_all x2, waiting for transfers between devices, from_groups(): lax.all_to_all(mine, 'z', 0, 0, tiled=True).reshape(2, nz // 2, t, width)  24.4 us
  transfers between devices with their start and end apart: 73, of which 29 were waited for; matrix products, arithmetic and copies ran while one was open for 9% of the time, Pallas kernels for 37%

profile of v7, /device:TPU:0, one launch (start us, length us, event | category | flops | bytes accessed | tf_op | source)
XLA Modules:
  0.0 680.3 jit_solution(12981828927307284356)
XLA Ops:
  16.7 12.2 %collective-permute-done.1 = bf16[2,256,512]{2,1,0:T(8,128)(2,1)} collective-permute-done((bf16[2,256,512]{2,1,0:T(8,128)(2,1)}, bf16[2,256,512]{2,1,0:T(8,128)(2,1)}, u32[]{:S(2)}, u32[]{:S(2)}) %collective-permute-start.1) | collective-permute-done | bytes 524320 | tf_op jit(solution)/shard_map/ppermute | solution.py:559
  43.2 51.6 %all-to-all-done = bf16[4,264,512]{2,1,0:T(8,128)(2,1)} async-done(((bf16[4,264,512]{2,1,0:T(8,128)(2,1)}), bf16[4,264,512]{2,1,0:T(8,128)(2,1)}, u32[]{:S(2)}, u32[]{:S(2)}) %all-to-all-start) | async-done | bytes 1081376 | tf_op jit(solution)/shard_map/all_to_all | solution.py:662
  123.5 16.7 %all-to-all-done.1 = bf16[4,256,512]{2,1,0:T(8,128)(2,1)S(1)} async-done(((bf16[4,256,512]{2,1,0:T(8,128)(2,1)}), bf16[4,256,512]{2,1,0:T(8,128)(2,1)S(1)}, u32[]{:S(2)}, u32[]{:S(2)}) %all-to-all-start.1) | async-done | bytes 1048608 | tf_op jit(solution)/shard_map/all_to_all | solution.py:662
  149.0 12.3 %product_nt.2.q_ref.k_ref.v_ref = bf16[1024,1536]{1,0:T(8,128)(2,1)} custom-call(s32[4]{0:T(128)} %add_multiply_fusion.starts_ref, bf16[2,256,512]{2,1,0:T(8,128)(2,1)} %copy-done.10, bf16[2,256,512]{2,1,0:T(8,128)(2,1)} %collective-permute-done.2.refs_1_.refs_3_, bf16[2,256,512]{2,1,0:T(8,128)(2,1)} %collective-permute-done.3.refs_2_.refs_4_, ...), custom_call_target="tpu_custom_call" | custom-call | flops 402653184 | bytes 851968 | tf_op jit(solution)/shard_map/product_nt/pallas_call | solution.py:78
  161.3 16.8 %attend.2 = (bf16[1024,256]{1,0:T(8,128)(2,1)}, f32[8,1024]{1,0:T(8,128)}) custom-call(s32[1]{0:T(128)} %dynamic_slice.51.length_ref, f32[8,32]{1,0:T(8,128)} %constant_dynamic-slice_fusion.4.table_ref, bf16[1024,1536]{1,0:T(8,128)(2,1)} %product_nt.2.q_ref.k_ref.v_ref, bf16[1024,1536]{1,0:T(8,128)(2,1)} %product_nt.2.q_ref.k_ref.v_ref, ...), custom_call_target="tpu_custom_call" | custom-call | flops 268435456 | bytes 131072 | tf_op jit(solution)/shard_map/attend/pallas_call | solution.py:454
  181.0 16.8 %attend.3 = (bf16[1024,256]{1,0:T(8,128)(2,1)}, f32[8,1024]{1,0:T(8,128)}) custom-call(s32[1]{0:T(128)} %dynamic_slice.51.length_ref, f32[8,32]{1,0:T(8,128)} %constant_dynamic-slice_fusion.4.table_ref, bf16[1024,1536]{1,0:T(8,128)(2,1)} %product_nt.2.q_ref.k_ref.v_ref, bf16[1024,1536]{1,0:T(8,128)(2,1)} %product_nt.2.q_ref.k_ref.v_ref, ...), custom_call_target="tpu_custom_call" | custom-call | flops 268435456 | bytes 131072 | tf_op jit(solution)/shard_map/attend/pallas_call | solution.py:454
  206.3 22.8 %collective-permute-done.15 = bf16[2,2,256,512]{3,2,1,0:T(8,128)(2,1)S(1)} collective-permute-done((bf16[2,2,256,512]{3,2,1,0:T(8,128)(2,1)}, bf16[2,2,256,512]{3,2,1,0:T(8,128)(2,1)S(1)}, u32[]{:S(2)}, u32[]{:S(2)}) %collective-permute-start.15) | collective-permute-done | bytes 1048608 | tf_op jit(solution)/shard_map/ppermute | solution.py:559
  232.8 9.3 %collective-permute-done.16 = bf16[2,256,512]{2,1,0:T(8,128)(2,1)S(1)} collective-permute-done((bf16[2,256,512]{2,1,0:T(8,128)(2,1)S(1)}, bf16[2,256,512]{2,1,0:T(8,128)(2,1)S(1)}, u32[]{:S(2)}, u32[]{:S(2)}) %collective-permute-start.16) | collective-permute-done | bytes 524320 | tf_op jit(solution)/shard_map/ppermute | solution.py:559
  250.1 10.8 %collective-permute-done.20.refs_2_.refs_3_ = bf16[2,256,512]{2,1,0:T(8,128)(2,1)S(1)} collective-permute-done((bf16[2,256,512]{2,1,0:T(8,128)(2,1)S(1)}, bf16[2,256,512]{2,1,0:T(8,128)(2,1)S(1)}, u32[]{:S(2)}, u32[]{:S(2)}) %collective-permute-start.20) | collective-permute-done | bytes 524320 | tf_op jit(solution)/shard_map/ppermute | solution.py:559
  262.9 9.5 %collective-permute-done.19.refs_1_.refs_2_ = bf16[2,256,512]{2,1,0:T(8,128)(2,1)S(1)} collective-permute-done((bf16[2,256,512]{2,1,0:T(8,128)(2,1)S(1)}, bf16[2,256,512]{2,1,0:T(8,128)(2,1)S(1)}, u32[]{:S(2)}, u32[]{:S(2)}) %collective-permute-start.19) | collective-permute-done | bytes 524320 | tf_op jit(solution)/shard_map/ppermute | solution.py:559
  280.0 17.6 %ffn_in.1 = (bf16[1024,1280]{1,0:T(8,128)(2,1)}, bf16[1024,1280]{1,0:T(8,128)(2,1)}, bf16[1024,1280]{1,0:T(8,128)(2,1)}) custom-call(s32[4]{0:T(128)} %add_multiply_fusion.starts_ref, bf16[2,256,512]{2,1,0:T(8,128)(2,1)} %copy-done.8, bf16[2,256,512]{2,1,0:T(8,128)(2,1)} %copy-done.18, bf16[2,256,512]{2,1,0:T(8,128)(2,1)} %copy-done.16, ...), custom_call_target="tpu_custom_call" | custom-call | flops 671088640 | bytes 1409024 | tf_op jit(solution)/shard_map/ffn_in/pallas_call | solution.py:214
  297.7 10.0 %product_tn.4 = bf16[4,1280,512]{2,1,0:T(8,128)(2,1)} custom-call(s32[4]{0:T(128)} %add_multiply_fusion.starts_ref, bf16[1024,1280]{1,0:T(8,128)(2,1)} %get-tuple-element.92.refs_0_, bf16[2,256,512]{2,1,0:T(8,128)(2,1)} %copy-done.6, bf16[2,256,512]{2,1,0:T(8,128)(2,1)} %copy-done.15, bf16[2,256,512]{2,1,0:T(8,128)(2,1)} %copy-done.13, ...), custom_call_target="tpu_custom_call" | custom-call | flops 335544320 | bytes 753664 | tf_op jit(solution)/shard_map/product_tn/pallas_call | solution.py:171
  307.7 15.3 %ffn_back.1.refs_0_ = bf16[1024,2560]{1,0:T(8,128)(2,1)} custom-call(s32[4]{0:T(128)} %add_multiply_fusion.starts_ref, bf16[2,256,512]{2,1,0:T(8,128)(2,1)} %copy-done.6, bf16[2,256,512]{2,1,0:T(8,128)(2,1)} %copy-done.15, bf16[2,256,512]{2,1,0:T(8,128)(2,1)} %copy-done.13, bf16[2,256,512]{2,1,0:T(8,128)(2,1)} %collective-permute-done.11.refs_4_.refs_3_, ...), custom_call_target="tpu_custom_call" | custom-call | flops 335544320 | bytes 1245184 | tf_op jit(solution)/shard_map/ffn_back/pallas_call | solution.py:245
  323.0 16.5 %product_nn.5 = (bf16[2,2,256,512]{3,2,1,0:T(8,128)(2,1)}, bf16[2,2,256,512]{3,2,1,0:T(8,128)(2,1)}, bf16[2,2,256,512]{3,2,1,0:T(8,128)(2,1)}, bf16[2,2,256,512]{3,2,1,0:T(8,128)(2,1)}) custom-call(s32[4]{0:T(128)} %add_multiply_fusion.starts_ref, bf16[1024,2560]{1,0:T(8,128)(2,1)} %ffn_back.1.refs_0_, bf16[4,2,1280,512]{3,2,1,0:T(8,128)(2,1)} %bitcast.101), custom_call_target="tpu_custom_call" | custom-call | flops 671088640 | bytes 1245184 | tf_op jit(solution)/shard_map/product_nn/pallas_call | solution.py:123
  342.5 15.9 %product_tn.5 = bf16[4,2560,512]{2,1,0:T(8,128)(2,1)} custom-call(s32[4]{0:T(128)} %add_multiply_fusion.starts_ref, bf16[1024,2560]{1,0:T(8,128)(2,1)} %ffn_back.1.refs_0_, bf16[2,256,512]{2,1,0:T(8,128)(2,1)} %copy-done.8, bf16[2,256,512]{2,1,0:T(8,128)(2,1)} %copy-done.18, bf16[2,256,512]{2,1,0:T(8,128)(2,1)} %copy-done.16, ...), custom_call_target="tpu_custom_call" | custom-call | flops 671088640 | bytes 1245184 | tf_op jit(solution)/shard_map/product_tn/pallas_call | solution.py:171
  373.2 10.2 %product_nn.6 = (bf16[2,2,256,512]{3,2,1,0:T(8,128)(2,1)}, bf16[2,2,256,512]{3,2,1,0:T(8,128)(2,1)}, bf16[2,2,256,512]{3,2,1,0:T(8,128)(2,1)}, bf16[2,2,256,512]{3,2,1,0:T(8,128)(2,1)}) custom-call(s32[4]{0:T(128)} %add_multiply_fusion.starts_ref, bf16[1024,1280]{1,0:T(8,128)(2,1)} %get-tuple-element.92.refs_0_, bf16[4,2,640,512]{3,2,1,0:T(8,128)(2,1)} %bitcast.106), custom_call_target="tpu_custom_call" | custom-call | flops 335544320 | bytes 753664 | tf_op jit(solution)/shard_map/product_nn/pallas_call | solution.py:123
  393.4 10.8 %collective-permute-done.30.refs_2_.refs_4_ = bf16[2,256,512]{2,1,0:T(8,128)(2,1)S(1)} collective-permute-done((bf16[2,256,512]{2,1,0:T(8,128)(2,1)S(1)}, bf16[2,256,512]{2,1,0:T(8,128)(2,1)S(1)}, u32[]{:S(2)}, u32[]{:S(2)}) %collective-permute-start.30) | collective-permute-done | bytes 524320 | tf_op jit(solution)/shard_map/ppermute | solution.py:559
  406.3 10.5 %collective-permute-done.29.refs_1_.refs_3_ = bf16[2,256,512]{2,1,0:T(8,128)(2,1)S(1)} collective-permute-done((bf16[2,256,512]{2,1,0:T(8,128)(2,1)S(1)}, bf16[2,256,512]{2,1,0:T(8,128)(2,1)S(1)}, u32[]{:S(2)}, u32[]{:S(2)}) %collective-permute-start.29) | collective-permute-done | bytes 524320 | tf_op jit(solution)/shard_map/ppermute | solution.py:559
  439.2 28.8 %attend_back.2 = (bf16[1024,768]{1,0:T(8,128)(2,1)}, f32[4,32,128]{2,1,0:T(8,128)}) custom-call(s32[1]{0:T(128)} %dynamic_slice.51.length_ref, f32[8,32]{1,0:T(8,128)} %constant_dynamic-slice_fusion.4.table_ref, bf16[1024,1536]{1,0:T(8,128)(2,1)} %product_nt.2.q_ref.k_ref.v_ref, bf16[1024,1536]{1,0:T(8,128)(2,1)} %product_nt.2.q_ref.k_ref.v_ref, ...), custom_call_target="tpu_custom_call" | custom-call | flops 671088640 | bytes 262144 | tf_op jit(solution)/shard_map/attend_back/pallas_call | solution.py:481
  484.8 28.8 %attend_back.3 = (bf16[1024,768]{1,0:T(8,128)(2,1)}, f32[4,32,128]{2,1,0:T(8,128)}) custom-call(s32[1]{0:T(128)} %dynamic_slice.51.length_ref, f32[8,32]{1,0:T(8,128)} %constant_dynamic-slice_fusion.4.table_ref, bf16[1024,1536]{1,0:T(8,128)(2,1)} %product_nt.2.q_ref.k_ref.v_ref, bf16[1024,1536]{1,0:T(8,128)(2,1)} %product_nt.2.q_ref.k_ref.v_ref, ...), custom_call_target="tpu_custom_call" | custom-call | flops 671088640 | bytes 262144 | tf_op jit(solution)/shard_map/attend_back/pallas_call | solution.py:481
  513.6 11.4 %product_tn.7 = bf16[4,1536,512]{2,1,0:T(8,128)(2,1)} custom-call(s32[4]{0:T(128)} %add_multiply_fusion.starts_ref, bf16[1024,768]{1,0:T(8,128)(2,1)} %get-tuple-element.107.refs_0_, bf16[1024,768]{1,0:T(8,128)(2,1)} %get-tuple-element.110.refs_1_, bf16[2,256,512]{2,1,0:T(8,128)(2,1)} %copy-done.10, ...), custom_call_target="tpu_custom_call" | custom-call | flops 402653184 | bytes 851968 | tf_op jit(solution)/shard_map/product_tn/pallas_call | solution.py:171
  525.1 11.5 %product_nn.7 = (bf16[2,2,256,512]{3,2,1,0:T(8,128)(2,1)}, bf16[2,2,256,512]{3,2,1,0:T(8,128)(2,1)}, bf16[2,2,256,512]{3,2,1,0:T(8,128)(2,1)}, bf16[2,2,256,512]{3,2,1,0:T(8,128)(2,1)}) custom-call(s32[4]{0:T(128)} %add_multiply_fusion.starts_ref, bf16[1024,768]{1,0:T(8,128)(2,1)} %get-tuple-element.107.refs_0_, ...), custom_call_target="tpu_custom_call" | custom-call | flops 402653184 | bytes 851968 | tf_op jit(solution)/shard_map/product_nn/pallas_call | solution.py:123
  546.5 12.3 %collective-permute-done.40 = bf16[2,2,256,512]{3,2,1,0:T(8,128)(2,1)} collective-permute-done((bf16[2,2,256,512]{3,2,1,0:T(8,128)(2,1)}, bf16[2,2,256,512]{3,2,1,0:T(8,128)(2,1)}, u32[]{:S(2)}, u32[]{:S(2)}) %collective-permute-start.40) | collective-permute-done | bytes 1048608 | tf_op jit(solution)/shard_map/ppermute | solution.py:559
  570.4 17.7 %all-to-all-done.2 = bf16[4,256,512]{2,1,0:T(8,128)(2,1)S(1)} async-done(((bf16[4,256,512]{2,1,0:T(8,128)(2,1)}), bf16[4,256,512]{2,1,0:T(8,128)(2,1)S(1)}, u32[]{:S(2)}, u32[]{:S(2)}) %all-to-all-start.2) | async-done | bytes 1048608 | tf_op jit(solution)/shard_map/all_to_all | solution.py:667
  (321 shorter events, 268.7 us)
Async XLA Ops:
  7.2 134.3 %all-gather.4.cloned.1.call-start = ((), (), s32[]{:S(2)}) async-start(), calls=%async_computation.8 | async-start | bytes 9437184 | tf_op jit(solution)/shard_map/all_gather | solution.py:761
  11.6 268.5 %all-gather.6.cloned.1.call-start = ((), (), s32[]{:S(2)}) async-start(), calls=%async_computation.9 | async-start | bytes 11796480 | tf_op jit(solution)/shard_map/all_gather | solution.py:761
  34.3 60.5 %all-to-all-start = ((bf16[4,264,512]{2,1,0:T(8,128)(2,1)}), bf16[4,264,512]{2,1,0:T(8,128)(2,1)}, u32[]{:S(2)}, u32[]{:S(2)}) async-start(bf16[4,264,512]{2,1,0:T(8,128)(2,1)} %pad_maximum_fusion.3), calls=%async_computation | async-start | bytes 2162688 | tf_op jit(solution)/shard_map/all_to_all | solution.py:662
  39.3 268.4 %all-gather.8.cloned.1.call-start = ((), (), s32[]{:S(2)}) async-start(), calls=%async_computation.10 | async-start | bytes 5898240 | tf_op jit(solution)/shard_map/all_gather | solution.py:761
  41.6 53.2 %collective-permute-start.8 = (bf16[2,256,512]{2,1,0:T(8,128)(2,1)S(1)}, bf16[2,256,512]{2,1,0:T(8,128)(2,1)S(1)}, u32[]{:S(2)}, u32[]{:S(2)}) collective-permute-start(bf16[2,256,512]{2,1,0:T(8,128)(2,1)S(1)} %get-tuple-element.149), channel_id=1, source_target_pairs={{0,16},{16,0},{1,17},{17,1},{2,18},{18,2},{3,19},{19,3},{4,20},{20... | collective-permute-start | bytes 1572872 | tf_op jit(solution)/shard_map/ppermute | solution.py:559
  95.9 44.3 %all-to-all-start.1 = ((bf16[4,256,512]{2,1,0:T(8,128)(2,1)}), bf16[4,256,512]{2,1,0:T(8,128)(2,1)S(1)}, u32[]{:S(2)}, u32[]{:S(2)}) async-start(bf16[4,256,512]{2,1,0:T(8,128)(2,1)} %bitcast.26), calls=%async_computation.1 | async-start | bytes 2097152 | tf_op jit(solution)/shard_map/all_to_all | solution.py:662
  101.7 264.3 %reduce-scatter.5.cloned.1.call-start = ((), (), s32[]{:S(2)}) async-start(), calls=%async_computation.11 | async-start | bytes 5898240 | tf_op jit(solution)/shard_map/reduce_scatter | solution.py:802
  142.8 35.3 %collective-permute-start.13 = (bf16[2,256,512]{2,1,0:T(8,128)(2,1)S(1)}, bf16[2,256,512]{2,1,0:T(8,128)(2,1)}, u32[]{:S(2)}, u32[]{:S(2)}) collective-permute-start(bf16[2,256,512]{2,1,0:T(8,128)(2,1)S(1)} %get-tuple-element.146.refs_5_.refs_4_), channel_id=1, source_target_pairs={{0,16},{16,0},{1,17},{17,1},{2,18},{18,2},{3,19},{19,3},{4,20},{20... | collective-permute-start | bytes 1572872 | tf_op jit(solution)/shard_map/ppermute | solution.py:559
  144.4 33.8 %collective-permute-start.10 = (bf16[2,256,512]{2,1,0:T(8,128)(2,1)S(1)}, bf16[2,256,512]{2,1,0:T(8,128)(2,1)S(1)}, u32[]{:S(2)}, u32[]{:S(2)}) collective-permute-start(bf16[2,256,512]{2,1,0:T(8,128)(2,1)S(1)} %get-tuple-element.147.refs_1_.refs_0_), channel_id=1, source_target_pairs={{0,4},{4,0},{1,5},{5,1},{2,6},{6,2},{3,7},{7,3},{8,12},{12,8},{9,1... | collective-permute-start | bytes 1572872 | tf_op jit(solution)/shard_map/ppermute | solution.py:559
  147.9 50.0 %collective-permute-start.12 = (bf16[2,256,512]{2,1,0:T(8,128)(2,1)S(1)}, bf16[2,256,512]{2,1,0:T(8,128)(2,1)S(1)}, u32[]{:S(2)}, u32[]{:S(2)}) collective-permute-start(bf16[2,256,512]{2,1,0:T(8,128)(2,1)S(1)} %get-tuple-element.146.refs_5_.refs_4_), channel_id=1, source_target_pairs={{0,4},{4,0},{1,5},{5,1},{2,6},{6,2},{3,7},{7,3},{8,12},{12,8},{9,1... | collective-permute-start | bytes 1572872 | tf_op jit(solution)/shard_map/ppermute | solution.py:559
  148.4 49.4 %collective-permute-start.9 = (bf16[2,256,512]{2,1,0:T(8,128)(2,1)S(1)}, bf16[2,256,512]{2,1,0:T(8,128)(2,1)S(1)}, u32[]{:S(2)}, u32[]{:S(2)}) collective-permute-start(bf16[2,256,512]{2,1,0:T(8,128)(2,1)S(1)} %get-tuple-element.147.refs_1_.refs_0_), channel_id=1, source_target_pairs={{0,16},{16,0},{1,17},{17,1},{2,18},{18,2},{3,19},{19,3},{4,20},{20... | collective-permute-start | bytes 1572872 | tf_op jit(solution)/shard_map/ppermute | solution.py:559
  307.7 168.8 %reduce-scatter.7.cloned.1.call-start = ((), (), s32[]{:S(2)}) async-start(), calls=%async_computation.12 | async-start | bytes 11796480 | tf_op jit(solution)/shard_map/reduce_scatter | solution.py:802
  366.0 159.1 %reduce-scatter.9.cloned.1.call-start = ((), (), s32[]{:S(2)}) async-start(), calls=%async_computation.13 | async-start | bytes 2359296 | tf_op jit(solution)/shard_map/reduce_scatter | solution.py:802
  423.6 44.3 %collective-permute-start.35 = (bf16[2,2,256,512]{3,2,1,0:T(8,128)(2,1)}, bf16[2,2,256,512]{3,2,1,0:T(8,128)(2,1)}, u32[]{:S(2)}, u32[]{:S(2)}) collective-permute-start(bf16[2,2,256,512]{3,2,1,0:T(8,128)(2,1)} %get-tuple-element.100), channel_id=1, source_target_pairs={{0,4},{4,0},{1,5},{5,1},{2,6},{6,2},{3,7},{7,3},{8,12},{12,8},{9,1... | collective-permute-start | bytes 3145736 | tf_op jit(solution)/shard_map/ppermute | solution.py:559
  424.9 43.0 %collective-permute-start.37 = (bf16[2,2,256,512]{3,2,1,0:T(8,128)(2,1)}, bf16[2,2,256,512]{3,2,1,0:T(8,128)(2,1)}, u32[]{:S(2)}, u32[]{:S(2)}) collective-permute-start(bf16[2,2,256,512]{3,2,1,0:T(8,128)(2,1)} %get-tuple-element.104), channel_id=1, source_target_pairs={{0,16},{16,0},{1,17},{17,1},{2,18},{18,2},{3,19},{19,3},{4,20},{20... | collective-permute-start | bytes 3145736 | tf_op jit(solution)/shard_map/ppermute | solution.py:559
  425.8 42.2 %collective-permute-start.46 = (bf16[640,512]{1,0:T(8,128)(2,1)}, bf16[640,512]{1,0:T(8,128)(2,1)}, u32[]{:S(2)}, u32[]{:S(2)}) collective-permute-start(bf16[640,512]{1,0:T(8,128)(2,1)} %reduce-scatter.5.cloned.1.call-done.refs_0_), channel_id=1, source_target_pairs={{0,16},{16,0},{1,17},{17,1},{2,18},{18,2},{3,19},{19,3},{4,20},{20... | collective-permute-start | bytes 1966088 | tf_op jit(solution)/shard_map/ppermute | solution.py:559
  476.5 149.3 %reduce-scatter.11.cloned.1.call-start = ((), (), s32[]{:S(2)}) async-start(), calls=%async_computation.14 | async-start | bytes 7077888 | tf_op jit(solution)/shard_map/reduce_scatter | solution.py:802
  477.8 47.2 %collective-permute-start.52 = (bf16[1280,512]{1,0:T(8,128)(2,1)S(1)}, bf16[1280,512]{1,0:T(8,128)(2,1)}, u32[]{:S(2)}, u32[]{:S(2)}) collective-permute-start(bf16[1280,512]{1,0:T(8,128)(2,1)S(1)} %copy-done.27), channel_id=1, source_target_pairs={{0,16},{16,0},{1,17},{17,1},{2,18},{18,2},{3,19},{19,3},{4,20},{20... | collective-permute-start | bytes 3932168 | tf_op jit(solution)/shard_map/ppermute | solution.py:559
  480.6 44.4 %collective-permute-start.36 = (bf16[2,256,512]{2,1,0:T(8,128)(2,1)S(1)}, bf16[2,256,512]{2,1,0:T(8,128)(2,1)}, u32[]{:S(2)}, u32[]{:S(2)}) collective-permute-start(bf16[2,256,512]{2,1,0:T(8,128)(2,1)S(1)} %fusion.19), channel_id=1, source_target_pairs={{0,16},{16,0},{1,17},{17,1},{2,18},{18,2},{3,19},{19,3},{4,20},{20... | collective-permute-start | bytes 1572872 | tf_op jit(solution)/shard_map/ppermute | solution.py:559
  483.3 41.7 %collective-permute-start.38 = (bf16[2,256,512]{2,1,0:T(8,128)(2,1)}, bf16[2,256,512]{2,1,0:T(8,128)(2,1)}, u32[]{:S(2)}, u32[]{:S(2)}) collective-permute-start(bf16[2,256,512]{2,1,0:T(8,128)(2,1)} %fusion.20), channel_id=1, source_target_pairs={{0,4},{4,0},{1,5},{5,1},{2,6},{6,2},{3,7},{7,3},{8,12},{12,8},{9,1... | collective-permute-start | bytes 1572872 | tf_op jit(solution)/shard_map/ppermute | solution.py:559
  542.9 45.2 %all-to-all-start.2 = ((bf16[4,256,512]{2,1,0:T(8,128)(2,1)}), bf16[4,256,512]{2,1,0:T(8,128)(2,1)S(1)}, u32[]{:S(2)}, u32[]{:S(2)}) async-start(bf16[4,256,512]{2,1,0:T(8,128)(2,1)} %fusion.13), calls=%async_computation.2 | async-start | bytes 2097152 | tf_op jit(solution)/shard_map/all_to_all | solution.py:667
  596.4 37.2 %all-to-all-start.3 = ((bf16[4,256,512]{2,1,0:T(8,128)(2,1)}), bf16[4,256,512]{2,1,0:T(8,128)(2,1)S(1)}, u32[]{:S(2)}, u32[]{:S(2)}) async-start(bf16[4,256,512]{2,1,0:T(8,128)(2,1)} %fusion.9), calls=%async_computation.3 | async-start | bytes 2097152 | tf_op jit(solution)/shard_map/all_to_all | solution.py:667
  601.9 32.5 %collective-permute-start.59 = (bf16[1280,512]{1,0:T(8,128)(2,1)S(1)}, bf16[1280,512]{1,0:T(8,128)(2,1)}, u32[]{:S(2)}, u32[]{:S(2)}) collective-permute-start(bf16[1280,512]{1,0:T(8,128)(2,1)S(1)} %copy-done.27), channel_id=1, source_target_pairs={{0,8},{8,0},{1,9},{9,1},{2,10},{10,2},{3,11},{11,3},{4,12},{12,4},... | collective-permute-start | bytes 3932168 | tf_op jit(solution)/shard_map/ppermute | solution.py:559
  603.4 40.0 %collective-permute-start.60 = (bf16[1280,512]{1,0:T(8,128)(2,1)}, bf16[1280,512]{1,0:T(8,128)(2,1)}, u32[]{:S(2)}, u32[]{:S(2)}) collective-permute-start(bf16[1280,512]{1,0:T(8,128)(2,1)} %collective-permute-done.52.refs_2_), channel_id=1, source_target_pairs={{0,8},{8,0},{1,9},{9,1},{2,10},{10,2},{3,11},{11,3},{4,12},{12,4},... | collective-permute-start | bytes 3932168 | tf_op jit(solution)/shard_map/ppermute | solution.py:559
  (92 other events, 1482.7 us)
Sparse Core Ops, SparseCore 0:
  11.7 129.7 all-gather.3
  143.7 97.5 all-gather.5
  242.9 54.4 all-gather.7
  307.8 58.1 reduce-scatter.4
  368.7 107.7 reduce-scatter.6
  479.2 33.9 reduce-scatter.8
  525.2 89.3 reduce-scatter.10

commit v8 on v7

--- a/solution.py
+++ b/solution.py
@@ -773,7 +773,13 @@
     w_down = spread(own_down)
     qkv_count, out_count = 3 * heads * 64, heads * 64
 
-    arrived = after(to_groups(stored_in, other, small), own_gate_up, own_down)
+    both_lengths = jnp.stack([lengths, lax.ppermute(lengths, "y", swap)])
+    both_lengths = jnp.where(y == 0, both_lengths, both_lengths[::-1]).reshape(-1)
+    length = lax.dynamic_slice_in_dim(both_lengths, z, 1, 0)
+    slots = (x * 2 + y) * count + jnp.arange(count, dtype=jnp.int32)
+    near_x, near_y = jnp.array([0, 0, 1, 1]) ^ x, jnp.array([0, 1, 0, 1]) ^ y
+    starts = ((near_x * 2 + near_y) * count).astype(jnp.int32)
+    arrived = after(to_groups(stored_in, other, small), own_gate_up, own_down, length, starts)
     tokens = arrived[:, :count].astype(F32)
     small = arrived[:, count:]
     gain_one = small[:, :1].astype(F32)
@@ -782,10 +788,6 @@
     table = table.reshape(-1, buckets).astype(F32)
     table = lax.dynamic_slice_in_dim(table, y * local_heads, local_heads, 0)
 
-    both_lengths = jnp.stack([lengths, lax.ppermute(lengths, "y", swap)])
-    both_lengths = jnp.where(y == 0, both_lengths, both_lengths[::-1]).reshape(-1)
-    length = lax.dynamic_slice_in_dim(both_lengths, z, 1, 0)
-    slots = (x * 2 + y) * count + jnp.arange(count, dtype=jnp.int32)
     live = (slots < length).astype(F32)[None, :, None]
 
     def scale_of(values):
@@ -810,9 +812,6 @@
         forward, backward, gather, scatter = attend_plain, attend_back_plain, gather_plain, scatter_plain
         nt, nn, tn, ffn_one, ffn_two = mm_nt_plain, mm_nn_plain, mm_tn_plain, ffn_in_plain, ffn_back_plain
         shared, stored_from = share_plain, settle_plain
-    near_x, near_y = jnp.array([0, 0, 1, 1]) ^ x, jnp.array([0, 1, 0, 1]) ^ y
-    starts = ((near_x * 2 + near_y) * count).astype(jnp.int32)
-
     def attend_back_all(grad, *last):
         if not fits:
             grads, table_grad = backward(projected, length, table, grad, lse, nc, heads)
@@ -822,7 +821,7 @@
         return (first[0], second[0]), jnp.concatenate([first[1], second[1]])
 
     scale_one = scale_of(tokens)
-    normed, _, _ = gather((tokens * scale_one * gain_one).astype(BF))
+    normed, _, _ = gather((tokens * scale_one * gain_one).astype(BF), table, live)
     cot_other = hop(pick(stored_cot, 1 - y, 1), "y")
     upstream = live * to_groups(stored_cot, after(cot_other, arrived), None).astype(F32)
     upstream_rounded = after(upstream.astype(BF), w_attn)
@@ -866,7 +865,31 @@
     gate_up_pieces, gate_up_last = shared(after(gate_up_part, grad_projected[0]))
     qkv_part = reduce(after(qkv_partial, out_part, *branch_last, gate_up_last))
     one_parts = nn(grad_projected, w_attn, 0, qkv_count, starts)
-    grad_one, _, one_last = scatter(one_parts, (), (outputs[0],))
+    if fits:
+        here = jnp.stack([y, c]).astype(jnp.int32)
+
+        def write_rows(source, outs):
+            outs[0][...] = source[...].astype(F32)
+
+        def write_qkv(source, outs):
+            for h in range(heads):
+                for i in range(3):
+                    value = source[(i * heads + h) * 64 : (i * heads + h + 1) * 64, :].astype(F32)
+                    if i == 2:
+                        outs[1][h] = value
+                    else:
+                        outs[0][h, i] = value
+
+        def write_gate_up(source, outs):
+            for u in range(units):
+                for i in range(2):
+                    first = (i * units + u) * unit
+                    outs[0][u, i] = source[first : first + unit, :].astype(F32)
+
+        (down_all,) = place(down_pieces, here, [(units * unit, width)], write_rows)
+        (gate_up_all,) = place(gate_up_pieces, here, [(units, 2, unit, width)], write_gate_up)
+    beside = (outputs[0], down_all, gate_up_all) if fits else ()
+    grad_one, _, one_last = scatter(one_parts, (), beside)
     through, attn_gain_part = norm_back(tokens, scale_one, gain_one, grad_one)
     input_grad, input_leaves = from_groups((grad_hidden + through).astype(BF))
 
@@ -882,32 +905,11 @@
     attn_gain_grad, ffn_gain_grad = all_sums[:nz], all_sums[nz : 2 * nz]
     every = all_sums[2 * nz :].reshape(-1)[: nx * 2 * local_heads * buckets].reshape(-1, buckets)
 
+    other_half = outputs[1]
     outputs = stored_from(outputs, BF)
     if fits:
-        here = jnp.stack([y, c]).astype(jnp.int32)
-
-        def write_rows(source, outs):
-            outs[0][...] = source[...].astype(F32)
-
-        def write_qkv(source, outs):
-            for h in range(heads):
-                for i in range(3):
-                    value = source[(i * heads + h) * 64 : (i * heads + h + 1) * 64, :].astype(F32)
-                    if i == 2:
-                        outs[1][h] = value
-                    else:
-                        outs[0][h, i] = value
-
-        def write_gate_up(source, outs):
-            for u in range(units):
-                for i in range(2):
-                    first = (i * units + u) * unit
-                    outs[0][u, i] = source[first : first + unit, :].astype(F32)
-
-        (down_all,) = place(down_pieces, here, [(units * unit, width)], write_rows)
         (out_all,) = place(out_pieces, here, [(heads * 64, width)], write_rows)
-        (gate_up_all,) = place(gate_up_pieces, here, [(units, 2, unit, width)], write_gate_up)
-        qkv_pieces, _ = shared(after(qkv_part, sums, *one_last), down_all, out_all, gate_up_all, outputs)
+        qkv_pieces, _ = shared(after(qkv_part, out_last, other_half, *one_last), out_all, outputs, sums)
         query_key_all, value_all = place(
             qkv_pieces, here, [(heads, 2, 64, width), (heads, 64, width)], write_qkv
         )

time: 686 us -> 689 us (level)
  starting transfers between devices: 84.7 us -> 104 us
  waiting for transfers between devices: 257 us -> 240 us
    all_to_all x2, waiting for transfers between devices: 24.4 us -> 11.9 us  [from_groups(): lax.all_to_all(mine, 'z', 0, 0, tiled=True).reshape(2, nz // 2, t, width)]
    ppermute x2, starting transfers between devices: 7.54 us -> 19 us  [sum_line(): value = value + lax.ppermute(value, 'z', [(i, i ^ step) for i in range(nz)])]
    ppermute x1, waiting for transfers between devices: 8.6 us -> 0.01 us  [body(): both_lengths = jnp.stack([lengths, lax.ppermute(lengths, 'y', swap)])]
    ppermute x59, starting transfers between devices: 57.8 us -> 64.8 us  [hop(): return lax.ppermute(value, axis, swap)]
  transfers between devices with their start and end apart: 73 -> 73, of which waited for: 29 -> 27; matrix products, arithmetic and copies ran while one was open for 9% -> 8% of each run, Pallas kernels for 37% -> 37%
where the time goes in v8:
time: 689 us; the launch traced here: 682 us
  Pallas kernels  256 us (37%)
  waiting for transfers between devices  240 us (35%)
  starting transfers between devices  104 us (15%)
  other arithmetic  47.3 us (7%)
  local copies, waits for them, and re-layouts  18.2 us (3%)
  between operations  15.4 us (2%)
    ppermute x59, waiting for transfers between devices, hop(): return lax.ppermute(value, axis, swap)  143 us
    all_to_all x2, waiting for transfers between devices, to_groups(): return lax.all_to_all(both, 'z', 0, 0, tiled=True)  66.1 us
    ppermute x59, starting transfers between devices, hop(): return lax.ppermute(value, axis, swap)  64.8 us
    pallas_call x2, Pallas kernels, attend_back(): pl.pallas_call(functools.partial(attend_back_kernel, group), grid=(1,), i...  57.6 us
    pallas_call x4, Pallas kernels, mm_nn(): pl.pallas_call(functools.partial(nn_kernel, len(grads)), grid=(nz,), in_s...  45 us
    pallas_call x4, Pallas kernels, mm_tn(): pl.pallas_call(functools.partial(tn_kernel, count), grid=(count * steps,)...  43.4 us
    pallas_call x2, Pallas kernels, attend(): pl.pallas_call(functools.partial(attend_kernel, group), grid=(1,), in_spe...  33.6 us
    pallas_call x4, Pallas kernels, place(): pl.pallas_call(functools.partial(place_kernel, write), grid=(4,), in_spec...  19.4 us
  transfers between devices with their start and end apart: 73, of which 27 were waited for; matrix products, arithmetic and copies ran while one was open for 8% of the time, Pallas kernels for 37%

profile of v8, /device:TPU:0, one launch (start us, length us, event | category | flops | bytes accessed | tf_op | source)
XLA Modules:
  0.0 682.0 jit_solution(1471865447817093882)
XLA Ops:
  16.7 12.2 %collective-permute-done.1 = bf16[2,256,512]{2,1,0:T(8,128)(2,1)} collective-permute-done((bf16[2,256,512]{2,1,0:T(8,128)(2,1)}, bf16[2,256,512]{2,1,0:T(8,128)(2,1)}, u32[]{:S(2)}, u32[]{:S(2)}) %collective-permute-start.1) | collective-permute-done | bytes 524320 | tf_op jit(solution)/shard_map/ppermute | solution.py:559
  45.2 49.8 %all-to-all-done = bf16[4,264,512]{2,1,0:T(8,128)(2,1)} async-done(((bf16[4,264,512]{2,1,0:T(8,128)(2,1)}), bf16[4,264,512]{2,1,0:T(8,128)(2,1)}, u32[]{:S(2)}, u32[]{:S(2)}) %all-to-all-start) | async-done | bytes 1081376 | tf_op jit(solution)/shard_map/all_to_all | solution.py:662
  123.9 16.3 %all-to-all-done.1 = bf16[4,256,512]{2,1,0:T(8,128)(2,1)S(1)} async-done(((bf16[4,256,512]{2,1,0:T(8,128)(2,1)}), bf16[4,256,512]{2,1,0:T(8,128)(2,1)S(1)}, u32[]{:S(2)}, u32[]{:S(2)}) %all-to-all-start.1) | async-done | bytes 1048608 | tf_op jit(solution)/shard_map/all_to_all | solution.py:662
  146.9 12.3 %product_nt.2.q_ref.k_ref.v_ref = bf16[1024,1536]{1,0:T(8,128)(2,1)} custom-call(s32[4]{0:T(128)} %add_multiply_fusion.starts_ref, bf16[2,256,512]{2,1,0:T(8,128)(2,1)} %copy-done.10, bf16[2,256,512]{2,1,0:T(8,128)(2,1)} %collective-permute-done.2.refs_1_.refs_3_, bf16[2,256,512]{2,1,0:T(8,128)(2,1)} %collective-permute-done.3.refs_2_.refs_4_, ...), custom_call_target="tpu_custom_call" | custom-call | flops 402653184 | bytes 851968 | tf_op jit(solution)/shard_map/product_nt/pallas_call | solution.py:78
  159.2 16.8 %attend.2 = (bf16[1024,256]{1,0:T(8,128)(2,1)}, f32[8,1024]{1,0:T(8,128)}) custom-call(s32[1]{0:T(128)} %dynamic_slice.51.length_ref, f32[8,32]{1,0:T(8,128)} %constant_dynamic-slice_fusion.4.table_ref, bf16[1024,1536]{1,0:T(8,128)(2,1)} %product_nt.2.q_ref.k_ref.v_ref, bf16[1024,1536]{1,0:T(8,128)(2,1)} %product_nt.2.q_ref.k_ref.v_ref, ...), custom_call_target="tpu_custom_call" | custom-call | flops 268435456 | bytes 131072 | tf_op jit(solution)/shard_map/attend/pallas_call | solution.py:454
  179.0 16.8 %attend.3 = (bf16[1024,256]{1,0:T(8,128)(2,1)}, f32[8,1024]{1,0:T(8,128)}) custom-call(s32[1]{0:T(128)} %dynamic_slice.51.length_ref, f32[8,32]{1,0:T(8,128)} %constant_dynamic-slice_fusion.4.table_ref, bf16[1024,1536]{1,0:T(8,128)(2,1)} %product_nt.2.q_ref.k_ref.v_ref, bf16[1024,1536]{1,0:T(8,128)(2,1)} %product_nt.2.q_ref.k_ref.v_ref, ...), custom_call_target="tpu_custom_call" | custom-call | flops 268435456 | bytes 131072 | tf_op jit(solution)/shard_map/attend/pallas_call | solution.py:454
  203.9 22.5 %collective-permute-done.15 = bf16[2,2,256,512]{3,2,1,0:T(8,128)(2,1)S(1)} collective-permute-done((bf16[2,2,256,512]{3,2,1,0:T(8,128)(2,1)}, bf16[2,2,256,512]{3,2,1,0:T(8,128)(2,1)S(1)}, u32[]{:S(2)}, u32[]{:S(2)}) %collective-permute-start.15) | collective-permute-done | bytes 1048608 | tf_op jit(solution)/shard_map/ppermute | solution.py:559
  246.8 10.8 %collective-permute-done.20.refs_2_.refs_3_ = bf16[2,256,512]{2,1,0:T(8,128)(2,1)S(1)} collective-permute-done((bf16[2,256,512]{2,1,0:T(8,128)(2,1)S(1)}, bf16[2,256,512]{2,1,0:T(8,128)(2,1)S(1)}, u32[]{:S(2)}, u32[]{:S(2)}) %collective-permute-start.20) | collective-permute-done | bytes 524320 | tf_op jit(solution)/shard_map/ppermute | solution.py:559
  259.7 10.0 %collective-permute-done.19.refs_1_.refs_2_ = bf16[2,256,512]{2,1,0:T(8,128)(2,1)S(1)} collective-permute-done((bf16[2,256,512]{2,1,0:T(8,128)(2,1)S(1)}, bf16[2,256,512]{2,1,0:T(8,128)(2,1)S(1)}, u32[]{:S(2)}, u32[]{:S(2)}) %collective-permute-start.19) | collective-permute-done | bytes 524320 | tf_op jit(solution)/shard_map/ppermute | solution.py:559
  276.9 17.6 %ffn_in.1 = (bf16[1024,1280]{1,0:T(8,128)(2,1)}, bf16[1024,1280]{1,0:T(8,128)(2,1)}, bf16[1024,1280]{1,0:T(8,128)(2,1)}) custom-call(s32[4]{0:T(128)} %add_multiply_fusion.starts_ref, bf16[2,256,512]{2,1,0:T(8,128)(2,1)} %copy-done.8, bf16[2,256,512]{2,1,0:T(8,128)(2,1)} %copy-done.18, bf16[2,256,512]{2,1,0:T(8,128)(2,1)} %copy-done.16, ...), custom_call_target="tpu_custom_call" | custom-call | flops 671088640 | bytes 1409024 | tf_op jit(solution)/shard_map/ffn_in/pallas_call | solution.py:214
  304.5 15.2 %ffn_back.1.refs_0_ = bf16[1024,2560]{1,0:T(8,128)(2,1)} custom-call(s32[4]{0:T(128)} %add_multiply_fusion.starts_ref, bf16[2,256,512]{2,1,0:T(8,128)(2,1)} %copy-done.6, bf16[2,256,512]{2,1,0:T(8,128)(2,1)} %collective-permute-done.9.refs_2_.refs_1_, bf16[2,256,512]{2,1,0:T(8,128)(2,1)} %copy-done.14, ...), custom_call_target="tpu_custom_call" | custom-call | flops 335544320 | bytes 1245184 | tf_op jit(solution)/shard_map/ffn_back/pallas_call | solution.py:245
  319.7 16.5 %product_nn.5 = (bf16[2,2,256,512]{3,2,1,0:T(8,128)(2,1)}, bf16[2,2,256,512]{3,2,1,0:T(8,128)(2,1)}, bf16[2,2,256,512]{3,2,1,0:T(8,128)(2,1)}, bf16[2,2,256,512]{3,2,1,0:T(8,128)(2,1)}) custom-call(s32[4]{0:T(128)} %add_multiply_fusion.starts_ref, bf16[1024,2560]{1,0:T(8,128)(2,1)} %ffn_back.1.refs_0_, bf16[4,2,1280,512]{3,2,1,0:T(8,128)(2,1)} %bitcast.101), custom_call_target="tpu_custom_call" | custom-call | flops 671088640 | bytes 1245184 | tf_op jit(solution)/shard_map/product_nn/pallas_call | solution.py:123
  338.8 15.9 %product_tn.5 = bf16[4,2560,512]{2,1,0:T(8,128)(2,1)} custom-call(s32[4]{0:T(128)} %add_multiply_fusion.starts_ref, bf16[1024,2560]{1,0:T(8,128)(2,1)} %ffn_back.1.refs_0_, bf16[2,256,512]{2,1,0:T(8,128)(2,1)} %copy-done.8, bf16[2,256,512]{2,1,0:T(8,128)(2,1)} %copy-done.18, bf16[2,256,512]{2,1,0:T(8,128)(2,1)} %copy-done.16, ...), custom_call_target="tpu_custom_call" | custom-call | flops 671088640 | bytes 1245184 | tf_op jit(solution)/shard_map/product_tn/pallas_call | solution.py:171
  369.7 10.2 %product_nn.6 = (bf16[2,2,256,512]{3,2,1,0:T(8,128)(2,1)}, bf16[2,2,256,512]{3,2,1,0:T(8,128)(2,1)}, bf16[2,2,256,512]{3,2,1,0:T(8,128)(2,1)}, bf16[2,2,256,512]{3,2,1,0:T(8,128)(2,1)}) custom-call(s32[4]{0:T(128)} %add_multiply_fusion.starts_ref, bf16[1024,1280]{1,0:T(8,128)(2,1)} %get-tuple-element.96.refs_0_, bf16[4,2,640,512]{3,2,1,0:T(8,128)(2,1)} %bitcast.106), custom_call_target="tpu_custom_call" | custom-call | flops 335544320 | bytes 753664 | tf_op jit(solution)/shard_map/product_nn/pallas_call | solution.py:123
  389.9 10.8 %collective-permute-done.30.refs_2_.refs_4_ = bf16[2,256,512]{2,1,0:T(8,128)(2,1)S(1)} collective-permute-done((bf16[2,256,512]{2,1,0:T(8,128)(2,1)S(1)}, bf16[2,256,512]{2,1,0:T(8,128)(2,1)S(1)}, u32[]{:S(2)}, u32[]{:S(2)}) %collective-permute-start.30) | collective-permute-done | bytes 524320 | tf_op jit(solution)/shard_map/ppermute | solution.py:559
  402.7 10.5 %collective-permute-done.29.refs_1_.refs_3_ = bf16[2,256,512]{2,1,0:T(8,128)(2,1)S(1)} collective-permute-done((bf16[2,256,512]{2,1,0:T(8,128)(2,1)S(1)}, bf16[2,256,512]{2,1,0:T(8,128)(2,1)S(1)}, u32[]{:S(2)}, u32[]{:S(2)}) %collective-permute-start.29) | collective-permute-done | bytes 524320 | tf_op jit(solution)/shard_map/ppermute | solution.py:559
  435.6 28.8 %attend_back.2 = (bf16[1024,768]{1,0:T(8,128)(2,1)}, f32[4,32,128]{2,1,0:T(8,128)}) custom-call(s32[1]{0:T(128)} %dynamic_slice.51.length_ref, f32[8,32]{1,0:T(8,128)} %constant_dynamic-slice_fusion.4.table_ref, bf16[1024,1536]{1,0:T(8,128)(2,1)} %product_nt.2.q_ref.k_ref.v_ref, bf16[1024,1536]{1,0:T(8,128)(2,1)} %product_nt.2.q_ref.k_ref.v_ref, ...), custom_call_target="tpu_custom_call" | custom-call | flops 671088640 | bytes 262144 | tf_op jit(solution)/shard_map/attend_back/pallas_call | solution.py:481
  481.4 28.8 %attend_back.3 = (bf16[1024,768]{1,0:T(8,128)(2,1)}, f32[4,32,128]{2,1,0:T(8,128)}) custom-call(s32[1]{0:T(128)} %dynamic_slice.51.length_ref, f32[8,32]{1,0:T(8,128)} %constant_dynamic-slice_fusion.4.table_ref, bf16[1024,1536]{1,0:T(8,128)(2,1)} %product_nt.2.q_ref.k_ref.v_ref, bf16[1024,1536]{1,0:T(8,128)(2,1)} %product_nt.2.q_ref.k_ref.v_ref, ...), custom_call_target="tpu_custom_call" | custom-call | flops 671088640 | bytes 262144 | tf_op jit(solution)/shard_map/attend_back/pallas_call | solution.py:481
  510.2 11.4 %product_tn.7 = bf16[4,1536,512]{2,1,0:T(8,128)(2,1)} custom-call(s32[4]{0:T(128)} %add_multiply_fusion.starts_ref, bf16[1024,768]{1,0:T(8,128)(2,1)} %get-tuple-element.111.refs_0_, bf16[1024,768]{1,0:T(8,128)(2,1)} %get-tuple-element.114.refs_1_, bf16[2,256,512]{2,1,0:T(8,128)(2,1)} %copy-done.10, ...), custom_call_target="tpu_custom_call" | custom-call | flops 402653184 | bytes 851968 | tf_op jit(solution)/shard_map/product_tn/pallas_call | solution.py:171
  521.7 11.5 %product_nn.7 = (bf16[2,2,256,512]{3,2,1,0:T(8,128)(2,1)}, bf16[2,2,256,512]{3,2,1,0:T(8,128)(2,1)}, bf16[2,2,256,512]{3,2,1,0:T(8,128)(2,1)}, bf16[2,2,256,512]{3,2,1,0:T(8,128)(2,1)}) custom-call(s32[4]{0:T(128)} %add_multiply_fusion.starts_ref, bf16[1024,768]{1,0:T(8,128)(2,1)} %get-tuple-element.111.refs_0_, ...), custom_call_target="tpu_custom_call" | custom-call | flops 402653184 | bytes 851968 | tf_op jit(solution)/shard_map/product_nn/pallas_call | solution.py:123
  543.8 11.5 %collective-permute-done.40 = bf16[2,2,256,512]{3,2,1,0:T(8,128)(2,1)} collective-permute-done((bf16[2,2,256,512]{3,2,1,0:T(8,128)(2,1)}, bf16[2,2,256,512]{3,2,1,0:T(8,128)(2,1)}, u32[]{:S(2)}, u32[]{:S(2)}) %collective-permute-start.40) | collective-permute-done | bytes 1048608 | tf_op jit(solution)/shard_map/ppermute | solution.py:559
  572.7 11.9 %all-to-all-done.2 = bf16[4,256,512]{2,1,0:T(8,128)(2,1)S(1)} async-done(((bf16[4,256,512]{2,1,0:T(8,128)(2,1)}), bf16[4,256,512]{2,1,0:T(8,128)(2,1)S(1)}, u32[]{:S(2)}, u32[]{:S(2)}) %all-to-all-start.2) | async-done | bytes 1048608 | tf_op jit(solution)/shard_map/all_to_all | solution.py:667
  599.1 11.1 %collective-permute-done.39.other_ref = bf16[2,256,512]{2,1,0:T(8,128)(2,1)S(1)} collective-permute-done((bf16[2,256,512]{2,1,0:T(8,128)(2,1)S(1)}, bf16[2,256,512]{2,1,0:T(8,128)(2,1)S(1)}, u32[]{:S(2)}, u32[]{:S(2)}) %collective-permute-start.39) | collective-permute-done | bytes 524320 | tf_op jit(solution)/shard_map/ppermute | solution.py:559
  640.5 17.6 %collective-permute-start.55 = (f32[10,512]{1,0:T(8,128)S(1)}, f32[10,512]{1,0:T(8,128)S(1)}, u32[]{:S(2)}, u32[]{:S(2)}) collective-permute-start(f32[10,512]{1,0:T(8,128)S(1)} %add.284), channel_id=1, source_target_pairs={{0,1},{1,0},{2,3},{3,2},{4,5},{5,4},{6,7},{7,6},{8,9},{9,8},{10,11... | collective-permute-start | bytes 61448 | tf_op jit(solution)/shard_map/ppermute | solution.py:721
  (331 shorter events, 270.0 us)
Async XLA Ops:
  7.2 134.3 %all-gather.4.cloned.1.call-start = ((), (), s32[]{:S(2)}) async-start(), calls=%async_computation.8 | async-start | bytes 9437184 | tf_op jit(solution)/shard_map/all_gather | solution.py:761
  11.6 265.3 %all-gather.6.cloned.1.call-start = ((), (), s32[]{:S(2)}) async-start(), calls=%async_computation.9 | async-start | bytes 11796480 | tf_op jit(solution)/shard_map/all_gather | solution.py:761
  34.3 60.7 %all-to-all-start = ((bf16[4,264,512]{2,1,0:T(8,128)(2,1)}), bf16[4,264,512]{2,1,0:T(8,128)(2,1)}, u32[]{:S(2)}, u32[]{:S(2)}) async-start(bf16[4,264,512]{2,1,0:T(8,128)(2,1)} %pad_maximum_fusion.3), calls=%async_computation | async-start | bytes 2162688 | tf_op jit(solution)/shard_map/all_to_all | solution.py:662
  39.5 265.0 %all-gather.8.cloned.1.call-start = ((), (), s32[]{:S(2)}) async-start(), calls=%async_computation.10 | async-start | bytes 5898240 | tf_op jit(solution)/shard_map/all_gather | solution.py:761
  43.3 51.6 %collective-permute-start.8 = (bf16[2,256,512]{2,1,0:T(8,128)(2,1)S(1)}, bf16[2,256,512]{2,1,0:T(8,128)(2,1)S(1)}, u32[]{:S(2)}, u32[]{:S(2)}) collective-permute-start(bf16[2,256,512]{2,1,0:T(8,128)(2,1)S(1)} %get-tuple-element.153), channel_id=1, source_target_pairs={{0,16},{16,0},{1,17},{17,1},{2,18},{18,2},{3,19},{19,3},{4,20},{20... | collective-permute-start | bytes 1572872 | tf_op jit(solution)/shard_map/ppermute | solution.py:559
  96.1 44.1 %all-to-all-start.1 = ((bf16[4,256,512]{2,1,0:T(8,128)(2,1)}), bf16[4,256,512]{2,1,0:T(8,128)(2,1)S(1)}, u32[]{:S(2)}, u32[]{:S(2)}) async-start(bf16[4,256,512]{2,1,0:T(8,128)(2,1)} %bitcast.26), calls=%async_computation.1 | async-start | bytes 2097152 | tf_op jit(solution)/shard_map/all_to_all | solution.py:662
  101.8 260.7 %reduce-scatter.5.cloned.1.call-start = ((), (), s32[]{:S(2)}) async-start(), calls=%async_computation.11 | async-start | bytes 5898240 | tf_op jit(solution)/shard_map/reduce_scatter | solution.py:804
  109.6 34.8 %collective-permute-start.2 = (bf16[2,256,512]{2,1,0:T(8,128)(2,1)S(1)}, bf16[2,256,512]{2,1,0:T(8,128)(2,1)}, u32[]{:S(2)}, u32[]{:S(2)}) collective-permute-start(bf16[2,256,512]{2,1,0:T(8,128)(2,1)S(1)} %get-tuple-element.155.refs_0_.refs_2_), channel_id=1, source_target_pairs={{0,16},{16,0},{1,17},{17,1},{2,18},{18,2},{3,19},{19,3},{4,20},{20... | collective-permute-start | bytes 1572872 | tf_op jit(solution)/shard_map/ppermute | solution.py:559
  110.1 35.6 %collective-permute-start.6 = (bf16[2,256,512]{2,1,0:T(8,128)(2,1)S(1)}, bf16[2,256,512]{2,1,0:T(8,128)(2,1)}, u32[]{:S(2)}, u32[]{:S(2)}) collective-permute-start(bf16[2,256,512]{2,1,0:T(8,128)(2,1)S(1)} %get-tuple-element.154.refs_4_.refs_6_), channel_id=1, source_target_pairs={{0,4},{4,0},{1,5},{5,1},{2,6},{6,2},{3,7},{7,3},{8,12},{12,8},{9,1... | collective-permute-start | bytes 1572872 | tf_op jit(solution)/shard_map/ppermute | solution.py:559
  142.8 33.2 %collective-permute-start.13 = (bf16[2,256,512]{2,1,0:T(8,128)(2,1)S(1)}, bf16[2,256,512]{2,1,0:T(8,128)(2,1)S(1)}, u32[]{:S(2)}, u32[]{:S(2)}) collective-permute-start(bf16[2,256,512]{2,1,0:T(8,128)(2,1)S(1)} %get-tuple-element.150.refs_5_.refs_4_), channel_id=1, source_target_pairs={{0,16},{16,0},{1,17},{17,1},{2,18},{18,2},{3,19},{19,3},{4,20},{20... | collective-permute-start | bytes 1572872 | tf_op jit(solution)/shard_map/ppermute | solution.py:559
  145.8 50.0 %collective-permute-start.12 = (bf16[2,256,512]{2,1,0:T(8,128)(2,1)S(1)}, bf16[2,256,512]{2,1,0:T(8,128)(2,1)S(1)}, u32[]{:S(2)}, u32[]{:S(2)}) collective-permute-start(bf16[2,256,512]{2,1,0:T(8,128)(2,1)S(1)} %get-tuple-element.150.refs_5_.refs_4_), channel_id=1, source_target_pairs={{0,4},{4,0},{1,5},{5,1},{2,6},{6,2},{3,7},{7,3},{8,12},{12,8},{9,1... | collective-permute-start | bytes 1572872 | tf_op jit(solution)/shard_map/ppermute | solution.py:559
  146.3 49.5 %collective-permute-start.9 = (bf16[2,256,512]{2,1,0:T(8,128)(2,1)S(1)}, bf16[2,256,512]{2,1,0:T(8,128)(2,1)}, u32[]{:S(2)}, u32[]{:S(2)}) collective-permute-start(bf16[2,256,512]{2,1,0:T(8,128)(2,1)S(1)} %get-tuple-element.151.refs_1_.refs_0_), channel_id=1, source_target_pairs={{0,16},{16,0},{1,17},{17,1},{2,18},{18,2},{3,19},{19,3},{4,20},{20... | collective-permute-start | bytes 1572872 | tf_op jit(solution)/shard_map/ppermute | solution.py:559
  304.4 168.5 %reduce-scatter.7.cloned.1.call-start = ((), (), s32[]{:S(2)}) async-start(), calls=%async_computation.12 | async-start | bytes 11796480 | tf_op jit(solution)/shard_map/reduce_scatter | solution.py:804
  362.4 159.2 %reduce-scatter.9.cloned.1.call-start = ((), (), s32[]{:S(2)}) async-start(), calls=%async_computation.13 | async-start | bytes 2359296 | tf_op jit(solution)/shard_map/reduce_scatter | solution.py:804
  420.1 44.3 %collective-permute-start.35 = (bf16[2,2,256,512]{3,2,1,0:T(8,128)(2,1)}, bf16[2,2,256,512]{3,2,1,0:T(8,128)(2,1)}, u32[]{:S(2)}, u32[]{:S(2)}) collective-permute-start(bf16[2,2,256,512]{3,2,1,0:T(8,128)(2,1)} %get-tuple-element.104), channel_id=1, source_target_pairs={{0,4},{4,0},{1,5},{5,1},{2,6},{6,2},{3,7},{7,3},{8,12},{12,8},{9,1... | collective-permute-start | bytes 3145736 | tf_op jit(solution)/shard_map/ppermute | solution.py:559
  421.3 43.0 %collective-permute-start.37 = (bf16[2,2,256,512]{3,2,1,0:T(8,128)(2,1)}, bf16[2,2,256,512]{3,2,1,0:T(8,128)(2,1)}, u32[]{:S(2)}, u32[]{:S(2)}) collective-permute-start(bf16[2,2,256,512]{3,2,1,0:T(8,128)(2,1)} %get-tuple-element.108), channel_id=1, source_target_pairs={{0,16},{16,0},{1,17},{17,1},{2,18},{18,2},{3,19},{19,3},{4,20},{20... | collective-permute-start | bytes 3145736 | tf_op jit(solution)/shard_map/ppermute | solution.py:559
  422.3 42.1 %collective-permute-start.43 = (bf16[640,512]{1,0:T(8,128)(2,1)}, bf16[640,512]{1,0:T(8,128)(2,1)}, u32[]{:S(2)}, u32[]{:S(2)}) collective-permute-start(bf16[640,512]{1,0:T(8,128)(2,1)} %reduce-scatter.5.cloned.1.call-done.refs_0_), channel_id=1, source_target_pairs={{0,16},{16,0},{1,17},{17,1},{2,18},{18,2},{3,19},{19,3},{4,20},{20... | collective-permute-start | bytes 1966088 | tf_op jit(solution)/shard_map/ppermute | solution.py:559
  473.0 140.0 %reduce-scatter.11.cloned.1.call-start = ((), (), s32[]{:S(2)}) async-start(), calls=%async_computation.14 | async-start | bytes 7077888 | tf_op jit(solution)/shard_map/reduce_scatter | solution.py:804
  474.3 47.4 %collective-permute-start.46 = (bf16[1280,512]{1,0:T(8,128)(2,1)S(1)}, bf16[1280,512]{1,0:T(8,128)(2,1)}, u32[]{:S(2)}, u32[]{:S(2)}) collective-permute-start(bf16[1280,512]{1,0:T(8,128)(2,1)S(1)} %copy-done.27), channel_id=1, source_target_pairs={{0,16},{16,0},{1,17},{17,1},{2,18},{18,2},{3,19},{19,3},{4,20},{20... | collective-permute-start | bytes 3932168 | tf_op jit(solution)/shard_map/ppermute | solution.py:559
  477.1 44.5 %collective-permute-start.36 = (bf16[2,256,512]{2,1,0:T(8,128)(2,1)S(1)}, bf16[2,256,512]{2,1,0:T(8,128)(2,1)}, u32[]{:S(2)}, u32[]{:S(2)}) collective-permute-start(bf16[2,256,512]{2,1,0:T(8,128)(2,1)S(1)} %fusion.19), channel_id=1, source_target_pairs={{0,16},{16,0},{1,17},{17,1},{2,18},{18,2},{3,19},{19,3},{4,20},{20... | collective-permute-start | bytes 1572872 | tf_op jit(solution)/shard_map/ppermute | solution.py:559
  479.8 41.8 %collective-permute-start.38 = (bf16[2,256,512]{2,1,0:T(8,128)(2,1)}, bf16[2,256,512]{2,1,0:T(8,128)(2,1)}, u32[]{:S(2)}, u32[]{:S(2)}) collective-permute-start(bf16[2,256,512]{2,1,0:T(8,128)(2,1)} %fusion.20), channel_id=1, source_target_pairs={{0,4},{4,0},{1,5},{5,1},{2,6},{6,2},{3,7},{7,3},{8,12},{12,8},{9,1... | collective-permute-start | bytes 1572872 | tf_op jit(solution)/shard_map/ppermute | solution.py:559
  539.4 45.2 %all-to-all-start.2 = ((bf16[4,256,512]{2,1,0:T(8,128)(2,1)}), bf16[4,256,512]{2,1,0:T(8,128)(2,1)S(1)}, u32[]{:S(2)}, u32[]{:S(2)}) async-start(bf16[4,256,512]{2,1,0:T(8,128)(2,1)} %fusion.13), calls=%async_computation.2 | async-start | bytes 2097152 | tf_op jit(solution)/shard_map/all_to_all | solution.py:667
  592.7 46.0 %all-to-all-start.3 = ((bf16[4,256,512]{2,1,0:T(8,128)(2,1)}), bf16[4,256,512]{2,1,0:T(8,128)(2,1)S(1)}, u32[]{:S(2)}, u32[]{:S(2)}) async-start(bf16[4,256,512]{2,1,0:T(8,128)(2,1)} %fusion.9), calls=%async_computation.5 | async-start | bytes 2097152 | tf_op jit(solution)/shard_map/all_to_all | solution.py:667
  635.2 34.6 %collective-permute-start.57 = (bf16[768,512]{1,0:T(8,128)(2,1)S(1)}, bf16[768,512]{1,0:T(8,128)(2,1)}, u32[]{:S(2)}, u32[]{:S(2)}) collective-permute-start(bf16[768,512]{1,0:T(8,128)(2,1)S(1)} %copy-done.34), channel_id=1, source_target_pairs={{0,8},{8,0},{1,9},{9,1},{2,10},{10,2},{3,11},{11,3},{4,12},{12,4},... | collective-permute-start | bytes 2359304 | tf_op jit(solution)/shard_map/ppermute | solution.py:559
  (97 other events, 1491.3 us)
Sparse Core Ops, SparseCore 0:
  11.7 129.7 all-gather.3
  143.7 97.5 all-gather.5
  242.9 54.4 all-gather.7
  304.6 57.8 reduce-scatter.4
  365.1 107.7 reduce-scatter.6
  475.7 33.9 reduce-scatter.8
  521.8 89.3 reduce-scatter.10

commit v9 on v8

--- a/solution.py
+++ b/solution.py
@@ -300,27 +300,79 @@
     return bucket_index(first + rows - (total - LB) - lanes)
 
 
-def build_strips(table_ref, strip_ref, total, group):
+def near_kernel(total, table_ref, out_ref):
+    heads = out_ref.shape[0]
+
+    def one_tile(tile, _):
+        index = near_buckets(tile, total)
+        vals = [jnp.full((LB, LB), table_ref[h, 0], F32) for h in range(heads)]
+        for b in range(1, 32):
+            hit = index == b
+            vals = [jnp.where(hit, table_ref[h, b], vals[h]) for h in range(heads)]
+        for h in range(heads):
+            out_ref[h, pl.ds(pl.multiple_of(tile * LB, LB), LB)] = vals[h]
+        return 0
+
+    lax.fori_loop(0, 3, one_tile, 0)
+
+
+def near_bias(table, total):
+    heads = table.shape[0]
+    return pl.pallas_call(
+        functools.partial(near_kernel, total),
+        in_specs=[pl.BlockSpec(memory_space=pltpu.SMEM)],
+        out_specs=pl.BlockSpec((heads, 3 * LB, LB), lambda: (0, 0, 0)),
+        out_shape=jax.ShapeDtypeStruct((heads, 3 * LB, LB), F32),
+        compiler_params=params(0),
+        cost_estimate=cost(0, heads * LB * LB),
+        name="near_bias",
+    )(table)
+
+
+def build_strips(table_ref, near_ref, strip_ref, total, group):
     heads = strip_ref.shape[0]
     near = (total // LB - 2) * LB
     for h in range(heads):
         head = group * heads + h
         strip_ref[h, :near] = jnp.full((near, LB), table_ref[head, 15], F32)
+        strip_ref[h, near : near + 3 * LB] = near_ref[h]
         strip_ref[h, near + 3 * LB :] = jnp.full((near, LB), table_ref[head, 31], F32)
 
-    def one_tile(tile, _):
-        index = near_buckets(tile, total)
-        vals = [jnp.full((LB, LB), table_ref[group * heads + h, 0], F32) for h in range(heads)]
-        for b in range(1, 32):
-            hit = index == b
-            vals = [
-                jnp.where(hit, table_ref[group * heads + h, b], vals[h]) for h in range(heads)
-            ]
-        for h in range(heads):
-            strip_ref[h, pl.ds(pl.multiple_of(near + tile * LB, LB), LB)] = vals[h]
-        return 0
-
-    lax.fori_loop(0, 3, one_tile, 0)
+
+def table_kernel(total, *refs):
+    parts, out_ref = refs[:-1], refs[-1]
+    index = [near_buckets(tile, total) for tile in range(3)]
+    buckets = [range(1, 16), [b for b in range(32) if b != 16], range(17, 32)]
+    for g, part_ref in enumerate(parts):
+        heads = part_ref.shape[0]
+
+        def one_head(h, _):
+            here = g * heads + h
+            out_ref[here] = jnp.zeros((32, LB), F32)
+            out_ref[here, 15:16] = part_ref[h, 3 * LB : 3 * LB + 1]
+            out_ref[here, 31:32] = part_ref[h, 3 * LB + 8 : 3 * LB + 9]
+            for tile in range(3):
+                grads = part_ref[h, tile * LB : (tile + 1) * LB]
+                for b in buckets[tile]:
+                    picked = jnp.where(index[tile] == b, grads, 0.0)
+                    out_ref[here, b : b + 1] += jnp.sum(picked, axis=0, keepdims=True)
+            return 0
+
+        lax.fori_loop(0, heads, one_head, 0)
+
+
+def table_sums(parts, total):
+    heads = len(parts) * parts[0].shape[0]
+    out = pl.pallas_call(
+        functools.partial(table_kernel, total),
+        in_specs=[pl.BlockSpec(part.shape, lambda: (0, 0, 0)) for part in parts],
+        out_specs=pl.BlockSpec((heads, 32, LB), lambda: (0, 0, 0)),
+        out_shape=jax.ShapeDtypeStruct((heads, 32, LB), F32),
+        compiler_params=params(0),
+        cost_estimate=cost(0, heads * LB * LB),
+        name="table_sums",
+    )(*parts)
+    return jnp.sum(out, axis=2)
 
 
 def head_lanes(shape, h):
@@ -352,10 +404,10 @@
     return jnp.concatenate([left, right], axis=1)
 
 
-def attend_kernel(group, length_ref, table_ref, q_ref, k_ref, v_ref, out_ref, lse_ref, strip, heads_k, turned_v, turned_out):
+def attend_kernel(group, length_ref, table_ref, near_ref, q_ref, k_ref, v_ref, out_ref, lse_ref, strip, heads_k, turned_v, turned_out):
     total = q_ref.shape[0]
     heads = strip.shape[0]
-    build_strips(table_ref, strip, total, group)
+    build_strips(table_ref, near_ref, strip, total, group)
     turned_v[...] = v_ref[...].astype(F32).T.astype(BF)
     for h in range(heads):
         heads_k[h] = mask_keys(k_ref[...], length_ref[0], h)
@@ -378,12 +430,12 @@
 
 
 def attend_back_kernel(
-    group, length_ref, table_ref, q_ref, k_ref, v_ref, grad_ref, lse_ref, out_ref, table_grad_ref,
+    group, length_ref, table_ref, near_ref, q_ref, k_ref, v_ref, grad_ref, lse_ref, out_ref, table_grad_ref,
     strip, strip_grad, heads_k, turned_k, turned_q, ds_ref, p_ref, dk_ref, dv_ref,
 ):
     total = q_ref.shape[0]
     heads = strip.shape[0]
-    build_strips(table_ref, strip, total, group)
+    build_strips(table_ref, near_ref, strip, total, group)
     strip_grad[...] = jnp.zeros_like(strip_grad)
     dk_ref[...] = jnp.zeros_like(dk_ref)
     dv_ref[...] = jnp.zeros_like(dv_ref)
@@ -423,21 +475,11 @@
 
     near = (total // LB - 2) * LB
     for h in range(heads):
-        table_grad_ref[h] = jnp.zeros((32, LB), F32)
-        table_grad_ref[h, 15:16] = jnp.sum(strip_grad[h, :near], axis=0, keepdims=True)
-        table_grad_ref[h, 31:32] = jnp.sum(strip_grad[h, near + 3 * LB :], axis=0, keepdims=True)
-
-    def one_tile(tile, _):
-        index = near_buckets(tile, total)
-        spot = pl.ds(pl.multiple_of(near + tile * LB, LB), LB)
-        for h in range(heads):
-            grads = strip_grad[h, spot]
-            for b in range(32):
-                picked = jnp.where(index == b, grads, 0.0)
-                table_grad_ref[h, b : b + 1] += jnp.sum(picked, axis=0, keepdims=True)
-        return 0
-
-    lax.fori_loop(0, 3, one_tile, 0)
+        table_grad_ref[h, : 3 * LB] = strip_grad[h, near : near + 3 * LB]
+        left = jnp.sum(strip_grad[h, :near], axis=0, keepdims=True)
+        right = jnp.sum(strip_grad[h, near + 3 * LB :], axis=0, keepdims=True)
+        table_grad_ref[h, 3 * LB : 3 * LB + 8] = jnp.broadcast_to(left, (8, LB))
+        table_grad_ref[h, 3 * LB + 8 :] = jnp.broadcast_to(right, (8, LB))
 
 
 def block_specs(total, group):
@@ -445,10 +487,11 @@
         return pl.BlockSpec((total, 256), lambda _: (0, 3 * group + i))
 
     smem = pl.BlockSpec(memory_space=pltpu.SMEM)
-    return [smem, smem, spec(0), spec(1), spec(2)]
-
-
-def attend(group, projected, length, table):
+    near = pl.BlockSpec((4, 3 * LB, LB), lambda _: (group, 0, 0))
+    return [smem, smem, near, spec(0), spec(1), spec(2)]
+
+
+def attend(group, projected, length, table, near):
     total = projected.shape[0]
     heads = 4
     return pl.pallas_call(
@@ -472,10 +515,10 @@
         compiler_params=params(1),
         cost_estimate=cost(heads * total * total * 2 * 256 * 2, 4 * total * 256 * 2),
         name="attend",
-    )(length, table, projected, projected, projected)
-
-
-def attend_back(group, projected, length, table, grad_out, lse):
+    )(length, table, near, projected, projected, projected)
+
+
+def attend_back(group, projected, length, table, near, grad_out, lse):
     total = projected.shape[0]
     heads = 4
     return pl.pallas_call(
@@ -488,11 +531,11 @@
         ],
         out_specs=[
             pl.BlockSpec((total, 768), lambda _: (0, 0)),
-            pl.BlockSpec((heads, 32, LB), lambda _: (0, 0, 0)),
+            pl.BlockSpec((heads, 3 * LB + 16, LB), lambda _: (0, 0, 0)),
         ],
         out_shape=[
             jax.ShapeDtypeStruct((total, 768), BF),
-            jax.ShapeDtypeStruct((heads, 32, LB), F32),
+            jax.ShapeDtypeStruct((heads, 3 * LB + 16, LB), F32),
         ],
         scratch_shapes=[
             pltpu.VMEM((heads, 2 * total - LB, LB), F32),
@@ -508,7 +551,7 @@
         compiler_params=params(1),
         cost_estimate=cost(heads * total * total * 2 * 256 * 5, 8 * total * 256 * 2),
         name="attend_back",
-    )(length, table, projected, projected, projected, grad_out, lse)
+    )(length, table, near, projected, projected, projected, grad_out, lse)
 
 
 def split_heads(projected, groups, heads):
@@ -815,21 +858,22 @@
     def attend_back_all(grad, *last):
         if not fits:
             grads, table_grad = backward(projected, length, table, grad, lse, nc, heads)
-            return (grads,), table_grad
-        first = backward(0, projected, length, table, grad, lse[0])
-        second = backward(1, after(projected, first[0], *last), length, table, grad, lse[1])
-        return (first[0], second[0]), jnp.concatenate([first[1], second[1]])
+            return (grads,), table_grad[:, :, 0]
+        first = backward(0, projected, length, table, near, grad, lse[0])
+        second = backward(1, after(projected, first[0], *last), length, table, near, grad, lse[1])
+        return (first[0], second[0]), (first[1], second[1])
 
     scale_one = scale_of(tokens)
-    normed, _, _ = gather((tokens * scale_one * gain_one).astype(BF), table, live)
+    near = near_bias(table, 4 * count) if fits else table
+    normed, _, _ = gather((tokens * scale_one * gain_one).astype(BF), near, live)
     cot_other = hop(pick(stored_cot, 1 - y, 1), "y")
     upstream = live * to_groups(stored_cot, after(cot_other, arrived), None).astype(F32)
     upstream_rounded = after(upstream.astype(BF), w_attn)
     projected = nt(normed, w_attn, 0, qkv_count, starts)
     if fits:
-        first = forward(0, projected, length, table)
+        first = forward(0, projected, length, table, near)
         grad_ffn, cot_first, cot_last = gather(upstream_rounded, first[0])
-        second = forward(1, after(projected, first[0], *cot_first), length, table)
+        second = forward(1, after(projected, first[0], *cot_first), length, table, near)
         attended, lse = (first[0], second[0]), (first[1], second[1])
     else:
         grad_ffn, _, cot_last = gather(upstream_rounded)
@@ -888,14 +932,14 @@
 
         (down_all,) = place(down_pieces, here, [(units * unit, width)], write_rows)
         (gate_up_all,) = place(gate_up_pieces, here, [(units, 2, unit, width)], write_gate_up)
-    beside = (outputs[0], down_all, gate_up_all) if fits else ()
-    grad_one, _, one_last = scatter(one_parts, (), beside)
+    beside = (down_all, gate_up_all) if fits else ()
+    table_part = table_sums(table_part, 4 * count) if fits else table_part
+    grad_one, _, one_last = scatter(one_parts, beside, (table_part, outputs[0]))
     through, attn_gain_part = norm_back(tokens, scale_one, gain_one, grad_one)
     input_grad, input_leaves = from_groups((grad_hidden + through).astype(BF))
 
     out_pieces, out_last = shared(out_part)
 
-    table_part = jnp.sum(table_part, axis=2)
     every = jnp.zeros((nx * 2 * local_heads, table_part.shape[1]), F32)
     every = lax.dynamic_update_slice_in_dim(every, table_part, (x * 2 + y) * local_heads, 0)
     spare = -every.size % width
@@ -905,11 +949,10 @@
     attn_gain_grad, ffn_gain_grad = all_sums[:nz], all_sums[nz : 2 * nz]
     every = all_sums[2 * nz :].reshape(-1)[: nx * 2 * local_heads * buckets].reshape(-1, buckets)
 
-    other_half = outputs[1]
     outputs = stored_from(outputs, BF)
     if fits:
         (out_all,) = place(out_pieces, here, [(heads * 64, width)], write_rows)
-        qkv_pieces, _ = shared(after(qkv_part, out_last, other_half, *one_last), out_all, outputs, sums)
+        qkv_pieces, _ = shared(after(qkv_part, sums, *one_last), out_all, outputs, input_leaves)
         query_key_all, value_all = place(
             qkv_pieces, here, [(heads, 2, 64, width), (heads, 64, width)], write_qkv
         )

time: 689 us -> 673 us (0.977)
  starting transfers between devices: 104 us -> 82.3 us
    ppermute x2, starting transfers between devices: 19 us -> 5.81 us  [sum_line(): value = value + lax.ppermute(value, 'z', [(i, i ^ step) for i in range(nz)])]
    pallas_call x0 -> x2, Pallas kernels: none -> 11.4 us  [the longest x1 5.89 us: table_sums(): pl.pallas_call(functools.partial(table_kernel, total), in_specs=[pl.Block...]
    ppermute x59, starting transfers between devices: 64.8 us -> 56.5 us  [hop(): return lax.ppermute(value, axis, swap)]
    pallas_call x2, Pallas kernels: 57.6 us -> 49.5 us  [attend_back(): pl.pallas_call(functools.partial(attend_back_kernel, group), grid=(1,), i...]
  transfers between devices with their start and end apart: 73 -> 73, of which waited for: 27 -> 28; matrix products, arithmetic and copies ran while one was open for 8% -> 9% of each run, Pallas kernels for 37% -> 38%
where the time goes in v9:
time: 673 us; the launch traced here: 666 us
  Pallas kernels  256 us (38%)
  waiting for transfers between devices  245 us (36%)
  starting transfers between devices  82.3 us (12%)
  other arithmetic  48.9 us (7%)
  local copies, waits for them, and re-layouts  18.1 us (3%)
  between operations  15.5 us (2%)
    ppermute x59, waiting for transfers between devices, hop(): return lax.ppermute(value, axis, swap)  141 us
    all_to_all x2, waiting for transfers between devices, to_groups(): return lax.all_to_all(both, 'z', 0, 0, tiled=True)  66.1 us
    ppermute x59, starting transfers between devices, hop(): return lax.ppermute(value, axis, swap)  56.5 us
    pallas_call x2, Pallas kernels, attend_back(): pl.pallas_call(functools.partial(attend_back_kernel, group), grid=(1,), i...  49.5 us
    pallas_call x4, Pallas kernels, mm_nn(): pl.pallas_call(functools.partial(nn_kernel, len(grads)), grid=(nz,), in_s...  44.8 us
    pallas_call x4, Pallas kernels, mm_tn(): pl.pallas_call(functools.partial(tn_kernel, count), grid=(count * steps,)...  43.5 us
    pallas_call x2, Pallas kernels, attend(): pl.pallas_call(functools.partial(attend_kernel, group), grid=(1,), in_spe...  30.1 us
    pallas_call x4, Pallas kernels, place(): pl.pallas_call(functools.partial(place_kernel, write), grid=(4,), in_spec...  19.5 us
  transfers between devices with their start and end apart: 73, of which 28 were waited for; matrix products, arithmetic and copies ran while one was open for 9% of the time, Pallas kernels for 38%

profile of v9, /device:TPU:0, one launch (start us, length us, event | category | flops | bytes accessed | tf_op | source)
XLA Modules:
  0.0 666.0 jit_solution(14097850560329682433)
XLA Ops:
  16.7 12.2 %collective-permute-done.1 = bf16[2,256,512]{2,1,0:T(8,128)(2,1)} collective-permute-done((bf16[2,256,512]{2,1,0:T(8,128)(2,1)}, bf16[2,256,512]{2,1,0:T(8,128)(2,1)}, u32[]{:S(2)}, u32[]{:S(2)}) %collective-permute-start.1) | collective-permute-done | bytes 524320 | tf_op jit(solution)/shard_map/ppermute | solution.py:602
  45.1 49.8 %all-to-all-done = bf16[4,264,512]{2,1,0:T(8,128)(2,1)} async-done(((bf16[4,264,512]{2,1,0:T(8,128)(2,1)}), bf16[4,264,512]{2,1,0:T(8,128)(2,1)}, u32[]{:S(2)}, u32[]{:S(2)}) %all-to-all-start) | async-done | bytes 1081376 | tf_op jit(solution)/shard_map/all_to_all | solution.py:705
  123.9 16.3 %all-to-all-done.1 = bf16[4,256,512]{2,1,0:T(8,128)(2,1)S(1)} async-done(((bf16[4,256,512]{2,1,0:T(8,128)(2,1)}), bf16[4,256,512]{2,1,0:T(8,128)(2,1)S(1)}, u32[]{:S(2)}, u32[]{:S(2)}) %all-to-all-start.1) | async-done | bytes 1048608 | tf_op jit(solution)/shard_map/all_to_all | solution.py:705
  146.9 12.1 %product_nt.2.q_ref.k_ref.v_ref = bf16[1024,1536]{1,0:T(8,128)(2,1)} custom-call(s32[4]{0:T(128)} %add_multiply_fusion.starts_ref, bf16[2,256,512]{2,1,0:T(8,128)(2,1)} %copy-done.10, bf16[2,256,512]{2,1,0:T(8,128)(2,1)} %collective-permute-done.2.refs_1_.refs_3_, bf16[2,256,512]{2,1,0:T(8,128)(2,1)} %collective-permute-done.3.refs_2_.refs_4_, ...), custom_call_target="tpu_custom_call" | custom-call | flops 402653184 | bytes 851968 | tf_op jit(solution)/shard_map/product_nt/pallas_call | solution.py:78
  159.0 15.0 %attend.2 = (bf16[1024,256]{1,0:T(8,128)(2,1)}, f32[8,1024]{1,0:T(8,128)}) custom-call(s32[1]{0:T(128)} %dynamic_slice.51.length_ref, f32[8,32]{1,0:T(8,128)} %constant_dynamic-slice_fusion.4.table_ref, f32[8,384,128]{2,1,0:T(8,128)} %near_bias.1.near_ref, bf16[1024,1536]{1,0:T(8,128)(2,1)} %product_nt.2.q_ref.k_ref.v_ref, ...), custom_call_target="tpu_custom_call" | custom-call | flops 268435456 | bytes 131072 | tf_op jit(solution)/shard_map/attend/pallas_call | solution.py:497
  176.9 15.1 %attend.3 = (bf16[1024,256]{1,0:T(8,128)(2,1)}, f32[8,1024]{1,0:T(8,128)}) custom-call(s32[1]{0:T(128)} %dynamic_slice.51.length_ref, f32[8,32]{1,0:T(8,128)} %constant_dynamic-slice_fusion.4.table_ref, f32[8,384,128]{2,1,0:T(8,128)} %near_bias.1.near_ref, bf16[1024,1536]{1,0:T(8,128)(2,1)} %product_nt.2.q_ref.k_ref.v_ref, ...), custom_call_target="tpu_custom_call" | custom-call | flops 268435456 | bytes 131072 | tf_op jit(solution)/shard_map/attend/pallas_call | solution.py:497
  200.4 22.3 %collective-permute-done.15 = bf16[2,2,256,512]{3,2,1,0:T(8,128)(2,1)S(1)} collective-permute-done((bf16[2,2,256,512]{3,2,1,0:T(8,128)(2,1)}, bf16[2,2,256,512]{3,2,1,0:T(8,128)(2,1)S(1)}, u32[]{:S(2)}, u32[]{:S(2)}) %collective-permute-start.15) | collective-permute-done | bytes 1048608 | tf_op jit(solution)/shard_map/ppermute | solution.py:602
  243.0 10.8 %collective-permute-done.20.refs_2_.refs_3_ = bf16[2,256,512]{2,1,0:T(8,128)(2,1)S(1)} collective-permute-done((bf16[2,256,512]{2,1,0:T(8,128)(2,1)S(1)}, bf16[2,256,512]{2,1,0:T(8,128)(2,1)S(1)}, u32[]{:S(2)}, u32[]{:S(2)}) %collective-permute-start.20) | collective-permute-done | bytes 524320 | tf_op jit(solution)/shard_map/ppermute | solution.py:602
  255.9 9.6 %collective-permute-done.19.refs_1_.refs_2_ = bf16[2,256,512]{2,1,0:T(8,128)(2,1)S(1)} collective-permute-done((bf16[2,256,512]{2,1,0:T(8,128)(2,1)S(1)}, bf16[2,256,512]{2,1,0:T(8,128)(2,1)S(1)}, u32[]{:S(2)}, u32[]{:S(2)}) %collective-permute-start.19) | collective-permute-done | bytes 524320 | tf_op jit(solution)/shard_map/ppermute | solution.py:602
  272.5 17.6 %ffn_in.1 = (bf16[1024,1280]{1,0:T(8,128)(2,1)}, bf16[1024,1280]{1,0:T(8,128)(2,1)}, bf16[1024,1280]{1,0:T(8,128)(2,1)}) custom-call(s32[4]{0:T(128)} %add_multiply_fusion.starts_ref, bf16[2,256,512]{2,1,0:T(8,128)(2,1)} %copy-done.8, bf16[2,256,512]{2,1,0:T(8,128)(2,1)} %copy-done.18, bf16[2,256,512]{2,1,0:T(8,128)(2,1)} %copy-done.16, ...), custom_call_target="tpu_custom_call" | custom-call | flops 671088640 | bytes 1409024 | tf_op jit(solution)/shard_map/ffn_in/pallas_call | solution.py:214
  290.2 9.9 %product_tn.4 = bf16[4,1280,512]{2,1,0:T(8,128)(2,1)} custom-call(s32[4]{0:T(128)} %add_multiply_fusion.starts_ref, bf16[1024,1280]{1,0:T(8,128)(2,1)} %get-tuple-element.98.refs_0_, bf16[2,256,512]{2,1,0:T(8,128)(2,1)} %copy-done.6, bf16[2,256,512]{2,1,0:T(8,128)(2,1)} %collective-permute-done.9.refs_2_.refs_1_, bf16[2,256,512]{2,1,0:T(8,128)(2,1)} %copy-done.14, ...), custom_call_target="tpu_custom_call" | custom-call | flops 335544320 | bytes 753664 | tf_op jit(solution)/shard_map/product_tn/pallas_call | solution.py:171
  300.2 15.2 %ffn_back.1.refs_0_ = bf16[1024,2560]{1,0:T(8,128)(2,1)} custom-call(s32[4]{0:T(128)} %add_multiply_fusion.starts_ref, bf16[2,256,512]{2,1,0:T(8,128)(2,1)} %copy-done.6, bf16[2,256,512]{2,1,0:T(8,128)(2,1)} %collective-permute-done.9.refs_2_.refs_1_, bf16[2,256,512]{2,1,0:T(8,128)(2,1)} %copy-done.14, ...), custom_call_target="tpu_custom_call" | custom-call | flops 335544320 | bytes 1245184 | tf_op jit(solution)/shard_map/ffn_back/pallas_call | solution.py:245
  315.4 16.4 %product_nn.5 = (bf16[2,2,256,512]{3,2,1,0:T(8,128)(2,1)}, bf16[2,2,256,512]{3,2,1,0:T(8,128)(2,1)}, bf16[2,2,256,512]{3,2,1,0:T(8,128)(2,1)}, bf16[2,2,256,512]{3,2,1,0:T(8,128)(2,1)}) custom-call(s32[4]{0:T(128)} %add_multiply_fusion.starts_ref, bf16[1024,2560]{1,0:T(8,128)(2,1)} %ffn_back.1.refs_0_, bf16[4,2,1280,512]{3,2,1,0:T(8,128)(2,1)} %bitcast.101), custom_call_target="tpu_custom_call" | custom-call | flops 671088640 | bytes 1245184 | tf_op jit(solution)/shard_map/product_nn/pallas_call | solution.py:123
  335.3 15.9 %product_tn.5 = bf16[4,2560,512]{2,1,0:T(8,128)(2,1)} custom-call(s32[4]{0:T(128)} %add_multiply_fusion.starts_ref, bf16[1024,2560]{1,0:T(8,128)(2,1)} %ffn_back.1.refs_0_, bf16[2,256,512]{2,1,0:T(8,128)(2,1)} %copy-done.8, bf16[2,256,512]{2,1,0:T(8,128)(2,1)} %copy-done.18, bf16[2,256,512]{2,1,0:T(8,128)(2,1)} %copy-done.16, ...), custom_call_target="tpu_custom_call" | custom-call | flops 671088640 | bytes 1245184 | tf_op jit(solution)/shard_map/product_tn/pallas_call | solution.py:171
  366.1 10.2 %product_nn.6 = (bf16[2,2,256,512]{3,2,1,0:T(8,128)(2,1)}, bf16[2,2,256,512]{3,2,1,0:T(8,128)(2,1)}, bf16[2,2,256,512]{3,2,1,0:T(8,128)(2,1)}, bf16[2,2,256,512]{3,2,1,0:T(8,128)(2,1)}) custom-call(s32[4]{0:T(128)} %add_multiply_fusion.starts_ref, bf16[1024,1280]{1,0:T(8,128)(2,1)} %get-tuple-element.98.refs_0_, bf16[4,2,640,512]{3,2,1,0:T(8,128)(2,1)} %bitcast.106), custom_call_target="tpu_custom_call" | custom-call | flops 335544320 | bytes 753664 | tf_op jit(solution)/shard_map/product_nn/pallas_call | solution.py:123
  386.3 10.8 %collective-permute-done.30.refs_2_.refs_4_ = bf16[2,256,512]{2,1,0:T(8,128)(2,1)S(1)} collective-permute-done((bf16[2,256,512]{2,1,0:T(8,128)(2,1)S(1)}, bf16[2,256,512]{2,1,0:T(8,128)(2,1)S(1)}, u32[]{:S(2)}, u32[]{:S(2)}) %collective-permute-start.30) | collective-permute-done | bytes 524320 | tf_op jit(solution)/shard_map/ppermute | solution.py:602
  399.1 10.5 %collective-permute-done.29.refs_1_.refs_3_ = bf16[2,256,512]{2,1,0:T(8,128)(2,1)S(1)} collective-permute-done((bf16[2,256,512]{2,1,0:T(8,128)(2,1)S(1)}, bf16[2,256,512]{2,1,0:T(8,128)(2,1)S(1)}, u32[]{:S(2)}, u32[]{:S(2)}) %collective-permute-start.29) | collective-permute-done | bytes 524320 | tf_op jit(solution)/shard_map/ppermute | solution.py:602
  432.0 24.8 %attend_back.2 = (bf16[1024,768]{1,0:T(8,128)(2,1)}, f32[4,400,128]{2,1,0:T(8,128)}) custom-call(s32[1]{0:T(128)} %dynamic_slice.51.length_ref, f32[8,32]{1,0:T(8,128)} %constant_dynamic-slice_fusion.4.table_ref, f32[8,384,128]{2,1,0:T(8,128)} %near_bias.1.near_ref, bf16[1024,1536]{1,0:T(8,128)(2,1)} %product_nt.2.q_ref.k_ref.v_ref, ...), custom_call_target="tpu_custom_call" | custom-call | flops 671088640 | bytes 262144 | tf_op jit(solution)/shard_map/attend_back/pallas_call | solution.py:524
  456.8 12.5 %reduce-scatter.7.cloned.1.call-done.refs_0_ = bf16[1280,512]{1,0:T(8,128)(2,1)} async-done(((bf16[10240,512]{1,0:T(8,128)(2,1)}), bf16[1280,512]{1,0:T(8,128)(2,1)}) %reduce-scatter.7.cloned.1.call-update) | async-done | bytes 1310736 | tf_op jit(solution)/shard_map/reduce_scatter | solution.py:847
  477.8 24.8 %attend_back.3 = (bf16[1024,768]{1,0:T(8,128)(2,1)}, f32[4,400,128]{2,1,0:T(8,128)}) custom-call(s32[1]{0:T(128)} %dynamic_slice.51.length_ref, f32[8,32]{1,0:T(8,128)} %constant_dynamic-slice_fusion.4.table_ref, f32[8,384,128]{2,1,0:T(8,128)} %near_bias.1.near_ref, bf16[1024,1536]{1,0:T(8,128)(2,1)} %product_nt.2.q_ref.k_ref.v_ref, ...), custom_call_target="tpu_custom_call" | custom-call | flops 671088640 | bytes 262144 | tf_op jit(solution)/shard_map/attend_back/pallas_call | solution.py:524
  502.5 11.5 %product_tn.7 = bf16[4,1536,512]{2,1,0:T(8,128)(2,1)} custom-call(s32[4]{0:T(128)} %add_multiply_fusion.starts_ref, bf16[1024,768]{1,0:T(8,128)(2,1)} %get-tuple-element.113.refs_0_, bf16[1024,768]{1,0:T(8,128)(2,1)} %get-tuple-element.116.refs_1_, bf16[2,256,512]{2,1,0:T(8,128)(2,1)} %copy-done.10, ...), custom_call_target="tpu_custom_call" | custom-call | flops 402653184 | bytes 851968 | tf_op jit(solution)/shard_map/product_tn/pallas_call | solution.py:171
  514.2 11.2 %product_nn.7 = (bf16[2,2,256,512]{3,2,1,0:T(8,128)(2,1)}, bf16[2,2,256,512]{3,2,1,0:T(8,128)(2,1)}, bf16[2,2,256,512]{3,2,1,0:T(8,128)(2,1)}, bf16[2,2,256,512]{3,2,1,0:T(8,128)(2,1)}) custom-call(s32[4]{0:T(128)} %add_multiply_fusion.starts_ref, bf16[1024,768]{1,0:T(8,128)(2,1)} %get-tuple-element.113.refs_0_, ...), custom_call_target="tpu_custom_call" | custom-call | flops 402653184 | bytes 851968 | tf_op jit(solution)/shard_map/product_nn/pallas_call | solution.py:123
  564.1 15.7 %all-to-all-done.2 = bf16[4,256,512]{2,1,0:T(8,128)(2,1)S(1)} async-done(((bf16[4,256,512]{2,1,0:T(8,128)(2,1)}), bf16[4,256,512]{2,1,0:T(8,128)(2,1)S(1)}, u32[]{:S(2)}, u32[]{:S(2)}) %all-to-all-start.2) | async-done | bytes 1048608 | tf_op jit(solution)/shard_map/all_to_all | solution.py:710
  593.9 12.6 %collective-permute-done.39.other_ref = bf16[2,256,512]{2,1,0:T(8,128)(2,1)S(1)} collective-permute-done((bf16[2,256,512]{2,1,0:T(8,128)(2,1)S(1)}, bf16[2,256,512]{2,1,0:T(8,128)(2,1)S(1)}, u32[]{:S(2)}, u32[]{:S(2)}) %collective-permute-start.39) | collective-permute-done | bytes 524320 | tf_op jit(solution)/shard_map/ppermute | solution.py:602
  (327 shorter events, 267.5 us)
Async XLA Ops:
  7.2 134.3 %all-gather.4.cloned.1.call-start = ((), (), s32[]{:S(2)}) async-start(), calls=%async_computation.8 | async-start | bytes 9437184 | tf_op jit(solution)/shard_map/all_gather | solution.py:804
  11.6 261.0 %all-gather.6.cloned.1.call-start = ((), (), s32[]{:S(2)}) async-start(), calls=%async_computation.9 | async-start | bytes 11796480 | tf_op jit(solution)/shard_map/all_gather | solution.py:804
  34.3 60.7 %all-to-all-start = ((bf16[4,264,512]{2,1,0:T(8,128)(2,1)}), bf16[4,264,512]{2,1,0:T(8,128)(2,1)}, u32[]{:S(2)}, u32[]{:S(2)}) async-start(bf16[4,264,512]{2,1,0:T(8,128)(2,1)} %pad_maximum_fusion.3), calls=%async_computation | async-start | bytes 2162688 | tf_op jit(solution)/shard_map/all_to_all | solution.py:705
  39.5 260.7 %all-gather.8.cloned.1.call-start = ((), (), s32[]{:S(2)}) async-start(), calls=%async_computation.10 | async-start | bytes 5898240 | tf_op jit(solution)/shard_map/all_gather | solution.py:804
  43.3 51.6 %collective-permute-start.8 = (bf16[2,256,512]{2,1,0:T(8,128)(2,1)S(1)}, bf16[2,256,512]{2,1,0:T(8,128)(2,1)S(1)}, u32[]{:S(2)}, u32[]{:S(2)}) collective-permute-start(bf16[2,256,512]{2,1,0:T(8,128)(2,1)S(1)} %get-tuple-element.157), channel_id=1, source_target_pairs={{0,16},{16,0},{1,17},{17,1},{2,18},{18,2},{3,19},{19,3},{4,20},{20... | collective-permute-start | bytes 1572872 | tf_op jit(solution)/shard_map/ppermute | solution.py:602
  96.1 44.1 %all-to-all-start.1 = ((bf16[4,256,512]{2,1,0:T(8,128)(2,1)}), bf16[4,256,512]{2,1,0:T(8,128)(2,1)S(1)}, u32[]{:S(2)}, u32[]{:S(2)}) async-start(bf16[4,256,512]{2,1,0:T(8,128)(2,1)} %bitcast.26), calls=%async_computation.1 | async-start | bytes 2097152 | tf_op jit(solution)/shard_map/all_to_all | solution.py:705
  101.8 257.0 %reduce-scatter.5.cloned.1.call-start = ((), (), s32[]{:S(2)}) async-start(), calls=%async_computation.11 | async-start | bytes 5898240 | tf_op jit(solution)/shard_map/reduce_scatter | solution.py:847
  109.6 34.8 %collective-permute-start.2 = (bf16[2,256,512]{2,1,0:T(8,128)(2,1)S(1)}, bf16[2,256,512]{2,1,0:T(8,128)(2,1)}, u32[]{:S(2)}, u32[]{:S(2)}) collective-permute-start(bf16[2,256,512]{2,1,0:T(8,128)(2,1)S(1)} %get-tuple-element.159.refs_0_.refs_2_), channel_id=1, source_target_pairs={{0,16},{16,0},{1,17},{17,1},{2,18},{18,2},{3,19},{19,3},{4,20},{20... | collective-permute-start | bytes 1572872 | tf_op jit(solution)/shard_map/ppermute | solution.py:602
  110.1 35.6 %collective-permute-start.6 = (bf16[2,256,512]{2,1,0:T(8,128)(2,1)S(1)}, bf16[2,256,512]{2,1,0:T(8,128)(2,1)}, u32[]{:S(2)}, u32[]{:S(2)}) collective-permute-start(bf16[2,256,512]{2,1,0:T(8,128)(2,1)S(1)} %get-tuple-element.158.refs_4_.refs_6_), channel_id=1, source_target_pairs={{0,4},{4,0},{1,5},{5,1},{2,6},{6,2},{3,7},{7,3},{8,12},{12,8},{9,1... | collective-permute-start | bytes 1572872 | tf_op jit(solution)/shard_map/ppermute | solution.py:602
  142.8 31.3 %collective-permute-start.13 = (bf16[2,256,512]{2,1,0:T(8,128)(2,1)S(1)}, bf16[2,256,512]{2,1,0:T(8,128)(2,1)S(1)}, u32[]{:S(2)}, u32[]{:S(2)}) collective-permute-start(bf16[2,256,512]{2,1,0:T(8,128)(2,1)S(1)} %get-tuple-element.154.refs_5_.refs_4_), channel_id=1, source_target_pairs={{0,16},{16,0},{1,17},{17,1},{2,18},{18,2},{3,19},{19,3},{4,20},{20... | collective-permute-start | bytes 1572872 | tf_op jit(solution)/shard_map/ppermute | solution.py:602
  144.3 29.7 %collective-permute-start.10 = (bf16[2,256,512]{2,1,0:T(8,128)(2,1)S(1)}, bf16[2,256,512]{2,1,0:T(8,128)(2,1)S(1)}, u32[]{:S(2)}, u32[]{:S(2)}) collective-permute-start(bf16[2,256,512]{2,1,0:T(8,128)(2,1)S(1)} %get-tuple-element.155.refs_1_.refs_0_), channel_id=1, source_target_pairs={{0,4},{4,0},{1,5},{5,1},{2,6},{6,2},{3,7},{7,3},{8,12},{12,8},{9,1... | collective-permute-start | bytes 1572872 | tf_op jit(solution)/shard_map/ppermute | solution.py:602
  145.8 46.2 %collective-permute-start.12 = (bf16[2,256,512]{2,1,0:T(8,128)(2,1)S(1)}, bf16[2,256,512]{2,1,0:T(8,128)(2,1)S(1)}, u32[]{:S(2)}, u32[]{:S(2)}) collective-permute-start(bf16[2,256,512]{2,1,0:T(8,128)(2,1)S(1)} %get-tuple-element.154.refs_5_.refs_4_), channel_id=1, source_target_pairs={{0,4},{4,0},{1,5},{5,1},{2,6},{6,2},{3,7},{7,3},{8,12},{12,8},{9,1... | collective-permute-start | bytes 1572872 | tf_op jit(solution)/shard_map/ppermute | solution.py:602
  146.4 45.6 %collective-permute-start.9 = (bf16[2,256,512]{2,1,0:T(8,128)(2,1)S(1)}, bf16[2,256,512]{2,1,0:T(8,128)(2,1)}, u32[]{:S(2)}, u32[]{:S(2)}) collective-permute-start(bf16[2,256,512]{2,1,0:T(8,128)(2,1)S(1)} %get-tuple-element.155.refs_1_.refs_0_), channel_id=1, source_target_pairs={{0,16},{16,0},{1,17},{17,1},{2,18},{18,2},{3,19},{19,3},{4,20},{20... | collective-permute-start | bytes 1572872 | tf_op jit(solution)/shard_map/ppermute | solution.py:602
  300.1 169.2 %reduce-scatter.7.cloned.1.call-start = ((), (), s32[]{:S(2)}) async-start(), calls=%async_computation.12 | async-start | bytes 11796480 | tf_op jit(solution)/shard_map/reduce_scatter | solution.py:847
  358.8 155.2 %reduce-scatter.9.cloned.1.call-start = ((), (), s32[]{:S(2)}) async-start(), calls=%async_computation.13 | async-start | bytes 2359296 | tf_op jit(solution)/shard_map/reduce_scatter | solution.py:847
  416.5 40.3 %collective-permute-start.35 = (bf16[2,2,256,512]{3,2,1,0:T(8,128)(2,1)}, bf16[2,2,256,512]{3,2,1,0:T(8,128)(2,1)}, u32[]{:S(2)}, u32[]{:S(2)}) collective-permute-start(bf16[2,2,256,512]{3,2,1,0:T(8,128)(2,1)} %get-tuple-element.106), channel_id=1, source_target_pairs={{0,4},{4,0},{1,5},{5,1},{2,6},{6,2},{3,7},{7,3},{8,12},{12,8},{9,1... | collective-permute-start | bytes 3145736 | tf_op jit(solution)/shard_map/ppermute | solution.py:602
  417.8 39.0 %collective-permute-start.37 = (bf16[2,2,256,512]{3,2,1,0:T(8,128)(2,1)}, bf16[2,2,256,512]{3,2,1,0:T(8,128)(2,1)}, u32[]{:S(2)}, u32[]{:S(2)}) collective-permute-start(bf16[2,2,256,512]{3,2,1,0:T(8,128)(2,1)} %get-tuple-element.110), channel_id=1, source_target_pairs={{0,16},{16,0},{1,17},{17,1},{2,18},{18,2},{3,19},{19,3},{4,20},{20... | collective-permute-start | bytes 3145736 | tf_op jit(solution)/shard_map/ppermute | solution.py:602
  418.6 38.2 %collective-permute-start.42 = (bf16[640,512]{1,0:T(8,128)(2,1)}, bf16[640,512]{1,0:T(8,128)(2,1)}, u32[]{:S(2)}, u32[]{:S(2)}) collective-permute-start(bf16[640,512]{1,0:T(8,128)(2,1)} %reduce-scatter.5.cloned.1.call-done.refs_0_), channel_id=1, source_target_pairs={{0,16},{16,0},{1,17},{17,1},{2,18},{18,2},{3,19},{19,3},{4,20},{20... | collective-permute-start | bytes 1966088 | tf_op jit(solution)/shard_map/ppermute | solution.py:602
  469.4 149.9 %reduce-scatter.11.cloned.1.call-start = ((), (), s32[]{:S(2)}) async-start(), calls=%async_computation.14 | async-start | bytes 7077888 | tf_op jit(solution)/shard_map/reduce_scatter | solution.py:847
  470.7 43.4 %collective-permute-start.45 = (bf16[1280,512]{1,0:T(8,128)(2,1)S(1)}, bf16[1280,512]{1,0:T(8,128)(2,1)}, u32[]{:S(2)}, u32[]{:S(2)}) collective-permute-start(bf16[1280,512]{1,0:T(8,128)(2,1)S(1)} %copy-done.27), channel_id=1, source_target_pairs={{0,16},{16,0},{1,17},{17,1},{2,18},{18,2},{3,19},{19,3},{4,20},{20... | collective-permute-start | bytes 3932168 | tf_op jit(solution)/shard_map/ppermute | solution.py:602
  473.5 40.5 %collective-permute-start.36 = (bf16[2,256,512]{2,1,0:T(8,128)(2,1)S(1)}, bf16[2,256,512]{2,1,0:T(8,128)(2,1)}, u32[]{:S(2)}, u32[]{:S(2)}) collective-permute-start(bf16[2,256,512]{2,1,0:T(8,128)(2,1)S(1)} %fusion.19), channel_id=1, source_target_pairs={{0,16},{16,0},{1,17},{17,1},{2,18},{18,2},{3,19},{19,3},{4,20},{20... | collective-permute-start | bytes 1572872 | tf_op jit(solution)/shard_map/ppermute | solution.py:602
  476.2 37.8 %collective-permute-start.38 = (bf16[2,256,512]{2,1,0:T(8,128)(2,1)}, bf16[2,256,512]{2,1,0:T(8,128)(2,1)}, u32[]{:S(2)}, u32[]{:S(2)}) collective-permute-start(bf16[2,256,512]{2,1,0:T(8,128)(2,1)} %fusion.20), channel_id=1, source_target_pairs={{0,4},{4,0},{1,5},{5,1},{2,6},{6,2},{3,7},{7,3},{8,12},{12,8},{9,1... | collective-permute-start | bytes 1572872 | tf_op jit(solution)/shard_map/ppermute | solution.py:602
  532.3 47.6 %all-to-all-start.2 = ((bf16[4,256,512]{2,1,0:T(8,128)(2,1)}), bf16[4,256,512]{2,1,0:T(8,128)(2,1)S(1)}, u32[]{:S(2)}, u32[]{:S(2)}) async-start(bf16[4,256,512]{2,1,0:T(8,128)(2,1)} %fusion.13), calls=%async_computation.2 | async-start | bytes 2097152 | tf_op jit(solution)/shard_map/all_to_all | solution.py:710
  588.0 39.8 %all-to-all-start.3 = ((bf16[4,256,512]{2,1,0:T(8,128)(2,1)}), bf16[4,256,512]{2,1,0:T(8,128)(2,1)S(1)}, u32[]{:S(2)}, u32[]{:S(2)}) async-start(bf16[4,256,512]{2,1,0:T(8,128)(2,1)} %fusion.9), calls=%async_computation.5 | async-start | bytes 2097152 | tf_op jit(solution)/shard_map/all_to_all | solution.py:710
  (94 other events, 1358.5 us)
Sparse Core Ops, SparseCore 0:
  11.7 129.7 all-gather.3
  143.7 97.5 all-gather.5
  242.9 54.3 all-gather.7
  300.2 58.5 reduce-scatter.4
  361.5 107.7 reduce-scatter.6
  472.1 33.8 reduce-scatter.8
  514.2 84.9 reduce-scatter.10

commit v10 on v9

--- a/solution.py
+++ b/solution.py
@@ -692,7 +692,7 @@
     return [part, hop(part, "c"), over_y, hop(over_y, "c")], over_y
 
 
-def share_plain(part):
+def share_plain(part, *beside):
     return lax.all_gather(part, ("y", "c"), axis=0), part
 
 
@@ -855,14 +855,6 @@
         forward, backward, gather, scatter = attend_plain, attend_back_plain, gather_plain, scatter_plain
         nt, nn, tn, ffn_one, ffn_two = mm_nt_plain, mm_nn_plain, mm_tn_plain, ffn_in_plain, ffn_back_plain
         shared, stored_from = share_plain, settle_plain
-    def attend_back_all(grad, *last):
-        if not fits:
-            grads, table_grad = backward(projected, length, table, grad, lse, nc, heads)
-            return (grads,), table_grad[:, :, 0]
-        first = backward(0, projected, length, table, near, grad, lse[0])
-        second = backward(1, after(projected, first[0], *last), length, table, near, grad, lse[1])
-        return (first[0], second[0]), (first[1], second[1])
-
     scale_one = scale_of(tokens)
     near = near_bias(table, 4 * count) if fits else table
     normed, _, _ = gather((tokens * scale_one * gain_one).astype(BF), near, live)
@@ -898,17 +890,28 @@
     grad_branch, _, branch_here = gather(after(grad_hidden.astype(BF), branch_parts[0]))
     grad_attended = nt(grad_branch, w_attn, qkv_count, out_count, starts)
     out_partial = tn(attended, grad_branch, starts)
+    grad_attended = after(grad_attended, out_partial)
     branch_parts = [after(part, *branch_here) for part in branch_parts]
-    branch, branch_first, branch_last = scatter(branch_parts)
+    if fits:
+        first = backward(0, projected, length, table, near, grad_attended, lse[0])
+        branch, branch_first, branch_last = scatter(branch_parts, (first[0],))
+    else:
+        branch, branch_first, branch_last = scatter(branch_parts)
     down_pieces, down_last = shared(after(down_part, *branch_here))
-    grad_projected, table_part = attend_back_all(after(grad_attended, out_partial), *branch_first)
-    out_part = reduce(after(out_partial, gate_up_part, grad_projected[0], *branch_first, down_last))
+    if fits:
+        second = backward(
+            1, after(projected, first[0], *branch_first), length, table, near, grad_attended, lse[1]
+        )
+        grad_projected, table_part = (first[0], second[0]), (first[1], second[1])
+    else:
+        grads, table_part = backward(projected, length, table, grad_attended, lse, nc, heads)
+        grad_projected, table_part = (grads,), table_part[:, :, 0]
+    out_part = reduce(after(out_partial, gate_up_part, grad_projected[-1], *branch_last, down_last))
     outputs = (live * (hidden + branch)).astype(BF)
     outputs, _ = from_groups(outputs)
-    qkv_partial = tn(grad_projected, normed, starts)
-    gate_up_pieces, gate_up_last = shared(after(gate_up_part, grad_projected[0]))
-    qkv_part = reduce(after(qkv_partial, out_part, *branch_last, gate_up_last))
     one_parts = nn(grad_projected, w_attn, 0, qkv_count, starts)
+    last = after(grad_projected[-1], one_parts[0])
+    qkv_partial = tn([*grad_projected[:-1], last], normed, starts)
     if fits:
         here = jnp.stack([y, c]).astype(jnp.int32)
 
@@ -931,28 +934,30 @@
                     outs[0][u, i] = source[first : first + unit, :].astype(F32)
 
         (down_all,) = place(down_pieces, here, [(units * unit, width)], write_rows)
-        (gate_up_all,) = place(gate_up_pieces, here, [(units, 2, unit, width)], write_gate_up)
-    beside = (down_all, gate_up_all) if fits else ()
+    beside = (qkv_partial, down_all, outputs[0]) if fits else ()
     table_part = table_sums(table_part, 4 * count) if fits else table_part
-    grad_one, _, one_last = scatter(one_parts, beside, (table_part, outputs[0]))
+    grad_one, one_first, one_last = scatter(one_parts, beside, (table_part,))
+    qkv_part = reduce(after(qkv_partial, gate_up_part, *one_first))
     through, attn_gain_part = norm_back(tokens, scale_one, gain_one, grad_one)
     input_grad, input_leaves = from_groups((grad_hidden + through).astype(BF))
 
     out_pieces, out_last = shared(out_part)
+    gate_up_pieces, _ = shared(after(gate_up_part, *one_first), input_leaves)
 
     every = jnp.zeros((nx * 2 * local_heads, table_part.shape[1]), F32)
     every = lax.dynamic_update_slice_in_dim(every, table_part, (x * 2 + y) * local_heads, 0)
     spare = -every.size % width
     every = jnp.pad(every.reshape(-1), (0, spare)).reshape(-1, width)
-    sums = sum_plane(jnp.concatenate([attn_gain_part, ffn_gain_part, every]), nx, out_last, outputs[1])
+    sums = sum_plane(jnp.concatenate([attn_gain_part, ffn_gain_part, every]), nx, out_last, outputs[1], input_grad[1])
     all_sums = sum_line(after(sums, input_leaves), nz)
     attn_gain_grad, ffn_gain_grad = all_sums[:nz], all_sums[nz : 2 * nz]
     every = all_sums[2 * nz :].reshape(-1)[: nx * 2 * local_heads * buckets].reshape(-1, buckets)
 
     outputs = stored_from(outputs, BF)
     if fits:
+        (gate_up_all,) = place(gate_up_pieces, here, [(units, 2, unit, width)], write_gate_up)
         (out_all,) = place(out_pieces, here, [(heads * 64, width)], write_rows)
-        qkv_pieces, _ = shared(after(qkv_part, sums, *one_last), out_all, outputs, input_leaves)
+        qkv_pieces, _ = shared(after(qkv_part, sums, *one_last), out_all, gate_up_all, outputs, input_leaves)
         query_key_all, value_all = place(
             qkv_pieces, here, [(heads, 2, 64, width), (heads, 64, width)], write_qkv
         )

time: 673 us -> 679 us (level)
  waiting for transfers between devices: 245 us -> 252 us
    all_to_all x2, waiting for transfers between devices: 15.7 us -> 43.2 us  [from_groups(): lax.all_to_all(mine, 'z', 0, 0, tiled=True).reshape(2, nz // 2, t, width)]
    reduce_scatter x4, waiting for transfers between devices: 15.6 us -> 3.07 us  [reduce(): return lax.psum_scatter(rows, ('z', 'c'), scatter_dimension=0, tiled=True)]
  transfers between devices with their start and end apart: 73 -> 73, of which waited for: 28 -> 29; matrix products, arithmetic and copies ran while one was open for 9% -> 9% of each run, Pallas kernels for 38% -> 37%
where the time goes in v10:
time: 679 us; the launch traced here: 674 us
  Pallas kernels  255 us (38%)
  waiting for transfers between devices  252 us (37%)
  starting transfers between devices  82.5 us (12%)
  other arithmetic  48.2 us (7%)
  local copies, waits for them, and re-layouts  19.8 us (3%)
  between operations  15.4 us (2%)
    ppermute x59, waiting for transfers between devices, hop(): return lax.ppermute(value, axis, swap)  138 us
    all_to_all x2, waiting for transfers between devices, to_groups(): return lax.all_to_all(both, 'z', 0, 0, tiled=True)  66.1 us
    ppermute x59, starting transfers between devices, hop(): return lax.ppermute(value, axis, swap)  56.8 us
    pallas_call x2, Pallas kernels, attend_back(): pl.pallas_call(functools.partial(attend_back_kernel, group), grid=(1,), i...  49.3 us
    pallas_call x4, Pallas kernels, mm_nn(): pl.pallas_call(functools.partial(nn_kernel, len(grads)), grid=(nz,), in_s...  44.8 us
    pallas_call x4, Pallas kernels, mm_tn(): pl.pallas_call(functools.partial(tn_kernel, count), grid=(count * steps,)...  43.4 us
    all_to_all x2, waiting for transfers between devices, from_groups(): lax.all_to_all(mine, 'z', 0, 0, tiled=True).reshape(2, nz // 2, t, width)  43.2 us
    pallas_call x2, Pallas kernels, attend(): pl.pallas_call(functools.partial(attend_kernel, group), grid=(1,), in_spe...  30.1 us
  transfers between devices with their start and end apart: 73, of which 29 were waited for; matrix products, arithmetic and copies ran while one was open for 9% of the time, Pallas kernels for 37%

profile of v10, /device:TPU:0, one launch (start us, length us, event | category | flops | bytes accessed | tf_op | source)
XLA Modules:
  0.0 673.6 jit_solution(1454624261345488198)
XLA Ops:
  16.7 12.2 %collective-permute-done.1 = bf16[2,256,512]{2,1,0:T(8,128)(2,1)} collective-permute-done((bf16[2,256,512]{2,1,0:T(8,128)(2,1)}, bf16[2,256,512]{2,1,0:T(8,128)(2,1)}, u32[]{:S(2)}, u32[]{:S(2)}) %collective-permute-start.1) | collective-permute-done | bytes 524320 | tf_op jit(solution)/shard_map/ppermute | solution.py:602
  45.2 49.8 %all-to-all-done = bf16[4,264,512]{2,1,0:T(8,128)(2,1)} async-done(((bf16[4,264,512]{2,1,0:T(8,128)(2,1)}), bf16[4,264,512]{2,1,0:T(8,128)(2,1)}, u32[]{:S(2)}, u32[]{:S(2)}) %all-to-all-start) | async-done | bytes 1081376 | tf_op jit(solution)/shard_map/all_to_all | solution.py:705
  123.9 16.3 %all-to-all-done.1 = bf16[4,256,512]{2,1,0:T(8,128)(2,1)S(1)} async-done(((bf16[4,256,512]{2,1,0:T(8,128)(2,1)}), bf16[4,256,512]{2,1,0:T(8,128)(2,1)S(1)}, u32[]{:S(2)}, u32[]{:S(2)}) %all-to-all-start.1) | async-done | bytes 1048608 | tf_op jit(solution)/shard_map/all_to_all | solution.py:705
  146.9 12.1 %product_nt.2.q_ref.k_ref.v_ref = bf16[1024,1536]{1,0:T(8,128)(2,1)} custom-call(s32[4]{0:T(128)} %add_multiply_fusion.starts_ref, bf16[2,256,512]{2,1,0:T(8,128)(2,1)} %copy-done.10, bf16[2,256,512]{2,1,0:T(8,128)(2,1)} %collective-permute-done.2.refs_1_.refs_3_, bf16[2,256,512]{2,1,0:T(8,128)(2,1)} %collective-permute-done.3.refs_2_.refs_4_, ...), custom_call_target="tpu_custom_call" | custom-call | flops 402653184 | bytes 851968 | tf_op jit(solution)/shard_map/product_nt/pallas_call | solution.py:78
  159.0 15.0 %attend.2 = (bf16[1024,256]{1,0:T(8,128)(2,1)}, f32[8,1024]{1,0:T(8,128)}) custom-call(s32[1]{0:T(128)} %dynamic_slice.51.length_ref, f32[8,32]{1,0:T(8,128)} %constant_dynamic-slice_fusion.4.table_ref, f32[8,384,128]{2,1,0:T(8,128)} %near_bias.1.near_ref, bf16[1024,1536]{1,0:T(8,128)(2,1)} %product_nt.2.q_ref.k_ref.v_ref, ...), custom_call_target="tpu_custom_call" | custom-call | flops 268435456 | bytes 131072 | tf_op jit(solution)/shard_map/attend/pallas_call | solution.py:497
  176.8 15.0 %attend.3 = (bf16[1024,256]{1,0:T(8,128)(2,1)}, f32[8,1024]{1,0:T(8,128)}) custom-call(s32[1]{0:T(128)} %dynamic_slice.51.length_ref, f32[8,32]{1,0:T(8,128)} %constant_dynamic-slice_fusion.4.table_ref, f32[8,384,128]{2,1,0:T(8,128)} %near_bias.1.near_ref, bf16[1024,1536]{1,0:T(8,128)(2,1)} %product_nt.2.q_ref.k_ref.v_ref, ...), custom_call_target="tpu_custom_call" | custom-call | flops 268435456 | bytes 131072 | tf_op jit(solution)/shard_map/attend/pallas_call | solution.py:497
  200.3 22.3 %collective-permute-done.15 = bf16[2,2,256,512]{3,2,1,0:T(8,128)(2,1)S(1)} collective-permute-done((bf16[2,2,256,512]{3,2,1,0:T(8,128)(2,1)}, bf16[2,2,256,512]{3,2,1,0:T(8,128)(2,1)S(1)}, u32[]{:S(2)}, u32[]{:S(2)}) %collective-permute-start.15) | collective-permute-done | bytes 1048608 | tf_op jit(solution)/shard_map/ppermute | solution.py:602
  226.3 8.9 %collective-permute-done.16 = bf16[2,256,512]{2,1,0:T(8,128)(2,1)S(1)} collective-permute-done((bf16[2,256,512]{2,1,0:T(8,128)(2,1)S(1)}, bf16[2,256,512]{2,1,0:T(8,128)(2,1)S(1)}, u32[]{:S(2)}, u32[]{:S(2)}) %collective-permute-start.16) | collective-permute-done | bytes 524320 | tf_op jit(solution)/shard_map/ppermute | solution.py:602
  243.0 10.8 %collective-permute-done.20.refs_2_.refs_3_ = bf16[2,256,512]{2,1,0:T(8,128)(2,1)S(1)} collective-permute-done((bf16[2,256,512]{2,1,0:T(8,128)(2,1)S(1)}, bf16[2,256,512]{2,1,0:T(8,128)(2,1)S(1)}, u32[]{:S(2)}, u32[]{:S(2)}) %collective-permute-start.20) | collective-permute-done | bytes 524320 | tf_op jit(solution)/shard_map/ppermute | solution.py:602
  255.9 9.7 %collective-permute-done.19.refs_1_.refs_2_ = bf16[2,256,512]{2,1,0:T(8,128)(2,1)S(1)} collective-permute-done((bf16[2,256,512]{2,1,0:T(8,128)(2,1)S(1)}, bf16[2,256,512]{2,1,0:T(8,128)(2,1)S(1)}, u32[]{:S(2)}, u32[]{:S(2)}) %collective-permute-start.19) | collective-permute-done | bytes 524320 | tf_op jit(solution)/shard_map/ppermute | solution.py:602
  272.5 17.6 %ffn_in.1 = (bf16[1024,1280]{1,0:T(8,128)(2,1)}, bf16[1024,1280]{1,0:T(8,128)(2,1)}, bf16[1024,1280]{1,0:T(8,128)(2,1)}) custom-call(s32[4]{0:T(128)} %add_multiply_fusion.starts_ref, bf16[2,256,512]{2,1,0:T(8,128)(2,1)} %copy-done.8, bf16[2,256,512]{2,1,0:T(8,128)(2,1)} %copy-done.18, bf16[2,256,512]{2,1,0:T(8,128)(2,1)} %copy-done.16, ...), custom_call_target="tpu_custom_call" | custom-call | flops 671088640 | bytes 1409024 | tf_op jit(solution)/shard_map/ffn_in/pallas_call | solution.py:214
  290.1 10.0 %product_tn.4 = bf16[4,1280,512]{2,1,0:T(8,128)(2,1)} custom-call(s32[4]{0:T(128)} %add_multiply_fusion.starts_ref, bf16[1024,1280]{1,0:T(8,128)(2,1)} %get-tuple-element.102.refs_0_, bf16[2,256,512]{2,1,0:T(8,128)(2,1)} %copy-done.6, bf16[2,256,512]{2,1,0:T(8,128)(2,1)} %collective-permute-done.9.refs_2_.refs_1_, bf16[2,256,512]{2,1,0:T(8,128)(2,1)} %copy-done.14, ...), custom_call_target="tpu_custom_call" | custom-call | flops 335544320 | bytes 753664 | tf_op jit(solution)/shard_map/product_tn/pallas_call | solution.py:171
  300.2 15.2 %ffn_back.1.refs_0_ = bf16[1024,2560]{1,0:T(8,128)(2,1)} custom-call(s32[4]{0:T(128)} %add_multiply_fusion.starts_ref, bf16[2,256,512]{2,1,0:T(8,128)(2,1)} %copy-done.6, bf16[2,256,512]{2,1,0:T(8,128)(2,1)} %collective-permute-done.9.refs_2_.refs_1_, bf16[2,256,512]{2,1,0:T(8,128)(2,1)} %copy-done.14, ...), custom_call_target="tpu_custom_call" | custom-call | flops 335544320 | bytes 1245184 | tf_op jit(solution)/shard_map/ffn_back/pallas_call | solution.py:245
  315.4 16.5 %product_nn.5 = (bf16[2,2,256,512]{3,2,1,0:T(8,128)(2,1)}, bf16[2,2,256,512]{3,2,1,0:T(8,128)(2,1)}, bf16[2,2,256,512]{3,2,1,0:T(8,128)(2,1)}, bf16[2,2,256,512]{3,2,1,0:T(8,128)(2,1)}) custom-call(s32[4]{0:T(128)} %add_multiply_fusion.starts_ref, bf16[1024,2560]{1,0:T(8,128)(2,1)} %ffn_back.1.refs_0_, bf16[4,2,1280,512]{3,2,1,0:T(8,128)(2,1)} %bitcast.101), custom_call_target="tpu_custom_call" | custom-call | flops 671088640 | bytes 1245184 | tf_op jit(solution)/shard_map/product_nn/pallas_call | solution.py:123
  335.2 15.9 %product_tn.5 = bf16[4,2560,512]{2,1,0:T(8,128)(2,1)} custom-call(s32[4]{0:T(128)} %add_multiply_fusion.starts_ref, bf16[1024,2560]{1,0:T(8,128)(2,1)} %ffn_back.1.refs_0_, bf16[2,256,512]{2,1,0:T(8,128)(2,1)} %copy-done.8, bf16[2,256,512]{2,1,0:T(8,128)(2,1)} %copy-done.18, bf16[2,256,512]{2,1,0:T(8,128)(2,1)} %copy-done.16, ...), custom_call_target="tpu_custom_call" | custom-call | flops 671088640 | bytes 1245184 | tf_op jit(solution)/shard_map/product_tn/pallas_call | solution.py:171
  366.0 10.3 %product_nn.6 = (bf16[2,2,256,512]{3,2,1,0:T(8,128)(2,1)}, bf16[2,2,256,512]{3,2,1,0:T(8,128)(2,1)}, bf16[2,2,256,512]{3,2,1,0:T(8,128)(2,1)}, bf16[2,2,256,512]{3,2,1,0:T(8,128)(2,1)}) custom-call(s32[4]{0:T(128)} %add_multiply_fusion.starts_ref, bf16[1024,1280]{1,0:T(8,128)(2,1)} %get-tuple-element.102.refs_0_, bf16[4,2,640,512]{3,2,1,0:T(8,128)(2,1)} %bitcast.106), custom_call_target="tpu_custom_call" | custom-call | flops 335544320 | bytes 753664 | tf_op jit(solution)/shard_map/product_nn/pallas_call | solution.py:123
  386.3 10.8 %collective-permute-done.30.refs_2_.refs_4_ = bf16[2,256,512]{2,1,0:T(8,128)(2,1)S(1)} collective-permute-done((bf16[2,256,512]{2,1,0:T(8,128)(2,1)S(1)}, bf16[2,256,512]{2,1,0:T(8,128)(2,1)S(1)}, u32[]{:S(2)}, u32[]{:S(2)}) %collective-permute-start.30) | collective-permute-done | bytes 524320 | tf_op jit(solution)/shard_map/ppermute | solution.py:602
  399.1 10.5 %collective-permute-done.29.refs_1_.refs_3_ = bf16[2,256,512]{2,1,0:T(8,128)(2,1)S(1)} collective-permute-done((bf16[2,256,512]{2,1,0:T(8,128)(2,1)S(1)}, bf16[2,256,512]{2,1,0:T(8,128)(2,1)S(1)}, u32[]{:S(2)}, u32[]{:S(2)}) %collective-permute-start.29) | collective-permute-done | bytes 524320 | tf_op jit(solution)/shard_map/ppermute | solution.py:602
  430.8 24.8 %attend_back.2 = (bf16[1024,768]{1,0:T(8,128)(2,1)}, f32[4,400,128]{2,1,0:T(8,128)}) custom-call(s32[1]{0:T(128)} %dynamic_slice.51.length_ref, f32[8,32]{1,0:T(8,128)} %constant_dynamic-slice_fusion.4.table_ref, f32[8,384,128]{2,1,0:T(8,128)} %near_bias.1.near_ref, bf16[1024,1536]{1,0:T(8,128)(2,1)} %product_nt.2.q_ref.k_ref.v_ref, ...), custom_call_target="tpu_custom_call" | custom-call | flops 671088640 | bytes 262144 | tf_op jit(solution)/shard_map/attend_back/pallas_call | solution.py:524
  461.8 24.5 %attend_back.3 = (bf16[1024,768]{1,0:T(8,128)(2,1)}, f32[4,400,128]{2,1,0:T(8,128)}) custom-call(s32[1]{0:T(128)} %dynamic_slice.51.length_ref, f32[8,32]{1,0:T(8,128)} %constant_dynamic-slice_fusion.4.table_ref, f32[8,384,128]{2,1,0:T(8,128)} %near_bias.1.near_ref, bf16[1024,1536]{1,0:T(8,128)(2,1)} %product_nt.2.q_ref.k_ref.v_ref, ...), custom_call_target="tpu_custom_call" | custom-call | flops 671088640 | bytes 262144 | tf_op jit(solution)/shard_map/attend_back/pallas_call | solution.py:524
  495.8 11.2 %product_nn.7 = (bf16[2,2,256,512]{3,2,1,0:T(8,128)(2,1)}, bf16[2,2,256,512]{3,2,1,0:T(8,128)(2,1)}, bf16[2,2,256,512]{3,2,1,0:T(8,128)(2,1)}, bf16[2,2,256,512]{3,2,1,0:T(8,128)(2,1)}) custom-call(s32[4]{0:T(128)} %add_multiply_fusion.starts_ref, bf16[1024,768]{1,0:T(8,128)(2,1)} %get-tuple-element.113.refs_0_, ...), custom_call_target="tpu_custom_call" | custom-call | flops 402653184 | bytes 851968 | tf_op jit(solution)/shard_map/product_nn/pallas_call | solution.py:123
  510.5 11.4 %product_tn.7 = bf16[4,1536,512]{2,1,0:T(8,128)(2,1)} custom-call(s32[4]{0:T(128)} %add_multiply_fusion.starts_ref, bf16[1024,768]{1,0:T(8,128)(2,1)} %get-tuple-element.113.refs_0_, bf16[1024,768]{1,0:T(8,128)(2,1)} %get-tuple-element.125.refs_1_, bf16[2,256,512]{2,1,0:T(8,128)(2,1)} %copy-done.10, ...), custom_call_target="tpu_custom_call" | custom-call | flops 402653184 | bytes 851968 | tf_op jit(solution)/shard_map/product_tn/pallas_call | solution.py:171
  568.4 39.1 %all-to-all-done.3 = bf16[4,256,512]{2,1,0:T(8,128)(2,1)S(1)} async-done(((bf16[4,256,512]{2,1,0:T(8,128)(2,1)}), bf16[4,256,512]{2,1,0:T(8,128)(2,1)S(1)}, u32[]{:S(2)}, u32[]{:S(2)}) %all-to-all-start.3) | async-done | bytes 1048608 | tf_op jit(solution)/shard_map/all_to_all | solution.py:710
  614.6 7.2 %collective-permute-done.47.other_ref = bf16[2,256,512]{2,1,0:T(8,128)(2,1)S(1)} collective-permute-done((bf16[2,256,512]{2,1,0:T(8,128)(2,1)S(1)}, bf16[2,256,512]{2,1,0:T(8,128)(2,1)S(1)}, u32[]{:S(2)}, u32[]{:S(2)}) %collective-permute-start.47) | collective-permute-done | bytes 524320 | tf_op jit(solution)/shard_map/ppermute | solution.py:602
  (333 shorter events, 261.2 us)
Async XLA Ops:
  7.2 134.3 %all-gather.4.cloned.1.call-start = ((), (), s32[]{:S(2)}) async-start(), calls=%async_computation.8 | async-start | bytes 9437184 | tf_op jit(solution)/shard_map/all_gather | solution.py:804
  11.6 261.0 %all-gather.6.cloned.1.call-start = ((), (), s32[]{:S(2)}) async-start(), calls=%async_computation.9 | async-start | bytes 11796480 | tf_op jit(solution)/shard_map/all_gather | solution.py:804
  34.3 60.7 %all-to-all-start = ((bf16[4,264,512]{2,1,0:T(8,128)(2,1)}), bf16[4,264,512]{2,1,0:T(8,128)(2,1)}, u32[]{:S(2)}, u32[]{:S(2)}) async-start(bf16[4,264,512]{2,1,0:T(8,128)(2,1)} %pad_maximum_fusion.3), calls=%async_computation | async-start | bytes 2162688 | tf_op jit(solution)/shard_map/all_to_all | solution.py:705
  39.5 260.7 %all-gather.8.cloned.1.call-start = ((), (), s32[]{:S(2)}) async-start(), calls=%async_computation.10 | async-start | bytes 5898240 | tf_op jit(solution)/shard_map/all_gather | solution.py:804
  43.3 51.6 %collective-permute-start.8 = (bf16[2,256,512]{2,1,0:T(8,128)(2,1)S(1)}, bf16[2,256,512]{2,1,0:T(8,128)(2,1)S(1)}, u32[]{:S(2)}, u32[]{:S(2)}) collective-permute-start(bf16[2,256,512]{2,1,0:T(8,128)(2,1)S(1)} %get-tuple-element.165), channel_id=1, source_target_pairs={{0,16},{16,0},{1,17},{17,1},{2,18},{18,2},{3,19},{19,3},{4,20},{20... | collective-permute-start | bytes 1572872 | tf_op jit(solution)/shard_map/ppermute | solution.py:602
  96.1 44.1 %all-to-all-start.1 = ((bf16[4,256,512]{2,1,0:T(8,128)(2,1)}), bf16[4,256,512]{2,1,0:T(8,128)(2,1)S(1)}, u32[]{:S(2)}, u32[]{:S(2)}) async-start(bf16[4,256,512]{2,1,0:T(8,128)(2,1)} %bitcast.26), calls=%async_computation.1 | async-start | bytes 2097152 | tf_op jit(solution)/shard_map/all_to_all | solution.py:705
  101.8 257.0 %reduce-scatter.5.cloned.1.call-start = ((), (), s32[]{:S(2)}) async-start(), calls=%async_computation.11 | async-start | bytes 5898240 | tf_op jit(solution)/shard_map/reduce_scatter | solution.py:847
  109.6 34.8 %collective-permute-start.2 = (bf16[2,256,512]{2,1,0:T(8,128)(2,1)S(1)}, bf16[2,256,512]{2,1,0:T(8,128)(2,1)}, u32[]{:S(2)}, u32[]{:S(2)}) collective-permute-start(bf16[2,256,512]{2,1,0:T(8,128)(2,1)S(1)} %get-tuple-element.167.refs_0_.refs_2_), channel_id=1, source_target_pairs={{0,16},{16,0},{1,17},{17,1},{2,18},{18,2},{3,19},{19,3},{4,20},{20... | collective-permute-start | bytes 1572872 | tf_op jit(solution)/shard_map/ppermute | solution.py:602
  110.1 35.6 %collective-permute-start.6 = (bf16[2,256,512]{2,1,0:T(8,128)(2,1)S(1)}, bf16[2,256,512]{2,1,0:T(8,128)(2,1)}, u32[]{:S(2)}, u32[]{:S(2)}) collective-permute-start(bf16[2,256,512]{2,1,0:T(8,128)(2,1)S(1)} %get-tuple-element.166.refs_4_.refs_6_), channel_id=1, source_target_pairs={{0,4},{4,0},{1,5},{5,1},{2,6},{6,2},{3,7},{7,3},{8,12},{12,8},{9,1... | collective-permute-start | bytes 1572872 | tf_op jit(solution)/shard_map/ppermute | solution.py:602
  142.8 31.3 %collective-permute-start.13 = (bf16[2,256,512]{2,1,0:T(8,128)(2,1)S(1)}, bf16[2,256,512]{2,1,0:T(8,128)(2,1)S(1)}, u32[]{:S(2)}, u32[]{:S(2)}) collective-permute-start(bf16[2,256,512]{2,1,0:T(8,128)(2,1)S(1)} %get-tuple-element.162.refs_5_.refs_4_), channel_id=1, source_target_pairs={{0,16},{16,0},{1,17},{17,1},{2,18},{18,2},{3,19},{19,3},{4,20},{20... | collective-permute-start | bytes 1572872 | tf_op jit(solution)/shard_map/ppermute | solution.py:602
  144.3 29.7 %collective-permute-start.10 = (bf16[2,256,512]{2,1,0:T(8,128)(2,1)S(1)}, bf16[2,256,512]{2,1,0:T(8,128)(2,1)S(1)}, u32[]{:S(2)}, u32[]{:S(2)}) collective-permute-start(bf16[2,256,512]{2,1,0:T(8,128)(2,1)S(1)} %get-tuple-element.163.refs_1_.refs_0_), channel_id=1, source_target_pairs={{0,4},{4,0},{1,5},{5,1},{2,6},{6,2},{3,7},{7,3},{8,12},{12,8},{9,1... | collective-permute-start | bytes 1572872 | tf_op jit(solution)/shard_map/ppermute | solution.py:602
  145.8 46.1 %collective-permute-start.12 = (bf16[2,256,512]{2,1,0:T(8,128)(2,1)S(1)}, bf16[2,256,512]{2,1,0:T(8,128)(2,1)S(1)}, u32[]{:S(2)}, u32[]{:S(2)}) collective-permute-start(bf16[2,256,512]{2,1,0:T(8,128)(2,1)S(1)} %get-tuple-element.162.refs_5_.refs_4_), channel_id=1, source_target_pairs={{0,4},{4,0},{1,5},{5,1},{2,6},{6,2},{3,7},{7,3},{8,12},{12,8},{9,1... | collective-permute-start | bytes 1572872 | tf_op jit(solution)/shard_map/ppermute | solution.py:602
  146.4 45.6 %collective-permute-start.9 = (bf16[2,256,512]{2,1,0:T(8,128)(2,1)S(1)}, bf16[2,256,512]{2,1,0:T(8,128)(2,1)}, u32[]{:S(2)}, u32[]{:S(2)}) collective-permute-start(bf16[2,256,512]{2,1,0:T(8,128)(2,1)S(1)} %get-tuple-element.163.refs_1_.refs_0_), channel_id=1, source_target_pairs={{0,16},{16,0},{1,17},{17,1},{2,18},{18,2},{3,19},{19,3},{4,20},{20... | collective-permute-start | bytes 1572872 | tf_op jit(solution)/shard_map/ppermute | solution.py:602
  300.1 186.3 %reduce-scatter.7.cloned.1.call-start = ((), (), s32[]{:S(2)}) async-start(), calls=%async_computation.12 | async-start | bytes 11796480 | tf_op jit(solution)/shard_map/reduce_scatter | solution.py:847
  358.8 249.3 %reduce-scatter.9.cloned.1.call-start = ((), (), s32[]{:S(2)}) async-start(), calls=%async_computation.13 | async-start | bytes 2359296 | tf_op jit(solution)/shard_map/reduce_scatter | solution.py:847
  416.5 39.2 %collective-permute-start.35 = (bf16[2,2,256,512]{3,2,1,0:T(8,128)(2,1)}, bf16[2,2,256,512]{3,2,1,0:T(8,128)(2,1)}, u32[]{:S(2)}, u32[]{:S(2)}) collective-permute-start(bf16[2,2,256,512]{3,2,1,0:T(8,128)(2,1)} %get-tuple-element.110), channel_id=1, source_target_pairs={{0,4},{4,0},{1,5},{5,1},{2,6},{6,2},{3,7},{7,3},{8,12},{12,8},{9,1... | collective-permute-start | bytes 3145736 | tf_op jit(solution)/shard_map/ppermute | solution.py:602
  417.6 38.0 %collective-permute-start.37 = (bf16[2,2,256,512]{3,2,1,0:T(8,128)(2,1)}, bf16[2,2,256,512]{3,2,1,0:T(8,128)(2,1)}, u32[]{:S(2)}, u32[]{:S(2)}) collective-permute-start(bf16[2,2,256,512]{3,2,1,0:T(8,128)(2,1)} %get-tuple-element.118), channel_id=1, source_target_pairs={{0,16},{16,0},{1,17},{17,1},{2,18},{18,2},{3,19},{19,3},{4,20},{20... | collective-permute-start | bytes 3145736 | tf_op jit(solution)/shard_map/ppermute | solution.py:602
  457.0 29.3 %collective-permute-start.36 = (bf16[2,256,512]{2,1,0:T(8,128)(2,1)S(1)}, bf16[2,256,512]{2,1,0:T(8,128)(2,1)}, u32[]{:S(2)}, u32[]{:S(2)}) collective-permute-start(bf16[2,256,512]{2,1,0:T(8,128)(2,1)S(1)} %fusion.19), channel_id=1, source_target_pairs={{0,16},{16,0},{1,17},{17,1},{2,18},{18,2},{3,19},{19,3},{4,20},{20... | collective-permute-start | bytes 1572872 | tf_op jit(solution)/shard_map/ppermute | solution.py:602
  458.1 28.3 %collective-permute-start.42 = (bf16[640,512]{1,0:T(8,128)(2,1)}, bf16[640,512]{1,0:T(8,128)(2,1)}, u32[]{:S(2)}, u32[]{:S(2)}) collective-permute-start(bf16[640,512]{1,0:T(8,128)(2,1)} %reduce-scatter.5.cloned.1.call-done.refs_0_), channel_id=1, source_target_pairs={{0,16},{16,0},{1,17},{17,1},{2,18},{18,2},{3,19},{19,3},{4,20},{20... | collective-permute-start | bytes 1966088 | tf_op jit(solution)/shard_map/ppermute | solution.py:602
  490.6 43.0 %all-to-all-start.2 = ((bf16[4,256,512]{2,1,0:T(8,128)(2,1)}), bf16[4,256,512]{2,1,0:T(8,128)(2,1)S(1)}, u32[]{:S(2)}, u32[]{:S(2)}) async-start(bf16[4,256,512]{2,1,0:T(8,128)(2,1)} %fusion.13), calls=%async_computation.2 | async-start | bytes 2097152 | tf_op jit(solution)/shard_map/all_to_all | solution.py:710
  495.8 136.8 %reduce-scatter.11.cloned.1.call-start = ((), (), s32[]{:S(2)}) async-start(), calls=%async_computation.14 | async-start | bytes 7077888 | tf_op jit(solution)/shard_map/reduce_scatter | solution.py:847
  561.5 46.0 %all-to-all-start.3 = ((bf16[4,256,512]{2,1,0:T(8,128)(2,1)}), bf16[4,256,512]{2,1,0:T(8,128)(2,1)S(1)}, u32[]{:S(2)}, u32[]{:S(2)}) async-start(bf16[4,256,512]{2,1,0:T(8,128)(2,1)} %fusion.9), calls=%async_computation.4 | async-start | bytes 2097152 | tf_op jit(solution)/shard_map/all_to_all | solution.py:710
  565.5 44.2 %collective-permute-start.59 = (bf16[1280,512]{1,0:T(8,128)(2,1)S(1)}, bf16[1280,512]{1,0:T(8,128)(2,1)}, u32[]{:S(2)}, u32[]{:S(2)}) collective-permute-start(bf16[1280,512]{1,0:T(8,128)(2,1)S(1)} %copy-done.27), channel_id=1, source_target_pairs={{0,16},{16,0},{1,17},{17,1},{2,18},{18,2},{3,19},{19,3},{4,20},{20... | collective-permute-start | bytes 3932168 | tf_op jit(solution)/shard_map/ppermute | solution.py:602
  566.9 43.4 %collective-permute-start.39 = (bf16[2,256,512]{2,1,0:T(8,128)(2,1)}, bf16[2,256,512]{2,1,0:T(8,128)(2,1)}, u32[]{:S(2)}, u32[]{:S(2)}) collective-permute-start(bf16[2,256,512]{2,1,0:T(8,128)(2,1)} %dynamic-slice_bitcast_fusion.1), channel_id=1, source_target_pairs={{0,16},{16,0},{1,17},{17,1},{2,18},{18,2},{3,19},{19,3},{4,20},{20... | collective-permute-start | bytes 1572872 | tf_op jit(solution)/shard_map/ppermute | solution.py:602
  (97 other events, 1426.6 us)
Sparse Core Ops, SparseCore 0:
  11.7 129.7 all-gather.3
  143.7 97.5 all-gather.5
  242.9 54.3 all-gather.7
  300.2 58.5 reduce-scatter.4
  361.5 107.7 reduce-scatter.6
  486.5 52.5 reduce-scatter.8
  542.0 88.1 reduce-scatter.10

commit v11 on v10

--- a/solution.py
+++ b/solution.py
@@ -692,7 +692,7 @@
     return [part, hop(part, "c"), over_y, hop(over_y, "c")], over_y
 
 
-def share_plain(part, *beside):
+def share_plain(part):
     return lax.all_gather(part, ("y", "c"), axis=0), part
 
 
@@ -892,26 +892,27 @@
     out_partial = tn(attended, grad_branch, starts)
     grad_attended = after(grad_attended, out_partial)
     branch_parts = [after(part, *branch_here) for part in branch_parts]
+    down_pieces, down_last = shared(after(down_part, *branch_here))
     if fits:
         first = backward(0, projected, length, table, near, grad_attended, lse[0])
-        branch, branch_first, branch_last = scatter(branch_parts, (first[0],))
+        branch, branch_first, branch_last = scatter(branch_parts, (first[0], down_last))
     else:
         branch, branch_first, branch_last = scatter(branch_parts)
-    down_pieces, down_last = shared(after(down_part, *branch_here))
     if fits:
         second = backward(
-            1, after(projected, first[0], *branch_first), length, table, near, grad_attended, lse[1]
+            1, after(projected, first[0], *branch_last), length, table, near, grad_attended, lse[1]
         )
         grad_projected, table_part = (first[0], second[0]), (first[1], second[1])
     else:
         grads, table_part = backward(projected, length, table, grad_attended, lse, nc, heads)
         grad_projected, table_part = (grads,), table_part[:, :, 0]
-    out_part = reduce(after(out_partial, gate_up_part, grad_projected[-1], *branch_last, down_last))
+    out_part = reduce(after(out_partial, gate_up_part, grad_projected[0], *branch_last))
     outputs = (live * (hidden + branch)).astype(BF)
     outputs, _ = from_groups(outputs)
+    qkv_partial = tn(grad_projected, normed, starts)
+    gate_up_pieces, gate_up_last = shared(after(gate_up_part, grad_projected[0]))
+    qkv_part = reduce(after(qkv_partial, out_part, gate_up_last, outputs[0]))
     one_parts = nn(grad_projected, w_attn, 0, qkv_count, starts)
-    last = after(grad_projected[-1], one_parts[0])
-    qkv_partial = tn([*grad_projected[:-1], last], normed, starts)
     if fits:
         here = jnp.stack([y, c]).astype(jnp.int32)
 
@@ -934,30 +935,28 @@
                     outs[0][u, i] = source[first : first + unit, :].astype(F32)
 
         (down_all,) = place(down_pieces, here, [(units * unit, width)], write_rows)
-    beside = (qkv_partial, down_all, outputs[0]) if fits else ()
+        (gate_up_all,) = place(gate_up_pieces, here, [(units, 2, unit, width)], write_gate_up)
+    beside = (down_all, gate_up_all, outputs[0]) if fits else ()
     table_part = table_sums(table_part, 4 * count) if fits else table_part
-    grad_one, one_first, one_last = scatter(one_parts, beside, (table_part,))
-    qkv_part = reduce(after(qkv_partial, gate_up_part, *one_first))
+    grad_one, _, one_last = scatter(one_parts, beside, (table_part,))
     through, attn_gain_part = norm_back(tokens, scale_one, gain_one, grad_one)
     input_grad, input_leaves = from_groups((grad_hidden + through).astype(BF))
 
     out_pieces, out_last = shared(out_part)
-    gate_up_pieces, _ = shared(after(gate_up_part, *one_first), input_leaves)
 
     every = jnp.zeros((nx * 2 * local_heads, table_part.shape[1]), F32)
     every = lax.dynamic_update_slice_in_dim(every, table_part, (x * 2 + y) * local_heads, 0)
     spare = -every.size % width
     every = jnp.pad(every.reshape(-1), (0, spare)).reshape(-1, width)
-    sums = sum_plane(jnp.concatenate([attn_gain_part, ffn_gain_part, every]), nx, out_last, outputs[1], input_grad[1])
+    sums = sum_plane(jnp.concatenate([attn_gain_part, ffn_gain_part, every]), nx, out_last, outputs[1])
     all_sums = sum_line(after(sums, input_leaves), nz)
     attn_gain_grad, ffn_gain_grad = all_sums[:nz], all_sums[nz : 2 * nz]
     every = all_sums[2 * nz :].reshape(-1)[: nx * 2 * local_heads * buckets].reshape(-1, buckets)
 
     outputs = stored_from(outputs, BF)
     if fits:
-        (gate_up_all,) = place(gate_up_pieces, here, [(units, 2, unit, width)], write_gate_up)
         (out_all,) = place(out_pieces, here, [(heads * 64, width)], write_rows)
-        qkv_pieces, _ = shared(after(qkv_part, sums, *one_last), out_all, gate_up_all, outputs, input_leaves)
+        qkv_pieces, _ = shared(after(qkv_part, sums, *one_last), out_all, outputs, input_leaves)
         query_key_all, value_all = place(
             qkv_pieces, here, [(heads, 2, 64, width), (heads, 64, width)], write_qkv
         )

time: 679 us -> 670 us (0.987)
  waiting for transfers between devices: 252 us -> 241 us
    all_to_all x2, waiting for transfers between devices: 43.2 us -> 0.01 us  [from_groups(): lax.all_to_all(mine, 'z', 0, 0, tiled=True).reshape(2, nz // 2, t, width)]
    ppermute x59, waiting for transfers between devices: 138 us -> 161 us  [hop(): return lax.ppermute(value, axis, swap)]
  transfers between devices with their start and end apart: 73 -> 73, of which waited for: 29 -> 32; matrix products, arithmetic and copies ran while one was open for 9% -> 9% of each run, Pallas kernels for 37% -> 38%
where the time goes in v11:
time: 670 us; the launch traced here: 665 us
  Pallas kernels  256 us (38%)
  waiting for transfers between devices  241 us (36%)
  starting transfers between devices  88 us (13%)
  other arithmetic  47.6 us (7%)
  local copies, waits for them, and re-layouts  16.9 us (3%)
  between operations  15.4 us (2%)
    ppermute x59, waiting for transfers between devices, hop(): return lax.ppermute(value, axis, swap)  161 us
    all_to_all x2, waiting for transfers between devices, to_groups(): return lax.all_to_all(both, 'z', 0, 0, tiled=True)  66.1 us
    ppermute x59, starting transfers between devices, hop(): return lax.ppermute(value, axis, swap)  60.2 us
    pallas_call x2, Pallas kernels, attend_back(): pl.pallas_call(functools.partial(attend_back_kernel, group), grid=(1,), i...  49.5 us
    pallas_call x4, Pallas kernels, mm_nn(): pl.pallas_call(functools.partial(nn_kernel, len(grads)), grid=(nz,), in_s...  44.7 us
    pallas_call x4, Pallas kernels, mm_tn(): pl.pallas_call(functools.partial(tn_kernel, count), grid=(count * steps,)...  43.4 us
    pallas_call x2, Pallas kernels, attend(): pl.pallas_call(functools.partial(attend_kernel, group), grid=(1,), in_spe...  30.1 us
    pallas_call x4, Pallas kernels, place(): pl.pallas_call(functools.partial(place_kernel, write), grid=(4,), in_spec...  19.5 us
  transfers between devices with their start and end apart: 73, of which 32 were waited for; matrix products, arithmetic and copies ran while one was open for 9% of the time, Pallas kernels for 38%

profile of v11, /device:TPU:0, one launch (start us, length us, event | category | flops | bytes accessed | tf_op | source)
XLA Modules:
  0.0 665.0 jit_solution(2892280829788321183)
XLA Ops:
  16.7 12.2 %collective-permute-done.1 = bf16[2,256,512]{2,1,0:T(8,128)(2,1)} collective-permute-done((bf16[2,256,512]{2,1,0:T(8,128)(2,1)}, bf16[2,256,512]{2,1,0:T(8,128)(2,1)}, u32[]{:S(2)}, u32[]{:S(2)}) %collective-permute-start.1) | collective-permute-done | bytes 524320 | tf_op jit(solution)/shard_map/ppermute | solution.py:602
  45.1 49.8 %all-to-all-done = bf16[4,264,512]{2,1,0:T(8,128)(2,1)} async-done(((bf16[4,264,512]{2,1,0:T(8,128)(2,1)}), bf16[4,264,512]{2,1,0:T(8,128)(2,1)}, u32[]{:S(2)}, u32[]{:S(2)}) %all-to-all-start) | async-done | bytes 1081376 | tf_op jit(solution)/shard_map/all_to_all | solution.py:705
  123.9 16.3 %all-to-all-done.1 = bf16[4,256,512]{2,1,0:T(8,128)(2,1)S(1)} async-done(((bf16[4,256,512]{2,1,0:T(8,128)(2,1)}), bf16[4,256,512]{2,1,0:T(8,128)(2,1)S(1)}, u32[]{:S(2)}, u32[]{:S(2)}) %all-to-all-start.1) | async-done | bytes 1048608 | tf_op jit(solution)/shard_map/all_to_all | solution.py:705
  146.9 12.1 %product_nt.2.q_ref.k_ref.v_ref = bf16[1024,1536]{1,0:T(8,128)(2,1)} custom-call(s32[4]{0:T(128)} %add_multiply_fusion.starts_ref, bf16[2,256,512]{2,1,0:T(8,128)(2,1)} %copy-done.10, bf16[2,256,512]{2,1,0:T(8,128)(2,1)} %collective-permute-done.2.refs_1_.refs_3_, bf16[2,256,512]{2,1,0:T(8,128)(2,1)} %collective-permute-done.3.refs_2_.refs_4_, ...), custom_call_target="tpu_custom_call" | custom-call | flops 402653184 | bytes 851968 | tf_op jit(solution)/shard_map/product_nt/pallas_call | solution.py:78
  159.0 15.0 %attend.2 = (bf16[1024,256]{1,0:T(8,128)(2,1)}, f32[8,1024]{1,0:T(8,128)}) custom-call(s32[1]{0:T(128)} %dynamic_slice.51.length_ref, f32[8,32]{1,0:T(8,128)} %constant_dynamic-slice_fusion.4.table_ref, f32[8,384,128]{2,1,0:T(8,128)} %near_bias.1.near_ref, bf16[1024,1536]{1,0:T(8,128)(2,1)} %product_nt.2.q_ref.k_ref.v_ref, ...), custom_call_target="tpu_custom_call" | custom-call | flops 268435456 | bytes 131072 | tf_op jit(solution)/shard_map/attend/pallas_call | solution.py:497
  176.9 15.1 %attend.3 = (bf16[1024,256]{1,0:T(8,128)(2,1)}, f32[8,1024]{1,0:T(8,128)}) custom-call(s32[1]{0:T(128)} %dynamic_slice.51.length_ref, f32[8,32]{1,0:T(8,128)} %constant_dynamic-slice_fusion.4.table_ref, f32[8,384,128]{2,1,0:T(8,128)} %near_bias.1.near_ref, bf16[1024,1536]{1,0:T(8,128)(2,1)} %product_nt.2.q_ref.k_ref.v_ref, ...), custom_call_target="tpu_custom_call" | custom-call | flops 268435456 | bytes 131072 | tf_op jit(solution)/shard_map/attend/pallas_call | solution.py:497
  200.4 22.3 %collective-permute-done.15 = bf16[2,2,256,512]{3,2,1,0:T(8,128)(2,1)S(1)} collective-permute-done((bf16[2,2,256,512]{3,2,1,0:T(8,128)(2,1)}, bf16[2,2,256,512]{3,2,1,0:T(8,128)(2,1)S(1)}, u32[]{:S(2)}, u32[]{:S(2)}) %collective-permute-start.15) | collective-permute-done | bytes 1048608 | tf_op jit(solution)/shard_map/ppermute | solution.py:602
  226.4 8.9 %collective-permute-done.16 = bf16[2,256,512]{2,1,0:T(8,128)(2,1)S(1)} collective-permute-done((bf16[2,256,512]{2,1,0:T(8,128)(2,1)S(1)}, bf16[2,256,512]{2,1,0:T(8,128)(2,1)S(1)}, u32[]{:S(2)}, u32[]{:S(2)}) %collective-permute-start.16) | collective-permute-done | bytes 524320 | tf_op jit(solution)/shard_map/ppermute | solution.py:602
  243.0 10.8 %collective-permute-done.20.refs_2_.refs_3_ = bf16[2,256,512]{2,1,0:T(8,128)(2,1)S(1)} collective-permute-done((bf16[2,256,512]{2,1,0:T(8,128)(2,1)S(1)}, bf16[2,256,512]{2,1,0:T(8,128)(2,1)S(1)}, u32[]{:S(2)}, u32[]{:S(2)}) %collective-permute-start.20) | collective-permute-done | bytes 524320 | tf_op jit(solution)/shard_map/ppermute | solution.py:602
  255.9 9.6 %collective-permute-done.19.refs_1_.refs_2_ = bf16[2,256,512]{2,1,0:T(8,128)(2,1)S(1)} collective-permute-done((bf16[2,256,512]{2,1,0:T(8,128)(2,1)S(1)}, bf16[2,256,512]{2,1,0:T(8,128)(2,1)S(1)}, u32[]{:S(2)}, u32[]{:S(2)}) %collective-permute-start.19) | collective-permute-done | bytes 524320 | tf_op jit(solution)/shard_map/ppermute | solution.py:602
  272.5 17.6 %ffn_in.1 = (bf16[1024,1280]{1,0:T(8,128)(2,1)}, bf16[1024,1280]{1,0:T(8,128)(2,1)}, bf16[1024,1280]{1,0:T(8,128)(2,1)}) custom-call(s32[4]{0:T(128)} %add_multiply_fusion.starts_ref, bf16[2,256,512]{2,1,0:T(8,128)(2,1)} %copy-done.8, bf16[2,256,512]{2,1,0:T(8,128)(2,1)} %copy-done.18, bf16[2,256,512]{2,1,0:T(8,128)(2,1)} %copy-done.16, ...), custom_call_target="tpu_custom_call" | custom-call | flops 671088640 | bytes 1409024 | tf_op jit(solution)/shard_map/ffn_in/pallas_call | solution.py:214
  290.1 9.9 %product_tn.4 = bf16[4,1280,512]{2,1,0:T(8,128)(2,1)} custom-call(s32[4]{0:T(128)} %add_multiply_fusion.starts_ref, bf16[1024,1280]{1,0:T(8,128)(2,1)} %get-tuple-element.100.refs_0_, bf16[2,256,512]{2,1,0:T(8,128)(2,1)} %copy-done.6, bf16[2,256,512]{2,1,0:T(8,128)(2,1)} %collective-permute-done.9.refs_2_.refs_1_, bf16[2,256,512]{2,1,0:T(8,128)(2,1)} %copy-done.14, ...), custom_call_target="tpu_custom_call" | custom-call | flops 335544320 | bytes 753664 | tf_op jit(solution)/shard_map/product_tn/pallas_call | solution.py:171
  300.2 15.2 %ffn_back.1.refs_0_ = bf16[1024,2560]{1,0:T(8,128)(2,1)} custom-call(s32[4]{0:T(128)} %add_multiply_fusion.starts_ref, bf16[2,256,512]{2,1,0:T(8,128)(2,1)} %copy-done.6, bf16[2,256,512]{2,1,0:T(8,128)(2,1)} %collective-permute-done.9.refs_2_.refs_1_, bf16[2,256,512]{2,1,0:T(8,128)(2,1)} %copy-done.14, ...), custom_call_target="tpu_custom_call" | custom-call | flops 335544320 | bytes 1245184 | tf_op jit(solution)/shard_map/ffn_back/pallas_call | solution.py:245
  315.3 16.4 %product_nn.5 = (bf16[2,2,256,512]{3,2,1,0:T(8,128)(2,1)}, bf16[2,2,256,512]{3,2,1,0:T(8,128)(2,1)}, bf16[2,2,256,512]{3,2,1,0:T(8,128)(2,1)}, bf16[2,2,256,512]{3,2,1,0:T(8,128)(2,1)}) custom-call(s32[4]{0:T(128)} %add_multiply_fusion.starts_ref, bf16[1024,2560]{1,0:T(8,128)(2,1)} %ffn_back.1.refs_0_, bf16[4,2,1280,512]{3,2,1,0:T(8,128)(2,1)} %bitcast.101), custom_call_target="tpu_custom_call" | custom-call | flops 671088640 | bytes 1245184 | tf_op jit(solution)/shard_map/product_nn/pallas_call | solution.py:123
  335.2 15.9 %product_tn.5 = bf16[4,2560,512]{2,1,0:T(8,128)(2,1)} custom-call(s32[4]{0:T(128)} %add_multiply_fusion.starts_ref, bf16[1024,2560]{1,0:T(8,128)(2,1)} %ffn_back.1.refs_0_, bf16[2,256,512]{2,1,0:T(8,128)(2,1)} %copy-done.8, bf16[2,256,512]{2,1,0:T(8,128)(2,1)} %copy-done.18, bf16[2,256,512]{2,1,0:T(8,128)(2,1)} %copy-done.16, ...), custom_call_target="tpu_custom_call" | custom-call | flops 671088640 | bytes 1245184 | tf_op jit(solution)/shard_map/product_tn/pallas_call | solution.py:171
  366.0 10.2 %product_nn.6 = (bf16[2,2,256,512]{3,2,1,0:T(8,128)(2,1)}, bf16[2,2,256,512]{3,2,1,0:T(8,128)(2,1)}, bf16[2,2,256,512]{3,2,1,0:T(8,128)(2,1)}, bf16[2,2,256,512]{3,2,1,0:T(8,128)(2,1)}) custom-call(s32[4]{0:T(128)} %add_multiply_fusion.starts_ref, bf16[1024,1280]{1,0:T(8,128)(2,1)} %get-tuple-element.100.refs_0_, bf16[4,2,640,512]{3,2,1,0:T(8,128)(2,1)} %bitcast.106), custom_call_target="tpu_custom_call" | custom-call | flops 335544320 | bytes 753664 | tf_op jit(solution)/shard_map/product_nn/pallas_call | solution.py:123
  386.3 10.8 %collective-permute-done.30.refs_2_.refs_4_ = bf16[2,256,512]{2,1,0:T(8,128)(2,1)S(1)} collective-permute-done((bf16[2,256,512]{2,1,0:T(8,128)(2,1)S(1)}, bf16[2,256,512]{2,1,0:T(8,128)(2,1)S(1)}, u32[]{:S(2)}, u32[]{:S(2)}) %collective-permute-start.30) | collective-permute-done | bytes 524320 | tf_op jit(solution)/shard_map/ppermute | solution.py:602
  399.1 10.5 %collective-permute-done.29.refs_1_.refs_3_ = bf16[2,256,512]{2,1,0:T(8,128)(2,1)S(1)} collective-permute-done((bf16[2,256,512]{2,1,0:T(8,128)(2,1)S(1)}, bf16[2,256,512]{2,1,0:T(8,128)(2,1)S(1)}, u32[]{:S(2)}, u32[]{:S(2)}) %collective-permute-start.29) | collective-permute-done | bytes 524320 | tf_op jit(solution)/shard_map/ppermute | solution.py:602
  432.0 24.8 %attend_back.2 = (bf16[1024,768]{1,0:T(8,128)(2,1)}, f32[4,400,128]{2,1,0:T(8,128)}) custom-call(s32[1]{0:T(128)} %dynamic_slice.51.length_ref, f32[8,32]{1,0:T(8,128)} %constant_dynamic-slice_fusion.4.table_ref, f32[8,384,128]{2,1,0:T(8,128)} %near_bias.1.near_ref, bf16[1024,1536]{1,0:T(8,128)(2,1)} %product_nt.2.q_ref.k_ref.v_ref, ...), custom_call_target="tpu_custom_call" | custom-call | flops 671088640 | bytes 262144 | tf_op jit(solution)/shard_map/attend_back/pallas_call | solution.py:524
  482.7 24.7 %attend_back.3 = (bf16[1024,768]{1,0:T(8,128)(2,1)}, f32[4,400,128]{2,1,0:T(8,128)}) custom-call(s32[1]{0:T(128)} %dynamic_slice.51.length_ref, f32[8,32]{1,0:T(8,128)} %constant_dynamic-slice_fusion.4.table_ref, f32[8,384,128]{2,1,0:T(8,128)} %near_bias.1.near_ref, bf16[1024,1536]{1,0:T(8,128)(2,1)} %product_nt.2.q_ref.k_ref.v_ref, ...), custom_call_target="tpu_custom_call" | custom-call | flops 671088640 | bytes 262144 | tf_op jit(solution)/shard_map/attend_back/pallas_call | solution.py:524
  507.5 11.4 %product_tn.7 = bf16[4,1536,512]{2,1,0:T(8,128)(2,1)} custom-call(s32[4]{0:T(128)} %add_multiply_fusion.starts_ref, bf16[1024,768]{1,0:T(8,128)(2,1)} %get-tuple-element.111.refs_0_, bf16[1024,768]{1,0:T(8,128)(2,1)} %get-tuple-element.121.refs_1_, bf16[2,256,512]{2,1,0:T(8,128)(2,1)} %copy-done.10, ...), custom_call_target="tpu_custom_call" | custom-call | flops 402653184 | bytes 851968 | tf_op jit(solution)/shard_map/product_tn/pallas_call | solution.py:171
  526.0 11.1 %product_nn.7 = (bf16[2,2,256,512]{3,2,1,0:T(8,128)(2,1)}, bf16[2,2,256,512]{3,2,1,0:T(8,128)(2,1)}, bf16[2,2,256,512]{3,2,1,0:T(8,128)(2,1)}, bf16[2,2,256,512]{3,2,1,0:T(8,128)(2,1)}) custom-call(s32[4]{0:T(128)} %add_multiply_fusion.starts_ref, bf16[1024,768]{1,0:T(8,128)(2,1)} %get-tuple-element.111.refs_0_, ...), custom_call_target="tpu_custom_call" | custom-call | flops 402653184 | bytes 851968 | tf_op jit(solution)/shard_map/product_nn/pallas_call | solution.py:123
  554.5 8.2 %collective-permute-done.41 = bf16[2,2,256,512]{3,2,1,0:T(8,128)(2,1)} collective-permute-done((bf16[2,2,256,512]{3,2,1,0:T(8,128)(2,1)}, bf16[2,2,256,512]{3,2,1,0:T(8,128)(2,1)}, u32[]{:S(2)}, u32[]{:S(2)}) %collective-permute-start.41) | collective-permute-done | bytes 1048608 | tf_op jit(solution)/shard_map/ppermute | solution.py:602
  596.0 12.6 %collective-permute-done.40.other_ref = bf16[2,256,512]{2,1,0:T(8,128)(2,1)S(1)} collective-permute-done((bf16[2,256,512]{2,1,0:T(8,128)(2,1)S(1)}, bf16[2,256,512]{2,1,0:T(8,128)(2,1)S(1)}, u32[]{:S(2)}, u32[]{:S(2)}) %collective-permute-start.40) | collective-permute-done | bytes 524320 | tf_op jit(solution)/shard_map/ppermute | solution.py:602
  (329 shorter events, 277.9 us)
Async XLA Ops:
  7.2 134.3 %all-gather.4.cloned.1.call-start = ((), (), s32[]{:S(2)}) async-start(), calls=%async_computation.8 | async-start | bytes 9437184 | tf_op jit(solution)/shard_map/all_gather | solution.py:804
  11.6 261.0 %all-gather.6.cloned.1.call-start = ((), (), s32[]{:S(2)}) async-start(), calls=%async_computation.9 | async-start | bytes 11796480 | tf_op jit(solution)/shard_map/all_gather | solution.py:804
  34.3 60.7 %all-to-all-start = ((bf16[4,264,512]{2,1,0:T(8,128)(2,1)}), bf16[4,264,512]{2,1,0:T(8,128)(2,1)}, u32[]{:S(2)}, u32[]{:S(2)}) async-start(bf16[4,264,512]{2,1,0:T(8,128)(2,1)} %pad_maximum_fusion.3), calls=%async_computation | async-start | bytes 2162688 | tf_op jit(solution)/shard_map/all_to_all | solution.py:705
  39.5 260.7 %all-gather.8.cloned.1.call-start = ((), (), s32[]{:S(2)}) async-start(), calls=%async_computation.10 | async-start | bytes 5898240 | tf_op jit(solution)/shard_map/all_gather | solution.py:804
  43.3 51.6 %collective-permute-start.8 = (bf16[2,256,512]{2,1,0:T(8,128)(2,1)S(1)}, bf16[2,256,512]{2,1,0:T(8,128)(2,1)S(1)}, u32[]{:S(2)}, u32[]{:S(2)}) collective-permute-start(bf16[2,256,512]{2,1,0:T(8,128)(2,1)S(1)} %get-tuple-element.161), channel_id=1, source_target_pairs={{0,16},{16,0},{1,17},{17,1},{2,18},{18,2},{3,19},{19,3},{4,20},{20... | collective-permute-start | bytes 1572872 | tf_op jit(solution)/shard_map/ppermute | solution.py:602
  96.1 44.1 %all-to-all-start.1 = ((bf16[4,256,512]{2,1,0:T(8,128)(2,1)}), bf16[4,256,512]{2,1,0:T(8,128)(2,1)S(1)}, u32[]{:S(2)}, u32[]{:S(2)}) async-start(bf16[4,256,512]{2,1,0:T(8,128)(2,1)} %bitcast.26), calls=%async_computation.1 | async-start | bytes 2097152 | tf_op jit(solution)/shard_map/all_to_all | solution.py:705
  101.8 257.0 %reduce-scatter.5.cloned.1.call-start = ((), (), s32[]{:S(2)}) async-start(), calls=%async_computation.11 | async-start | bytes 5898240 | tf_op jit(solution)/shard_map/reduce_scatter | solution.py:847
  109.6 34.8 %collective-permute-start.2 = (bf16[2,256,512]{2,1,0:T(8,128)(2,1)S(1)}, bf16[2,256,512]{2,1,0:T(8,128)(2,1)}, u32[]{:S(2)}, u32[]{:S(2)}) collective-permute-start(bf16[2,256,512]{2,1,0:T(8,128)(2,1)S(1)} %get-tuple-element.163.refs_0_.refs_2_), channel_id=1, source_target_pairs={{0,16},{16,0},{1,17},{17,1},{2,18},{18,2},{3,19},{19,3},{4,20},{20... | collective-permute-start | bytes 1572872 | tf_op jit(solution)/shard_map/ppermute | solution.py:602
  110.1 35.6 %collective-permute-start.6 = (bf16[2,256,512]{2,1,0:T(8,128)(2,1)S(1)}, bf16[2,256,512]{2,1,0:T(8,128)(2,1)}, u32[]{:S(2)}, u32[]{:S(2)}) collective-permute-start(bf16[2,256,512]{2,1,0:T(8,128)(2,1)S(1)} %get-tuple-element.162.refs_4_.refs_6_), channel_id=1, source_target_pairs={{0,4},{4,0},{1,5},{5,1},{2,6},{6,2},{3,7},{7,3},{8,12},{12,8},{9,1... | collective-permute-start | bytes 1572872 | tf_op jit(solution)/shard_map/ppermute | solution.py:602
  142.8 31.3 %collective-permute-start.13 = (bf16[2,256,512]{2,1,0:T(8,128)(2,1)S(1)}, bf16[2,256,512]{2,1,0:T(8,128)(2,1)S(1)}, u32[]{:S(2)}, u32[]{:S(2)}) collective-permute-start(bf16[2,256,512]{2,1,0:T(8,128)(2,1)S(1)} %get-tuple-element.158.refs_5_.refs_4_), channel_id=1, source_target_pairs={{0,16},{16,0},{1,17},{17,1},{2,18},{18,2},{3,19},{19,3},{4,20},{20... | collective-permute-start | bytes 1572872 | tf_op jit(solution)/shard_map/ppermute | solution.py:602
  144.3 29.7 %collective-permute-start.10 = (bf16[2,256,512]{2,1,0:T(8,128)(2,1)S(1)}, bf16[2,256,512]{2,1,0:T(8,128)(2,1)S(1)}, u32[]{:S(2)}, u32[]{:S(2)}) collective-permute-start(bf16[2,256,512]{2,1,0:T(8,128)(2,1)S(1)} %get-tuple-element.159.refs_1_.refs_0_), channel_id=1, source_target_pairs={{0,4},{4,0},{1,5},{5,1},{2,6},{6,2},{3,7},{7,3},{8,12},{12,8},{9,1... | collective-permute-start | bytes 1572872 | tf_op jit(solution)/shard_map/ppermute | solution.py:602
  145.8 46.1 %collective-permute-start.12 = (bf16[2,256,512]{2,1,0:T(8,128)(2,1)S(1)}, bf16[2,256,512]{2,1,0:T(8,128)(2,1)S(1)}, u32[]{:S(2)}, u32[]{:S(2)}) collective-permute-start(bf16[2,256,512]{2,1,0:T(8,128)(2,1)S(1)} %get-tuple-element.158.refs_5_.refs_4_), channel_id=1, source_target_pairs={{0,4},{4,0},{1,5},{5,1},{2,6},{6,2},{3,7},{7,3},{8,12},{12,8},{9,1... | collective-permute-start | bytes 1572872 | tf_op jit(solution)/shard_map/ppermute | solution.py:602
  146.4 45.6 %collective-permute-start.9 = (bf16[2,256,512]{2,1,0:T(8,128)(2,1)S(1)}, bf16[2,256,512]{2,1,0:T(8,128)(2,1)}, u32[]{:S(2)}, u32[]{:S(2)}) collective-permute-start(bf16[2,256,512]{2,1,0:T(8,128)(2,1)S(1)} %get-tuple-element.159.refs_1_.refs_0_), channel_id=1, source_target_pairs={{0,16},{16,0},{1,17},{17,1},{2,18},{18,2},{3,19},{19,3},{4,20},{20... | collective-permute-start | bytes 1572872 | tf_op jit(solution)/shard_map/ppermute | solution.py:602
  300.1 169.5 %reduce-scatter.7.cloned.1.call-start = ((), (), s32[]{:S(2)}) async-start(), calls=%async_computation.12 | async-start | bytes 11796480 | tf_op jit(solution)/shard_map/reduce_scatter | solution.py:847
  358.8 164.8 %reduce-scatter.9.cloned.1.call-start = ((), (), s32[]{:S(2)}) async-start(), calls=%async_computation.13 | async-start | bytes 2359296 | tf_op jit(solution)/shard_map/reduce_scatter | solution.py:847
  383.6 26.0 %collective-permute-start.29 = (bf16[2,256,512]{2,1,0:T(8,128)(2,1)S(1)}, bf16[2,256,512]{2,1,0:T(8,128)(2,1)S(1)}, u32[]{:S(2)}, u32[]{:S(2)}) collective-permute-start(bf16[2,256,512]{2,1,0:T(8,128)(2,1)S(1)} %get-tuple-element.155.refs_0_.refs_2_), channel_id=1, source_target_pairs={{0,16},{16,0},{1,17},{17,1},{2,18},{18,2},{3,19},{19,3},{4,20},{20... | collective-permute-start | bytes 1572872 | tf_op jit(solution)/shard_map/ppermute | solution.py:602
  416.4 40.3 %collective-permute-start.35 = (bf16[2,2,256,512]{3,2,1,0:T(8,128)(2,1)}, bf16[2,2,256,512]{3,2,1,0:T(8,128)(2,1)}, u32[]{:S(2)}, u32[]{:S(2)}) collective-permute-start(bf16[2,2,256,512]{3,2,1,0:T(8,128)(2,1)} %get-tuple-element.108), channel_id=1, source_target_pairs={{0,4},{4,0},{1,5},{5,1},{2,6},{6,2},{3,7},{7,3},{8,12},{12,8},{9,1... | collective-permute-start | bytes 3145736 | tf_op jit(solution)/shard_map/ppermute | solution.py:602
  417.7 41.3 %collective-permute-start.38 = (bf16[2,2,256,512]{3,2,1,0:T(8,128)(2,1)}, bf16[2,2,256,512]{3,2,1,0:T(8,128)(2,1)}, u32[]{:S(2)}, u32[]{:S(2)}) collective-permute-start(bf16[2,2,256,512]{3,2,1,0:T(8,128)(2,1)} %get-tuple-element.117), channel_id=1, source_target_pairs={{0,16},{16,0},{1,17},{17,1},{2,18},{18,2},{3,19},{19,3},{4,20},{20... | collective-permute-start | bytes 3145736 | tf_op jit(solution)/shard_map/ppermute | solution.py:602
  418.6 38.2 %collective-permute-start.36 = (bf16[640,512]{1,0:T(8,128)(2,1)}, bf16[640,512]{1,0:T(8,128)(2,1)}, u32[]{:S(2)}, u32[]{:S(2)}) collective-permute-start(bf16[640,512]{1,0:T(8,128)(2,1)} %reduce-scatter.5.cloned.1.call-done.refs_0_), channel_id=1, source_target_pairs={{0,16},{16,0},{1,17},{17,1},{2,18},{18,2},{3,19},{19,3},{4,20},{20... | collective-permute-start | bytes 1966088 | tf_op jit(solution)/shard_map/ppermute | solution.py:602
  473.8 45.1 %all-to-all-start.2 = ((bf16[4,256,512]{2,1,0:T(8,128)(2,1)}), bf16[4,256,512]{2,1,0:T(8,128)(2,1)S(1)}, u32[]{:S(2)}, u32[]{:S(2)}) async-start(bf16[4,256,512]{2,1,0:T(8,128)(2,1)} %fusion.13), calls=%async_computation.3 | async-start | bytes 2097152 | tf_op jit(solution)/shard_map/all_to_all | solution.py:710
  481.0 138.8 %reduce-scatter.11.cloned.1.call-start = ((), (), s32[]{:S(2)}) async-start(), calls=%async_computation.14 | async-start | bytes 7077888 | tf_op jit(solution)/shard_map/reduce_scatter | solution.py:847
  481.0 37.9 %collective-permute-start.45 = (bf16[1280,512]{1,0:T(8,128)(2,1)S(1)}, bf16[1280,512]{1,0:T(8,128)(2,1)}, u32[]{:S(2)}, u32[]{:S(2)}) collective-permute-start(bf16[1280,512]{1,0:T(8,128)(2,1)S(1)} %copy-done.27), channel_id=1, source_target_pairs={{0,16},{16,0},{1,17},{17,1},{2,18},{18,2},{3,19},{19,3},{4,20},{20... | collective-permute-start | bytes 3932168 | tf_op jit(solution)/shard_map/ppermute | solution.py:602
  539.0 27.2 %collective-permute-start.48 = (bf16[2,2,256,512]{3,2,1,0:T(8,128)(2,1)}, bf16[2,2,256,512]{3,2,1,0:T(8,128)(2,1)}, u32[]{:S(2)}, u32[]{:S(2)}) collective-permute-start(bf16[2,2,256,512]{3,2,1,0:T(8,128)(2,1)} %get-tuple-element.131), channel_id=1, source_target_pairs={{0,16},{16,0},{1,17},{17,1},{2,18},{18,2},{3,19},{19,3},{4,20},{20... | collective-permute-start | bytes 3145736 | tf_op jit(solution)/shard_map/ppermute | solution.py:602
  589.1 39.1 %all-to-all-start.3 = ((bf16[4,256,512]{2,1,0:T(8,128)(2,1)}), bf16[4,256,512]{2,1,0:T(8,128)(2,1)S(1)}, u32[]{:S(2)}, u32[]{:S(2)}) async-start(bf16[4,256,512]{2,1,0:T(8,128)(2,1)} %fusion.9), calls=%async_computation.5 | async-start | bytes 2097152 | tf_op jit(solution)/shard_map/all_to_all | solution.py:710
  (95 other events, 1407.5 us)
Sparse Core Ops, SparseCore 0:
  11.7 129.7 all-gather.3
  143.7 97.5 all-gather.5
  242.9 54.3 all-gather.7
  300.2 58.5 reduce-scatter.4
  361.5 107.7 reduce-scatter.6
  472.0 51.5 reduce-scatter.8
  525.9 71.8 reduce-scatter.10

commit v12 on v11

--- a/solution.py
+++ b/solution.py
@@ -934,6 +934,7 @@
                     first = (i * units + u) * unit
                     outs[0][u, i] = source[first : first + unit, :].astype(F32)
 
+        down_pieces = [after(down_pieces[0], outputs[1]), *down_pieces[1:]]
         (down_all,) = place(down_pieces, here, [(units * unit, width)], write_rows)
         (gate_up_all,) = place(gate_up_pieces, here, [(units, 2, unit, width)], write_gate_up)
     beside = (down_all, gate_up_all, outputs[0]) if fits else ()
@@ -948,7 +949,7 @@
     every = lax.dynamic_update_slice_in_dim(every, table_part, (x * 2 + y) * local_heads, 0)
     spare = -every.size % width
     every = jnp.pad(every.reshape(-1), (0, spare)).reshape(-1, width)
-    sums = sum_plane(jnp.concatenate([attn_gain_part, ffn_gain_part, every]), nx, out_last, outputs[1])
+    sums = sum_plane(jnp.concatenate([attn_gain_part, ffn_gain_part, every]), nx, out_last)
     all_sums = sum_line(after(sums, input_leaves), nz)
     attn_gain_grad, ffn_gain_grad = all_sums[:nz], all_sums[nz : 2 * nz]
     every = all_sums[2 * nz :].reshape(-1)[: nx * 2 * local_heads * buckets].reshape(-1, buckets)
@@ -956,7 +957,7 @@
     outputs = stored_from(outputs, BF)
     if fits:
         (out_all,) = place(out_pieces, here, [(heads * 64, width)], write_rows)
-        qkv_pieces, _ = shared(after(qkv_part, sums, *one_last), out_all, outputs, input_leaves)
+        qkv_pieces, _ = shared(after(qkv_part, sums, *one_last), out_all, outputs)
         query_key_all, value_all = place(
             qkv_pieces, here, [(heads, 2, 64, width), (heads, 64, width)], write_qkv
         )

time: 670 us -> 660 us (0.985)
  waiting for transfers between devices: 241 us -> 227 us
    ppermute x59, waiting for transfers between devices: 161 us -> 148 us  [hop(): return lax.ppermute(value, axis, swap)]
where the time goes in v12:
time: 660 us; the launch traced here: 655 us
  Pallas kernels  256 us (39%)
  waiting for transfers between devices  227 us (34%)
  starting transfers between devices  91 us (14%)
  other arithmetic  47.2 us (7%)
  local copies, waits for them, and re-layouts  17.8 us (3%)
  between operations  15.4 us (2%)
    ppermute x59, waiting for transfers between devices, hop(): return lax.ppermute(value, axis, swap)  148 us
    all_to_all x2, waiting for transfers between devices, to_groups(): return lax.all_to_all(both, 'z', 0, 0, tiled=True)  66.1 us
    ppermute x59, starting transfers between devices, hop(): return lax.ppermute(value, axis, swap)  62.1 us
    pallas_call x2, Pallas kernels, attend_back(): pl.pallas_call(functools.partial(attend_back_kernel, group), grid=(1,), i...  49.5 us
    pallas_call x4, Pallas kernels, mm_nn(): pl.pallas_call(functools.partial(nn_kernel, len(grads)), grid=(nz,), in_s...  44.7 us
    pallas_call x4, Pallas kernels, mm_tn(): pl.pallas_call(functools.partial(tn_kernel, count), grid=(count * steps,)...  43.4 us
    pallas_call x2, Pallas kernels, attend(): pl.pallas_call(functools.partial(attend_kernel, group), grid=(1,), in_spe...  30.1 us
    pallas_call x4, Pallas kernels, place(): pl.pallas_call(functools.partial(place_kernel, write), grid=(4,), in_spec...  19.5 us
  transfers between devices with their start and end apart: 73, of which 32 were waited for; matrix products, arithmetic and copies ran while one was open for 9% of the time, Pallas kernels for 38%

profile of v12, /device:TPU:0, one launch (start us, length us, event | category | flops | bytes accessed | tf_op | source)
XLA Modules:
  0.0 654.5 jit_solution(18211218434293863134)
XLA Ops:
  16.7 12.2 %collective-permute-done.1 = bf16[2,256,512]{2,1,0:T(8,128)(2,1)} collective-permute-done((bf16[2,256,512]{2,1,0:T(8,128)(2,1)}, bf16[2,256,512]{2,1,0:T(8,128)(2,1)}, u32[]{:S(2)}, u32[]{:S(2)}) %collective-permute-start.1) | collective-permute-done | bytes 524320 | tf_op jit(solution)/shard_map/ppermute | solution.py:602
  45.1 49.8 %all-to-all-done = bf16[4,264,512]{2,1,0:T(8,128)(2,1)} async-done(((bf16[4,264,512]{2,1,0:T(8,128)(2,1)}), bf16[4,264,512]{2,1,0:T(8,128)(2,1)}, u32[]{:S(2)}, u32[]{:S(2)}) %all-to-all-start) | async-done | bytes 1081376 | tf_op jit(solution)/shard_map/all_to_all | solution.py:705
  123.9 16.3 %all-to-all-done.1 = bf16[4,256,512]{2,1,0:T(8,128)(2,1)S(1)} async-done(((bf16[4,256,512]{2,1,0:T(8,128)(2,1)}), bf16[4,256,512]{2,1,0:T(8,128)(2,1)S(1)}, u32[]{:S(2)}, u32[]{:S(2)}) %all-to-all-start.1) | async-done | bytes 1048608 | tf_op jit(solution)/shard_map/all_to_all | solution.py:705
  146.9 12.1 %product_nt.2.q_ref.k_ref.v_ref = bf16[1024,1536]{1,0:T(8,128)(2,1)} custom-call(s32[4]{0:T(128)} %add_multiply_fusion.starts_ref, bf16[2,256,512]{2,1,0:T(8,128)(2,1)} %copy-done.10, bf16[2,256,512]{2,1,0:T(8,128)(2,1)} %collective-permute-done.2.refs_1_.refs_3_, bf16[2,256,512]{2,1,0:T(8,128)(2,1)} %collective-permute-done.3.refs_2_.refs_4_, ...), custom_call_target="tpu_custom_call" | custom-call | flops 402653184 | bytes 851968 | tf_op jit(solution)/shard_map/product_nt/pallas_call | solution.py:78
  159.0 15.0 %attend.2 = (bf16[1024,256]{1,0:T(8,128)(2,1)}, f32[8,1024]{1,0:T(8,128)}) custom-call(s32[1]{0:T(128)} %dynamic_slice.51.length_ref, f32[8,32]{1,0:T(8,128)} %constant_dynamic-slice_fusion.4.table_ref, f32[8,384,128]{2,1,0:T(8,128)} %near_bias.1.near_ref, bf16[1024,1536]{1,0:T(8,128)(2,1)} %product_nt.2.q_ref.k_ref.v_ref, ...), custom_call_target="tpu_custom_call" | custom-call | flops 268435456 | bytes 131072 | tf_op jit(solution)/shard_map/attend/pallas_call | solution.py:497
  176.8 15.1 %attend.3 = (bf16[1024,256]{1,0:T(8,128)(2,1)}, f32[8,1024]{1,0:T(8,128)}) custom-call(s32[1]{0:T(128)} %dynamic_slice.51.length_ref, f32[8,32]{1,0:T(8,128)} %constant_dynamic-slice_fusion.4.table_ref, f32[8,384,128]{2,1,0:T(8,128)} %near_bias.1.near_ref, bf16[1024,1536]{1,0:T(8,128)(2,1)} %product_nt.2.q_ref.k_ref.v_ref, ...), custom_call_target="tpu_custom_call" | custom-call | flops 268435456 | bytes 131072 | tf_op jit(solution)/shard_map/attend/pallas_call | solution.py:497
  200.3 22.3 %collective-permute-done.15 = bf16[2,2,256,512]{3,2,1,0:T(8,128)(2,1)S(1)} collective-permute-done((bf16[2,2,256,512]{3,2,1,0:T(8,128)(2,1)}, bf16[2,2,256,512]{3,2,1,0:T(8,128)(2,1)S(1)}, u32[]{:S(2)}, u32[]{:S(2)}) %collective-permute-start.15) | collective-permute-done | bytes 1048608 | tf_op jit(solution)/shard_map/ppermute | solution.py:602
  226.4 8.9 %collective-permute-done.16 = bf16[2,256,512]{2,1,0:T(8,128)(2,1)S(1)} collective-permute-done((bf16[2,256,512]{2,1,0:T(8,128)(2,1)S(1)}, bf16[2,256,512]{2,1,0:T(8,128)(2,1)S(1)}, u32[]{:S(2)}, u32[]{:S(2)}) %collective-permute-start.16) | collective-permute-done | bytes 524320 | tf_op jit(solution)/shard_map/ppermute | solution.py:602
  243.0 10.8 %collective-permute-done.20.refs_2_.refs_3_ = bf16[2,256,512]{2,1,0:T(8,128)(2,1)S(1)} collective-permute-done((bf16[2,256,512]{2,1,0:T(8,128)(2,1)S(1)}, bf16[2,256,512]{2,1,0:T(8,128)(2,1)S(1)}, u32[]{:S(2)}, u32[]{:S(2)}) %collective-permute-start.20) | collective-permute-done | bytes 524320 | tf_op jit(solution)/shard_map/ppermute | solution.py:602
  255.9 9.7 %collective-permute-done.19.refs_1_.refs_2_ = bf16[2,256,512]{2,1,0:T(8,128)(2,1)S(1)} collective-permute-done((bf16[2,256,512]{2,1,0:T(8,128)(2,1)S(1)}, bf16[2,256,512]{2,1,0:T(8,128)(2,1)S(1)}, u32[]{:S(2)}, u32[]{:S(2)}) %collective-permute-start.19) | collective-permute-done | bytes 524320 | tf_op jit(solution)/shard_map/ppermute | solution.py:602
  272.5 17.6 %ffn_in.1 = (bf16[1024,1280]{1,0:T(8,128)(2,1)}, bf16[1024,1280]{1,0:T(8,128)(2,1)}, bf16[1024,1280]{1,0:T(8,128)(2,1)}) custom-call(s32[4]{0:T(128)} %add_multiply_fusion.starts_ref, bf16[2,256,512]{2,1,0:T(8,128)(2,1)} %copy-done.8, bf16[2,256,512]{2,1,0:T(8,128)(2,1)} %copy-done.18, bf16[2,256,512]{2,1,0:T(8,128)(2,1)} %copy-done.16, ...), custom_call_target="tpu_custom_call" | custom-call | flops 671088640 | bytes 1409024 | tf_op jit(solution)/shard_map/ffn_in/pallas_call | solution.py:214
  290.1 9.9 %product_tn.4 = bf16[4,1280,512]{2,1,0:T(8,128)(2,1)} custom-call(s32[4]{0:T(128)} %add_multiply_fusion.starts_ref, bf16[1024,1280]{1,0:T(8,128)(2,1)} %get-tuple-element.101.refs_0_, bf16[2,256,512]{2,1,0:T(8,128)(2,1)} %copy-done.6, bf16[2,256,512]{2,1,0:T(8,128)(2,1)} %collective-permute-done.9.refs_2_.refs_1_, bf16[2,256,512]{2,1,0:T(8,128)(2,1)} %copy-done.14, ...), custom_call_target="tpu_custom_call" | custom-call | flops 335544320 | bytes 753664 | tf_op jit(solution)/shard_map/product_tn/pallas_call | solution.py:171
  300.2 15.2 %ffn_back.1.refs_0_ = bf16[1024,2560]{1,0:T(8,128)(2,1)} custom-call(s32[4]{0:T(128)} %add_multiply_fusion.starts_ref, bf16[2,256,512]{2,1,0:T(8,128)(2,1)} %copy-done.6, bf16[2,256,512]{2,1,0:T(8,128)(2,1)} %collective-permute-done.9.refs_2_.refs_1_, bf16[2,256,512]{2,1,0:T(8,128)(2,1)} %copy-done.14, ...), custom_call_target="tpu_custom_call" | custom-call | flops 335544320 | bytes 1245184 | tf_op jit(solution)/shard_map/ffn_back/pallas_call | solution.py:245
  315.3 16.4 %product_nn.5 = (bf16[2,2,256,512]{3,2,1,0:T(8,128)(2,1)}, bf16[2,2,256,512]{3,2,1,0:T(8,128)(2,1)}, bf16[2,2,256,512]{3,2,1,0:T(8,128)(2,1)}, bf16[2,2,256,512]{3,2,1,0:T(8,128)(2,1)}) custom-call(s32[4]{0:T(128)} %add_multiply_fusion.starts_ref, bf16[1024,2560]{1,0:T(8,128)(2,1)} %ffn_back.1.refs_0_, bf16[4,2,1280,512]{3,2,1,0:T(8,128)(2,1)} %bitcast.101), custom_call_target="tpu_custom_call" | custom-call | flops 671088640 | bytes 1245184 | tf_op jit(solution)/shard_map/product_nn/pallas_call | solution.py:123
  335.2 15.9 %product_tn.5 = bf16[4,2560,512]{2,1,0:T(8,128)(2,1)} custom-call(s32[4]{0:T(128)} %add_multiply_fusion.starts_ref, bf16[1024,2560]{1,0:T(8,128)(2,1)} %ffn_back.1.refs_0_, bf16[2,256,512]{2,1,0:T(8,128)(2,1)} %copy-done.8, bf16[2,256,512]{2,1,0:T(8,128)(2,1)} %copy-done.18, bf16[2,256,512]{2,1,0:T(8,128)(2,1)} %copy-done.16, ...), custom_call_target="tpu_custom_call" | custom-call | flops 671088640 | bytes 1245184 | tf_op jit(solution)/shard_map/product_tn/pallas_call | solution.py:171
  366.1 10.2 %product_nn.6 = (bf16[2,2,256,512]{3,2,1,0:T(8,128)(2,1)}, bf16[2,2,256,512]{3,2,1,0:T(8,128)(2,1)}, bf16[2,2,256,512]{3,2,1,0:T(8,128)(2,1)}, bf16[2,2,256,512]{3,2,1,0:T(8,128)(2,1)}) custom-call(s32[4]{0:T(128)} %add_multiply_fusion.starts_ref, bf16[1024,1280]{1,0:T(8,128)(2,1)} %get-tuple-element.101.refs_0_, bf16[4,2,640,512]{3,2,1,0:T(8,128)(2,1)} %bitcast.106), custom_call_target="tpu_custom_call" | custom-call | flops 335544320 | bytes 753664 | tf_op jit(solution)/shard_map/product_nn/pallas_call | solution.py:123
  386.3 10.8 %collective-permute-done.30.refs_2_.refs_4_ = bf16[2,256,512]{2,1,0:T(8,128)(2,1)S(1)} collective-permute-done((bf16[2,256,512]{2,1,0:T(8,128)(2,1)S(1)}, bf16[2,256,512]{2,1,0:T(8,128)(2,1)S(1)}, u32[]{:S(2)}, u32[]{:S(2)}) %collective-permute-start.30) | collective-permute-done | bytes 524320 | tf_op jit(solution)/shard_map/ppermute | solution.py:602
  399.1 10.5 %collective-permute-done.29.refs_1_.refs_3_ = bf16[2,256,512]{2,1,0:T(8,128)(2,1)S(1)} collective-permute-done((bf16[2,256,512]{2,1,0:T(8,128)(2,1)S(1)}, bf16[2,256,512]{2,1,0:T(8,128)(2,1)S(1)}, u32[]{:S(2)}, u32[]{:S(2)}) %collective-permute-start.29) | collective-permute-done | bytes 524320 | tf_op jit(solution)/shard_map/ppermute | solution.py:602
  432.0 24.8 %attend_back.2 = (bf16[1024,768]{1,0:T(8,128)(2,1)}, f32[4,400,128]{2,1,0:T(8,128)}) custom-call(s32[1]{0:T(128)} %dynamic_slice.51.length_ref, f32[8,32]{1,0:T(8,128)} %constant_dynamic-slice_fusion.4.table_ref, f32[8,384,128]{2,1,0:T(8,128)} %near_bias.1.near_ref, bf16[1024,1536]{1,0:T(8,128)(2,1)} %product_nt.2.q_ref.k_ref.v_ref, ...), custom_call_target="tpu_custom_call" | custom-call | flops 671088640 | bytes 262144 | tf_op jit(solution)/shard_map/attend_back/pallas_call | solution.py:524
  473.9 7.3 %all-to-all-start.2 = ((bf16[4,256,512]{2,1,0:T(8,128)(2,1)}), bf16[4,256,512]{2,1,0:T(8,128)(2,1)S(1)}, u32[]{:S(2)}, u32[]{:S(2)}) async-start(bf16[4,256,512]{2,1,0:T(8,128)(2,1)} %fusion.13), calls=%async_computation.3 | async-start | bytes 2097152 | tf_op jit(solution)/shard_map/all_to_all | solution.py:710
  482.7 24.7 %attend_back.3 = (bf16[1024,768]{1,0:T(8,128)(2,1)}, f32[4,400,128]{2,1,0:T(8,128)}) custom-call(s32[1]{0:T(128)} %dynamic_slice.51.length_ref, f32[8,32]{1,0:T(8,128)} %constant_dynamic-slice_fusion.4.table_ref, f32[8,384,128]{2,1,0:T(8,128)} %near_bias.1.near_ref, bf16[1024,1536]{1,0:T(8,128)(2,1)} %product_nt.2.q_ref.k_ref.v_ref, ...), custom_call_target="tpu_custom_call" | custom-call | flops 671088640 | bytes 262144 | tf_op jit(solution)/shard_map/attend_back/pallas_call | solution.py:524
  507.5 11.4 %product_tn.7 = bf16[4,1536,512]{2,1,0:T(8,128)(2,1)} custom-call(s32[4]{0:T(128)} %add_multiply_fusion.starts_ref, bf16[1024,768]{1,0:T(8,128)(2,1)} %get-tuple-element.112.refs_0_, bf16[1024,768]{1,0:T(8,128)(2,1)} %get-tuple-element.122.refs_1_, bf16[2,256,512]{2,1,0:T(8,128)(2,1)} %copy-done.10, ...), custom_call_target="tpu_custom_call" | custom-call | flops 402653184 | bytes 851968 | tf_op jit(solution)/shard_map/product_tn/pallas_call | solution.py:171
  527.9 11.1 %product_nn.7 = (bf16[2,2,256,512]{3,2,1,0:T(8,128)(2,1)}, bf16[2,2,256,512]{3,2,1,0:T(8,128)(2,1)}, bf16[2,2,256,512]{3,2,1,0:T(8,128)(2,1)}, bf16[2,2,256,512]{3,2,1,0:T(8,128)(2,1)}) custom-call(s32[4]{0:T(128)} %add_multiply_fusion.starts_ref, bf16[1024,768]{1,0:T(8,128)(2,1)} %get-tuple-element.112.refs_0_, ...), custom_call_target="tpu_custom_call" | custom-call | flops 402653184 | bytes 851968 | tf_op jit(solution)/shard_map/product_nn/pallas_call | solution.py:123
  555.9 8.3 %collective-permute-done.41 = bf16[2,2,256,512]{3,2,1,0:T(8,128)(2,1)} collective-permute-done((bf16[2,2,256,512]{3,2,1,0:T(8,128)(2,1)}, bf16[2,2,256,512]{3,2,1,0:T(8,128)(2,1)}, u32[]{:S(2)}, u32[]{:S(2)}) %collective-permute-start.41) | collective-permute-done | bytes 1048608 | tf_op jit(solution)/shard_map/ppermute | solution.py:602
  (331 shorter events, 272.7 us)
Async XLA Ops:
  7.2 134.3 %all-gather.4.cloned.1.call-start = ((), (), s32[]{:S(2)}) async-start(), calls=%async_computation.8 | async-start | bytes 9437184 | tf_op jit(solution)/shard_map/all_gather | solution.py:804
  11.6 261.0 %all-gather.6.cloned.1.call-start = ((), (), s32[]{:S(2)}) async-start(), calls=%async_computation.9 | async-start | bytes 11796480 | tf_op jit(solution)/shard_map/all_gather | solution.py:804
  34.3 60.7 %all-to-all-start = ((bf16[4,264,512]{2,1,0:T(8,128)(2,1)}), bf16[4,264,512]{2,1,0:T(8,128)(2,1)}, u32[]{:S(2)}, u32[]{:S(2)}) async-start(bf16[4,264,512]{2,1,0:T(8,128)(2,1)} %pad_maximum_fusion.3), calls=%async_computation | async-start | bytes 2162688 | tf_op jit(solution)/shard_map/all_to_all | solution.py:705
  39.5 260.7 %all-gather.8.cloned.1.call-start = ((), (), s32[]{:S(2)}) async-start(), calls=%async_computation.10 | async-start | bytes 5898240 | tf_op jit(solution)/shard_map/all_gather | solution.py:804
  43.3 51.6 %collective-permute-start.8 = (bf16[2,256,512]{2,1,0:T(8,128)(2,1)S(1)}, bf16[2,256,512]{2,1,0:T(8,128)(2,1)S(1)}, u32[]{:S(2)}, u32[]{:S(2)}) collective-permute-start(bf16[2,256,512]{2,1,0:T(8,128)(2,1)S(1)} %get-tuple-element.163), channel_id=1, source_target_pairs={{0,16},{16,0},{1,17},{17,1},{2,18},{18,2},{3,19},{19,3},{4,20},{20... | collective-permute-start | bytes 1572872 | tf_op jit(solution)/shard_map/ppermute | solution.py:602
  96.1 44.1 %all-to-all-start.1 = ((bf16[4,256,512]{2,1,0:T(8,128)(2,1)}), bf16[4,256,512]{2,1,0:T(8,128)(2,1)S(1)}, u32[]{:S(2)}, u32[]{:S(2)}) async-start(bf16[4,256,512]{2,1,0:T(8,128)(2,1)} %bitcast.26), calls=%async_computation.1 | async-start | bytes 2097152 | tf_op jit(solution)/shard_map/all_to_all | solution.py:705
  101.8 257.0 %reduce-scatter.5.cloned.1.call-start = ((), (), s32[]{:S(2)}) async-start(), calls=%async_computation.11 | async-start | bytes 5898240 | tf_op jit(solution)/shard_map/reduce_scatter | solution.py:847
  109.6 34.8 %collective-permute-start.2 = (bf16[2,256,512]{2,1,0:T(8,128)(2,1)S(1)}, bf16[2,256,512]{2,1,0:T(8,128)(2,1)}, u32[]{:S(2)}, u32[]{:S(2)}) collective-permute-start(bf16[2,256,512]{2,1,0:T(8,128)(2,1)S(1)} %get-tuple-element.165.refs_0_.refs_2_), channel_id=1, source_target_pairs={{0,16},{16,0},{1,17},{17,1},{2,18},{18,2},{3,19},{19,3},{4,20},{20... | collective-permute-start | bytes 1572872 | tf_op jit(solution)/shard_map/ppermute | solution.py:602
  110.1 35.6 %collective-permute-start.6 = (bf16[2,256,512]{2,1,0:T(8,128)(2,1)S(1)}, bf16[2,256,512]{2,1,0:T(8,128)(2,1)}, u32[]{:S(2)}, u32[]{:S(2)}) collective-permute-start(bf16[2,256,512]{2,1,0:T(8,128)(2,1)S(1)} %get-tuple-element.164.refs_4_.refs_6_), channel_id=1, source_target_pairs={{0,4},{4,0},{1,5},{5,1},{2,6},{6,2},{3,7},{7,3},{8,12},{12,8},{9,1... | collective-permute-start | bytes 1572872 | tf_op jit(solution)/shard_map/ppermute | solution.py:602
  142.8 31.3 %collective-permute-start.13 = (bf16[2,256,512]{2,1,0:T(8,128)(2,1)S(1)}, bf16[2,256,512]{2,1,0:T(8,128)(2,1)S(1)}, u32[]{:S(2)}, u32[]{:S(2)}) collective-permute-start(bf16[2,256,512]{2,1,0:T(8,128)(2,1)S(1)} %get-tuple-element.160.refs_5_.refs_4_), channel_id=1, source_target_pairs={{0,16},{16,0},{1,17},{17,1},{2,18},{18,2},{3,19},{19,3},{4,20},{20... | collective-permute-start | bytes 1572872 | tf_op jit(solution)/shard_map/ppermute | solution.py:602
  144.3 29.7 %collective-permute-start.10 = (bf16[2,256,512]{2,1,0:T(8,128)(2,1)S(1)}, bf16[2,256,512]{2,1,0:T(8,128)(2,1)S(1)}, u32[]{:S(2)}, u32[]{:S(2)}) collective-permute-start(bf16[2,256,512]{2,1,0:T(8,128)(2,1)S(1)} %get-tuple-element.161.refs_1_.refs_0_), channel_id=1, source_target_pairs={{0,4},{4,0},{1,5},{5,1},{2,6},{6,2},{3,7},{7,3},{8,12},{12,8},{9,1... | collective-permute-start | bytes 1572872 | tf_op jit(solution)/shard_map/ppermute | solution.py:602
  145.8 46.1 %collective-permute-start.12 = (bf16[2,256,512]{2,1,0:T(8,128)(2,1)S(1)}, bf16[2,256,512]{2,1,0:T(8,128)(2,1)S(1)}, u32[]{:S(2)}, u32[]{:S(2)}) collective-permute-start(bf16[2,256,512]{2,1,0:T(8,128)(2,1)S(1)} %get-tuple-element.160.refs_5_.refs_4_), channel_id=1, source_target_pairs={{0,4},{4,0},{1,5},{5,1},{2,6},{6,2},{3,7},{7,3},{8,12},{12,8},{9,1... | collective-permute-start | bytes 1572872 | tf_op jit(solution)/shard_map/ppermute | solution.py:602
  146.4 45.6 %collective-permute-start.9 = (bf16[2,256,512]{2,1,0:T(8,128)(2,1)S(1)}, bf16[2,256,512]{2,1,0:T(8,128)(2,1)}, u32[]{:S(2)}, u32[]{:S(2)}) collective-permute-start(bf16[2,256,512]{2,1,0:T(8,128)(2,1)S(1)} %get-tuple-element.161.refs_1_.refs_0_), channel_id=1, source_target_pairs={{0,16},{16,0},{1,17},{17,1},{2,18},{18,2},{3,19},{19,3},{4,20},{20... | collective-permute-start | bytes 1572872 | tf_op jit(solution)/shard_map/ppermute | solution.py:602
  300.1 169.5 %reduce-scatter.7.cloned.1.call-start = ((), (), s32[]{:S(2)}) async-start(), calls=%async_computation.12 | async-start | bytes 11796480 | tf_op jit(solution)/shard_map/reduce_scatter | solution.py:847
  358.8 165.4 %reduce-scatter.9.cloned.1.call-start = ((), (), s32[]{:S(2)}) async-start(), calls=%async_computation.13 | async-start | bytes 2359296 | tf_op jit(solution)/shard_map/reduce_scatter | solution.py:847
  383.6 26.0 %collective-permute-start.29 = (bf16[2,256,512]{2,1,0:T(8,128)(2,1)S(1)}, bf16[2,256,512]{2,1,0:T(8,128)(2,1)S(1)}, u32[]{:S(2)}, u32[]{:S(2)}) collective-permute-start(bf16[2,256,512]{2,1,0:T(8,128)(2,1)S(1)} %get-tuple-element.157.refs_0_.refs_2_), channel_id=1, source_target_pairs={{0,16},{16,0},{1,17},{17,1},{2,18},{18,2},{3,19},{19,3},{4,20},{20... | collective-permute-start | bytes 1572872 | tf_op jit(solution)/shard_map/ppermute | solution.py:602
  416.5 40.3 %collective-permute-start.35 = (bf16[2,2,256,512]{3,2,1,0:T(8,128)(2,1)}, bf16[2,2,256,512]{3,2,1,0:T(8,128)(2,1)}, u32[]{:S(2)}, u32[]{:S(2)}) collective-permute-start(bf16[2,2,256,512]{3,2,1,0:T(8,128)(2,1)} %get-tuple-element.109), channel_id=1, source_target_pairs={{0,4},{4,0},{1,5},{5,1},{2,6},{6,2},{3,7},{7,3},{8,12},{12,8},{9,1... | collective-permute-start | bytes 3145736 | tf_op jit(solution)/shard_map/ppermute | solution.py:602
  417.8 41.3 %collective-permute-start.38 = (bf16[2,2,256,512]{3,2,1,0:T(8,128)(2,1)}, bf16[2,2,256,512]{3,2,1,0:T(8,128)(2,1)}, u32[]{:S(2)}, u32[]{:S(2)}) collective-permute-start(bf16[2,2,256,512]{3,2,1,0:T(8,128)(2,1)} %get-tuple-element.118), channel_id=1, source_target_pairs={{0,16},{16,0},{1,17},{17,1},{2,18},{18,2},{3,19},{19,3},{4,20},{20... | collective-permute-start | bytes 3145736 | tf_op jit(solution)/shard_map/ppermute | solution.py:602
  418.6 38.2 %collective-permute-start.36 = (bf16[640,512]{1,0:T(8,128)(2,1)}, bf16[640,512]{1,0:T(8,128)(2,1)}, u32[]{:S(2)}, u32[]{:S(2)}) collective-permute-start(bf16[640,512]{1,0:T(8,128)(2,1)} %reduce-scatter.5.cloned.1.call-done.refs_0_), channel_id=1, source_target_pairs={{0,16},{16,0},{1,17},{17,1},{2,18},{18,2},{3,19},{19,3},{4,20},{20... | collective-permute-start | bytes 1966088 | tf_op jit(solution)/shard_map/ppermute | solution.py:602
  473.9 45.0 %all-to-all-start.2 = ((bf16[4,256,512]{2,1,0:T(8,128)(2,1)}), bf16[4,256,512]{2,1,0:T(8,128)(2,1)S(1)}, u32[]{:S(2)}, u32[]{:S(2)}) async-start(bf16[4,256,512]{2,1,0:T(8,128)(2,1)} %fusion.13), calls=%async_computation.3 | async-start | bytes 2097152 | tf_op jit(solution)/shard_map/all_to_all | solution.py:710
  481.1 126.9 %reduce-scatter.11.cloned.1.call-start = ((), (), s32[]{:S(2)}) async-start(), calls=%async_computation.14 | async-start | bytes 7077888 | tf_op jit(solution)/shard_map/reduce_scatter | solution.py:847
  481.1 37.8 %collective-permute-start.45 = (bf16[1280,512]{1,0:T(8,128)(2,1)S(1)}, bf16[1280,512]{1,0:T(8,128)(2,1)}, u32[]{:S(2)}, u32[]{:S(2)}) collective-permute-start(bf16[1280,512]{1,0:T(8,128)(2,1)S(1)} %copy-done.27), channel_id=1, source_target_pairs={{0,16},{16,0},{1,17},{17,1},{2,18},{18,2},{3,19},{19,3},{4,20},{20... | collective-permute-start | bytes 3932168 | tf_op jit(solution)/shard_map/ppermute | solution.py:602
  540.6 26.5 %collective-permute-start.48 = (bf16[2,2,256,512]{3,2,1,0:T(8,128)(2,1)}, bf16[2,2,256,512]{3,2,1,0:T(8,128)(2,1)}, u32[]{:S(2)}, u32[]{:S(2)}) collective-permute-start(bf16[2,2,256,512]{3,2,1,0:T(8,128)(2,1)} %get-tuple-element.133), channel_id=1, source_target_pairs={{0,16},{16,0},{1,17},{17,1},{2,18},{18,2},{3,19},{19,3},{4,20},{20... | collective-permute-start | bytes 3145736 | tf_op jit(solution)/shard_map/ppermute | solution.py:602
  589.1 34.2 %all-to-all-start.3 = ((bf16[4,256,512]{2,1,0:T(8,128)(2,1)}), bf16[4,256,512]{2,1,0:T(8,128)(2,1)S(1)}, u32[]{:S(2)}, u32[]{:S(2)}) async-start(bf16[4,256,512]{2,1,0:T(8,128)(2,1)} %fusion.9), calls=%async_computation.5 | async-start | bytes 2097152 | tf_op jit(solution)/shard_map/all_to_all | solution.py:710
  (96 other events, 1312.9 us)
Sparse Core Ops, SparseCore 0:
  11.7 129.7 all-gather.3
  143.7 97.5 all-gather.5
  242.9 54.3 all-gather.7
  300.2 58.5 reduce-scatter.4
  361.5 107.7 reduce-scatter.6
  472.0 52.1 reduce-scatter.8
  526.6 71.3 reduce-scatter.10

commit v13 on v12

--- a/solution.py
+++ b/solution.py
@@ -911,7 +911,7 @@
     outputs, _ = from_groups(outputs)
     qkv_partial = tn(grad_projected, normed, starts)
     gate_up_pieces, gate_up_last = shared(after(gate_up_part, grad_projected[0]))
-    qkv_part = reduce(after(qkv_partial, out_part, gate_up_last, outputs[0]))
+    qkv_part = reduce(after(qkv_partial, gate_up_last, outputs[0]))
     one_parts = nn(grad_projected, w_attn, 0, qkv_count, starts)
     if fits:
         here = jnp.stack([y, c]).astype(jnp.int32)
@@ -968,7 +968,8 @@
         qkv_all = shared(qkv_part)[0].astype(F32).reshape(parts, 3, heads, 64, width)
         qkv_all = qkv_all.transpose(0, 2, 1, 3, 4).reshape(-1, 3, 64, width)
         query_key_all, value_all = qkv_all[:, :2], qkv_all[:, 2]
-    input_grad = stored_from(input_grad, F32)
+    back, other = input_grad
+    input_grad = stored_from((back, after(other, query_key_all)), F32)
     down_all, out_all = down_all.reshape(down_proj.shape), out_all.reshape(out_proj.shape)
 
     table_grad = lax.dynamic_slice_in_dim(every, (x * nz + z) * mine, mine, 0).T

time: 660 us -> 665 us (level)
  transfers between devices with their start and end apart: 73 -> 73, of which waited for: 32 -> 31; matrix products, arithmetic and copies ran while one was open for 9% -> 9% of each run, Pallas kernels for 38% -> 38%
where the time goes in v13:
time: 665 us; the launch traced here: 660 us
  Pallas kernels  256 us (38%)
  waiting for transfers between devices  229 us (34%)
  starting transfers between devices  92.2 us (14%)
  other arithmetic  47.3 us (7%)
  local copies, waits for them, and re-layouts  19.8 us (3%)
  between operations  15.4 us (2%)
    ppermute x59, waiting for transfers between devices, hop(): return lax.ppermute(value, axis, swap)  150 us
    all_to_all x2, waiting for transfers between devices, to_groups(): return lax.all_to_all(both, 'z', 0, 0, tiled=True)  66.1 us
    ppermute x59, starting transfers between devices, hop(): return lax.ppermute(value, axis, swap)  62.2 us
    pallas_call x2, Pallas kernels, attend_back(): pl.pallas_call(functools.partial(attend_back_kernel, group), grid=(1,), i...  49.5 us
    pallas_call x4, Pallas kernels, mm_nn(): pl.pallas_call(functools.partial(nn_kernel, len(grads)), grid=(nz,), in_s...  44.8 us
    pallas_call x4, Pallas kernels, mm_tn(): pl.pallas_call(functools.partial(tn_kernel, count), grid=(count * steps,)...  43.4 us
    pallas_call x2, Pallas kernels, attend(): pl.pallas_call(functools.partial(attend_kernel, group), grid=(1,), in_spe...  30.1 us
    pallas_call x4, Pallas kernels, place(): pl.pallas_call(functools.partial(place_kernel, write), grid=(4,), in_spec...  19.7 us
  transfers between devices with their start and end apart: 73, of which 31 were waited for; matrix products, arithmetic and copies ran while one was open for 9% of the time, Pallas kernels for 38%

profile of v13, /device:TPU:0, one launch (start us, length us, event | category | flops | bytes accessed | tf_op | source)
XLA Modules:
  0.0 659.6 jit_solution(5131340758567426966)
XLA Ops:
  16.7 12.2 %collective-permute-done.1 = bf16[2,256,512]{2,1,0:T(8,128)(2,1)} collective-permute-done((bf16[2,256,512]{2,1,0:T(8,128)(2,1)}, bf16[2,256,512]{2,1,0:T(8,128)(2,1)}, u32[]{:S(2)}, u32[]{:S(2)}) %collective-permute-start.1) | collective-permute-done | bytes 524320 | tf_op jit(solution)/shard_map/ppermute | solution.py:602
  45.1 49.8 %all-to-all-done = bf16[4,264,512]{2,1,0:T(8,128)(2,1)} async-done(((bf16[4,264,512]{2,1,0:T(8,128)(2,1)}), bf16[4,264,512]{2,1,0:T(8,128)(2,1)}, u32[]{:S(2)}, u32[]{:S(2)}) %all-to-all-start) | async-done | bytes 1081376 | tf_op jit(solution)/shard_map/all_to_all | solution.py:705
  123.9 16.3 %all-to-all-done.1 = bf16[4,256,512]{2,1,0:T(8,128)(2,1)S(1)} async-done(((bf16[4,256,512]{2,1,0:T(8,128)(2,1)}), bf16[4,256,512]{2,1,0:T(8,128)(2,1)S(1)}, u32[]{:S(2)}, u32[]{:S(2)}) %all-to-all-start.1) | async-done | bytes 1048608 | tf_op jit(solution)/shard_map/all_to_all | solution.py:705
  146.9 12.1 %product_nt.2.q_ref.k_ref.v_ref = bf16[1024,1536]{1,0:T(8,128)(2,1)} custom-call(s32[4]{0:T(128)} %add_multiply_fusion.starts_ref, bf16[2,256,512]{2,1,0:T(8,128)(2,1)} %copy-done.10, bf16[2,256,512]{2,1,0:T(8,128)(2,1)} %collective-permute-done.2.refs_1_.refs_3_, bf16[2,256,512]{2,1,0:T(8,128)(2,1)} %collective-permute-done.3.refs_2_.refs_4_, ...), custom_call_target="tpu_custom_call" | custom-call | flops 402653184 | bytes 851968 | tf_op jit(solution)/shard_map/product_nt/pallas_call | solution.py:78
  159.0 15.0 %attend.2 = (bf16[1024,256]{1,0:T(8,128)(2,1)}, f32[8,1024]{1,0:T(8,128)}) custom-call(s32[1]{0:T(128)} %dynamic_slice.51.length_ref, f32[8,32]{1,0:T(8,128)} %constant_dynamic-slice_fusion.4.table_ref, f32[8,384,128]{2,1,0:T(8,128)} %near_bias.1.near_ref, bf16[1024,1536]{1,0:T(8,128)(2,1)} %product_nt.2.q_ref.k_ref.v_ref, ...), custom_call_target="tpu_custom_call" | custom-call | flops 268435456 | bytes 131072 | tf_op jit(solution)/shard_map/attend/pallas_call | solution.py:497
  176.8 15.0 %attend.3 = (bf16[1024,256]{1,0:T(8,128)(2,1)}, f32[8,1024]{1,0:T(8,128)}) custom-call(s32[1]{0:T(128)} %dynamic_slice.51.length_ref, f32[8,32]{1,0:T(8,128)} %constant_dynamic-slice_fusion.4.table_ref, f32[8,384,128]{2,1,0:T(8,128)} %near_bias.1.near_ref, bf16[1024,1536]{1,0:T(8,128)(2,1)} %product_nt.2.q_ref.k_ref.v_ref, ...), custom_call_target="tpu_custom_call" | custom-call | flops 268435456 | bytes 131072 | tf_op jit(solution)/shard_map/attend/pallas_call | solution.py:497
  200.3 22.3 %collective-permute-done.15 = bf16[2,2,256,512]{3,2,1,0:T(8,128)(2,1)S(1)} collective-permute-done((bf16[2,2,256,512]{3,2,1,0:T(8,128)(2,1)}, bf16[2,2,256,512]{3,2,1,0:T(8,128)(2,1)S(1)}, u32[]{:S(2)}, u32[]{:S(2)}) %collective-permute-start.15) | collective-permute-done | bytes 1048608 | tf_op jit(solution)/shard_map/ppermute | solution.py:602
  226.3 8.9 %collective-permute-done.16 = bf16[2,256,512]{2,1,0:T(8,128)(2,1)S(1)} collective-permute-done((bf16[2,256,512]{2,1,0:T(8,128)(2,1)S(1)}, bf16[2,256,512]{2,1,0:T(8,128)(2,1)S(1)}, u32[]{:S(2)}, u32[]{:S(2)}) %collective-permute-start.16) | collective-permute-done | bytes 524320 | tf_op jit(solution)/shard_map/ppermute | solution.py:602
  243.0 10.8 %collective-permute-done.20.refs_2_.refs_3_ = bf16[2,256,512]{2,1,0:T(8,128)(2,1)S(1)} collective-permute-done((bf16[2,256,512]{2,1,0:T(8,128)(2,1)S(1)}, bf16[2,256,512]{2,1,0:T(8,128)(2,1)S(1)}, u32[]{:S(2)}, u32[]{:S(2)}) %collective-permute-start.20) | collective-permute-done | bytes 524320 | tf_op jit(solution)/shard_map/ppermute | solution.py:602
  255.9 9.7 %collective-permute-done.19.refs_1_.refs_2_ = bf16[2,256,512]{2,1,0:T(8,128)(2,1)S(1)} collective-permute-done((bf16[2,256,512]{2,1,0:T(8,128)(2,1)S(1)}, bf16[2,256,512]{2,1,0:T(8,128)(2,1)S(1)}, u32[]{:S(2)}, u32[]{:S(2)}) %collective-permute-start.19) | collective-permute-done | bytes 524320 | tf_op jit(solution)/shard_map/ppermute | solution.py:602
  272.5 17.6 %ffn_in.1 = (bf16[1024,1280]{1,0:T(8,128)(2,1)}, bf16[1024,1280]{1,0:T(8,128)(2,1)}, bf16[1024,1280]{1,0:T(8,128)(2,1)}) custom-call(s32[4]{0:T(128)} %add_multiply_fusion.starts_ref, bf16[2,256,512]{2,1,0:T(8,128)(2,1)} %copy-done.8, bf16[2,256,512]{2,1,0:T(8,128)(2,1)} %copy-done.18, bf16[2,256,512]{2,1,0:T(8,128)(2,1)} %copy-done.16, ...), custom_call_target="tpu_custom_call" | custom-call | flops 671088640 | bytes 1409024 | tf_op jit(solution)/shard_map/ffn_in/pallas_call | solution.py:214
  290.1 10.0 %product_tn.4 = bf16[4,1280,512]{2,1,0:T(8,128)(2,1)} custom-call(s32[4]{0:T(128)} %add_multiply_fusion.starts_ref, bf16[1024,1280]{1,0:T(8,128)(2,1)} %get-tuple-element.102.refs_0_, bf16[2,256,512]{2,1,0:T(8,128)(2,1)} %copy-done.6, bf16[2,256,512]{2,1,0:T(8,128)(2,1)} %collective-permute-done.9.refs_2_.refs_1_, bf16[2,256,512]{2,1,0:T(8,128)(2,1)} %copy-done.14, ...), custom_call_target="tpu_custom_call" | custom-call | flops 335544320 | bytes 753664 | tf_op jit(solution)/shard_map/product_tn/pallas_call | solution.py:171
  300.2 15.2 %ffn_back.1.refs_0_ = bf16[1024,2560]{1,0:T(8,128)(2,1)} custom-call(s32[4]{0:T(128)} %add_multiply_fusion.starts_ref, bf16[2,256,512]{2,1,0:T(8,128)(2,1)} %copy-done.6, bf16[2,256,512]{2,1,0:T(8,128)(2,1)} %collective-permute-done.9.refs_2_.refs_1_, bf16[2,256,512]{2,1,0:T(8,128)(2,1)} %copy-done.14, ...), custom_call_target="tpu_custom_call" | custom-call | flops 335544320 | bytes 1245184 | tf_op jit(solution)/shard_map/ffn_back/pallas_call | solution.py:245
  315.3 16.5 %product_nn.5 = (bf16[2,2,256,512]{3,2,1,0:T(8,128)(2,1)}, bf16[2,2,256,512]{3,2,1,0:T(8,128)(2,1)}, bf16[2,2,256,512]{3,2,1,0:T(8,128)(2,1)}, bf16[2,2,256,512]{3,2,1,0:T(8,128)(2,1)}) custom-call(s32[4]{0:T(128)} %add_multiply_fusion.starts_ref, bf16[1024,2560]{1,0:T(8,128)(2,1)} %ffn_back.1.refs_0_, bf16[4,2,1280,512]{3,2,1,0:T(8,128)(2,1)} %bitcast.101), custom_call_target="tpu_custom_call" | custom-call | flops 671088640 | bytes 1245184 | tf_op jit(solution)/shard_map/product_nn/pallas_call | solution.py:123
  335.2 15.9 %product_tn.5 = bf16[4,2560,512]{2,1,0:T(8,128)(2,1)} custom-call(s32[4]{0:T(128)} %add_multiply_fusion.starts_ref, bf16[1024,2560]{1,0:T(8,128)(2,1)} %ffn_back.1.refs_0_, bf16[2,256,512]{2,1,0:T(8,128)(2,1)} %copy-done.8, bf16[2,256,512]{2,1,0:T(8,128)(2,1)} %copy-done.18, bf16[2,256,512]{2,1,0:T(8,128)(2,1)} %copy-done.16, ...), custom_call_target="tpu_custom_call" | custom-call | flops 671088640 | bytes 1245184 | tf_op jit(solution)/shard_map/product_tn/pallas_call | solution.py:171
  366.0 10.2 %product_nn.6 = (bf16[2,2,256,512]{3,2,1,0:T(8,128)(2,1)}, bf16[2,2,256,512]{3,2,1,0:T(8,128)(2,1)}, bf16[2,2,256,512]{3,2,1,0:T(8,128)(2,1)}, bf16[2,2,256,512]{3,2,1,0:T(8,128)(2,1)}) custom-call(s32[4]{0:T(128)} %add_multiply_fusion.starts_ref, bf16[1024,1280]{1,0:T(8,128)(2,1)} %get-tuple-element.102.refs_0_, bf16[4,2,640,512]{3,2,1,0:T(8,128)(2,1)} %bitcast.106), custom_call_target="tpu_custom_call" | custom-call | flops 335544320 | bytes 753664 | tf_op jit(solution)/shard_map/product_nn/pallas_call | solution.py:123
  386.2 10.8 %collective-permute-done.30.refs_2_.refs_4_ = bf16[2,256,512]{2,1,0:T(8,128)(2,1)S(1)} collective-permute-done((bf16[2,256,512]{2,1,0:T(8,128)(2,1)S(1)}, bf16[2,256,512]{2,1,0:T(8,128)(2,1)S(1)}, u32[]{:S(2)}, u32[]{:S(2)}) %collective-permute-start.30) | collective-permute-done | bytes 524320 | tf_op jit(solution)/shard_map/ppermute | solution.py:602
  399.1 10.5 %collective-permute-done.29.refs_1_.refs_3_ = bf16[2,256,512]{2,1,0:T(8,128)(2,1)S(1)} collective-permute-done((bf16[2,256,512]{2,1,0:T(8,128)(2,1)S(1)}, bf16[2,256,512]{2,1,0:T(8,128)(2,1)S(1)}, u32[]{:S(2)}, u32[]{:S(2)}) %collective-permute-start.29) | collective-permute-done | bytes 524320 | tf_op jit(solution)/shard_map/ppermute | solution.py:602
  432.0 24.8 %attend_back.2 = (bf16[1024,768]{1,0:T(8,128)(2,1)}, f32[4,400,128]{2,1,0:T(8,128)}) custom-call(s32[1]{0:T(128)} %dynamic_slice.51.length_ref, f32[8,32]{1,0:T(8,128)} %constant_dynamic-slice_fusion.4.table_ref, f32[8,384,128]{2,1,0:T(8,128)} %near_bias.1.near_ref, bf16[1024,1536]{1,0:T(8,128)(2,1)} %product_nt.2.q_ref.k_ref.v_ref, ...), custom_call_target="tpu_custom_call" | custom-call | flops 671088640 | bytes 262144 | tf_op jit(solution)/shard_map/attend_back/pallas_call | solution.py:524
  473.8 7.2 %all-to-all-start.2 = ((bf16[4,256,512]{2,1,0:T(8,128)(2,1)}), bf16[4,256,512]{2,1,0:T(8,128)(2,1)S(1)}, u32[]{:S(2)}, u32[]{:S(2)}) async-start(bf16[4,256,512]{2,1,0:T(8,128)(2,1)} %fusion.13), calls=%async_computation.3 | async-start | bytes 2097152 | tf_op jit(solution)/shard_map/all_to_all | solution.py:710
  482.7 24.7 %attend_back.3 = (bf16[1024,768]{1,0:T(8,128)(2,1)}, f32[4,400,128]{2,1,0:T(8,128)}) custom-call(s32[1]{0:T(128)} %dynamic_slice.51.length_ref, f32[8,32]{1,0:T(8,128)} %constant_dynamic-slice_fusion.4.table_ref, f32[8,384,128]{2,1,0:T(8,128)} %near_bias.1.near_ref, bf16[1024,1536]{1,0:T(8,128)(2,1)} %product_nt.2.q_ref.k_ref.v_ref, ...), custom_call_target="tpu_custom_call" | custom-call | flops 671088640 | bytes 262144 | tf_op jit(solution)/shard_map/attend_back/pallas_call | solution.py:524
  507.5 11.4 %product_tn.7 = bf16[4,1536,512]{2,1,0:T(8,128)(2,1)} custom-call(s32[4]{0:T(128)} %add_multiply_fusion.starts_ref, bf16[1024,768]{1,0:T(8,128)(2,1)} %get-tuple-element.113.refs_0_, bf16[1024,768]{1,0:T(8,128)(2,1)} %get-tuple-element.123.refs_1_, bf16[2,256,512]{2,1,0:T(8,128)(2,1)} %copy-done.10, ...), custom_call_target="tpu_custom_call" | custom-call | flops 402653184 | bytes 851968 | tf_op jit(solution)/shard_map/product_tn/pallas_call | solution.py:171
  521.3 11.2 %product_nn.7 = (bf16[2,2,256,512]{3,2,1,0:T(8,128)(2,1)}, bf16[2,2,256,512]{3,2,1,0:T(8,128)(2,1)}, bf16[2,2,256,512]{3,2,1,0:T(8,128)(2,1)}, bf16[2,2,256,512]{3,2,1,0:T(8,128)(2,1)}) custom-call(s32[4]{0:T(128)} %add_multiply_fusion.starts_ref, bf16[1024,768]{1,0:T(8,128)(2,1)} %get-tuple-element.113.refs_0_, ...), custom_call_target="tpu_custom_call" | custom-call | flops 402653184 | bytes 851968 | tf_op jit(solution)/shard_map/product_nn/pallas_call | solution.py:123
  548.9 8.9 %collective-permute-done.41 = bf16[2,2,256,512]{3,2,1,0:T(8,128)(2,1)} collective-permute-done((bf16[2,2,256,512]{3,2,1,0:T(8,128)(2,1)}, bf16[2,2,256,512]{3,2,1,0:T(8,128)(2,1)}, u32[]{:S(2)}, u32[]{:S(2)}) %collective-permute-start.41) | collective-permute-done | bytes 1048608 | tf_op jit(solution)/shard_map/ppermute | solution.py:602
  (333 shorter events, 277.3 us)
Async XLA Ops:
  7.2 134.3 %all-gather.4.cloned.1.call-start = ((), (), s32[]{:S(2)}) async-start(), calls=%async_computation.8 | async-start | bytes 9437184 | tf_op jit(solution)/shard_map/all_gather | solution.py:804
  11.6 260.9 %all-gather.6.cloned.1.call-start = ((), (), s32[]{:S(2)}) async-start(), calls=%async_computation.9 | async-start | bytes 11796480 | tf_op jit(solution)/shard_map/all_gather | solution.py:804
  34.3 60.7 %all-to-all-start = ((bf16[4,264,512]{2,1,0:T(8,128)(2,1)}), bf16[4,264,512]{2,1,0:T(8,128)(2,1)}, u32[]{:S(2)}, u32[]{:S(2)}) async-start(bf16[4,264,512]{2,1,0:T(8,128)(2,1)} %pad_maximum_fusion.3), calls=%async_computation | async-start | bytes 2162688 | tf_op jit(solution)/shard_map/all_to_all | solution.py:705
  39.5 260.7 %all-gather.8.cloned.1.call-start = ((), (), s32[]{:S(2)}) async-start(), calls=%async_computation.10 | async-start | bytes 5898240 | tf_op jit(solution)/shard_map/all_gather | solution.py:804
  43.3 51.6 %collective-permute-start.8 = (bf16[2,256,512]{2,1,0:T(8,128)(2,1)S(1)}, bf16[2,256,512]{2,1,0:T(8,128)(2,1)S(1)}, u32[]{:S(2)}, u32[]{:S(2)}) collective-permute-start(bf16[2,256,512]{2,1,0:T(8,128)(2,1)S(1)} %get-tuple-element.165), channel_id=1, source_target_pairs={{0,16},{16,0},{1,17},{17,1},{2,18},{18,2},{3,19},{19,3},{4,20},{20... | collective-permute-start | bytes 1572872 | tf_op jit(solution)/shard_map/ppermute | solution.py:602
  96.1 44.1 %all-to-all-start.1 = ((bf16[4,256,512]{2,1,0:T(8,128)(2,1)}), bf16[4,256,512]{2,1,0:T(8,128)(2,1)S(1)}, u32[]{:S(2)}, u32[]{:S(2)}) async-start(bf16[4,256,512]{2,1,0:T(8,128)(2,1)} %bitcast.26), calls=%async_computation.1 | async-start | bytes 2097152 | tf_op jit(solution)/shard_map/all_to_all | solution.py:705
  101.8 257.0 %reduce-scatter.5.cloned.1.call-start = ((), (), s32[]{:S(2)}) async-start(), calls=%async_computation.11 | async-start | bytes 5898240 | tf_op jit(solution)/shard_map/reduce_scatter | solution.py:847
  109.6 34.8 %collective-permute-start.2 = (bf16[2,256,512]{2,1,0:T(8,128)(2,1)S(1)}, bf16[2,256,512]{2,1,0:T(8,128)(2,1)}, u32[]{:S(2)}, u32[]{:S(2)}) collective-permute-start(bf16[2,256,512]{2,1,0:T(8,128)(2,1)S(1)} %get-tuple-element.167.refs_0_.refs_2_), channel_id=1, source_target_pairs={{0,16},{16,0},{1,17},{17,1},{2,18},{18,2},{3,19},{19,3},{4,20},{20... | collective-permute-start | bytes 1572872 | tf_op jit(solution)/shard_map/ppermute | solution.py:602
  110.1 35.6 %collective-permute-start.6 = (bf16[2,256,512]{2,1,0:T(8,128)(2,1)S(1)}, bf16[2,256,512]{2,1,0:T(8,128)(2,1)}, u32[]{:S(2)}, u32[]{:S(2)}) collective-permute-start(bf16[2,256,512]{2,1,0:T(8,128)(2,1)S(1)} %get-tuple-element.166.refs_4_.refs_6_), channel_id=1, source_target_pairs={{0,4},{4,0},{1,5},{5,1},{2,6},{6,2},{3,7},{7,3},{8,12},{12,8},{9,1... | collective-permute-start | bytes 1572872 | tf_op jit(solution)/shard_map/ppermute | solution.py:602
  142.8 31.3 %collective-permute-start.13 = (bf16[2,256,512]{2,1,0:T(8,128)(2,1)S(1)}, bf16[2,256,512]{2,1,0:T(8,128)(2,1)S(1)}, u32[]{:S(2)}, u32[]{:S(2)}) collective-permute-start(bf16[2,256,512]{2,1,0:T(8,128)(2,1)S(1)} %get-tuple-element.162.refs_5_.refs_4_), channel_id=1, source_target_pairs={{0,16},{16,0},{1,17},{17,1},{2,18},{18,2},{3,19},{19,3},{4,20},{20... | collective-permute-start | bytes 1572872 | tf_op jit(solution)/shard_map/ppermute | solution.py:602
  144.3 29.7 %collective-permute-start.10 = (bf16[2,256,512]{2,1,0:T(8,128)(2,1)S(1)}, bf16[2,256,512]{2,1,0:T(8,128)(2,1)S(1)}, u32[]{:S(2)}, u32[]{:S(2)}) collective-permute-start(bf16[2,256,512]{2,1,0:T(8,128)(2,1)S(1)} %get-tuple-element.163.refs_1_.refs_0_), channel_id=1, source_target_pairs={{0,4},{4,0},{1,5},{5,1},{2,6},{6,2},{3,7},{7,3},{8,12},{12,8},{9,1... | collective-permute-start | bytes 1572872 | tf_op jit(solution)/shard_map/ppermute | solution.py:602
  145.8 46.1 %collective-permute-start.12 = (bf16[2,256,512]{2,1,0:T(8,128)(2,1)S(1)}, bf16[2,256,512]{2,1,0:T(8,128)(2,1)S(1)}, u32[]{:S(2)}, u32[]{:S(2)}) collective-permute-start(bf16[2,256,512]{2,1,0:T(8,128)(2,1)S(1)} %get-tuple-element.162.refs_5_.refs_4_), channel_id=1, source_target_pairs={{0,4},{4,0},{1,5},{5,1},{2,6},{6,2},{3,7},{7,3},{8,12},{12,8},{9,1... | collective-permute-start | bytes 1572872 | tf_op jit(solution)/shard_map/ppermute | solution.py:602
  146.4 45.6 %collective-permute-start.9 = (bf16[2,256,512]{2,1,0:T(8,128)(2,1)S(1)}, bf16[2,256,512]{2,1,0:T(8,128)(2,1)}, u32[]{:S(2)}, u32[]{:S(2)}) collective-permute-start(bf16[2,256,512]{2,1,0:T(8,128)(2,1)S(1)} %get-tuple-element.163.refs_1_.refs_0_), channel_id=1, source_target_pairs={{0,16},{16,0},{1,17},{17,1},{2,18},{18,2},{3,19},{19,3},{4,20},{20... | collective-permute-start | bytes 1572872 | tf_op jit(solution)/shard_map/ppermute | solution.py:602
  300.1 169.5 %reduce-scatter.7.cloned.1.call-start = ((), (), s32[]{:S(2)}) async-start(), calls=%async_computation.12 | async-start | bytes 11796480 | tf_op jit(solution)/shard_map/reduce_scatter | solution.py:847
  358.8 228.8 %reduce-scatter.11.cloned.1.call-start = ((), (), s32[]{:S(2)}) async-start(), calls=%async_computation.14 | async-start | bytes 2359296 | tf_op jit(solution)/shard_map/reduce_scatter | solution.py:847
  383.5 26.0 %collective-permute-start.29 = (bf16[2,256,512]{2,1,0:T(8,128)(2,1)S(1)}, bf16[2,256,512]{2,1,0:T(8,128)(2,1)S(1)}, u32[]{:S(2)}, u32[]{:S(2)}) collective-permute-start(bf16[2,256,512]{2,1,0:T(8,128)(2,1)S(1)} %get-tuple-element.159.refs_0_.refs_2_), channel_id=1, source_target_pairs={{0,16},{16,0},{1,17},{17,1},{2,18},{18,2},{3,19},{19,3},{4,20},{20... | collective-permute-start | bytes 1572872 | tf_op jit(solution)/shard_map/ppermute | solution.py:602
  416.4 40.4 %collective-permute-start.35 = (bf16[2,2,256,512]{3,2,1,0:T(8,128)(2,1)}, bf16[2,2,256,512]{3,2,1,0:T(8,128)(2,1)}, u32[]{:S(2)}, u32[]{:S(2)}) collective-permute-start(bf16[2,2,256,512]{3,2,1,0:T(8,128)(2,1)} %get-tuple-element.110), channel_id=1, source_target_pairs={{0,4},{4,0},{1,5},{5,1},{2,6},{6,2},{3,7},{7,3},{8,12},{12,8},{9,1... | collective-permute-start | bytes 3145736 | tf_op jit(solution)/shard_map/ppermute | solution.py:602
  417.7 41.3 %collective-permute-start.38 = (bf16[2,2,256,512]{3,2,1,0:T(8,128)(2,1)}, bf16[2,2,256,512]{3,2,1,0:T(8,128)(2,1)}, u32[]{:S(2)}, u32[]{:S(2)}) collective-permute-start(bf16[2,2,256,512]{3,2,1,0:T(8,128)(2,1)} %get-tuple-element.119), channel_id=1, source_target_pairs={{0,16},{16,0},{1,17},{17,1},{2,18},{18,2},{3,19},{19,3},{4,20},{20... | collective-permute-start | bytes 3145736 | tf_op jit(solution)/shard_map/ppermute | solution.py:602
  418.6 38.2 %collective-permute-start.36 = (bf16[640,512]{1,0:T(8,128)(2,1)}, bf16[640,512]{1,0:T(8,128)(2,1)}, u32[]{:S(2)}, u32[]{:S(2)}) collective-permute-start(bf16[640,512]{1,0:T(8,128)(2,1)} %reduce-scatter.5.cloned.1.call-done.refs_0_), channel_id=1, source_target_pairs={{0,16},{16,0},{1,17},{17,1},{2,18},{18,2},{3,19},{19,3},{4,20},{20... | collective-permute-start | bytes 1966088 | tf_op jit(solution)/shard_map/ppermute | solution.py:602
  473.8 45.1 %all-to-all-start.2 = ((bf16[4,256,512]{2,1,0:T(8,128)(2,1)}), bf16[4,256,512]{2,1,0:T(8,128)(2,1)S(1)}, u32[]{:S(2)}, u32[]{:S(2)}) async-start(bf16[4,256,512]{2,1,0:T(8,128)(2,1)} %fusion.13), calls=%async_computation.3 | async-start | bytes 2097152 | tf_op jit(solution)/shard_map/all_to_all | solution.py:710
  481.1 126.2 %reduce-scatter.9.cloned.1.call-start = ((), (), s32[]{:S(2)}) async-start(), calls=%async_computation.13 | async-start | bytes 7077888 | tf_op jit(solution)/shard_map/reduce_scatter | solution.py:847
  481.1 37.9 %collective-permute-start.45 = (bf16[1280,512]{1,0:T(8,128)(2,1)S(1)}, bf16[1280,512]{1,0:T(8,128)(2,1)}, u32[]{:S(2)}, u32[]{:S(2)}) collective-permute-start(bf16[1280,512]{1,0:T(8,128)(2,1)S(1)} %copy-done.27), channel_id=1, source_target_pairs={{0,16},{16,0},{1,17},{17,1},{2,18},{18,2},{3,19},{19,3},{4,20},{20... | collective-permute-start | bytes 3932168 | tf_op jit(solution)/shard_map/ppermute | solution.py:602
  532.5 27.9 %collective-permute-start.48 = (bf16[2,2,256,512]{3,2,1,0:T(8,128)(2,1)}, bf16[2,2,256,512]{3,2,1,0:T(8,128)(2,1)}, u32[]{:S(2)}, u32[]{:S(2)}) collective-permute-start(bf16[2,2,256,512]{3,2,1,0:T(8,128)(2,1)} %get-tuple-element.134), channel_id=1, source_target_pairs={{0,16},{16,0},{1,17},{17,1},{2,18},{18,2},{3,19},{19,3},{4,20},{20... | collective-permute-start | bytes 3145736 | tf_op jit(solution)/shard_map/ppermute | solution.py:602
  582.6 45.6 %all-to-all-start.3 = ((bf16[4,256,512]{2,1,0:T(8,128)(2,1)}), bf16[4,256,512]{2,1,0:T(8,128)(2,1)S(1)}, u32[]{:S(2)}, u32[]{:S(2)}) async-start(bf16[4,256,512]{2,1,0:T(8,128)(2,1)} %fusion.9), calls=%async_computation.5 | async-start | bytes 2097152 | tf_op jit(solution)/shard_map/all_to_all | solution.py:710
  (97 other events, 1333.5 us)
Sparse Core Ops, SparseCore 0:
  11.7 129.7 all-gather.3
  143.7 97.5 all-gather.5
  242.9 54.3 all-gather.7
  300.2 58.5 reduce-scatter.4
  361.5 107.7 reduce-scatter.6
  472.0 53.9 reduce-scatter.10
  528.4 78.7 reduce-scatter.8

commit v14 on v13

--- a/solution.py
+++ b/solution.py
@@ -911,7 +911,7 @@
     outputs, _ = from_groups(outputs)
     qkv_partial = tn(grad_projected, normed, starts)
     gate_up_pieces, gate_up_last = shared(after(gate_up_part, grad_projected[0]))
-    qkv_part = reduce(after(qkv_partial, gate_up_last, outputs[0]))
+    qkv_part = reduce(after(qkv_partial, out_part, gate_up_last, outputs[0]))
     one_parts = nn(grad_projected, w_attn, 0, qkv_count, starts)
     if fits:
         here = jnp.stack([y, c]).astype(jnp.int32)

time: 665 us -> 659 us (level)
  transfers between devices with their start and end apart: 73 -> 73, of which waited for: 31 -> 31; matrix products, arithmetic and copies ran while one was open for 9% -> 9% of each run, Pallas kernels for 38% -> 39%
where the time goes in v14:
time: 659 us; the launch traced here: 653 us
  Pallas kernels  256 us (39%)
  waiting for transfers between devices  225 us (34%)
  starting transfers between devices  90.3 us (14%)
  other arithmetic  47.1 us (7%)
  local copies, waits for them, and re-layouts  19.6 us (3%)
  between operations  15.4 us (2%)
    ppermute x59, waiting for transfers between devices, hop(): return lax.ppermute(value, axis, swap)  146 us
    all_to_all x2, waiting for transfers between devices, to_groups(): return lax.all_to_all(both, 'z', 0, 0, tiled=True)  66.1 us
    ppermute x59, starting transfers between devices, hop(): return lax.ppermute(value, axis, swap)  61.7 us
    pallas_call x2, Pallas kernels, attend_back(): pl.pallas_call(functools.partial(attend_back_kernel, group), grid=(1,), i...  49.5 us
    pallas_call x4, Pallas kernels, mm_nn(): pl.pallas_call(functools.partial(nn_kernel, len(grads)), grid=(nz,), in_s...  44.7 us
    pallas_call x4, Pallas kernels, mm_tn(): pl.pallas_call(functools.partial(tn_kernel, count), grid=(count * steps,)...  43.4 us
    pallas_call x2, Pallas kernels, attend(): pl.pallas_call(functools.partial(attend_kernel, group), grid=(1,), in_spe...  30.1 us
    pallas_call x4, Pallas kernels, place(): pl.pallas_call(functools.partial(place_kernel, write), grid=(4,), in_spec...  19.7 us
  transfers between devices with their start and end apart: 73, of which 31 were waited for; matrix products, arithmetic and copies ran while one was open for 9% of the time, Pallas kernels for 39%

profile of v14, /device:TPU:0, one launch (start us, length us, event | category | flops | bytes accessed | tf_op | source)
XLA Modules:
  0.0 653.3 jit_solution(17524563201375234192)
XLA Ops:
  16.7 12.2 %collective-permute-done.1 = bf16[2,256,512]{2,1,0:T(8,128)(2,1)} collective-permute-done((bf16[2,256,512]{2,1,0:T(8,128)(2,1)}, bf16[2,256,512]{2,1,0:T(8,128)(2,1)}, u32[]{:S(2)}, u32[]{:S(2)}) %collective-permute-start.1) | collective-permute-done | bytes 524320 | tf_op jit(solution)/shard_map/ppermute | solution.py:602
  45.1 49.8 %all-to-all-done = bf16[4,264,512]{2,1,0:T(8,128)(2,1)} async-done(((bf16[4,264,512]{2,1,0:T(8,128)(2,1)}), bf16[4,264,512]{2,1,0:T(8,128)(2,1)}, u32[]{:S(2)}, u32[]{:S(2)}) %all-to-all-start) | async-done | bytes 1081376 | tf_op jit(solution)/shard_map/all_to_all | solution.py:705
  123.9 16.3 %all-to-all-done.1 = bf16[4,256,512]{2,1,0:T(8,128)(2,1)S(1)} async-done(((bf16[4,256,512]{2,1,0:T(8,128)(2,1)}), bf16[4,256,512]{2,1,0:T(8,128)(2,1)S(1)}, u32[]{:S(2)}, u32[]{:S(2)}) %all-to-all-start.1) | async-done | bytes 1048608 | tf_op jit(solution)/shard_map/all_to_all | solution.py:705
  146.9 12.1 %product_nt.2.q_ref.k_ref.v_ref = bf16[1024,1536]{1,0:T(8,128)(2,1)} custom-call(s32[4]{0:T(128)} %add_multiply_fusion.starts_ref, bf16[2,256,512]{2,1,0:T(8,128)(2,1)} %copy-done.10, bf16[2,256,512]{2,1,0:T(8,128)(2,1)} %collective-permute-done.2.refs_1_.refs_3_, bf16[2,256,512]{2,1,0:T(8,128)(2,1)} %collective-permute-done.3.refs_2_.refs_4_, ...), custom_call_target="tpu_custom_call" | custom-call | flops 402653184 | bytes 851968 | tf_op jit(solution)/shard_map/product_nt/pallas_call | solution.py:78
  159.0 15.0 %attend.2 = (bf16[1024,256]{1,0:T(8,128)(2,1)}, f32[8,1024]{1,0:T(8,128)}) custom-call(s32[1]{0:T(128)} %dynamic_slice.51.length_ref, f32[8,32]{1,0:T(8,128)} %constant_dynamic-slice_fusion.4.table_ref, f32[8,384,128]{2,1,0:T(8,128)} %near_bias.1.near_ref, bf16[1024,1536]{1,0:T(8,128)(2,1)} %product_nt.2.q_ref.k_ref.v_ref, ...), custom_call_target="tpu_custom_call" | custom-call | flops 268435456 | bytes 131072 | tf_op jit(solution)/shard_map/attend/pallas_call | solution.py:497
  176.8 15.1 %attend.3 = (bf16[1024,256]{1,0:T(8,128)(2,1)}, f32[8,1024]{1,0:T(8,128)}) custom-call(s32[1]{0:T(128)} %dynamic_slice.51.length_ref, f32[8,32]{1,0:T(8,128)} %constant_dynamic-slice_fusion.4.table_ref, f32[8,384,128]{2,1,0:T(8,128)} %near_bias.1.near_ref, bf16[1024,1536]{1,0:T(8,128)(2,1)} %product_nt.2.q_ref.k_ref.v_ref, ...), custom_call_target="tpu_custom_call" | custom-call | flops 268435456 | bytes 131072 | tf_op jit(solution)/shard_map/attend/pallas_call | solution.py:497
  200.3 22.3 %collective-permute-done.15 = bf16[2,2,256,512]{3,2,1,0:T(8,128)(2,1)S(1)} collective-permute-done((bf16[2,2,256,512]{3,2,1,0:T(8,128)(2,1)}, bf16[2,2,256,512]{3,2,1,0:T(8,128)(2,1)S(1)}, u32[]{:S(2)}, u32[]{:S(2)}) %collective-permute-start.15) | collective-permute-done | bytes 1048608 | tf_op jit(solution)/shard_map/ppermute | solution.py:602
  226.4 8.9 %collective-permute-done.16 = bf16[2,256,512]{2,1,0:T(8,128)(2,1)S(1)} collective-permute-done((bf16[2,256,512]{2,1,0:T(8,128)(2,1)S(1)}, bf16[2,256,512]{2,1,0:T(8,128)(2,1)S(1)}, u32[]{:S(2)}, u32[]{:S(2)}) %collective-permute-start.16) | collective-permute-done | bytes 524320 | tf_op jit(solution)/shard_map/ppermute | solution.py:602
  243.0 10.8 %collective-permute-done.20.refs_2_.refs_3_ = bf16[2,256,512]{2,1,0:T(8,128)(2,1)S(1)} collective-permute-done((bf16[2,256,512]{2,1,0:T(8,128)(2,1)S(1)}, bf16[2,256,512]{2,1,0:T(8,128)(2,1)S(1)}, u32[]{:S(2)}, u32[]{:S(2)}) %collective-permute-start.20) | collective-permute-done | bytes 524320 | tf_op jit(solution)/shard_map/ppermute | solution.py:602
  255.9 9.6 %collective-permute-done.19.refs_1_.refs_2_ = bf16[2,256,512]{2,1,0:T(8,128)(2,1)S(1)} collective-permute-done((bf16[2,256,512]{2,1,0:T(8,128)(2,1)S(1)}, bf16[2,256,512]{2,1,0:T(8,128)(2,1)S(1)}, u32[]{:S(2)}, u32[]{:S(2)}) %collective-permute-start.19) | collective-permute-done | bytes 524320 | tf_op jit(solution)/shard_map/ppermute | solution.py:602
  272.5 17.6 %ffn_in.1 = (bf16[1024,1280]{1,0:T(8,128)(2,1)}, bf16[1024,1280]{1,0:T(8,128)(2,1)}, bf16[1024,1280]{1,0:T(8,128)(2,1)}) custom-call(s32[4]{0:T(128)} %add_multiply_fusion.starts_ref, bf16[2,256,512]{2,1,0:T(8,128)(2,1)} %copy-done.8, bf16[2,256,512]{2,1,0:T(8,128)(2,1)} %copy-done.18, bf16[2,256,512]{2,1,0:T(8,128)(2,1)} %copy-done.16, ...), custom_call_target="tpu_custom_call" | custom-call | flops 671088640 | bytes 1409024 | tf_op jit(solution)/shard_map/ffn_in/pallas_call | solution.py:214
  290.1 9.9 %product_tn.4 = bf16[4,1280,512]{2,1,0:T(8,128)(2,1)} custom-call(s32[4]{0:T(128)} %add_multiply_fusion.starts_ref, bf16[1024,1280]{1,0:T(8,128)(2,1)} %get-tuple-element.102.refs_0_, bf16[2,256,512]{2,1,0:T(8,128)(2,1)} %copy-done.6, bf16[2,256,512]{2,1,0:T(8,128)(2,1)} %collective-permute-done.9.refs_2_.refs_1_, bf16[2,256,512]{2,1,0:T(8,128)(2,1)} %copy-done.14, ...), custom_call_target="tpu_custom_call" | custom-call | flops 335544320 | bytes 753664 | tf_op jit(solution)/shard_map/product_tn/pallas_call | solution.py:171
  300.1 15.2 %ffn_back.1.refs_0_ = bf16[1024,2560]{1,0:T(8,128)(2,1)} custom-call(s32[4]{0:T(128)} %add_multiply_fusion.starts_ref, bf16[2,256,512]{2,1,0:T(8,128)(2,1)} %copy-done.6, bf16[2,256,512]{2,1,0:T(8,128)(2,1)} %collective-permute-done.9.refs_2_.refs_1_, bf16[2,256,512]{2,1,0:T(8,128)(2,1)} %copy-done.14, ...), custom_call_target="tpu_custom_call" | custom-call | flops 335544320 | bytes 1245184 | tf_op jit(solution)/shard_map/ffn_back/pallas_call | solution.py:245
  315.3 16.5 %product_nn.5 = (bf16[2,2,256,512]{3,2,1,0:T(8,128)(2,1)}, bf16[2,2,256,512]{3,2,1,0:T(8,128)(2,1)}, bf16[2,2,256,512]{3,2,1,0:T(8,128)(2,1)}, bf16[2,2,256,512]{3,2,1,0:T(8,128)(2,1)}) custom-call(s32[4]{0:T(128)} %add_multiply_fusion.starts_ref, bf16[1024,2560]{1,0:T(8,128)(2,1)} %ffn_back.1.refs_0_, bf16[4,2,1280,512]{3,2,1,0:T(8,128)(2,1)} %bitcast.101), custom_call_target="tpu_custom_call" | custom-call | flops 671088640 | bytes 1245184 | tf_op jit(solution)/shard_map/product_nn/pallas_call | solution.py:123
  335.2 15.9 %product_tn.5 = bf16[4,2560,512]{2,1,0:T(8,128)(2,1)} custom-call(s32[4]{0:T(128)} %add_multiply_fusion.starts_ref, bf16[1024,2560]{1,0:T(8,128)(2,1)} %ffn_back.1.refs_0_, bf16[2,256,512]{2,1,0:T(8,128)(2,1)} %copy-done.8, bf16[2,256,512]{2,1,0:T(8,128)(2,1)} %copy-done.18, bf16[2,256,512]{2,1,0:T(8,128)(2,1)} %copy-done.16, ...), custom_call_target="tpu_custom_call" | custom-call | flops 671088640 | bytes 1245184 | tf_op jit(solution)/shard_map/product_tn/pallas_call | solution.py:171
  366.0 10.2 %product_nn.6 = (bf16[2,2,256,512]{3,2,1,0:T(8,128)(2,1)}, bf16[2,2,256,512]{3,2,1,0:T(8,128)(2,1)}, bf16[2,2,256,512]{3,2,1,0:T(8,128)(2,1)}, bf16[2,2,256,512]{3,2,1,0:T(8,128)(2,1)}) custom-call(s32[4]{0:T(128)} %add_multiply_fusion.starts_ref, bf16[1024,1280]{1,0:T(8,128)(2,1)} %get-tuple-element.102.refs_0_, bf16[4,2,640,512]{3,2,1,0:T(8,128)(2,1)} %bitcast.106), custom_call_target="tpu_custom_call" | custom-call | flops 335544320 | bytes 753664 | tf_op jit(solution)/shard_map/product_nn/pallas_call | solution.py:123
  386.2 10.8 %collective-permute-done.30.refs_2_.refs_4_ = bf16[2,256,512]{2,1,0:T(8,128)(2,1)S(1)} collective-permute-done((bf16[2,256,512]{2,1,0:T(8,128)(2,1)S(1)}, bf16[2,256,512]{2,1,0:T(8,128)(2,1)S(1)}, u32[]{:S(2)}, u32[]{:S(2)}) %collective-permute-start.30) | collective-permute-done | bytes 524320 | tf_op jit(solution)/shard_map/ppermute | solution.py:602
  399.1 10.5 %collective-permute-done.29.refs_1_.refs_3_ = bf16[2,256,512]{2,1,0:T(8,128)(2,1)S(1)} collective-permute-done((bf16[2,256,512]{2,1,0:T(8,128)(2,1)S(1)}, bf16[2,256,512]{2,1,0:T(8,128)(2,1)S(1)}, u32[]{:S(2)}, u32[]{:S(2)}) %collective-permute-start.29) | collective-permute-done | bytes 524320 | tf_op jit(solution)/shard_map/ppermute | solution.py:602
  432.0 24.8 %attend_back.2 = (bf16[1024,768]{1,0:T(8,128)(2,1)}, f32[4,400,128]{2,1,0:T(8,128)}) custom-call(s32[1]{0:T(128)} %dynamic_slice.51.length_ref, f32[8,32]{1,0:T(8,128)} %constant_dynamic-slice_fusion.4.table_ref, f32[8,384,128]{2,1,0:T(8,128)} %near_bias.1.near_ref, bf16[1024,1536]{1,0:T(8,128)(2,1)} %product_nt.2.q_ref.k_ref.v_ref, ...), custom_call_target="tpu_custom_call" | custom-call | flops 671088640 | bytes 262144 | tf_op jit(solution)/shard_map/attend_back/pallas_call | solution.py:524
  473.8 7.2 %all-to-all-start.2 = ((bf16[4,256,512]{2,1,0:T(8,128)(2,1)}), bf16[4,256,512]{2,1,0:T(8,128)(2,1)S(1)}, u32[]{:S(2)}, u32[]{:S(2)}) async-start(bf16[4,256,512]{2,1,0:T(8,128)(2,1)} %fusion.13), calls=%async_computation.3 | async-start | bytes 2097152 | tf_op jit(solution)/shard_map/all_to_all | solution.py:710
  482.7 24.7 %attend_back.3 = (bf16[1024,768]{1,0:T(8,128)(2,1)}, f32[4,400,128]{2,1,0:T(8,128)}) custom-call(s32[1]{0:T(128)} %dynamic_slice.51.length_ref, f32[8,32]{1,0:T(8,128)} %constant_dynamic-slice_fusion.4.table_ref, f32[8,384,128]{2,1,0:T(8,128)} %near_bias.1.near_ref, bf16[1024,1536]{1,0:T(8,128)(2,1)} %product_nt.2.q_ref.k_ref.v_ref, ...), custom_call_target="tpu_custom_call" | custom-call | flops 671088640 | bytes 262144 | tf_op jit(solution)/shard_map/attend_back/pallas_call | solution.py:524
  507.4 11.4 %product_tn.7 = bf16[4,1536,512]{2,1,0:T(8,128)(2,1)} custom-call(s32[4]{0:T(128)} %add_multiply_fusion.starts_ref, bf16[1024,768]{1,0:T(8,128)(2,1)} %get-tuple-element.113.refs_0_, bf16[1024,768]{1,0:T(8,128)(2,1)} %get-tuple-element.123.refs_1_, bf16[2,256,512]{2,1,0:T(8,128)(2,1)} %copy-done.10, ...), custom_call_target="tpu_custom_call" | custom-call | flops 402653184 | bytes 851968 | tf_op jit(solution)/shard_map/product_tn/pallas_call | solution.py:171
  527.9 11.1 %product_nn.7 = (bf16[2,2,256,512]{3,2,1,0:T(8,128)(2,1)}, bf16[2,2,256,512]{3,2,1,0:T(8,128)(2,1)}, bf16[2,2,256,512]{3,2,1,0:T(8,128)(2,1)}, bf16[2,2,256,512]{3,2,1,0:T(8,128)(2,1)}) custom-call(s32[4]{0:T(128)} %add_multiply_fusion.starts_ref, bf16[1024,768]{1,0:T(8,128)(2,1)} %get-tuple-element.113.refs_0_, ...), custom_call_target="tpu_custom_call" | custom-call | flops 402653184 | bytes 851968 | tf_op jit(solution)/shard_map/product_nn/pallas_call | solution.py:123
  555.9 8.3 %collective-permute-done.41 = bf16[2,2,256,512]{3,2,1,0:T(8,128)(2,1)} collective-permute-done((bf16[2,2,256,512]{3,2,1,0:T(8,128)(2,1)}, bf16[2,2,256,512]{3,2,1,0:T(8,128)(2,1)}, u32[]{:S(2)}, u32[]{:S(2)}) %collective-permute-start.41) | collective-permute-done | bytes 1048608 | tf_op jit(solution)/shard_map/ppermute | solution.py:602
  (335 shorter events, 271.6 us)
Async XLA Ops:
  7.2 134.3 %all-gather.4.cloned.1.call-start = ((), (), s32[]{:S(2)}) async-start(), calls=%async_computation.8 | async-start | bytes 9437184 | tf_op jit(solution)/shard_map/all_gather | solution.py:804
  11.6 261.0 %all-gather.6.cloned.1.call-start = ((), (), s32[]{:S(2)}) async-start(), calls=%async_computation.9 | async-start | bytes 11796480 | tf_op jit(solution)/shard_map/all_gather | solution.py:804
  34.3 60.7 %all-to-all-start = ((bf16[4,264,512]{2,1,0:T(8,128)(2,1)}), bf16[4,264,512]{2,1,0:T(8,128)(2,1)}, u32[]{:S(2)}, u32[]{:S(2)}) async-start(bf16[4,264,512]{2,1,0:T(8,128)(2,1)} %pad_maximum_fusion.3), calls=%async_computation | async-start | bytes 2162688 | tf_op jit(solution)/shard_map/all_to_all | solution.py:705
  39.5 260.7 %all-gather.8.cloned.1.call-start = ((), (), s32[]{:S(2)}) async-start(), calls=%async_computation.10 | async-start | bytes 5898240 | tf_op jit(solution)/shard_map/all_gather | solution.py:804
  43.3 51.6 %collective-permute-start.8 = (bf16[2,256,512]{2,1,0:T(8,128)(2,1)S(1)}, bf16[2,256,512]{2,1,0:T(8,128)(2,1)S(1)}, u32[]{:S(2)}, u32[]{:S(2)}) collective-permute-start(bf16[2,256,512]{2,1,0:T(8,128)(2,1)S(1)} %get-tuple-element.165), channel_id=1, source_target_pairs={{0,16},{16,0},{1,17},{17,1},{2,18},{18,2},{3,19},{19,3},{4,20},{20... | collective-permute-start | bytes 1572872 | tf_op jit(solution)/shard_map/ppermute | solution.py:602
  96.1 44.1 %all-to-all-start.1 = ((bf16[4,256,512]{2,1,0:T(8,128)(2,1)}), bf16[4,256,512]{2,1,0:T(8,128)(2,1)S(1)}, u32[]{:S(2)}, u32[]{:S(2)}) async-start(bf16[4,256,512]{2,1,0:T(8,128)(2,1)} %bitcast.26), calls=%async_computation.1 | async-start | bytes 2097152 | tf_op jit(solution)/shard_map/all_to_all | solution.py:705
  101.8 257.0 %reduce-scatter.5.cloned.1.call-start = ((), (), s32[]{:S(2)}) async-start(), calls=%async_computation.11 | async-start | bytes 5898240 | tf_op jit(solution)/shard_map/reduce_scatter | solution.py:847
  109.6 34.8 %collective-permute-start.2 = (bf16[2,256,512]{2,1,0:T(8,128)(2,1)S(1)}, bf16[2,256,512]{2,1,0:T(8,128)(2,1)}, u32[]{:S(2)}, u32[]{:S(2)}) collective-permute-start(bf16[2,256,512]{2,1,0:T(8,128)(2,1)S(1)} %get-tuple-element.167.refs_0_.refs_2_), channel_id=1, source_target_pairs={{0,16},{16,0},{1,17},{17,1},{2,18},{18,2},{3,19},{19,3},{4,20},{20... | collective-permute-start | bytes 1572872 | tf_op jit(solution)/shard_map/ppermute | solution.py:602
  110.1 35.6 %collective-permute-start.6 = (bf16[2,256,512]{2,1,0:T(8,128)(2,1)S(1)}, bf16[2,256,512]{2,1,0:T(8,128)(2,1)}, u32[]{:S(2)}, u32[]{:S(2)}) collective-permute-start(bf16[2,256,512]{2,1,0:T(8,128)(2,1)S(1)} %get-tuple-element.166.refs_4_.refs_6_), channel_id=1, source_target_pairs={{0,4},{4,0},{1,5},{5,1},{2,6},{6,2},{3,7},{7,3},{8,12},{12,8},{9,1... | collective-permute-start | bytes 1572872 | tf_op jit(solution)/shard_map/ppermute | solution.py:602
  142.8 31.3 %collective-permute-start.13 = (bf16[2,256,512]{2,1,0:T(8,128)(2,1)S(1)}, bf16[2,256,512]{2,1,0:T(8,128)(2,1)S(1)}, u32[]{:S(2)}, u32[]{:S(2)}) collective-permute-start(bf16[2,256,512]{2,1,0:T(8,128)(2,1)S(1)} %get-tuple-element.162.refs_5_.refs_4_), channel_id=1, source_target_pairs={{0,16},{16,0},{1,17},{17,1},{2,18},{18,2},{3,19},{19,3},{4,20},{20... | collective-permute-start | bytes 1572872 | tf_op jit(solution)/shard_map/ppermute | solution.py:602
  144.3 29.7 %collective-permute-start.10 = (bf16[2,256,512]{2,1,0:T(8,128)(2,1)S(1)}, bf16[2,256,512]{2,1,0:T(8,128)(2,1)S(1)}, u32[]{:S(2)}, u32[]{:S(2)}) collective-permute-start(bf16[2,256,512]{2,1,0:T(8,128)(2,1)S(1)} %get-tuple-element.163.refs_1_.refs_0_), channel_id=1, source_target_pairs={{0,4},{4,0},{1,5},{5,1},{2,6},{6,2},{3,7},{7,3},{8,12},{12,8},{9,1... | collective-permute-start | bytes 1572872 | tf_op jit(solution)/shard_map/ppermute | solution.py:602
  145.8 46.1 %collective-permute-start.12 = (bf16[2,256,512]{2,1,0:T(8,128)(2,1)S(1)}, bf16[2,256,512]{2,1,0:T(8,128)(2,1)S(1)}, u32[]{:S(2)}, u32[]{:S(2)}) collective-permute-start(bf16[2,256,512]{2,1,0:T(8,128)(2,1)S(1)} %get-tuple-element.162.refs_5_.refs_4_), channel_id=1, source_target_pairs={{0,4},{4,0},{1,5},{5,1},{2,6},{6,2},{3,7},{7,3},{8,12},{12,8},{9,1... | collective-permute-start | bytes 1572872 | tf_op jit(solution)/shard_map/ppermute | solution.py:602
  146.4 45.6 %collective-permute-start.9 = (bf16[2,256,512]{2,1,0:T(8,128)(2,1)S(1)}, bf16[2,256,512]{2,1,0:T(8,128)(2,1)}, u32[]{:S(2)}, u32[]{:S(2)}) collective-permute-start(bf16[2,256,512]{2,1,0:T(8,128)(2,1)S(1)} %get-tuple-element.163.refs_1_.refs_0_), channel_id=1, source_target_pairs={{0,16},{16,0},{1,17},{17,1},{2,18},{18,2},{3,19},{19,3},{4,20},{20... | collective-permute-start | bytes 1572872 | tf_op jit(solution)/shard_map/ppermute | solution.py:602
  300.1 169.5 %reduce-scatter.7.cloned.1.call-start = ((), (), s32[]{:S(2)}) async-start(), calls=%async_computation.12 | async-start | bytes 11796480 | tf_op jit(solution)/shard_map/reduce_scatter | solution.py:847
  358.8 165.2 %reduce-scatter.9.cloned.1.call-start = ((), (), s32[]{:S(2)}) async-start(), calls=%async_computation.13 | async-start | bytes 2359296 | tf_op jit(solution)/shard_map/reduce_scatter | solution.py:847
  383.5 26.0 %collective-permute-start.29 = (bf16[2,256,512]{2,1,0:T(8,128)(2,1)S(1)}, bf16[2,256,512]{2,1,0:T(8,128)(2,1)S(1)}, u32[]{:S(2)}, u32[]{:S(2)}) collective-permute-start(bf16[2,256,512]{2,1,0:T(8,128)(2,1)S(1)} %get-tuple-element.159.refs_0_.refs_2_), channel_id=1, source_target_pairs={{0,16},{16,0},{1,17},{17,1},{2,18},{18,2},{3,19},{19,3},{4,20},{20... | collective-permute-start | bytes 1572872 | tf_op jit(solution)/shard_map/ppermute | solution.py:602
  416.4 40.4 %collective-permute-start.35 = (bf16[2,2,256,512]{3,2,1,0:T(8,128)(2,1)}, bf16[2,2,256,512]{3,2,1,0:T(8,128)(2,1)}, u32[]{:S(2)}, u32[]{:S(2)}) collective-permute-start(bf16[2,2,256,512]{3,2,1,0:T(8,128)(2,1)} %get-tuple-element.110), channel_id=1, source_target_pairs={{0,4},{4,0},{1,5},{5,1},{2,6},{6,2},{3,7},{7,3},{8,12},{12,8},{9,1... | collective-permute-start | bytes 3145736 | tf_op jit(solution)/shard_map/ppermute | solution.py:602
  417.7 41.3 %collective-permute-start.38 = (bf16[2,2,256,512]{3,2,1,0:T(8,128)(2,1)}, bf16[2,2,256,512]{3,2,1,0:T(8,128)(2,1)}, u32[]{:S(2)}, u32[]{:S(2)}) collective-permute-start(bf16[2,2,256,512]{3,2,1,0:T(8,128)(2,1)} %get-tuple-element.119), channel_id=1, source_target_pairs={{0,16},{16,0},{1,17},{17,1},{2,18},{18,2},{3,19},{19,3},{4,20},{20... | collective-permute-start | bytes 3145736 | tf_op jit(solution)/shard_map/ppermute | solution.py:602
  418.6 38.2 %collective-permute-start.36 = (bf16[640,512]{1,0:T(8,128)(2,1)}, bf16[640,512]{1,0:T(8,128)(2,1)}, u32[]{:S(2)}, u32[]{:S(2)}) collective-permute-start(bf16[640,512]{1,0:T(8,128)(2,1)} %reduce-scatter.5.cloned.1.call-done.refs_0_), channel_id=1, source_target_pairs={{0,16},{16,0},{1,17},{17,1},{2,18},{18,2},{3,19},{19,3},{4,20},{20... | collective-permute-start | bytes 1966088 | tf_op jit(solution)/shard_map/ppermute | solution.py:602
  473.8 45.0 %all-to-all-start.2 = ((bf16[4,256,512]{2,1,0:T(8,128)(2,1)}), bf16[4,256,512]{2,1,0:T(8,128)(2,1)S(1)}, u32[]{:S(2)}, u32[]{:S(2)}) async-start(bf16[4,256,512]{2,1,0:T(8,128)(2,1)} %fusion.13), calls=%async_computation.3 | async-start | bytes 2097152 | tf_op jit(solution)/shard_map/all_to_all | solution.py:710
  481.1 127.1 %reduce-scatter.11.cloned.1.call-start = ((), (), s32[]{:S(2)}) async-start(), calls=%async_computation.14 | async-start | bytes 7077888 | tf_op jit(solution)/shard_map/reduce_scatter | solution.py:847
  481.1 37.8 %collective-permute-start.45 = (bf16[1280,512]{1,0:T(8,128)(2,1)S(1)}, bf16[1280,512]{1,0:T(8,128)(2,1)}, u32[]{:S(2)}, u32[]{:S(2)}) collective-permute-start(bf16[1280,512]{1,0:T(8,128)(2,1)S(1)} %copy-done.27), channel_id=1, source_target_pairs={{0,16},{16,0},{1,17},{17,1},{2,18},{18,2},{3,19},{19,3},{4,20},{20... | collective-permute-start | bytes 3932168 | tf_op jit(solution)/shard_map/ppermute | solution.py:602
  540.7 26.3 %collective-permute-start.48 = (bf16[2,2,256,512]{3,2,1,0:T(8,128)(2,1)}, bf16[2,2,256,512]{3,2,1,0:T(8,128)(2,1)}, u32[]{:S(2)}, u32[]{:S(2)}) collective-permute-start(bf16[2,2,256,512]{3,2,1,0:T(8,128)(2,1)} %get-tuple-element.134), channel_id=1, source_target_pairs={{0,16},{16,0},{1,17},{17,1},{2,18},{18,2},{3,19},{19,3},{4,20},{20... | collective-permute-start | bytes 3145736 | tf_op jit(solution)/shard_map/ppermute | solution.py:602
  589.1 34.3 %all-to-all-start.3 = ((bf16[4,256,512]{2,1,0:T(8,128)(2,1)}), bf16[4,256,512]{2,1,0:T(8,128)(2,1)S(1)}, u32[]{:S(2)}, u32[]{:S(2)}) async-start(bf16[4,256,512]{2,1,0:T(8,128)(2,1)} %fusion.9), calls=%async_computation.5 | async-start | bytes 2097152 | tf_op jit(solution)/shard_map/all_to_all | solution.py:710
  (98 other events, 1320.5 us)
Sparse Core Ops, SparseCore 0:
  11.7 129.7 all-gather.3
  143.7 97.5 all-gather.5
  242.9 54.3 all-gather.7
  300.2 58.5 reduce-scatter.4
  361.5 107.7 reduce-scatter.6
  472.0 51.9 reduce-scatter.8
  526.3 71.6 reduce-scatter.10
